TPU v7x, 512 devices: a whole 4x4x16 slice. The times are simulated.
512 devices in a mesh: gx: 16 (over z_lo, core), gy: 4 (over y), gz: 8 (over z_hi, x).
Axes of the slice: x: 4, y: 4, z: 16 (z_hi: 2, z_lo: 8; z = z_hi * 8 + z_lo), core: 2. Of those that a mesh axis runs over, the one named last changes fastest.
Arguments:
- positions: float32 [3, 16, 4, 8, 512], P(None, 'gx', 'gy', 'gz'), may hold values from 0 to 6
- species: int32 [16, 4, 8, 512], P('gx', 'gy', 'gz'), may hold values from 0 to 5
- send_lists: int32 [32, 8, 16, 8], P('gx', 'gy', 'gz'), may hold values from 0 to 511
- pair_center: int32 [16, 4, 8, 8, 128], P('gx', 'gy', 'gz'), may hold values from 0 to 511
- pair_partner: int32 [16, 4, 8, 8, 128], P('gx', 'gy', 'gz'), may hold values from 0 to 959, as said below
- pair_slot_live: int32 [16, 4, 8, 8, 128], P('gx', 'gy', 'gz'), may hold values from 0 to 1, as said below
- w_basis: float32 [8, 128], replicated, may hold values from -2 to 2
- emb_center: float32 [6, 128], replicated, may hold values from -6 to 6
- emb_partner: float32 [6, 128], replicated, may hold values from -6 to 6
- w_env: float32 [128, 64], replicated, may hold values from -0.5 to 0.5
- w_value: float32 [128, 64], replicated, may hold values from -0.5 to 0.5
- w_mix: float32 [192, 128], replicated, may hold values from -0.4375 to 0.4375
- w_out: float32 [128], replicated, may hold values from -0.5 to 0.5
Outputs:
- forces: float32 [3, 16, 4, 8, 512], P(None, 'gx', 'gy', 'gz')
- atom_energy: float32 [16, 4, 8, 512], P('gx', 'gy', 'gz')
Inputs may be any that keep to these rules, and one draw needn't show every extreme that they name: `pair_partner`: never the pair's centre. `pair_slot_live`: in every domain the first 8, 4, 2 or 1 blocks hold pairs and the later blocks none; a block that holds pairs has them in its first 64 to 128 slots. Some domain has all 8 blocks holding pairs, one of them full.
All inputs are finite; a program needn't handle non-finite values.
Results may differ from a plain program's by a relative error of at most 0.0003.
Values sent between devices are 32-bit elements; how exact they have to be, the bound alone decides.
No kernel may reach another device: no remote copies, remote signals or barrier semaphores. Data moves between devices by JAX's collectives and lax.ppermute only.
A program may use at most 64 MiB of HBM per device.

v0:
```python
import math

import jax
import jax.numpy as jnp
import numpy as np
from jax import lax
from jax.experimental import pallas as pl
from jax.experimental.pallas import tpu as pltpu
from jax.sharding import PartitionSpec as P

AXES = ("gx", "gy", "gz")
SHAPE = (16, 4, 8)
ATOMS = 512
PAIRS = 1024
LIST = 64
CHAN = 64
STEP = math.pi / 12.0
F32 = jnp.float32
BF16 = jnp.bfloat16


def flat(x, y, z):
    return (x * SHAPE[1] + y) * SHAPE[2] + z


def home(x, y, z):
    x, y, z = x % SHAPE[0], y % SHAPE[1], z % SHAPE[2]
    chip_z, chip_x, core = x, z // 2, z % 2
    return flat((chip_z % 8) * 2 + core, y, (chip_z // 8) * 4 + chip_x)


CELLS = [(x, y, z) for x in range(SHAPE[0]) for y in range(SHAPE[1]) for z in range(SHAPE[2])]
MOVE_IN = [(flat(*c), home(*c)) for c in CELLS]
MOVE_OUT = [(b, a) for a, b in MOVE_IN]


def shifted(axis, by):
    step = [0, 0, 0]
    step[axis] = by
    return [(home(x, y, z), home(x + step[0], y + step[1], z + step[2])) for x, y, z in CELLS]


def spread(cells):
    for axis in (2, 1, 0):
        last = lax.slice_in_dim(cells, 1, 2, axis=axis)
        first = lax.slice_in_dim(cells, 0, 1, axis=axis)
        before = lax.ppermute(last, AXES, shifted(axis, 1))
        after = lax.ppermute(first, AXES, shifted(axis, -1))
        cells = jnp.concatenate([before, cells, after], axis=axis)
    return cells


def collect(cells):
    for axis in (0, 1, 2):
        to_down = lax.slice_in_dim(cells, 0, 1, axis=axis)
        to_up = lax.slice_in_dim(cells, 3, 4, axis=axis)
        from_down = lax.ppermute(to_up, AXES, shifted(axis, 1))
        from_up = lax.ppermute(to_down, AXES, shifted(axis, -1))
        cells = lax.slice_in_dim(cells, 1, 3, axis=axis) + jnp.concatenate([from_down, from_up], axis=axis)
    return cells


def split2(x):
    high = x.astype(BF16)
    low = (x - high.astype(F32)).astype(BF16)
    return high, low


def split3(x):
    high = x.astype(BF16)
    rest = x - high.astype(F32)
    mid = rest.astype(BF16)
    return high, mid, (rest - mid.astype(F32)).astype(BF16)


def dot(a, b, ca, cb):
    return lax.dot_general(a, b, (((ca,), (cb,)), ((), ())), preferred_element_type=F32)


def weighted(w, x):
    wh, wl = split2(w)
    xh, xl = split2(x)
    return dot(wh, xh, 0, 0) + (dot(wl, xh, 0, 0) + dot(wh, xl, 0, 0))


def weighted_t(w, x):
    wh, wl = split2(w)
    xh, xl = split2(x)
    return dot(wh, xh, 1, 0) + (dot(wl, xh, 1, 0) + dot(wh, xl, 1, 0))


def pick(table, onehot, parts=2):
    rows = table.shape[0]
    pieces = split3(table) if parts == 3 else split2(table)
    full = dot(jnp.concatenate(pieces, axis=0), onehot, 1, 0)
    out = full[:rows]
    for i in range(1, parts):
        out = out + full[rows * i : rows * (i + 1)]
    return out


def put(values, onehot, parts=2):
    rows = values.shape[0]
    pieces = split3(values) if parts == 3 else split2(values)
    full = dot(jnp.concatenate(pieces, axis=0), onehot, 1, 1)
    out = full[:rows]
    for i in range(1, parts):
        out = out + full[rows * i : rows * (i + 1)]
    return out


def put_rows(values, onehot):
    high, low = split2(values)
    return dot(onehot, high, 1, 1) + dot(onehot, low, 1, 1)


def lanes(block):
    return jnp.concatenate([block[i : i + 1] for i in range(block.shape[0])], axis=1)


def match(index, count):
    ids = lax.broadcasted_iota(jnp.int32, (count, index.shape[1]), 0)
    return jnp.where(ids == index, 1.0, 0.0).astype(BF16)


def centers_of(packed):
    return lanes(packed[16:24]).astype(jnp.int32)


def partners_of(packed):
    return lanes(packed[24:32]).astype(jnp.int32)


def live_of(packed):
    return lanes(packed[32:40])


def own_table(packed):
    return jnp.concatenate([lanes(packed[4 * k : 4 * k + 4]) for k in range(4)], axis=0)


def ghost_slot(partners):
    rows = partners - ATOMS
    cell = rows >> 3
    skip = jnp.zeros_like(cell)
    for start in (21, 23, 33, 35):
        skip = skip + jnp.where(cell >= start, 16, 0)
    return rows + skip


def k_lists(packed_ref, out_ref, column_ref):
    packed = packed_ref[...]
    names = packed[40:41].astype(jnp.int32)
    found = pick(own_table(packed), match(names, ATOMS), 3)
    wide = jnp.concatenate([found, jnp.zeros((4, 128), F32)], axis=0)
    out_ref[...] = wide.T[:LIST, :4]
    column_ref[...] = jnp.broadcast_to(packed[40:41], (8, 128)).T[:LIST]


def k_own_pairs(packed_ref, out_ref):
    packed = packed_ref[...]
    table = own_table(packed)
    at_center = pick(table, match(centers_of(packed), ATOMS), 3)
    at_partner = pick(table, match(partners_of(packed), ATOMS), 3)
    out_ref[0:3] = at_partner[0:3] - at_center[0:3]
    out_ref[3:4] = at_partner[3:4]
    out_ref[4:5] = at_center[3:4]
    out_ref[5:8] = jnp.zeros((3, PAIRS), F32)


def k_features(packed_ref, part_ref, ghost_ref, shift_ref, column_ref, wb_ref, wav_ref, msg_ref, scal_ref, pre_ref, av_ref):
    packed = packed_ref[...]
    part = part_ref[...]
    ghost = ghost_ref[...] + shift_ref[...]
    slots = match(ghost_slot(partners_of(packed)), 512)
    pieces = split3(ghost)
    far = dot(pieces[0], slots, 0, 0) + (dot(pieces[1], slots, 0, 0) + dot(pieces[2], slots, 0, 0))
    disp = part[0:3] + far[0:3]
    partner_kind = part[3:4] + far[3:4]
    center_kind = part[4:5]
    radius = jnp.sqrt(jnp.sum(disp * disp, axis=0, keepdims=True) + 0.25)
    inv = 1.0 / radius
    unit = disp * inv
    scaled = radius * 0.2
    base = 1.0 + scaled * scaled
    live = live_of(packed)
    cut = live / (base * base)
    orders = lax.broadcasted_iota(jnp.int32, (8, 1), 0).astype(F32) + 1.0
    angle = radius * orders * STEP
    basis = jnp.sin(angle) * inv
    kinds = lax.broadcasted_iota(jnp.int32, (8, 1), 0).astype(F32)
    first = jnp.where(center_kind == kinds, 1.0, 0.0)
    second = jnp.where(partner_kind == kinds, 1.0, 0.0)
    pre = weighted(wb_ref[...], jnp.concatenate([basis, first, second], axis=0))
    latent = cut * (pre * jax.nn.sigmoid(pre))
    av = weighted(wav_ref[...], latent)
    a = av[:CHAN]
    terms = jnp.concatenate([unit[k : k + 1] * a for k in range(3)], axis=0)
    named = jnp.where(column_ref[:, 0:1].astype(jnp.int32) == centers_of(packed), 1.0, 0.0).astype(BF16)
    msg_ref[...] = put_rows(terms, named)
    scal_ref[0:3] = unit
    scal_ref[3:4] = radius
    scal_ref[4:5] = inv
    scal_ref[5:6] = cut
    scal_ref[6:7] = live * (-0.8) * scaled / (base * base * base)
    scal_ref[7:8] = live
    pre_ref[...] = pre
    av_ref[...] = av


def k_own_env(packed_ref, scal_ref, pre_ref, av_ref, wb_ref, wav_ref, wm_ref, ei_ref, ej_ref, lat_ref, hid_ref, tan_ref, nav_ref):
    packed = packed_ref[...]
    scal = scal_ref[...]
    unit, radius, inv, cut, slope = scal[0:3], scal[3:4], scal[4:5], scal[5:6], scal[6:7]
    av = av_ref[...]
    a = av[:CHAN]
    terms = jnp.concatenate([unit[k : k + 1] * a for k in range(3)], axis=0)
    at_center = match(centers_of(packed), ATOMS)
    env = put(terms, at_center)
    ei_ref[...] = pick(env, at_center)
    ej_ref[...] = pick(env, match(partners_of(packed), ATOMS))
    pre = pre_ref[...]
    gate = jax.nn.sigmoid(pre)
    act = pre * gate
    latent = cut * act
    lat_ref[...] = latent
    hid_ref[...] = weighted(wm_ref[0:128], latent)
    orders = lax.broadcasted_iota(jnp.int32, (8, 1), 0).astype(F32) + 1.0
    angle = radius * orders * STEP
    change = (jnp.cos(angle) * (orders * STEP) - jnp.sin(angle) * inv) * inv
    tangent = slope * act + cut * (gate * (1.0 + pre * (1.0 - gate))) * weighted(wb_ref[0:8], change)
    tan_ref[...] = tangent
    nav_ref[...] = weighted(wav_ref[...], tangent)


def k_energy(packed_ref, scal_ref, av_ref, ghost_ref, ei_ref, ejown_ref, hid_ref, wm_ref, wo_ref, msg_ref, ej_ref, h_ref, tb_ref):
    packed = packed_ref[...]
    scal = scal_ref[...]
    unit, cut = scal[0:3], scal[5:6]
    slots = match(ghost_slot(partners_of(packed)), 512)
    high, low = split2(ghost_ref[...])
    ej = ejown_ref[...] + (dot(high, slots, 0, 0) + dot(low, slots, 0, 0))
    ei = ei_ref[...]
    coupling = 0.0
    for k in range(3):
        rows = slice(k * CHAN, (k + 1) * CHAN)
        coupling = coupling + ei[rows] * (unit[k : k + 1] + ej[rows])
    v = av_ref[CHAN:]
    mix = wm_ref[128:]
    h = hid_ref[...] + weighted(mix, v * coupling)
    gate = jax.nn.sigmoid(h)
    out = wo_ref[...]
    hbar = (cut * out) * (gate * (1.0 + h * (1.0 - gate)))
    tbar = weighted_t(mix, hbar)
    cbar = tbar * v
    back = jnp.concatenate([cbar * ei[k * CHAN : (k + 1) * CHAN] for k in range(3)], axis=0)
    msg_ref[...] = put_rows(back, slots)
    ej_ref[...] = ej
    h_ref[...] = h
    tb_ref[...] = tbar


def k_direct(
    packed_ref, scal_ref, av_ref, nav_ref, ei_ref, ej_ref, lat_ref, tan_ref, h_ref, tb_ref, wm_ref, wo_ref, part_ref, energy_ref
):
    packed = packed_ref[...]
    scal = scal_ref[...]
    unit, cut, slope = scal[0:3], scal[5:6], scal[6:7]
    at_center = match(centers_of(packed), ATOMS)
    at_partner = match(partners_of(packed), ATOMS)
    ei, ej = ei_ref[...], ej_ref[...]
    a, v = av_ref[:CHAN], av_ref[CHAN:]
    na, nv = nav_ref[:CHAN], nav_ref[CHAN:]
    tbar = tb_ref[...]
    cbar = tbar * v
    h = h_ref[...]
    gate = jax.nn.sigmoid(h)
    out = wo_ref[...]
    score = jnp.sum(out * (lat_ref[...] + h * gate), axis=0, keepdims=True)
    energy_ref[...] = put(jnp.concatenate([cut * score, jnp.zeros((7, PAIRS), F32)], axis=0), at_center)[0:4]
    ubar = cut * out
    hbar = ubar * (gate * (1.0 + h * (1.0 - gate)))
    lbar = ubar + weighted_t(wm_ref[0:128], hbar)
    coupling = 0.0
    to_center, to_partner, along = [], [], []
    for k in range(3):
        rows = slice(k * CHAN, (k + 1) * CHAN)
        mixed = unit[k : k + 1] + ej[rows]
        coupling = coupling + ei[rows] * mixed
        to_center.append(cbar * mixed)
        to_partner.append(cbar * ei[rows])
        along.append(jnp.sum(to_partner[k], axis=0, keepdims=True))
    vbar = tbar * coupling
    rbar = slope * score + jnp.sum(lbar * tan_ref[...], axis=0, keepdims=True) + jnp.sum(vbar * nv, axis=0, keepdims=True)
    grad = put(jnp.concatenate(to_center, axis=0), at_center) + put(jnp.concatenate(to_partner, axis=0), at_partner)
    gi = pick(grad, at_center)
    for k in range(3):
        rows = slice(k * CHAN, (k + 1) * CHAN)
        along[k] = along[k] + jnp.sum(a * gi[rows], axis=0, keepdims=True)
        rbar = rbar + unit[k : k + 1] * jnp.sum(na * gi[rows], axis=0, keepdims=True)
    part_ref[...] = jnp.concatenate(along + [rbar, jnp.zeros((4, PAIRS), F32)], axis=0)


def k_env_back(packed_ref, scal_ref, av_ref, nav_ref, part_ref, back_ref, column_ref, msg_ref, dbar_ref):
    packed = packed_ref[...]
    scal = scal_ref[...]
    unit, inv = scal[0:3], scal[4:5]
    part = part_ref[...]
    named = jnp.where(column_ref[:, 0:1].astype(jnp.int32) == centers_of(packed), 1.0, 0.0).astype(BF16)
    high, low = split2(back_ref[...])
    gi = dot(high, named, 0, 0) + dot(low, named, 0, 0)
    a, na = av_ref[:CHAN], nav_ref[:CHAN]
    along = []
    rbar = part[3:4]
    for k in range(3):
        rows = slice(k * CHAN, (k + 1) * CHAN)
        along.append(part[k : k + 1] + jnp.sum(a * gi[rows], axis=0, keepdims=True))
        rbar = rbar + unit[k : k + 1] * jnp.sum(na * gi[rows], axis=0, keepdims=True)
    for k in range(3):
        rbar = rbar - inv * along[k] * unit[k : k + 1]
    dbar = jnp.concatenate([along[k] * inv + rbar * unit[k : k + 1] for k in range(3)] + [jnp.zeros((5, PAIRS), F32)], axis=0)
    slots = match(ghost_slot(partners_of(packed)), 512)
    msg_ref[...] = put_rows(dbar, slots)[:, :4]
    dbar_ref[...] = dbar


def k_own_force(packed_ref, dbar_ref, out_ref):
    packed = packed_ref[...]
    dbar = dbar_ref[...]
    out_ref[...] = put(dbar, match(partners_of(packed), ATOMS)) - put(dbar, match(centers_of(packed), ATOMS))


def k_force(own_ref, back_ref, column_ref, energy_ref, out_ref):
    named = jnp.where(
        column_ref[:, 0:1].astype(jnp.int32) == lax.broadcasted_iota(jnp.int32, (LIST, ATOMS), 1), 1.0, 0.0
    ).astype(BF16)
    high, mid, low = split3(back_ref[...])
    returned = dot(high, named, 0, 0) + (dot(mid, named, 0, 0) + dot(low, named, 0, 0))
    total = -(own_ref[0:3] + returned[0:3])
    energy = energy_ref[...]
    for k in range(3):
        for i in range(4):
            out_ref[4 * k + i : 4 * k + i + 1] = total[k : k + 1, 128 * i : 128 * i + 128]
    for i in range(4):
        out_ref[12 + i : 13 + i] = energy[0:1, 128 * i : 128 * i + 128]


def call(kernel, outs, *args):
    shapes = [jax.ShapeDtypeStruct(s, F32) for s in outs]
    spec = pl.BlockSpec(memory_space=pltpu.VMEM)
    return pl.pallas_call(
        kernel,
        out_shape=shapes,
        in_specs=[spec] * len(args),
        out_specs=[spec] * len(outs),
        compiler_params=pltpu.CompilerParams(vmem_limit_bytes=48 * 1024 * 1024),
        name=kernel.__name__,
    )(*args)


GRID_SHIFT = np.zeros((4, 4, 4, 8, 4), np.float32)
for _axis in range(3):
    _at = [slice(None)] * 3
    _at[_axis] = 0
    GRID_SHIFT[tuple(_at) + (slice(None), _axis)] = -6.0
    _at[_axis] = 3
    GRID_SHIFT[tuple(_at) + (slice(None), _axis)] = 6.0
GRID_SHIFT = GRID_SHIFT.reshape(512, 4)


def shards(
    positions,
    species,
    send_lists,
    pair_center,
    pair_partner,
    pair_slot_live,
    w_basis,
    emb_center,
    emb_partner,
    w_env,
    w_value,
    w_mix,
    w_out,
):
    packed = jnp.concatenate(
        [
            positions.reshape(12, 128),
            species.reshape(4, 128).astype(F32),
            pair_center.reshape(8, 128).astype(F32),
            pair_partner.reshape(8, 128).astype(F32),
            pair_slot_live.reshape(8, 128).astype(F32),
            jnp.pad(send_lists.reshape(1, LIST).astype(F32), ((0, 7), (0, 64)), constant_values=-1.0),
        ],
        axis=0,
    )
    zeros = jnp.zeros((2, 128), F32)
    wb = jnp.concatenate([w_basis, emb_center, zeros, emb_partner, zeros], axis=0)
    wav = jnp.concatenate([w_env, w_value], axis=1)
    wo = w_out.reshape(128, 1)

    packed = lax.ppermute(packed, AXES, MOVE_IN)
    msg, column = call(k_lists, [(LIST, 4), (LIST, 8)], packed)
    (part,) = call(k_own_pairs, [(8, PAIRS)], packed)
    ghost = spread(msg.reshape(2, 2, 2, 8, 4)).reshape(512, 4)
    msg, scal, pre, av = call(
        k_features,
        [(LIST, 192), (8, PAIRS), (128, PAIRS), (128, PAIRS)],
        packed,
        part,
        ghost,
        jnp.asarray(GRID_SHIFT),
        column,
        wb,
        wav,
    )
    ei, ej, latent, hid, tangent, nav = call(
        k_own_env,
        [(192, PAIRS), (192, PAIRS)] + [(128, PAIRS)] * 4,
        packed,
        scal,
        pre,
        av,
        wb,
        wav,
        w_mix,
    )
    ghost = spread(msg.reshape(2, 2, 2, 8, 192)).reshape(512, 192)
    msg, ej, h, tbar = call(
        k_energy,
        [(512, 192), (192, PAIRS), (128, PAIRS), (CHAN, PAIRS)],
        packed,
        scal,
        av,
        ghost,
        ei,
        ej,
        hid,
        w_mix,
        wo,
    )
    part, energy = call(
        k_direct,
        [(8, PAIRS), (4, ATOMS)],
        packed,
        scal,
        av,
        nav,
        ei,
        ej,
        latent,
        tangent,
        h,
        tbar,
        w_mix,
        wo,
    )
    back = collect(msg.reshape(4, 4, 4, 8, 192)).reshape(LIST, 192)
    msg, dbar = call(k_env_back, [(512, 4), (8, PAIRS)], packed, scal, av, nav, part, back, column)
    (own,) = call(k_own_force, [(8, ATOMS)], packed, dbar)
    back = collect(msg.reshape(4, 4, 4, 8, 4)).reshape(LIST, 4)
    (out,) = call(k_force, [(16, 128)], own, back, column, energy)
    out = lax.ppermute(out, AXES, MOVE_OUT)
    return out[:12].reshape(3, 1, 1, 1, ATOMS), out[12:].reshape(1, 1, 1, ATOMS)


def solution(mesh):
    in_specs = (
        P(None, "gx", "gy", "gz", None),
        P("gx", "gy", "gz", None),
        P("gx", "gy", "gz", None),
        P("gx", "gy", "gz", None, None),
        P("gx", "gy", "gz", None, None),
        P("gx", "gy", "gz", None, None),
        P(),
        P(),
        P(),
        P(),
        P(),
        P(),
        P(),
    )
    out_specs = (P(None, "gx", "gy", "gz", None), P("gx", "gy", "gz", None))
    return jax.shard_map(shards, mesh=mesh, in_specs=in_specs, out_specs=out_specs, check_vma=False)
```

profile of v0, /device:TPU:23, one launch (start us, length us, event | category | flops | bytes accessed | tf_op | source)
XLA Modules:
  0.0 136.4 jit_solution(8609189075780526580)
XLA Ops:
  0.6 0.7 convert_element_type.38
  1.4 0.6 copy-done.6
  2.1 0.6 copy-done.8
  2.8 4.4 %collective-permute-start = (f32[48,128]{1,0:T(8,128)S(1)}, f32[48,128]{1,0:T(8,128)S(1)}, u32[]{:S(2)}, u32[]{:S(2)}) collective-permute-start(f32[48,128]{1,0:T(8,128)S(1)} %concatenate.45), channel_id=1, source_target_pairs={{0,0},{1,32},{2,1},{3,33},{4,2},{5,34},{6,3},{7,35},{8,8},{9,40},{... | collective-permute-start | bytes 73736 | tf_op jit(solution)/shard_map/ppermute | solution.py:402
  7.2 13.4 %collective-permute-done.packed_ref = f32[48,128]{1,0:T(8,128)S(1)} collective-permute-done((f32[48,128]{1,0:T(8,128)S(1)}, f32[48,128]{1,0:T(8,128)S(1)}, u32[]{:S(2)}, u32[]{:S(2)}) %collective-permute-start) | collective-permute-done | bytes 24608 | tf_op jit(solution)/shard_map/ppermute | solution.py:402
  20.9 0.7 collective-permute-start.2
  21.6 0.7 collective-permute-done.1
  22.2 3.1 %collective-permute-done.2 = f32[2,2,1,8,4]{4,3,2,1,0:T(8,128)S(1)} collective-permute-done((f32[2,2,1,8,4]{4,3,2,1,0:T(8,128)S(1)}, f32[2,2,1,8,4]{4,3,2,1,0:T(8,128)S(1)}, u32[]{:S(2)}, u32[]{:S(2)}) %collective-permute-start.2) | collective-permute-done | bytes 544 | tf_op jit(solution)/shard_map/ppermute | solution.py:48
  25.3 2.9 %collective-permute-start.3 = (f32[2,1,4,8,4]{4,3,2,1,0:T(8,128)S(1)}, f32[2,1,4,8,4]{4,3,2,1,0:T(8,128)S(1)}, u32[]{:S(2)}, u32[]{:S(2)}) collective-permute-start(f32[2,1,4,8,4]{4,3,2,1,0:T(8,128)S(1)} %get-tuple-element.66), channel_id=1, source_target_pairs={{0,8},{32,40},{1,9},{33,41},{2,10},{34,42},{3,11},{35,43},{8,16},{... | collective-permute-start | bytes 3080 | tf_op jit(solution)/shard_map/ppermute | solution.py:47
  28.2 2.4 %collective-permute-start.4 = (f32[2,1,4,8,4]{4,3,2,1,0:T(8,128)S(1)}, f32[2,1,4,8,4]{4,3,2,1,0:T(8,128)S(1)}, u32[]{:S(2)}, u32[]{:S(2)}) collective-permute-start(f32[2,1,4,8,4]{4,3,2,1,0:T(8,128)S(1)} %get-tuple-element.67), channel_id=1, source_target_pairs={{0,24},{32,56},{1,25},{33,57},{2,26},{34,58},{3,27},{35,59},{8,0},... | collective-permute-start | bytes 3080 | tf_op jit(solution)/shard_map/ppermute | solution.py:48
  30.8 2.5 %collective-permute-done.4 = f32[2,1,4,8,4]{4,3,2,1,0:T(8,128)S(1)} collective-permute-done((f32[2,1,4,8,4]{4,3,2,1,0:T(8,128)S(1)}, f32[2,1,4,8,4]{4,3,2,1,0:T(8,128)S(1)}, u32[]{:S(2)}, u32[]{:S(2)}) %collective-permute-start.4) | collective-permute-done | bytes 1056 | tf_op jit(solution)/shard_map/ppermute | solution.py:48
  33.4 1.9 %collective-permute-start.5 = (f32[1,4,4,8,4]{4,3,2,1,0:T(8,128)S(1)}, f32[1,4,4,8,4]{4,3,2,1,0:T(8,128)S(1)}, u32[]{:S(2)}, u32[]{:S(2)}) collective-permute-start(f32[1,4,4,8,4]{4,3,2,1,0:T(8,128)S(1)} %get-tuple-element.60), channel_id=1, source_target_pairs={{0,64},{32,96},{1,65},{33,97},{2,66},{34,98},{3,67},{35,99},{8,72}... | collective-permute-start | bytes 6152 | tf_op jit(solution)/shard_map/ppermute | solution.py:47
  35.3 7.7 %collective-permute-start.6 = (f32[1,4,4,8,4]{4,3,2,1,0:T(8,128)S(1)}, f32[1,4,4,8,4]{4,3,2,1,0:T(8,128)S(1)}, u32[]{:S(2)}, u32[]{:S(2)}) collective-permute-start(f32[1,4,4,8,4]{4,3,2,1,0:T(8,128)S(1)} %get-tuple-element.61), channel_id=1, source_target_pairs={{0,452},{32,484},{1,453},{33,485},{2,454},{34,486},{3,455},{35,487... | collective-permute-start | bytes 6152 | tf_op jit(solution)/shard_map/ppermute | solution.py:48
  44.4 0.8 copy-done.1
  45.1 1.7 %k_features.1 = (f32[64,192]{1,0:T(8,128)S(1)}, f32[8,1024]{1,0:T(8,128)S(1)}, f32[128,1024]{1,0:T(8,128)S(1)}, f32[128,1024]{1,0:T(8,128)S(1)}) custom-call(f32[48,128]{1,0:T(8,128)S(1)} %collective-permute-done.packed_ref, f32[8,1024]{1,0:T(8,128)S(1)} %k_own_pairs.1.part_ref, f32[512,4]{1,0:T(8,128)S(1)} %bitcast.23, f32[512,4]{1,0:T(8,128)S(1)} %copy-done.1, ...), custom_call_target="tpu_custom_call" | custom-call | tf_op jit(solution)/shard_map/k_features/pallas_call | solution.py:351
  46.9 2.1 %collective-permute-start.7 = (f32[2,2,1,8,192]{4,3,2,1,0:T(8,128)S(1)}, f32[2,2,1,8,192]{4,3,2,1,0:T(8,128)S(1)}, u32[]{:S(2)}, u32[]{:S(2)}) collective-permute-start(f32[2,2,1,8,192]{4,3,2,1,0:T(8,128)S(1)} %get-tuple-element.64), channel_id=1, source_target_pairs={{0,32},{32,1},{1,33},{33,2},{2,34},{34,3},{3,35},{35,0},{8,40},{40... | collective-permute-start | bytes 73736 | tf_op jit(solution)/shard_map/ppermute | solution.py:47
  49.0 1.0 collective-permute-done.7
  50.0 3.5 %collective-permute-done.8 = f32[2,2,1,8,192]{4,3,2,1,0:T(8,128)S(1)} collective-permute-done((f32[2,2,1,8,192]{4,3,2,1,0:T(8,128)S(1)}, f32[2,2,1,8,192]{4,3,2,1,0:T(8,128)S(1)}, u32[]{:S(2)}, u32[]{:S(2)}) %collective-permute-start.8) | collective-permute-done | bytes 24608 | tf_op jit(solution)/shard_map/ppermute | solution.py:48
  53.5 3.0 %collective-permute-start.9 = (f32[2,1,4,8,192]{4,3,2,1,0:T(8,128)S(1)}, f32[2,1,4,8,192]{4,3,2,1,0:T(8,128)S(1)}, u32[]{:S(2)}, u32[]{:S(2)}) collective-permute-start(f32[2,1,4,8,192]{4,3,2,1,0:T(8,128)S(1)} %get-tuple-element.58), channel_id=1, source_target_pairs={{0,8},{32,40},{1,9},{33,41},{2,10},{34,42},{3,11},{35,43},{8,16},{... | collective-permute-start | bytes 147464 | tf_op jit(solution)/shard_map/ppermute | solution.py:47
  56.6 2.2 %collective-permute-start.10 = (f32[2,1,4,8,192]{4,3,2,1,0:T(8,128)S(1)}, f32[2,1,4,8,192]{4,3,2,1,0:T(8,128)S(1)}, u32[]{:S(2)}, u32[]{:S(2)}) collective-permute-start(f32[2,1,4,8,192]{4,3,2,1,0:T(8,128)S(1)} %get-tuple-element.59), channel_id=1, source_target_pairs={{0,24},{32,56},{1,25},{33,57},{2,26},{34,58},{3,27},{35,59},{8,0},... | collective-permute-start | bytes 147464 | tf_op jit(solution)/shard_map/ppermute | solution.py:48
  58.9 2.8 %collective-permute-done.10 = f32[2,1,4,8,192]{4,3,2,1,0:T(8,128)S(1)} collective-permute-done((f32[2,1,4,8,192]{4,3,2,1,0:T(8,128)S(1)}, f32[2,1,4,8,192]{4,3,2,1,0:T(8,128)S(1)}, u32[]{:S(2)}, u32[]{:S(2)}) %collective-permute-start.10) | collective-permute-done | bytes 49184 | tf_op jit(solution)/shard_map/ppermute | solution.py:48
  61.7 1.9 %collective-permute-start.11 = (f32[1,4,4,8,192]{4,3,2,1,0:T(8,128)S(1)}, f32[1,4,4,8,192]{4,3,2,1,0:T(8,128)S(1)}, u32[]{:S(2)}, u32[]{:S(2)}) collective-permute-start(f32[1,4,4,8,192]{4,3,2,1,0:T(8,128)S(1)} %get-tuple-element.52), channel_id=1, source_target_pairs={{0,64},{32,96},{1,65},{33,97},{2,66},{34,98},{3,67},{35,99},{8,72}... | collective-permute-start | bytes 294920 | tf_op jit(solution)/shard_map/ppermute | solution.py:47
  63.6 5.0 %collective-permute-start.12 = (f32[1,4,4,8,192]{4,3,2,1,0:T(8,128)S(1)}, f32[1,4,4,8,192]{4,3,2,1,0:T(8,128)S(1)}, u32[]{:S(2)}, u32[]{:S(2)}) collective-permute-start(f32[1,4,4,8,192]{4,3,2,1,0:T(8,128)S(1)} %get-tuple-element.53), channel_id=1, source_target_pairs={{0,452},{32,484},{1,453},{33,485},{2,454},{34,486},{3,455},{35,487... | collective-permute-start | bytes 294920 | tf_op jit(solution)/shard_map/ppermute | solution.py:48
  68.8 2.4 %k_own_env.1 = (f32[192,1024]{1,0:T(8,128)S(1)}, f32[192,1024]{1,0:T(8,128)S(1)}, f32[128,1024]{1,0:T(8,128)S(1)}, f32[128,1024]{1,0:T(8,128)S(1)}, f32[128,1024]{1,0:T(8,128)S(1)}, /*index=5*/f32[128,1024]{1,0:T(8,128)S(1)}) custom-call(f32[48,128]{1,0:T(8,128)S(1)} %collective-permute-done.packed_ref, f32[8,1024]{1,0:T(8,128)S(1)} %get-tuple-element.24.scal_ref, ...), custom_call_target="tpu_custom_call" | custom-call | tf_op jit(solution)/shard_map/k_own_env/pallas_call | solution.py:351
  71.3 2.2 %k_energy.1 = (f32[512,192]{1,0:T(8,128)S(1)}, f32[192,1024]{1,0:T(8,128)S(1)}, f32[128,1024]{1,0:T(8,128)S(1)}, f32[64,1024]{1,0:T(8,128)S(1)}) custom-call(f32[48,128]{1,0:T(8,128)S(1)} %collective-permute-done.packed_ref, f32[8,1024]{1,0:T(8,128)S(1)} %get-tuple-element.24.scal_ref, f32[128,1024]{1,0:T(8,128)S(1)} %get-tuple-element.25.av_ref, ...), custom_call_target="tpu_custom_call" | custom-call | tf_op jit(solution)/shard_map/k_energy/pallas_call | solution.py:351
  73.5 4.3 %collective-permute-start.14 = (f32[1,4,4,8,192]{4,3,2,1,0:T(8,128)S(1)}, f32[1,4,4,8,192]{4,3,2,1,0:T(8,128)S(1)}, u32[]{:S(2)}, u32[]{:S(2)}) collective-permute-start(f32[1,4,4,8,192]{4,3,2,1,0:T(8,128)S(1)} %bitcast.37), channel_id=1, source_target_pairs={{0,452},{32,484},{1,453},{33,485},{2,454},{34,486},{3,455},{35,487... | collective-permute-start | bytes 294920 | tf_op jit(solution)/shard_map/ppermute | solution.py:58
  77.8 1.9 %collective-permute-start.13 = (f32[1,4,4,8,192]{4,3,2,1,0:T(8,128)S(1)}, f32[1,4,4,8,192]{4,3,2,1,0:T(8,128)S(1)}, u32[]{:S(2)}, u32[]{:S(2)}) collective-permute-start(f32[1,4,4,8,192]{4,3,2,1,0:T(8,128)S(1)} %bitcast.36), channel_id=1, source_target_pairs={{0,64},{32,96},{1,65},{33,97},{2,66},{34,98},{3,67},{35,99},{8,72}... | collective-permute-start | bytes 294920 | tf_op jit(solution)/shard_map/ppermute | solution.py:57
  79.7 1.0 collective-permute-done.14
  80.8 5.6 %collective-permute-done.13 = f32[1,4,4,8,192]{4,3,2,1,0:T(8,128)S(1)} collective-permute-done((f32[1,4,4,8,192]{4,3,2,1,0:T(8,128)S(1)}, f32[1,4,4,8,192]{4,3,2,1,0:T(8,128)S(1)}, u32[]{:S(2)}, u32[]{:S(2)}) %collective-permute-start.13) | collective-permute-done | bytes 98336 | tf_op jit(solution)/shard_map/ppermute | solution.py:57
  86.4 3.2 %collective-permute-start.15 = (f32[2,1,4,8,192]{4,3,2,1,0:T(8,128)S(1)}, f32[2,1,4,8,192]{4,3,2,1,0:T(8,128)S(1)}, u32[]{:S(2)}, u32[]{:S(2)}) collective-permute-start(f32[2,1,4,8,192]{4,3,2,1,0:T(8,128)S(1)} %get-tuple-element.50), channel_id=1, source_target_pairs={{0,8},{32,40},{1,9},{33,41},{2,10},{34,42},{3,11},{35,43},{8,16},{... | collective-permute-start | bytes 147464 | tf_op jit(solution)/shard_map/ppermute | solution.py:57
  89.6 2.1 %collective-permute-start.16 = (f32[2,1,4,8,192]{4,3,2,1,0:T(8,128)S(1)}, f32[2,1,4,8,192]{4,3,2,1,0:T(8,128)S(1)}, u32[]{:S(2)}, u32[]{:S(2)}) collective-permute-start(f32[2,1,4,8,192]{4,3,2,1,0:T(8,128)S(1)} %get-tuple-element.51), channel_id=1, source_target_pairs={{0,24},{32,56},{1,25},{33,57},{2,26},{34,58},{3,27},{35,59},{8,0},... | collective-permute-start | bytes 147464 | tf_op jit(solution)/shard_map/ppermute | solution.py:58
  91.7 2.9 %collective-permute-done.16 = f32[2,1,4,8,192]{4,3,2,1,0:T(8,128)S(1)} collective-permute-done((f32[2,1,4,8,192]{4,3,2,1,0:T(8,128)S(1)}, f32[2,1,4,8,192]{4,3,2,1,0:T(8,128)S(1)}, u32[]{:S(2)}, u32[]{:S(2)}) %collective-permute-start.16) | collective-permute-done | bytes 49184 | tf_op jit(solution)/shard_map/ppermute | solution.py:58
  94.7 3.8 %collective-permute-start.17 = (f32[2,2,1,8,192]{4,3,2,1,0:T(8,128)S(1)}, f32[2,2,1,8,192]{4,3,2,1,0:T(8,128)S(1)}, u32[]{:S(2)}, u32[]{:S(2)}) collective-permute-start(f32[2,2,1,8,192]{4,3,2,1,0:T(8,128)S(1)} %get-tuple-element.56), channel_id=1, source_target_pairs={{0,32},{32,1},{1,33},{33,2},{2,34},{34,3},{3,35},{35,0},{8,40},{40... | collective-permute-start | bytes 73736 | tf_op jit(solution)/shard_map/ppermute | solution.py:57
  98.5 2.4 %k_direct.1 = (f32[8,1024]{1,0:T(8,128)S(1)}, f32[4,512]{1,0:T(4,128)S(1)}) custom-call(f32[48,128]{1,0:T(8,128)S(1)} %collective-permute-done.packed_ref, f32[8,1024]{1,0:T(8,128)S(1)} %get-tuple-element.24.scal_ref, f32[128,1024]{1,0:T(8,128)S(1)} %get-tuple-element.25.av_ref, f32[128,1024]{1,0:T(8,128)S(1)} %get-tuple-element.27.nav_ref, ...), custom_call_target="tpu_custom_call" | custom-call | tf_op jit(solution)/shard_map/k_direct/pallas_call | solution.py:351
  100.9 2.1 %collective-permute-done.18 = f32[2,2,1,8,192]{4,3,2,1,0:T(8,128)S(1)} collective-permute-done((f32[2,2,1,8,192]{4,3,2,1,0:T(8,128)S(1)}, f32[2,2,1,8,192]{4,3,2,1,0:T(8,128)S(1)}, u32[]{:S(2)}, u32[]{:S(2)}) %collective-permute-start.18) | collective-permute-done | bytes 24608 | tf_op jit(solution)/shard_map/ppermute | solution.py:58
  103.1 1.2 k_env_back.1
  104.3 1.9 %collective-permute-start.20 = (f32[1,4,4,8,4]{4,3,2,1,0:T(8,128)S(1)}, f32[1,4,4,8,4]{4,3,2,1,0:T(8,128)S(1)}, u32[]{:S(2)}, u32[]{:S(2)}) collective-permute-start(f32[1,4,4,8,4]{4,3,2,1,0:T(8,128)S(1)} %bitcast.39), channel_id=1, source_target_pairs={{0,452},{32,484},{1,453},{33,485},{2,454},{34,486},{3,455},{35,487... | collective-permute-start | bytes 6152 | tf_op jit(solution)/shard_map/ppermute | solution.py:58
  106.2 3.4 %collective-permute-start.19 = (f32[1,4,4,8,4]{4,3,2,1,0:T(8,128)S(1)}, f32[1,4,4,8,4]{4,3,2,1,0:T(8,128)S(1)}, u32[]{:S(2)}, u32[]{:S(2)}) collective-permute-start(f32[1,4,4,8,4]{4,3,2,1,0:T(8,128)S(1)} %bitcast.38), channel_id=1, source_target_pairs={{0,64},{32,96},{1,65},{33,97},{2,66},{34,98},{3,67},{35,99},{8,72}... | collective-permute-start | bytes 6152 | tf_op jit(solution)/shard_map/ppermute | solution.py:57
  109.6 2.8 %collective-permute-done.19 = f32[1,4,4,8,4]{4,3,2,1,0:T(8,128)S(1)} collective-permute-done((f32[1,4,4,8,4]{4,3,2,1,0:T(8,128)S(1)}, f32[1,4,4,8,4]{4,3,2,1,0:T(8,128)S(1)}, u32[]{:S(2)}, u32[]{:S(2)}) %collective-permute-start.19) | collective-permute-done | bytes 2080 | tf_op jit(solution)/shard_map/ppermute | solution.py:57
  112.5 3.2 %collective-permute-start.21 = (f32[2,1,4,8,4]{4,3,2,1,0:T(8,128)S(1)}, f32[2,1,4,8,4]{4,3,2,1,0:T(8,128)S(1)}, u32[]{:S(2)}, u32[]{:S(2)}) collective-permute-start(f32[2,1,4,8,4]{4,3,2,1,0:T(8,128)S(1)} %get-tuple-element.54), channel_id=1, source_target_pairs={{0,8},{32,40},{1,9},{33,41},{2,10},{34,42},{3,11},{35,43},{8,16},{... | collective-permute-start | bytes 3080 | tf_op jit(solution)/shard_map/ppermute | solution.py:57
  115.7 2.1 %collective-permute-start.22 = (f32[2,1,4,8,4]{4,3,2,1,0:T(8,128)S(1)}, f32[2,1,4,8,4]{4,3,2,1,0:T(8,128)S(1)}, u32[]{:S(2)}, u32[]{:S(2)}) collective-permute-start(f32[2,1,4,8,4]{4,3,2,1,0:T(8,128)S(1)} %get-tuple-element.55), channel_id=1, source_target_pairs={{0,24},{32,56},{1,25},{33,57},{2,26},{34,58},{3,27},{35,59},{8,0},... | collective-permute-start | bytes 3080 | tf_op jit(solution)/shard_map/ppermute | solution.py:58
  117.8 2.6 %collective-permute-done.22 = f32[2,1,4,8,4]{4,3,2,1,0:T(8,128)S(1)} collective-permute-done((f32[2,1,4,8,4]{4,3,2,1,0:T(8,128)S(1)}, f32[2,1,4,8,4]{4,3,2,1,0:T(8,128)S(1)}, u32[]{:S(2)}, u32[]{:S(2)}) %collective-permute-start.22) | collective-permute-done | bytes 1056 | tf_op jit(solution)/shard_map/ppermute | solution.py:58
  120.4 3.4 %collective-permute-start.23 = (f32[2,2,1,8,4]{4,3,2,1,0:T(8,128)S(1)}, f32[2,2,1,8,4]{4,3,2,1,0:T(8,128)S(1)}, u32[]{:S(2)}, u32[]{:S(2)}) collective-permute-start(f32[2,2,1,8,4]{4,3,2,1,0:T(8,128)S(1)} %get-tuple-element.62), channel_id=1, source_target_pairs={{0,32},{32,1},{1,33},{33,2},{2,34},{34,3},{3,35},{35,0},{8,40},{40... | collective-permute-start | bytes 1544 | tf_op jit(solution)/shard_map/ppermute | solution.py:57
  123.8 0.6 k_own_force.1.own_ref
  124.6 3.5 %collective-permute-done.24 = f32[2,2,1,8,4]{4,3,2,1,0:T(8,128)S(1)} collective-permute-done((f32[2,2,1,8,4]{4,3,2,1,0:T(8,128)S(1)}, f32[2,2,1,8,4]{4,3,2,1,0:T(8,128)S(1)}, u32[]{:S(2)}, u32[]{:S(2)}) %collective-permute-start.24) | collective-permute-done | bytes 544 | tf_op jit(solution)/shard_map/ppermute | solution.py:58
  128.4 2.2 %collective-permute-start.25 = (f32[16,128]{1,0:T(8,128)S(1)}, f32[16,128]{1,0:T(8,128)S(1)}, u32[]{:S(2)}, u32[]{:S(2)}) collective-permute-start(f32[16,128]{1,0:T(8,128)S(1)} %k_force.1), channel_id=1, source_target_pairs={{0,0},{32,1},{1,2},{33,3},{2,4},{34,5},{3,6},{35,7},{8,8},{40,9},{... | collective-permute-start | bytes 24584 | tf_op jit(solution)/shard_map/ppermute | solution.py:463
  130.6 4.6 %collective-permute-done.25 = f32[16,128]{1,0:T(8,128)S(1)} collective-permute-done((f32[16,128]{1,0:T(8,128)S(1)}, f32[16,128]{1,0:T(8,128)S(1)}, u32[]{:S(2)}, u32[]{:S(2)}) %collective-permute-start.25) | collective-permute-done | bytes 8224 | tf_op jit(solution)/shard_map/ppermute | solution.py:463
  135.2 0.6 reshape.74
  (82 shorter events, 3.5 us)
Async XLA Ops:
  0.6 0.7 copy-start.5
  1.3 0.7 copy-start.6
  1.3 0.7 copy-start.4
  2.1 0.7 copy-start.8
  2.1 0.7 copy-start.7
  2.8 17.8 %collective-permute-start = (f32[48,128]{1,0:T(8,128)S(1)}, f32[48,128]{1,0:T(8,128)S(1)}, u32[]{:S(2)}, u32[]{:S(2)}) collective-permute-start(f32[48,128]{1,0:T(8,128)S(1)} %concatenate.45), channel_id=1, source_target_pairs={{0,0},{1,32},{2,1},{3,33},{4,2},{5,34},{6,3},{7,35},{8,8},{9,40},{... | collective-permute-start | bytes 73736 | tf_op jit(solution)/shard_map/ppermute | solution.py:402
  20.9 1.4 collective-permute-start.1
  20.9 4.4 %collective-permute-start.2 = (f32[2,2,1,8,4]{4,3,2,1,0:T(8,128)S(1)}, f32[2,2,1,8,4]{4,3,2,1,0:T(8,128)S(1)}, u32[]{:S(2)}, u32[]{:S(2)}) collective-permute-start(f32[2,2,1,8,4]{4,3,2,1,0:T(8,128)S(1)} %get-tuple-element.69), channel_id=1, source_target_pairs={{0,35},{32,0},{1,32},{33,1},{2,33},{34,2},{3,34},{35,3},{8,43},{40... | collective-permute-start | bytes 1544 | tf_op jit(solution)/shard_map/ppermute | solution.py:48
  25.3 5.3 %copy-start.2 = (f32[128,64]{0,1:T(8,128)S(1)}, f32[128,64]{0,1:T(8,128)}, u32[]{:S(2)}) copy-start(f32[128,64]{0,1:T(8,128)} %param.23) | copy-start | bytes 98308
  25.3 5.5 %collective-permute-start.3 = (f32[2,1,4,8,4]{4,3,2,1,0:T(8,128)S(1)}, f32[2,1,4,8,4]{4,3,2,1,0:T(8,128)S(1)}, u32[]{:S(2)}, u32[]{:S(2)}) collective-permute-start(f32[2,1,4,8,4]{4,3,2,1,0:T(8,128)S(1)} %get-tuple-element.66), channel_id=1, source_target_pairs={{0,8},{32,40},{1,9},{33,41},{2,10},{34,42},{3,11},{35,43},{8,16},{... | collective-permute-start | bytes 3080 | tf_op jit(solution)/shard_map/ppermute | solution.py:47
  28.2 2.5 %copy-start.3 = (f32[128,64]{0,1:T(8,128)S(1)}, f32[128,64]{0,1:T(8,128)}, u32[]{:S(2)}) copy-start(f32[128,64]{0,1:T(8,128)} %param.24) | copy-start | bytes 98308
  28.2 5.1 %collective-permute-start.4 = (f32[2,1,4,8,4]{4,3,2,1,0:T(8,128)S(1)}, f32[2,1,4,8,4]{4,3,2,1,0:T(8,128)S(1)}, u32[]{:S(2)}, u32[]{:S(2)}) collective-permute-start(f32[2,1,4,8,4]{4,3,2,1,0:T(8,128)S(1)} %get-tuple-element.67), channel_id=1, source_target_pairs={{0,24},{32,56},{1,25},{33,57},{2,26},{34,58},{3,27},{35,59},{8,0},... | collective-permute-start | bytes 3080 | tf_op jit(solution)/shard_map/ppermute | solution.py:48
  33.4 10.8 %collective-permute-start.5 = (f32[1,4,4,8,4]{4,3,2,1,0:T(8,128)S(1)}, f32[1,4,4,8,4]{4,3,2,1,0:T(8,128)S(1)}, u32[]{:S(2)}, u32[]{:S(2)}) collective-permute-start(f32[1,4,4,8,4]{4,3,2,1,0:T(8,128)S(1)} %get-tuple-element.60), channel_id=1, source_target_pairs={{0,64},{32,96},{1,65},{33,97},{2,66},{34,98},{3,67},{35,99},{8,72}... | collective-permute-start | bytes 6152 | tf_op jit(solution)/shard_map/ppermute | solution.py:47
  35.3 9.0 %collective-permute-start.6 = (f32[1,4,4,8,4]{4,3,2,1,0:T(8,128)S(1)}, f32[1,4,4,8,4]{4,3,2,1,0:T(8,128)S(1)}, u32[]{:S(2)}, u32[]{:S(2)}) collective-permute-start(f32[1,4,4,8,4]{4,3,2,1,0:T(8,128)S(1)} %get-tuple-element.61), channel_id=1, source_target_pairs={{0,452},{32,484},{1,453},{33,485},{2,454},{34,486},{3,455},{35,487... | collective-permute-start | bytes 6152 | tf_op jit(solution)/shard_map/ppermute | solution.py:48
  43.0 0.7 copy-start.9
  43.0 0.7 copy-start.10
  43.0 0.7 copy-start.11
  44.2 1.0 copy-start.1
  46.9 3.1 %collective-permute-start.7 = (f32[2,2,1,8,192]{4,3,2,1,0:T(8,128)S(1)}, f32[2,2,1,8,192]{4,3,2,1,0:T(8,128)S(1)}, u32[]{:S(2)}, u32[]{:S(2)}) collective-permute-start(f32[2,2,1,8,192]{4,3,2,1,0:T(8,128)S(1)} %get-tuple-element.64), channel_id=1, source_target_pairs={{0,32},{32,1},{1,33},{33,2},{2,34},{34,3},{3,35},{35,0},{8,40},{40... | collective-permute-start | bytes 73736 | tf_op jit(solution)/shard_map/ppermute | solution.py:47
  49.0 4.6 %collective-permute-start.8 = (f32[2,2,1,8,192]{4,3,2,1,0:T(8,128)S(1)}, f32[2,2,1,8,192]{4,3,2,1,0:T(8,128)S(1)}, u32[]{:S(2)}, u32[]{:S(2)}) collective-permute-start(f32[2,2,1,8,192]{4,3,2,1,0:T(8,128)S(1)} %get-tuple-element.65), channel_id=1, source_target_pairs={{0,35},{32,0},{1,32},{33,1},{2,33},{34,2},{3,34},{35,3},{8,43},{40... | collective-permute-start | bytes 73736 | tf_op jit(solution)/shard_map/ppermute | solution.py:48
  53.5 5.3 %collective-permute-start.9 = (f32[2,1,4,8,192]{4,3,2,1,0:T(8,128)S(1)}, f32[2,1,4,8,192]{4,3,2,1,0:T(8,128)S(1)}, u32[]{:S(2)}, u32[]{:S(2)}) collective-permute-start(f32[2,1,4,8,192]{4,3,2,1,0:T(8,128)S(1)} %get-tuple-element.58), channel_id=1, source_target_pairs={{0,8},{32,40},{1,9},{33,41},{2,10},{34,42},{3,11},{35,43},{8,16},{... | collective-permute-start | bytes 147464 | tf_op jit(solution)/shard_map/ppermute | solution.py:47
  56.6 5.0 %collective-permute-start.10 = (f32[2,1,4,8,192]{4,3,2,1,0:T(8,128)S(1)}, f32[2,1,4,8,192]{4,3,2,1,0:T(8,128)S(1)}, u32[]{:S(2)}, u32[]{:S(2)}) collective-permute-start(f32[2,1,4,8,192]{4,3,2,1,0:T(8,128)S(1)} %get-tuple-element.59), channel_id=1, source_target_pairs={{0,24},{32,56},{1,25},{33,57},{2,26},{34,58},{3,27},{35,59},{8,0},... | collective-permute-start | bytes 147464 | tf_op jit(solution)/shard_map/ppermute | solution.py:48
  61.6 7.1 %copy-start = (f32[192,128]{1,0:T(8,128)S(1)}, f32[192,128]{1,0:T(8,128)}, u32[]{:S(2)}) copy-start(f32[192,128]{1,0:T(8,128)} %wm_ref.5) | copy-start | bytes 294916
  61.7 9.5 %collective-permute-start.11 = (f32[1,4,4,8,192]{4,3,2,1,0:T(8,128)S(1)}, f32[1,4,4,8,192]{4,3,2,1,0:T(8,128)S(1)}, u32[]{:S(2)}, u32[]{:S(2)}) collective-permute-start(f32[1,4,4,8,192]{4,3,2,1,0:T(8,128)S(1)} %get-tuple-element.52), channel_id=1, source_target_pairs={{0,64},{32,96},{1,65},{33,97},{2,66},{34,98},{3,67},{35,99},{8,72}... | collective-permute-start | bytes 294920 | tf_op jit(solution)/shard_map/ppermute | solution.py:47
  63.6 5.0 %copy-start.12 = (f32[128]{0:T(128)S(1)}, f32[128]{0:T(128)}, u32[]{:S(2)}) copy-start(f32[128]{0:T(128)} %param.26) | copy-start | bytes 1540
  63.6 7.6 %collective-permute-start.12 = (f32[1,4,4,8,192]{4,3,2,1,0:T(8,128)S(1)}, f32[1,4,4,8,192]{4,3,2,1,0:T(8,128)S(1)}, u32[]{:S(2)}, u32[]{:S(2)}) collective-permute-start(f32[1,4,4,8,192]{4,3,2,1,0:T(8,128)S(1)} %get-tuple-element.53), channel_id=1, source_target_pairs={{0,452},{32,484},{1,453},{33,485},{2,454},{34,486},{3,455},{35,487... | collective-permute-start | bytes 294920 | tf_op jit(solution)/shard_map/ppermute | solution.py:48
  73.5 7.3 %collective-permute-start.14 = (f32[1,4,4,8,192]{4,3,2,1,0:T(8,128)S(1)}, f32[1,4,4,8,192]{4,3,2,1,0:T(8,128)S(1)}, u32[]{:S(2)}, u32[]{:S(2)}) collective-permute-start(f32[1,4,4,8,192]{4,3,2,1,0:T(8,128)S(1)} %bitcast.37), channel_id=1, source_target_pairs={{0,452},{32,484},{1,453},{33,485},{2,454},{34,486},{3,455},{35,487... | collective-permute-start | bytes 294920 | tf_op jit(solution)/shard_map/ppermute | solution.py:58
  77.8 8.6 %collective-permute-start.13 = (f32[1,4,4,8,192]{4,3,2,1,0:T(8,128)S(1)}, f32[1,4,4,8,192]{4,3,2,1,0:T(8,128)S(1)}, u32[]{:S(2)}, u32[]{:S(2)}) collective-permute-start(f32[1,4,4,8,192]{4,3,2,1,0:T(8,128)S(1)} %bitcast.36), channel_id=1, source_target_pairs={{0,64},{32,96},{1,65},{33,97},{2,66},{34,98},{3,67},{35,99},{8,72}... | collective-permute-start | bytes 294920 | tf_op jit(solution)/shard_map/ppermute | solution.py:57
  86.4 5.3 %collective-permute-start.15 = (f32[2,1,4,8,192]{4,3,2,1,0:T(8,128)S(1)}, f32[2,1,4,8,192]{4,3,2,1,0:T(8,128)S(1)}, u32[]{:S(2)}, u32[]{:S(2)}) collective-permute-start(f32[2,1,4,8,192]{4,3,2,1,0:T(8,128)S(1)} %get-tuple-element.50), channel_id=1, source_target_pairs={{0,8},{32,40},{1,9},{33,41},{2,10},{34,42},{3,11},{35,43},{8,16},{... | collective-permute-start | bytes 147464 | tf_op jit(solution)/shard_map/ppermute | solution.py:57
  89.6 5.0 %collective-permute-start.16 = (f32[2,1,4,8,192]{4,3,2,1,0:T(8,128)S(1)}, f32[2,1,4,8,192]{4,3,2,1,0:T(8,128)S(1)}, u32[]{:S(2)}, u32[]{:S(2)}) collective-permute-start(f32[2,1,4,8,192]{4,3,2,1,0:T(8,128)S(1)} %get-tuple-element.51), channel_id=1, source_target_pairs={{0,24},{32,56},{1,25},{33,57},{2,26},{34,58},{3,27},{35,59},{8,0},... | collective-permute-start | bytes 147464 | tf_op jit(solution)/shard_map/ppermute | solution.py:58
  94.7 6.2 %collective-permute-start.17 = (f32[2,2,1,8,192]{4,3,2,1,0:T(8,128)S(1)}, f32[2,2,1,8,192]{4,3,2,1,0:T(8,128)S(1)}, u32[]{:S(2)}, u32[]{:S(2)}) collective-permute-start(f32[2,2,1,8,192]{4,3,2,1,0:T(8,128)S(1)} %get-tuple-element.56), channel_id=1, source_target_pairs={{0,32},{32,1},{1,33},{33,2},{2,34},{34,3},{3,35},{35,0},{8,40},{40... | collective-permute-start | bytes 73736 | tf_op jit(solution)/shard_map/ppermute | solution.py:57
  98.5 4.6 %collective-permute-start.18 = (f32[2,2,1,8,192]{4,3,2,1,0:T(8,128)S(1)}, f32[2,2,1,8,192]{4,3,2,1,0:T(8,128)S(1)}, u32[]{:S(2)}, u32[]{:S(2)}) collective-permute-start(f32[2,2,1,8,192]{4,3,2,1,0:T(8,128)S(1)} %get-tuple-element.57), channel_id=1, source_target_pairs={{0,35},{32,0},{1,32},{33,1},{2,33},{34,2},{3,34},{35,3},{8,43},{40... | collective-permute-start | bytes 73736 | tf_op jit(solution)/shard_map/ppermute | solution.py:58
  104.3 5.3 %collective-permute-start.20 = (f32[1,4,4,8,4]{4,3,2,1,0:T(8,128)S(1)}, f32[1,4,4,8,4]{4,3,2,1,0:T(8,128)S(1)}, u32[]{:S(2)}, u32[]{:S(2)}) collective-permute-start(f32[1,4,4,8,4]{4,3,2,1,0:T(8,128)S(1)} %bitcast.39), channel_id=1, source_target_pairs={{0,452},{32,484},{1,453},{33,485},{2,454},{34,486},{3,455},{35,487... | collective-permute-start | bytes 6152 | tf_op jit(solution)/shard_map/ppermute | solution.py:58
  106.2 6.2 %collective-permute-start.19 = (f32[1,4,4,8,4]{4,3,2,1,0:T(8,128)S(1)}, f32[1,4,4,8,4]{4,3,2,1,0:T(8,128)S(1)}, u32[]{:S(2)}, u32[]{:S(2)}) collective-permute-start(f32[1,4,4,8,4]{4,3,2,1,0:T(8,128)S(1)} %bitcast.38), channel_id=1, source_target_pairs={{0,64},{32,96},{1,65},{33,97},{2,66},{34,98},{3,67},{35,99},{8,72}... | collective-permute-start | bytes 6152 | tf_op jit(solution)/shard_map/ppermute | solution.py:57
  112.5 5.3 %collective-permute-start.21 = (f32[2,1,4,8,4]{4,3,2,1,0:T(8,128)S(1)}, f32[2,1,4,8,4]{4,3,2,1,0:T(8,128)S(1)}, u32[]{:S(2)}, u32[]{:S(2)}) collective-permute-start(f32[2,1,4,8,4]{4,3,2,1,0:T(8,128)S(1)} %get-tuple-element.54), channel_id=1, source_target_pairs={{0,8},{32,40},{1,9},{33,41},{2,10},{34,42},{3,11},{35,43},{8,16},{... | collective-permute-start | bytes 3080 | tf_op jit(solution)/shard_map/ppermute | solution.py:57
  115.7 4.7 %collective-permute-start.22 = (f32[2,1,4,8,4]{4,3,2,1,0:T(8,128)S(1)}, f32[2,1,4,8,4]{4,3,2,1,0:T(8,128)S(1)}, u32[]{:S(2)}, u32[]{:S(2)}) collective-permute-start(f32[2,1,4,8,4]{4,3,2,1,0:T(8,128)S(1)} %get-tuple-element.55), channel_id=1, source_target_pairs={{0,24},{32,56},{1,25},{33,57},{2,26},{34,58},{3,27},{35,59},{8,0},... | collective-permute-start | bytes 3080 | tf_op jit(solution)/shard_map/ppermute | solution.py:58
  120.4 4.3 %collective-permute-start.23 = (f32[2,2,1,8,4]{4,3,2,1,0:T(8,128)S(1)}, f32[2,2,1,8,4]{4,3,2,1,0:T(8,128)S(1)}, u32[]{:S(2)}, u32[]{:S(2)}) collective-permute-start(f32[2,2,1,8,4]{4,3,2,1,0:T(8,128)S(1)} %get-tuple-element.62), channel_id=1, source_target_pairs={{0,32},{32,1},{1,33},{33,2},{2,34},{34,3},{3,35},{35,0},{8,40},{40... | collective-permute-start | bytes 1544 | tf_op jit(solution)/shard_map/ppermute | solution.py:57
  123.8 4.4 %collective-permute-start.24 = (f32[2,2,1,8,4]{4,3,2,1,0:T(8,128)S(1)}, f32[2,2,1,8,4]{4,3,2,1,0:T(8,128)S(1)}, u32[]{:S(2)}, u32[]{:S(2)}) collective-permute-start(f32[2,2,1,8,4]{4,3,2,1,0:T(8,128)S(1)} %get-tuple-element.63), channel_id=1, source_target_pairs={{0,35},{32,0},{1,32},{33,1},{2,33},{34,2},{3,34},{35,3},{8,43},{40... | collective-permute-start | bytes 1544 | tf_op jit(solution)/shard_map/ppermute | solution.py:58
  128.4 6.8 %collective-permute-start.25 = (f32[16,128]{1,0:T(8,128)S(1)}, f32[16,128]{1,0:T(8,128)S(1)}, u32[]{:S(2)}, u32[]{:S(2)}) collective-permute-start(f32[16,128]{1,0:T(8,128)S(1)} %k_force.1), channel_id=1, source_target_pairs={{0,0},{32,1},{1,2},{33,3},{2,4},{34,5},{3,6},{35,7},{8,8},{40,9},{... | collective-permute-start | bytes 24584 | tf_op jit(solution)/shard_map/ppermute | solution.py:463
where the time goes:
time: 137 us; the launch traced here: 136 us
  starting transfers between devices  65.8 us (48%)
  waiting for transfers between devices  52.5 us (38%)
  Pallas kernels  11.4 us (8%)
  local copies, waits for them, and re-layouts  4.47 us (3%)
    ppermute x6, starting transfers between devices, collect(): from_down = lax.ppermute(to_up, AXES, shifted(axis, 1))  18.9 us
    ppermute x6, starting transfers between devices, spread(): after = lax.ppermute(first, AXES, shifted(axis, -1))  18 us
    ppermute x1, waiting for transfers between devices, shards(): packed = lax.ppermute(packed, AXES, MOVE_IN)  13.4 us
    ppermute x6, waiting for transfers between devices, collect(): from_up = lax.ppermute(to_down, AXES, shifted(axis, -1))  12.2 us
    ppermute x6, waiting for transfers between devices, spread(): after = lax.ppermute(first, AXES, shifted(axis, -1))  12 us
    ppermute x6, starting transfers between devices, spread(): before = lax.ppermute(last, AXES, shifted(axis, 1))  11.9 us
    pallas_call x9, Pallas kernels, call(): pl.pallas_call(kernel, out_shape=shapes, in_specs=[spec] * len(args), out...  11.4 us
    ppermute x6, starting transfers between devices, collect(): from_up = lax.ppermute(to_down, AXES, shifted(axis, -1))  10.4 us
  transfers between devices with their start and end apart: 26, of which 17 were waited for; matrix products, arithmetic and copies ran while one was open for 0% of the time, Pallas kernels for 4%

commit v1 on v0

--- a/solution.py
+++ b/solution.py
@@ -2,7 +2,7 @@
 
 import jax
 import jax.numpy as jnp
-import numpy as np
+
 from jax import lax
 from jax.experimental import pallas as pl
 from jax.experimental.pallas import tpu as pltpu
@@ -23,40 +23,91 @@
     return (x * SHAPE[1] + y) * SHAPE[2] + z
 
 
+def device(chip_x, chip_y, chip_z, core):
+    return flat((chip_z % 8) * 2 + core, chip_y, (chip_z // 8) * 4 + chip_x)
+
+
 def home(x, y, z):
     x, y, z = x % SHAPE[0], y % SHAPE[1], z % SHAPE[2]
-    chip_z, chip_x, core = x, z // 2, z % 2
-    return flat((chip_z % 8) * 2 + core, y, (chip_z // 8) * 4 + chip_x)
+    return device(*PLACE(x, y, z))
+
+
+def PLACE(x, y, z):
+    return z // 2, y, x, z % 2
 
 
 CELLS = [(x, y, z) for x in range(SHAPE[0]) for y in range(SHAPE[1]) for z in range(SHAPE[2])]
+CHIPS = [(x, y, z, c) for x in range(4) for y in range(4) for z in range(16) for c in range(2)]
 MOVE_IN = [(flat(*c), home(*c)) for c in CELLS]
 MOVE_OUT = [(b, a) for a, b in MOVE_IN]
-
-
-def shifted(axis, by):
-    step = [0, 0, 0]
-    step[axis] = by
-    return [(home(x, y, z), home(x + step[0], y + step[1], z + step[2])) for x, y, z in CELLS]
-
-
-def spread(cells):
-    for axis in (2, 1, 0):
-        last = lax.slice_in_dim(cells, 1, 2, axis=axis)
+UP = [(home(x, y, z), home(x, y, z + 1)) for x, y, z in CELLS]
+DOWN = [(b, a) for a, b in UP]
+
+
+def along(spot, axis, position, core):
+    spot = list(spot)
+    spot[axis], spot[3] = position, core
+    return device(*spot)
+
+
+def snake(axis, count):
+    pairs = []
+    for spot in CHIPS:
+        at, core = spot[axis], spot[3]
+        then = at + 1 - 2 * core
+        goal = along(spot, axis, then, core) if 0 <= then < count else along(spot, axis, at, 1 - core)
+        pairs.append((device(*spot), goal))
+    return pairs
+
+
+def ends(axis, count):
+    return [(device(*s), along(s, axis, count - 1 - s[axis], s[3])) for s in CHIPS if s[axis] in (0, count - 1)]
+
+
+RINGS = {0: (2, 16), 1: (1, 4)}
+FORTH = {a: snake(*r) for a, r in RINGS.items()}
+BACK = {a: [(j, i) for i, j in p] for a, p in FORTH.items()}
+ENDS = {a: ends(*r) for a, r in RINGS.items()}
+
+
+def send(x, pairs):
+    return lax.ppermute(x, AXES, pairs)
+
+
+def spots():
+    gx, gy, gz = (lax.axis_index(a) for a in AXES)
+    return {0: (gz // 4) * 8 + gx // 2, 1: gy, 2: gx % 2}
+
+
+def swap(axis, first, last, here):
+    at, upward, count = here[axis], here[2] == 0, RINGS[axis][1]
+    forth = send(jnp.where(upward, last, first), FORTH[axis])
+    ring = send(jnp.where(at == 0, first, last), ENDS[axis])
+    back = send(jnp.where(upward, first, last), BACK[axis])
+    before = jnp.where(at != 0, jnp.where(upward, forth, back), ring)
+    after = jnp.where(at != count - 1, jnp.where(upward, back, forth), ring)
+    return before, after
+
+
+def spread(low, high, here):
+    before, after = swap(0, low, high, here)
+    cells = jnp.concatenate([before, low, high, after], axis=0)
+    before, after = swap(1, cells[:, 0:1], cells[:, 1:2], here)
+    cells = jnp.concatenate([before, cells, after], axis=1)
+    before = send(cells[:, :, 1], UP)
+    after = send(cells[:, :, 0], DOWN)
+    return before, after, cells
+
+
+def collect(before, after, cells, here):
+    first = send(after, UP)
+    last = send(before, DOWN)
+    cells = cells + jnp.stack([first, last], axis=2)
+    for axis in (1, 0):
         first = lax.slice_in_dim(cells, 0, 1, axis=axis)
-        before = lax.ppermute(last, AXES, shifted(axis, 1))
-        after = lax.ppermute(first, AXES, shifted(axis, -1))
-        cells = jnp.concatenate([before, cells, after], axis=axis)
-    return cells
-
-
-def collect(cells):
-    for axis in (0, 1, 2):
-        to_down = lax.slice_in_dim(cells, 0, 1, axis=axis)
-        to_up = lax.slice_in_dim(cells, 3, 4, axis=axis)
-        from_down = lax.ppermute(to_up, AXES, shifted(axis, 1))
-        from_up = lax.ppermute(to_down, AXES, shifted(axis, -1))
-        cells = lax.slice_in_dim(cells, 1, 3, axis=axis) + jnp.concatenate([from_down, from_up], axis=axis)
+        last = lax.slice_in_dim(cells, 3, 4, axis=axis)
+        from_before, from_after = swap(axis, first, last, here)
+        cells = lax.slice_in_dim(cells, 1, 3, axis=axis) + jnp.concatenate([from_before, from_after], axis=axis)
     return cells
 
 
@@ -139,21 +190,74 @@
     return jnp.concatenate([lanes(packed[4 * k : 4 * k + 4]) for k in range(4)], axis=0)
 
 
-def ghost_slot(partners):
+def ghost_cell(partners):
     rows = partners - ATOMS
     cell = rows >> 3
     skip = jnp.zeros_like(cell)
     for start in (21, 23, 33, 35):
-        skip = skip + jnp.where(cell >= start, 16, 0)
-    return rows + skip
-
-
-def k_lists(packed_ref, out_ref, column_ref):
+        skip = skip + jnp.where(cell >= start, 2, 0)
+    full = cell + skip
+    return full >> 4, (full >> 2) & 3, full & 3, rows & 7
+
+
+def ghost_slot(partners):
+    p, q, r, atom = ghost_cell(partners)
+    column = p * 4 + q
+    slot = jnp.where(r == 0, column * 8, jnp.where(r == 3, column * 8 + 128, 256 + (column * 2 + r - 1) * 8)) + atom
+    return jnp.where(partners >= ATOMS, slot, -1)
+
+
+def k_pack(pos_in, kind_in, names_in, center_in, partner_in, live_in, out_ref, pos_ref, kind_ref, names_ref, center_ref, partner_ref, live_ref, sems):
+    moves = [
+        pltpu.make_async_copy(source, target, sems.at[i])
+        for i, (source, target) in enumerate(
+            [
+                (pos_in, pos_ref),
+                (kind_in, kind_ref),
+                (names_in, names_ref),
+                (center_in, center_ref),
+                (partner_in, partner_ref),
+                (live_in, live_ref),
+            ]
+        )
+    ]
+    for move in moves:
+        move.start()
+    out_ref[40:48] = jnp.zeros((8, 128), F32)
+    for move in moves:
+        move.wait()
+    for k in range(3):
+        for i in range(4):
+            out_ref[4 * k + i : 4 * k + i + 1] = pos_ref[k, 0, 0, 0:1, 128 * i : 128 * i + 128]
+    for i in range(4):
+        out_ref[12 + i : 13 + i] = kind_ref[0, 0, 0:1, 128 * i : 128 * i + 128].astype(F32)
+    out_ref[16:24] = center_ref[0, 0, 0].astype(F32)
+    out_ref[24:32] = partner_ref[0, 0, 0].astype(F32)
+    out_ref[32:40] = live_ref[0, 0, 0].astype(F32)
+    names = [names_ref[i, j, k : k + 1] for i in range(2) for j in range(2) for k in range(2)]
+    names.append(jnp.full((1, 64), -1, jnp.int32))
+    out_ref[40:41] = jnp.concatenate(names, axis=1).astype(F32)
+
+
+def pack(*args):
+    return pl.pallas_call(
+        k_pack,
+        out_shape=jax.ShapeDtypeStruct((48, 128), F32),
+        in_specs=[pl.BlockSpec(memory_space=pltpu.MemorySpace.HBM)] * len(args),
+        out_specs=pl.BlockSpec(memory_space=pltpu.VMEM),
+        scratch_shapes=[pltpu.VMEM(a.shape, a.dtype) for a in args] + [pltpu.SemaphoreType.DMA((len(args),))],
+        compiler_params=pltpu.CompilerParams(vmem_limit_bytes=48 * 1024 * 1024),
+        name="k_pack",
+    )(*args)
+
+
+def k_lists(packed_ref, low_ref, high_ref, column_ref):
     packed = packed_ref[...]
     names = packed[40:41].astype(jnp.int32)
     found = pick(own_table(packed), match(names, ATOMS), 3)
-    wide = jnp.concatenate([found, jnp.zeros((4, 128), F32)], axis=0)
-    out_ref[...] = wide.T[:LIST, :4]
+    wide = jnp.concatenate([found, jnp.zeros((124, 128), F32)], axis=0).T
+    low_ref[...] = wide[:32]
+    high_ref[...] = wide[32:64]
     column_ref[...] = jnp.broadcast_to(packed[40:41], (8, 128)).T[:LIST]
 
 
@@ -168,14 +272,20 @@
     out_ref[5:8] = jnp.zeros((3, PAIRS), F32)
 
 
-def k_features(packed_ref, part_ref, ghost_ref, shift_ref, column_ref, wb_ref, wav_ref, msg_ref, scal_ref, pre_ref, av_ref):
+def k_features(
+    packed_ref, part_ref, before_ref, after_ref, cells_ref, column_ref, wb_ref, wav_ref, low_ref, high_ref, scal_ref, pre_ref, av_ref
+):
     packed = packed_ref[...]
     part = part_ref[...]
-    ghost = ghost_ref[...] + shift_ref[...]
-    slots = match(ghost_slot(partners_of(packed)), 512)
+    ghost = jnp.concatenate([before_ref[...], after_ref[...], cells_ref[...]], axis=0).T[0:8]
+    partners = partners_of(packed)
+    slots = match(ghost_slot(partners), 512)
     pieces = split3(ghost)
-    far = dot(pieces[0], slots, 0, 0) + (dot(pieces[1], slots, 0, 0) + dot(pieces[2], slots, 0, 0))
-    disp = part[0:3] + far[0:3]
+    far = dot(jnp.concatenate(pieces, axis=0), slots, 1, 0)
+    far = far[0:8] + (far[8:16] + far[16:24])
+    moved = [jnp.where(c == 0, -6.0, jnp.where(c == 3, 6.0, 0.0)) for c in ghost_cell(partners)[:3]]
+    moved = jnp.where(partners >= ATOMS, jnp.concatenate(moved, axis=0), 0.0)
+    disp = part[0:3] + (far[0:3] + moved)
     partner_kind = part[3:4] + far[3:4]
     center_kind = part[4:5]
     radius = jnp.sqrt(jnp.sum(disp * disp, axis=0, keepdims=True) + 0.25)
@@ -197,7 +307,9 @@
     a = av[:CHAN]
     terms = jnp.concatenate([unit[k : k + 1] * a for k in range(3)], axis=0)
     named = jnp.where(column_ref[:, 0:1].astype(jnp.int32) == centers_of(packed), 1.0, 0.0).astype(BF16)
-    msg_ref[...] = put_rows(terms, named)
+    msg = put_rows(terms, named)
+    low_ref[...] = msg[:32]
+    high_ref[...] = msg[32:]
     scal_ref[0:3] = unit
     scal_ref[3:4] = radius
     scal_ref[4:5] = inv
@@ -233,12 +345,30 @@
     nav_ref[...] = weighted(wav_ref[...], tangent)
 
 
-def k_energy(packed_ref, scal_ref, av_ref, ghost_ref, ei_ref, ejown_ref, hid_ref, wm_ref, wo_ref, msg_ref, ej_ref, h_ref, tb_ref):
+def k_energy(
+    packed_ref,
+    scal_ref,
+    av_ref,
+    before_ref,
+    after_ref,
+    cells_ref,
+    ei_ref,
+    ejown_ref,
+    hid_ref,
+    wm_ref,
+    wo_ref,
+    to_before_ref,
+    to_after_ref,
+    to_cells_ref,
+    ej_ref,
+    h_ref,
+    tb_ref,
+):
     packed = packed_ref[...]
     scal = scal_ref[...]
     unit, cut = scal[0:3], scal[5:6]
     slots = match(ghost_slot(partners_of(packed)), 512)
-    high, low = split2(ghost_ref[...])
+    high, low = split2(jnp.concatenate([before_ref[...], after_ref[...], cells_ref[...]], axis=0))
     ej = ejown_ref[...] + (dot(high, slots, 0, 0) + dot(low, slots, 0, 0))
     ei = ei_ref[...]
     coupling = 0.0
@@ -254,7 +384,10 @@
     tbar = weighted_t(mix, hbar)
     cbar = tbar * v
     back = jnp.concatenate([cbar * ei[k * CHAN : (k + 1) * CHAN] for k in range(3)], axis=0)
-    msg_ref[...] = put_rows(back, slots)
+    msg = put_rows(back, slots)
+    to_before_ref[...] = msg[:128]
+    to_after_ref[...] = msg[128:256]
+    to_cells_ref[...] = msg[256:]
     ej_ref[...] = ej
     h_ref[...] = h
     tb_ref[...] = tbar
@@ -301,7 +434,19 @@
     part_ref[...] = jnp.concatenate(along + [rbar, jnp.zeros((4, PAIRS), F32)], axis=0)
 
 
-def k_env_back(packed_ref, scal_ref, av_ref, nav_ref, part_ref, back_ref, column_ref, msg_ref, dbar_ref):
+def k_env_back(
+    packed_ref,
+    scal_ref,
+    av_ref,
+    nav_ref,
+    part_ref,
+    back_ref,
+    column_ref,
+    to_before_ref,
+    to_after_ref,
+    to_cells_ref,
+    dbar_ref,
+):
     packed = packed_ref[...]
     scal = scal_ref[...]
     unit, inv = scal[0:3], scal[4:5]
@@ -320,7 +465,10 @@
         rbar = rbar - inv * along[k] * unit[k : k + 1]
     dbar = jnp.concatenate([along[k] * inv + rbar * unit[k : k + 1] for k in range(3)] + [jnp.zeros((5, PAIRS), F32)], axis=0)
     slots = match(ghost_slot(partners_of(packed)), 512)
-    msg_ref[...] = put_rows(dbar, slots)[:, :4]
+    msg = jnp.concatenate([put_rows(dbar, slots), jnp.zeros((512, 120), F32)], axis=1)
+    to_before_ref[...] = msg[:128]
+    to_after_ref[...] = msg[128:256]
+    to_cells_ref[...] = msg[256:]
     dbar_ref[...] = dbar
 
 
@@ -334,8 +482,7 @@
     named = jnp.where(
         column_ref[:, 0:1].astype(jnp.int32) == lax.broadcasted_iota(jnp.int32, (LIST, ATOMS), 1), 1.0, 0.0
     ).astype(BF16)
-    high, mid, low = split3(back_ref[...])
-    returned = dot(high, named, 0, 0) + (dot(mid, named, 0, 0) + dot(low, named, 0, 0))
+    returned = pick(back_ref[...].T[0:8], named, 3)
     total = -(own_ref[0:3] + returned[0:3])
     energy = energy_ref[...]
     for k in range(3):
@@ -343,6 +490,14 @@
             out_ref[4 * k + i : 4 * k + i + 1] = total[k : k + 1, 128 * i : 128 * i + 128]
     for i in range(4):
         out_ref[12 + i : 13 + i] = energy[0:1, 128 * i : 128 * i + 128]
+
+
+def k_unpack(in_ref, force_ref, energy_ref):
+    for k in range(3):
+        for i in range(4):
+            force_ref[k, 0, 0, 0:1, 128 * i : 128 * i + 128] = in_ref[4 * k + i : 4 * k + i + 1]
+    for i in range(4):
+        energy_ref[0, 0, 0:1, 128 * i : 128 * i + 128] = in_ref[12 + i : 13 + i]
 
 
 def call(kernel, outs, *args):
@@ -356,16 +511,6 @@
         compiler_params=pltpu.CompilerParams(vmem_limit_bytes=48 * 1024 * 1024),
         name=kernel.__name__,
     )(*args)
-
-
-GRID_SHIFT = np.zeros((4, 4, 4, 8, 4), np.float32)
-for _axis in range(3):
-    _at = [slice(None)] * 3
-    _at[_axis] = 0
-    GRID_SHIFT[tuple(_at) + (slice(None), _axis)] = -6.0
-    _at[_axis] = 3
-    GRID_SHIFT[tuple(_at) + (slice(None), _axis)] = 6.0
-GRID_SHIFT = GRID_SHIFT.reshape(512, 4)
 
 
 def shards(
@@ -383,33 +528,24 @@
     w_mix,
     w_out,
 ):
-    packed = jnp.concatenate(
-        [
-            positions.reshape(12, 128),
-            species.reshape(4, 128).astype(F32),
-            pair_center.reshape(8, 128).astype(F32),
-            pair_partner.reshape(8, 128).astype(F32),
-            pair_slot_live.reshape(8, 128).astype(F32),
-            jnp.pad(send_lists.reshape(1, LIST).astype(F32), ((0, 7), (0, 64)), constant_values=-1.0),
-        ],
-        axis=0,
-    )
+    packed = pack(positions, species, send_lists, pair_center, pair_partner, pair_slot_live)
+    here = spots()
     zeros = jnp.zeros((2, 128), F32)
     wb = jnp.concatenate([w_basis, emb_center, zeros, emb_partner, zeros], axis=0)
     wav = jnp.concatenate([w_env, w_value], axis=1)
     wo = w_out.reshape(128, 1)
 
-    packed = lax.ppermute(packed, AXES, MOVE_IN)
-    msg, column = call(k_lists, [(LIST, 4), (LIST, 8)], packed)
+    packed = send(packed, MOVE_IN)
+    low, high, column = call(k_lists, [(32, 128), (32, 128), (LIST, 8)], packed)
     (part,) = call(k_own_pairs, [(8, PAIRS)], packed)
-    ghost = spread(msg.reshape(2, 2, 2, 8, 4)).reshape(512, 4)
-    msg, scal, pre, av = call(
+    low, high = low.reshape(1, 2, 2, 8, 128), high.reshape(1, 2, 2, 8, 128)
+    ghosts = [g.reshape(-1, 128) for g in spread(low, high, here)]
+    low, high, scal, pre, av = call(
         k_features,
-        [(LIST, 192), (8, PAIRS), (128, PAIRS), (128, PAIRS)],
+        [(32, 192), (32, 192), (8, PAIRS), (128, PAIRS), (128, PAIRS)],
         packed,
         part,
-        ghost,
-        jnp.asarray(GRID_SHIFT),
+        *ghosts,
         column,
         wb,
         wav,
@@ -425,14 +561,15 @@
         wav,
         w_mix,
     )
-    ghost = spread(msg.reshape(2, 2, 2, 8, 192)).reshape(512, 192)
-    msg, ej, h, tbar = call(
+    low, high = low.reshape(1, 2, 2, 8, 192), high.reshape(1, 2, 2, 8, 192)
+    ghosts = [g.reshape(-1, 192) for g in spread(low, high, here)]
+    before, after, cells, ej, h, tbar = call(
         k_energy,
-        [(512, 192), (192, PAIRS), (128, PAIRS), (CHAN, PAIRS)],
+        [(128, 192), (128, 192), (256, 192), (192, PAIRS), (128, PAIRS), (CHAN, PAIRS)],
         packed,
         scal,
         av,
-        ghost,
+        *ghosts,
         ei,
         ej,
         hid,
@@ -455,13 +592,17 @@
         w_mix,
         wo,
     )
-    back = collect(msg.reshape(4, 4, 4, 8, 192)).reshape(LIST, 192)
-    msg, dbar = call(k_env_back, [(512, 4), (8, PAIRS)], packed, scal, av, nav, part, back, column)
+    before, after = before.reshape(4, 4, 8, 192), after.reshape(4, 4, 8, 192)
+    back = collect(before, after, cells.reshape(4, 4, 2, 8, 192), here).reshape(LIST, 192)
+    before, after, cells, dbar = call(
+        k_env_back, [(128, 128), (128, 128), (256, 128), (8, PAIRS)], packed, scal, av, nav, part, back, column
+    )
     (own,) = call(k_own_force, [(8, ATOMS)], packed, dbar)
-    back = collect(msg.reshape(4, 4, 4, 8, 4)).reshape(LIST, 4)
+    before, after = before.reshape(4, 4, 8, 128), after.reshape(4, 4, 8, 128)
+    back = collect(before, after, cells.reshape(4, 4, 2, 8, 128), here).reshape(LIST, 128)
     (out,) = call(k_force, [(16, 128)], own, back, column, energy)
-    out = lax.ppermute(out, AXES, MOVE_OUT)
-    return out[:12].reshape(3, 1, 1, 1, ATOMS), out[12:].reshape(1, 1, 1, ATOMS)
+    out = send(out, MOVE_OUT)
+    return call(k_unpack, [(3, 1, 1, 1, ATOMS), (1, 1, 1, ATOMS)], out)
 
 
 def solution(mesh):

time: 137 us -> 123 us (0.90)
  the two profiles are of different devices: /device:TPU:23 before, /device:TPU:6 now
where the time goes in v1:
time: 123 us; the launch traced here: 122 us
  waiting for transfers between devices  55.2 us (45%)
  starting transfers between devices  46.8 us (38%)
  Pallas kernels  12 us (10%)
  local copies, waits for them, and re-layouts  6.41 us (5%)
    ppermute x34, waiting for transfers between devices, send(): return lax.ppermute(x, AXES, pairs)  55.2 us
    ppermute x34, starting transfers between devices, send(): return lax.ppermute(x, AXES, pairs)  46.8 us
    pallas_call x10, Pallas kernels, call(): pl.pallas_call(kernel, out_shape=shapes, in_specs=[spec] * len(args), out...  11.8 us
    unnamed x28, local copies, waits for them, and re-layouts  6.23 us
  transfers between devices with their start and end apart: 34, of which 19 were waited for; matrix products, arithmetic and copies ran while one was open for 0% of the time, Pallas kernels for 5%

profile of v1, /device:TPU:6, one launch (start us, length us, event | category | flops | bytes accessed | tf_op | source)
XLA Modules:
  0.0 122.0 jit_solution(12093684205557759974)
XLA Ops:
  0.6 0.7 copy-done.1
  1.3 0.7 copy-done.2
  2.0 0.7 copy-done.3
  2.7 0.7 copy-done.4
  3.4 0.7 copy-done.5
  4.1 0.7 copy-done.6
  4.9 2.8 %collective-permute-start = (f32[48,128]{1,0:T(8,128)S(1)}, f32[48,128]{1,0:T(8,128)S(1)}, u32[]{:S(2)}, u32[]{:S(2)}) collective-permute-start(f32[48,128]{1,0:T(8,128)S(1)} %k_pack.1), channel_id=1, source_target_pairs={{0,0},{1,32},{2,1},{3,33},{4,2},{5,34},{6,3},{7,35},{8,8},{9,40},{... | collective-permute-start | bytes 73736 | tf_op jit(solution)/shard_map/ppermute | solution.py:74
  7.7 15.0 %collective-permute-done.packed_ref = f32[48,128]{1,0:T(8,128)S(1)} collective-permute-done((f32[48,128]{1,0:T(8,128)S(1)}, f32[48,128]{1,0:T(8,128)S(1)}, u32[]{:S(2)}, u32[]{:S(2)}) %collective-permute-start) | collective-permute-done | bytes 24608 | tf_op jit(solution)/shard_map/ppermute | solution.py:74
  23.0 1.9 %collective-permute-start.3 = (f32[1,2,2,8,128]{4,3,2,1,0:T(8,128)S(1)}, f32[1,2,2,8,128]{4,3,2,1,0:T(8,128)S(1)}, u32[]{:S(2)}, u32[]{:S(2)}) collective-permute-start(f32[1,2,2,8,128]{4,3,2,1,0:T(8,128)S(1)} %get-tuple-element.96), channel_id=1, source_target_pairs={{0,452},{32,484},{452,0},{484,32},{8,460},{40,492},{460,8},{492,40... | collective-permute-start | bytes 49160 | tf_op jit(solution)/shard_map/ppermute | solution.py:74
  25.4 4.4 %collective-permute-done.3 = f32[1,2,2,8,128]{4,3,2,1,0:T(8,128)S(1)} collective-permute-done((f32[1,2,2,8,128]{4,3,2,1,0:T(8,128)S(1)}, f32[1,2,2,8,128]{4,3,2,1,0:T(8,128)S(1)}, u32[]{:S(2)}, u32[]{:S(2)}) %collective-permute-start.3) | collective-permute-done | bytes 16416 | tf_op jit(solution)/shard_map/ppermute | solution.py:74
  29.9 1.6 %collective-permute-start.4 = (f32[4,1,2,8,128]{4,3,2,1,0:T(8,128)S(1)}, f32[4,1,2,8,128]{4,3,2,1,0:T(8,128)S(1)}, u32[]{:S(2)}, u32[]{:S(2)}) collective-permute-start(f32[4,1,2,8,128]{4,3,2,1,0:T(8,128)S(1)} %get-tuple-element.88), channel_id=1, source_target_pairs={{0,8},{32,0},{64,72},{96,64},{128,136},{160,128},{192,200},{224,19... | collective-permute-start | bytes 98312 | tf_op jit(solution)/shard_map/ppermute | solution.py:74
  31.5 3.4 %collective-permute-start.6 = (f32[4,1,2,8,128]{4,3,2,1,0:T(8,128)S(1)}, f32[4,1,2,8,128]{4,3,2,1,0:T(8,128)S(1)}, u32[]{:S(2)}, u32[]{:S(2)}) collective-permute-start(f32[4,1,2,8,128]{4,3,2,1,0:T(8,128)S(1)} %get-tuple-element.89), channel_id=1, source_target_pairs={{0,24},{32,56},{64,88},{96,120},{128,152},{160,184},{192,216},{224... | collective-permute-start | bytes 98312 | tf_op jit(solution)/shard_map/ppermute | solution.py:74
  35.0 0.7 copy-done.8
  35.8 0.6 copy-done.9
  36.4 2.1 %collective-permute-done.6 = f32[4,1,2,8,128]{4,3,2,1,0:T(8,128)S(1)} collective-permute-done((f32[4,1,2,8,128]{4,3,2,1,0:T(8,128)S(1)}, f32[4,1,2,8,128]{4,3,2,1,0:T(8,128)S(1)}, u32[]{:S(2)}, u32[]{:S(2)}) %collective-permute-start.6) | collective-permute-done | bytes 32800 | tf_op jit(solution)/shard_map/ppermute | solution.py:74
  39.9 0.9 collective-permute-done.8
  40.8 1.8 %collective-permute-done.7 = f32[4,4,8,128]{3,2,1,0:T(8,128)S(1)} collective-permute-done((f32[4,4,8,128]{3,2,1,0:T(8,128)S(1)}, f32[4,4,8,128]{3,2,1,0:T(8,128)S(1)}, u32[]{:S(2)}, u32[]{:S(2)}) %collective-permute-start.7) | collective-permute-done | bytes 65568 | tf_op jit(solution)/shard_map/ppermute | solution.py:74
  42.6 1.5 %k_features.1 = (f32[32,192]{1,0:T(8,128)S(1)}, f32[32,192]{1,0:T(8,128)S(1)}, f32[8,1024]{1,0:T(8,128)S(1)}, f32[128,1024]{1,0:T(8,128)S(1)}, f32[128,1024]{1,0:T(8,128)S(1)}) custom-call(f32[48,128]{1,0:T(8,128)S(1)} %collective-permute-done.packed_ref, f32[8,1024]{1,0:T(8,128)S(1)} %k_own_pairs.1.part_ref, f32[128,128]{1,0:T(8,128)S(1)} %bitcast.52, ...), custom_call_target="tpu_custom_call" | custom-call | tf_op jit(solution)/shard_map/k_features/pallas_call | solution.py:506
  44.2 7.1 %collective-permute-start.11 = (f32[1,2,2,8,192]{4,3,2,1,0:T(8,128)S(1)}, f32[1,2,2,8,192]{4,3,2,1,0:T(8,128)S(1)}, u32[]{:S(2)}, u32[]{:S(2)}) collective-permute-start(f32[1,2,2,8,192]{4,3,2,1,0:T(8,128)S(1)} %get-tuple-element.86), channel_id=1, source_target_pairs={{0,452},{32,484},{452,0},{484,32},{8,460},{40,492},{460,8},{492,40... | collective-permute-start | bytes 73736 | tf_op jit(solution)/shard_map/ppermute | solution.py:74
  51.3 1.8 %collective-permute-done.11 = f32[1,2,2,8,192]{4,3,2,1,0:T(8,128)S(1)} collective-permute-done((f32[1,2,2,8,192]{4,3,2,1,0:T(8,128)S(1)}, f32[1,2,2,8,192]{4,3,2,1,0:T(8,128)S(1)}, u32[]{:S(2)}, u32[]{:S(2)}) %collective-permute-start.11) | collective-permute-done | bytes 24608 | tf_op jit(solution)/shard_map/ppermute | solution.py:74
  53.1 2.1 %collective-permute-done.10 = f32[1,2,2,8,192]{4,3,2,1,0:T(8,128)S(1)} collective-permute-done((f32[1,2,2,8,192]{4,3,2,1,0:T(8,128)S(1)}, f32[1,2,2,8,192]{4,3,2,1,0:T(8,128)S(1)}, u32[]{:S(2)}, u32[]{:S(2)}) %collective-permute-start.10) | collective-permute-done | bytes 24608 | tf_op jit(solution)/shard_map/ppermute | solution.py:74
  55.3 3.1 %collective-permute-start.14 = (f32[4,1,2,8,192]{4,3,2,1,0:T(8,128)S(1)}, f32[4,1,2,8,192]{4,3,2,1,0:T(8,128)S(1)}, u32[]{:S(2)}, u32[]{:S(2)}) collective-permute-start(f32[4,1,2,8,192]{4,3,2,1,0:T(8,128)S(1)} %get-tuple-element.70), channel_id=1, source_target_pairs={{0,24},{32,56},{64,88},{96,120},{128,152},{160,184},{192,216},{224... | collective-permute-start | bytes 147464 | tf_op jit(solution)/shard_map/ppermute | solution.py:74
  58.4 4.5 %collective-permute-done.14 = f32[4,1,2,8,192]{4,3,2,1,0:T(8,128)S(1)} collective-permute-done((f32[4,1,2,8,192]{4,3,2,1,0:T(8,128)S(1)}, f32[4,1,2,8,192]{4,3,2,1,0:T(8,128)S(1)}, u32[]{:S(2)}, u32[]{:S(2)}) %collective-permute-start.14) | collective-permute-done | bytes 49184 | tf_op jit(solution)/shard_map/ppermute | solution.py:74
  62.9 1.2 collective-permute-start.16
  64.1 0.7 copy-done.12
  64.9 2.4 %k_own_env.1 = (f32[192,1024]{1,0:T(8,128)S(1)}, f32[192,1024]{1,0:T(8,128)S(1)}, f32[128,1024]{1,0:T(8,128)S(1)}, f32[128,1024]{1,0:T(8,128)S(1)}, f32[128,1024]{1,0:T(8,128)S(1)}, /*index=5*/f32[128,1024]{1,0:T(8,128)S(1)}) custom-call(f32[48,128]{1,0:T(8,128)S(1)} %collective-permute-done.packed_ref, f32[8,1024]{1,0:T(8,128)S(1)} %get-tuple-element.31.scal_ref, ...), custom_call_target="tpu_custom_call" | custom-call | tf_op jit(solution)/shard_map/k_own_env/pallas_call | solution.py:506
  67.3 1.2 collective-permute-done.15
  68.5 2.2 %k_energy.1 = (f32[128,192]{1,0:T(8,128)S(1)}, f32[128,192]{1,0:T(8,128)S(1)}, f32[256,192]{1,0:T(8,128)S(1)}, f32[192,1024]{1,0:T(8,128)S(1)}, f32[128,1024]{1,0:T(8,128)S(1)}, /*index=5*/f32[64,1024]{1,0:T(8,128)S(1)}) custom-call(f32[48,128]{1,0:T(8,128)S(1)} %collective-permute-done.packed_ref, f32[8,1024]{1,0:T(8,128)S(1)} %get-tuple-element.31.scal_ref, ...), custom_call_target="tpu_custom_call" | custom-call | tf_op jit(solution)/shard_map/k_energy/pallas_call | solution.py:506
  71.0 1.5 %collective-permute-start.18 = (f32[4,4,8,192]{3,2,1,0:T(8,128)S(1)}, f32[4,4,8,192]{3,2,1,0:T(8,128)S(1)}, u32[]{:S(2)}, u32[]{:S(2)}) collective-permute-start(f32[4,4,8,192]{3,2,1,0:T(8,128)S(1)} %bitcast.53), channel_id=1, source_target_pairs={{32,0},{1,32},{33,1},{2,33},{34,2},{3,34},{35,3},{0,35},{40,8},{9,... | collective-permute-start | bytes 294920 | tf_op jit(solution)/shard_map/ppermute | solution.py:74
  72.5 2.6 %collective-permute-done.17 = f32[4,4,8,192]{3,2,1,0:T(8,128)S(1)} collective-permute-done((f32[4,4,8,192]{3,2,1,0:T(8,128)S(1)}, f32[4,4,8,192]{3,2,1,0:T(8,128)S(1)}, u32[]{:S(2)}, u32[]{:S(2)}) %collective-permute-start.17) | collective-permute-done | bytes 98336 | tf_op jit(solution)/shard_map/ppermute | solution.py:74
  75.2 7.3 %collective-permute-start.21 = (f32[4,1,2,8,192]{4,3,2,1,0:T(8,128)S(1)}, f32[4,1,2,8,192]{4,3,2,1,0:T(8,128)S(1)}, u32[]{:S(2)}, u32[]{:S(2)}) collective-permute-start(f32[4,1,2,8,192]{4,3,2,1,0:T(8,128)S(1)} %get-tuple-element.55), channel_id=1, source_target_pairs={{0,24},{32,56},{64,88},{96,120},{128,152},{160,184},{192,216},{224... | collective-permute-start | bytes 147464 | tf_op jit(solution)/shard_map/ppermute | solution.py:74
  82.8 1.9 %collective-permute-done.21 = f32[4,1,2,8,192]{4,3,2,1,0:T(8,128)S(1)} collective-permute-done((f32[4,1,2,8,192]{4,3,2,1,0:T(8,128)S(1)}, f32[4,1,2,8,192]{4,3,2,1,0:T(8,128)S(1)}, u32[]{:S(2)}, u32[]{:S(2)}) %collective-permute-start.21) | collective-permute-done | bytes 49184 | tf_op jit(solution)/shard_map/ppermute | solution.py:74
  84.7 2.1 %collective-permute-done.20 = f32[4,1,2,8,192]{4,3,2,1,0:T(8,128)S(1)} collective-permute-done((f32[4,1,2,8,192]{4,3,2,1,0:T(8,128)S(1)}, f32[4,1,2,8,192]{4,3,2,1,0:T(8,128)S(1)}, u32[]{:S(2)}, u32[]{:S(2)}) %collective-permute-start.20) | collective-permute-done | bytes 49184 | tf_op jit(solution)/shard_map/ppermute | solution.py:74
  86.9 3.1 %collective-permute-start.24 = (f32[1,2,2,8,192]{4,3,2,1,0:T(8,128)S(1)}, f32[1,2,2,8,192]{4,3,2,1,0:T(8,128)S(1)}, u32[]{:S(2)}, u32[]{:S(2)}) collective-permute-start(f32[1,2,2,8,192]{4,3,2,1,0:T(8,128)S(1)} %get-tuple-element.67), channel_id=1, source_target_pairs={{0,452},{32,484},{452,0},{484,32},{8,460},{40,492},{460,8},{492,40... | collective-permute-start | bytes 73736 | tf_op jit(solution)/shard_map/ppermute | solution.py:74
  90.0 2.4 %k_direct.1 = (f32[8,1024]{1,0:T(8,128)S(1)}, f32[4,512]{1,0:T(4,128)S(1)}) custom-call(f32[48,128]{1,0:T(8,128)S(1)} %collective-permute-done.packed_ref, f32[8,1024]{1,0:T(8,128)S(1)} %get-tuple-element.31.scal_ref, f32[128,1024]{1,0:T(8,128)S(1)} %get-tuple-element.32.av_ref, f32[128,1024]{1,0:T(8,128)S(1)} %get-tuple-element.34.nav_ref, ...), custom_call_target="tpu_custom_call" | custom-call | tf_op jit(solution)/shard_map/k_direct/pallas_call | solution.py:506
  92.4 1.5 %collective-permute-done.24 = f32[1,2,2,8,192]{4,3,2,1,0:T(8,128)S(1)} collective-permute-done((f32[1,2,2,8,192]{4,3,2,1,0:T(8,128)S(1)}, f32[1,2,2,8,192]{4,3,2,1,0:T(8,128)S(1)}, u32[]{:S(2)}, u32[]{:S(2)}) %collective-permute-start.24) | collective-permute-done | bytes 24608 | tf_op jit(solution)/shard_map/ppermute | solution.py:74
  93.9 1.2 k_env_back.1
  95.2 1.7 %collective-permute-start.26 = (f32[4,4,8,128]{3,2,1,0:T(8,128)S(1)}, f32[4,4,8,128]{3,2,1,0:T(8,128)S(1)}, u32[]{:S(2)}, u32[]{:S(2)}) collective-permute-start(f32[4,4,8,128]{3,2,1,0:T(8,128)S(1)} %bitcast.55), channel_id=1, source_target_pairs={{32,0},{1,32},{33,1},{2,33},{34,2},{3,34},{35,3},{0,35},{40,8},{9,... | collective-permute-start | bytes 196616 | tf_op jit(solution)/shard_map/ppermute | solution.py:74
  96.9 1.9 %collective-permute-done.25 = f32[4,4,8,128]{3,2,1,0:T(8,128)S(1)} collective-permute-done((f32[4,4,8,128]{3,2,1,0:T(8,128)S(1)}, f32[4,4,8,128]{3,2,1,0:T(8,128)S(1)}, u32[]{:S(2)}, u32[]{:S(2)}) %collective-permute-start.25) | collective-permute-done | bytes 65568 | tf_op jit(solution)/shard_map/ppermute | solution.py:74
  98.9 4.4 %collective-permute-start.29 = (f32[4,1,2,8,128]{4,3,2,1,0:T(8,128)S(1)}, f32[4,1,2,8,128]{4,3,2,1,0:T(8,128)S(1)}, u32[]{:S(2)}, u32[]{:S(2)}) collective-permute-start(f32[4,1,2,8,128]{4,3,2,1,0:T(8,128)S(1)} %get-tuple-element.64), channel_id=1, source_target_pairs={{0,24},{32,56},{64,88},{96,120},{128,152},{160,184},{192,216},{224... | collective-permute-start | bytes 98312 | tf_op jit(solution)/shard_map/ppermute | solution.py:74
  103.8 2.2 %collective-permute-done.29 = f32[4,1,2,8,128]{4,3,2,1,0:T(8,128)S(1)} collective-permute-done((f32[4,1,2,8,128]{4,3,2,1,0:T(8,128)S(1)}, f32[4,1,2,8,128]{4,3,2,1,0:T(8,128)S(1)}, u32[]{:S(2)}, u32[]{:S(2)}) %collective-permute-start.29) | collective-permute-done | bytes 32800 | tf_op jit(solution)/shard_map/ppermute | solution.py:74
  105.9 1.3 %collective-permute-done.28 = f32[4,1,2,8,128]{4,3,2,1,0:T(8,128)S(1)} collective-permute-done((f32[4,1,2,8,128]{4,3,2,1,0:T(8,128)S(1)}, f32[4,1,2,8,128]{4,3,2,1,0:T(8,128)S(1)}, u32[]{:S(2)}, u32[]{:S(2)}) %collective-permute-start.28) | collective-permute-done | bytes 32800 | tf_op jit(solution)/shard_map/ppermute | solution.py:74
  107.9 2.9 %collective-permute-start.32 = (f32[1,2,2,8,128]{4,3,2,1,0:T(8,128)S(1)}, f32[1,2,2,8,128]{4,3,2,1,0:T(8,128)S(1)}, u32[]{:S(2)}, u32[]{:S(2)}) collective-permute-start(f32[1,2,2,8,128]{4,3,2,1,0:T(8,128)S(1)} %get-tuple-element.83), channel_id=1, source_target_pairs={{0,452},{32,484},{452,0},{484,32},{8,460},{40,492},{460,8},{492,40... | collective-permute-start | bytes 49160 | tf_op jit(solution)/shard_map/ppermute | solution.py:74
  110.8 0.6 k_own_force.1.own_ref
  111.5 3.2 %collective-permute-done.32 = f32[1,2,2,8,128]{4,3,2,1,0:T(8,128)S(1)} collective-permute-done((f32[1,2,2,8,128]{4,3,2,1,0:T(8,128)S(1)}, f32[1,2,2,8,128]{4,3,2,1,0:T(8,128)S(1)}, u32[]{:S(2)}, u32[]{:S(2)}) %collective-permute-start.32) | collective-permute-done | bytes 16416 | tf_op jit(solution)/shard_map/ppermute | solution.py:74
  115.0 2.0 %collective-permute-start.33 = (f32[16,128]{1,0:T(8,128)S(1)}, f32[16,128]{1,0:T(8,128)S(1)}, u32[]{:S(2)}, u32[]{:S(2)}) collective-permute-start(f32[16,128]{1,0:T(8,128)S(1)} %k_force.1), channel_id=1, source_target_pairs={{0,0},{32,1},{1,2},{33,3},{2,4},{34,5},{3,6},{35,7},{8,8},{40,9},{... | collective-permute-start | bytes 24584 | tf_op jit(solution)/shard_map/ppermute | solution.py:74
  117.0 4.4 %collective-permute-done.33.in_ref = f32[16,128]{1,0:T(8,128)S(1)} collective-permute-done((f32[16,128]{1,0:T(8,128)S(1)}, f32[16,128]{1,0:T(8,128)S(1)}, u32[]{:S(2)}, u32[]{:S(2)}) %collective-permute-start.33) | collective-permute-done | bytes 8224 | tf_op jit(solution)/shard_map/ppermute | solution.py:74
  121.4 0.6 k_unpack.1
  (91 shorter events, 5.0 us)
Async XLA Ops:
  0.6 0.7 copy-start.1
  1.3 0.7 copy-start.2
  2.0 0.7 copy-start.3
  2.7 0.7 copy-start.4
  3.4 0.7 copy-start.5
  4.1 0.7 copy-start.6
  4.9 17.8 %collective-permute-start = (f32[48,128]{1,0:T(8,128)S(1)}, f32[48,128]{1,0:T(8,128)S(1)}, u32[]{:S(2)}, u32[]{:S(2)}) collective-permute-start(f32[48,128]{1,0:T(8,128)S(1)} %k_pack.1), channel_id=1, source_target_pairs={{0,0},{1,32},{2,1},{3,33},{4,2},{5,34},{6,3},{7,35},{8,8},{9,40},{... | collective-permute-start | bytes 73736 | tf_op jit(solution)/shard_map/ppermute | solution.py:74
  23.0 2.5 %collective-permute-start.1 = (f32[1,2,2,8,128]{4,3,2,1,0:T(8,128)S(1)}, f32[1,2,2,8,128]{4,3,2,1,0:T(8,128)S(1)}, u32[]{:S(2)}, u32[]{:S(2)}) collective-permute-start(f32[1,2,2,8,128]{4,3,2,1,0:T(8,128)S(1)} %get-tuple-element.95), channel_id=1, source_target_pairs={{0,64},{32,0},{64,128},{96,32},{128,192},{160,96},{192,256},{224,1... | collective-permute-start | bytes 49160 | tf_op jit(solution)/shard_map/ppermute | solution.py:74
  23.0 6.8 %collective-permute-start.3 = (f32[1,2,2,8,128]{4,3,2,1,0:T(8,128)S(1)}, f32[1,2,2,8,128]{4,3,2,1,0:T(8,128)S(1)}, u32[]{:S(2)}, u32[]{:S(2)}) collective-permute-start(f32[1,2,2,8,128]{4,3,2,1,0:T(8,128)S(1)} %get-tuple-element.96), channel_id=1, source_target_pairs={{0,452},{32,484},{452,0},{484,32},{8,460},{40,492},{460,8},{492,40... | collective-permute-start | bytes 49160 | tf_op jit(solution)/shard_map/ppermute | solution.py:74
  24.9 4.9 %collective-permute-start.2 = (f32[1,2,2,8,128]{4,3,2,1,0:T(8,128)S(1)}, f32[1,2,2,8,128]{4,3,2,1,0:T(8,128)S(1)}, u32[]{:S(2)}, u32[]{:S(2)}) collective-permute-start(f32[1,2,2,8,128]{4,3,2,1,0:T(8,128)S(1)} %get-tuple-element.97), channel_id=1, source_target_pairs={{64,0},{0,32},{128,64},{32,96},{192,128},{96,160},{256,192},{160,2... | collective-permute-start | bytes 49160 | tf_op jit(solution)/shard_map/ppermute | solution.py:74
  29.9 5.0 %copy-start.7 = (f32[128,64]{0,1:T(8,128)S(1)}, f32[128,64]{0,1:T(8,128)}, u32[]{:S(2)}) copy-start(f32[128,64]{0,1:T(8,128)} %param.22) | copy-start | bytes 98308
  29.9 6.5 %collective-permute-start.4 = (f32[4,1,2,8,128]{4,3,2,1,0:T(8,128)S(1)}, f32[4,1,2,8,128]{4,3,2,1,0:T(8,128)S(1)}, u32[]{:S(2)}, u32[]{:S(2)}) collective-permute-start(f32[4,1,2,8,128]{4,3,2,1,0:T(8,128)S(1)} %get-tuple-element.88), channel_id=1, source_target_pairs={{0,8},{32,0},{64,72},{96,64},{128,136},{160,128},{192,200},{224,19... | collective-permute-start | bytes 98312 | tf_op jit(solution)/shard_map/ppermute | solution.py:74
  31.5 7.0 %collective-permute-start.6 = (f32[4,1,2,8,128]{4,3,2,1,0:T(8,128)S(1)}, f32[4,1,2,8,128]{4,3,2,1,0:T(8,128)S(1)}, u32[]{:S(2)}, u32[]{:S(2)}) collective-permute-start(f32[4,1,2,8,128]{4,3,2,1,0:T(8,128)S(1)} %get-tuple-element.89), channel_id=1, source_target_pairs={{0,24},{32,56},{64,88},{96,120},{128,152},{160,184},{192,216},{224... | collective-permute-start | bytes 98312 | tf_op jit(solution)/shard_map/ppermute | solution.py:74
  34.9 3.9 %collective-permute-start.5 = (f32[4,1,2,8,128]{4,3,2,1,0:T(8,128)S(1)}, f32[4,1,2,8,128]{4,3,2,1,0:T(8,128)S(1)}, u32[]{:S(2)}, u32[]{:S(2)}) collective-permute-start(f32[4,1,2,8,128]{4,3,2,1,0:T(8,128)S(1)} %get-tuple-element.90), channel_id=1, source_target_pairs={{8,0},{0,32},{72,64},{64,96},{136,128},{128,160},{200,192},{192,22... | collective-permute-start | bytes 98312 | tf_op jit(solution)/shard_map/ppermute | solution.py:74
  34.9 0.8 copy-start.8
  35.7 0.7 copy-start.9
  35.7 0.7 copy-start.10
  35.7 0.7 copy-start.11
  38.8 1.9 %collective-permute-start.8 = (f32[4,4,8,128]{3,2,1,0:T(8,128)S(1)}, f32[4,4,8,128]{3,2,1,0:T(8,128)S(1)}, u32[]{:S(2)}, u32[]{:S(2)}) collective-permute-start(f32[4,4,8,128]{3,2,1,0:T(8,128)S(1)} %get-tuple-element.72), channel_id=1, source_target_pairs={{32,0},{1,32},{33,1},{2,33},{34,2},{3,34},{35,3},{0,35},{40,8},{9,... | collective-permute-start | bytes 196616 | tf_op jit(solution)/shard_map/ppermute | solution.py:74
  38.9 3.7 %collective-permute-start.7 = (f32[4,4,8,128]{3,2,1,0:T(8,128)S(1)}, f32[4,4,8,128]{3,2,1,0:T(8,128)S(1)}, u32[]{:S(2)}, u32[]{:S(2)}) collective-permute-start(f32[4,4,8,128]{3,2,1,0:T(8,128)S(1)} %get-tuple-element.73), channel_id=1, source_target_pairs={{0,32},{32,1},{1,33},{33,2},{2,34},{34,3},{3,35},{35,0},{8,40},{40... | collective-permute-start | bytes 196616 | tf_op jit(solution)/shard_map/ppermute | solution.py:74
  44.1 7.1 %collective-permute-start.9 = (f32[1,2,2,8,192]{4,3,2,1,0:T(8,128)S(1)}, f32[1,2,2,8,192]{4,3,2,1,0:T(8,128)S(1)}, u32[]{:S(2)}, u32[]{:S(2)}) collective-permute-start(f32[1,2,2,8,192]{4,3,2,1,0:T(8,128)S(1)} %get-tuple-element.85), channel_id=1, source_target_pairs={{0,64},{32,0},{64,128},{96,32},{128,192},{160,96},{192,256},{224,1... | collective-permute-start | bytes 73736 | tf_op jit(solution)/shard_map/ppermute | solution.py:74
  44.2 9.0 %collective-permute-start.11 = (f32[1,2,2,8,192]{4,3,2,1,0:T(8,128)S(1)}, f32[1,2,2,8,192]{4,3,2,1,0:T(8,128)S(1)}, u32[]{:S(2)}, u32[]{:S(2)}) collective-permute-start(f32[1,2,2,8,192]{4,3,2,1,0:T(8,128)S(1)} %get-tuple-element.86), channel_id=1, source_target_pairs={{0,452},{32,484},{452,0},{484,32},{8,460},{40,492},{460,8},{492,40... | collective-permute-start | bytes 73736 | tf_op jit(solution)/shard_map/ppermute | solution.py:74
  51.2 3.9 %collective-permute-start.10 = (f32[1,2,2,8,192]{4,3,2,1,0:T(8,128)S(1)}, f32[1,2,2,8,192]{4,3,2,1,0:T(8,128)S(1)}, u32[]{:S(2)}, u32[]{:S(2)}) collective-permute-start(f32[1,2,2,8,192]{4,3,2,1,0:T(8,128)S(1)} %get-tuple-element.87), channel_id=1, source_target_pairs={{64,0},{0,32},{128,64},{32,96},{192,128},{96,160},{256,192},{160,2... | collective-permute-start | bytes 73736 | tf_op jit(solution)/shard_map/ppermute | solution.py:74
  55.2 3.2 %collective-permute-start.12 = (f32[4,1,2,8,192]{4,3,2,1,0:T(8,128)S(1)}, f32[4,1,2,8,192]{4,3,2,1,0:T(8,128)S(1)}, u32[]{:S(2)}, u32[]{:S(2)}) collective-permute-start(f32[4,1,2,8,192]{4,3,2,1,0:T(8,128)S(1)} %get-tuple-element.69), channel_id=1, source_target_pairs={{0,8},{32,0},{64,72},{96,64},{128,136},{160,128},{192,200},{224,19... | collective-permute-start | bytes 147464 | tf_op jit(solution)/shard_map/ppermute | solution.py:74
  55.3 7.6 %collective-permute-start.14 = (f32[4,1,2,8,192]{4,3,2,1,0:T(8,128)S(1)}, f32[4,1,2,8,192]{4,3,2,1,0:T(8,128)S(1)}, u32[]{:S(2)}, u32[]{:S(2)}) collective-permute-start(f32[4,1,2,8,192]{4,3,2,1,0:T(8,128)S(1)} %get-tuple-element.70), channel_id=1, source_target_pairs={{0,24},{32,56},{64,88},{96,120},{128,152},{160,184},{192,216},{224... | collective-permute-start | bytes 147464 | tf_op jit(solution)/shard_map/ppermute | solution.py:74
  58.4 4.5 %collective-permute-start.13 = (f32[4,1,2,8,192]{4,3,2,1,0:T(8,128)S(1)}, f32[4,1,2,8,192]{4,3,2,1,0:T(8,128)S(1)}, u32[]{:S(2)}, u32[]{:S(2)}) collective-permute-start(f32[4,1,2,8,192]{4,3,2,1,0:T(8,128)S(1)} %get-tuple-element.71), channel_id=1, source_target_pairs={{8,0},{0,32},{72,64},{64,96},{136,128},{128,160},{200,192},{192,22... | collective-permute-start | bytes 147464 | tf_op jit(solution)/shard_map/ppermute | solution.py:74
  62.9 2.0 %copy-start = (f32[192,128]{1,0:T(8,128)S(1)}, f32[192,128]{1,0:T(8,128)}, u32[]{:S(2)}) copy-start(f32[192,128]{1,0:T(8,128)} %wm_ref.5) | copy-start | bytes 294916
  62.9 4.4 %collective-permute-start.16 = (f32[4,4,8,192]{3,2,1,0:T(8,128)S(1)}, f32[4,4,8,192]{3,2,1,0:T(8,128)S(1)}, u32[]{:S(2)}, u32[]{:S(2)}) collective-permute-start(f32[4,4,8,192]{3,2,1,0:T(8,128)S(1)} %get-tuple-element.57), channel_id=1, source_target_pairs={{32,0},{1,32},{33,1},{2,33},{34,2},{3,34},{35,3},{0,35},{40,8},{9,... | collective-permute-start | bytes 294920 | tf_op jit(solution)/shard_map/ppermute | solution.py:74
  64.1 0.7 copy-start.12
  64.1 4.4 %collective-permute-start.15 = (f32[4,4,8,192]{3,2,1,0:T(8,128)S(1)}, f32[4,4,8,192]{3,2,1,0:T(8,128)S(1)}, u32[]{:S(2)}, u32[]{:S(2)}) collective-permute-start(f32[4,4,8,192]{3,2,1,0:T(8,128)S(1)} %get-tuple-element.58), channel_id=1, source_target_pairs={{0,32},{32,1},{1,33},{33,2},{2,34},{34,3},{3,35},{35,0},{8,40},{40... | collective-permute-start | bytes 294920 | tf_op jit(solution)/shard_map/ppermute | solution.py:74
  70.7 4.4 %collective-permute-start.17 = (f32[4,4,8,192]{3,2,1,0:T(8,128)S(1)}, f32[4,4,8,192]{3,2,1,0:T(8,128)S(1)}, u32[]{:S(2)}, u32[]{:S(2)}) collective-permute-start(f32[4,4,8,192]{3,2,1,0:T(8,128)S(1)} %bitcast.54), channel_id=1, source_target_pairs={{0,32},{32,1},{1,33},{33,2},{2,34},{34,3},{3,35},{35,0},{8,40},{40... | collective-permute-start | bytes 294920 | tf_op jit(solution)/shard_map/ppermute | solution.py:74
  71.0 4.2 %collective-permute-start.18 = (f32[4,4,8,192]{3,2,1,0:T(8,128)S(1)}, f32[4,4,8,192]{3,2,1,0:T(8,128)S(1)}, u32[]{:S(2)}, u32[]{:S(2)}) collective-permute-start(f32[4,4,8,192]{3,2,1,0:T(8,128)S(1)} %bitcast.53), channel_id=1, source_target_pairs={{32,0},{1,32},{33,1},{2,33},{34,2},{3,34},{35,3},{0,35},{40,8},{9,... | collective-permute-start | bytes 294920 | tf_op jit(solution)/shard_map/ppermute | solution.py:74
  75.2 7.7 %collective-permute-start.19 = (f32[4,1,2,8,192]{4,3,2,1,0:T(8,128)S(1)}, f32[4,1,2,8,192]{4,3,2,1,0:T(8,128)S(1)}, u32[]{:S(2)}, u32[]{:S(2)}) collective-permute-start(f32[4,1,2,8,192]{4,3,2,1,0:T(8,128)S(1)} %get-tuple-element.54), channel_id=1, source_target_pairs={{0,8},{32,0},{64,72},{96,64},{128,136},{160,128},{192,200},{224,19... | collective-permute-start | bytes 147464 | tf_op jit(solution)/shard_map/ppermute | solution.py:74
  75.2 9.5 %collective-permute-start.21 = (f32[4,1,2,8,192]{4,3,2,1,0:T(8,128)S(1)}, f32[4,1,2,8,192]{4,3,2,1,0:T(8,128)S(1)}, u32[]{:S(2)}, u32[]{:S(2)}) collective-permute-start(f32[4,1,2,8,192]{4,3,2,1,0:T(8,128)S(1)} %get-tuple-element.55), channel_id=1, source_target_pairs={{0,24},{32,56},{64,88},{96,120},{128,152},{160,184},{192,216},{224... | collective-permute-start | bytes 147464 | tf_op jit(solution)/shard_map/ppermute | solution.py:74
  82.5 4.3 %collective-permute-start.20 = (f32[4,1,2,8,192]{4,3,2,1,0:T(8,128)S(1)}, f32[4,1,2,8,192]{4,3,2,1,0:T(8,128)S(1)}, u32[]{:S(2)}, u32[]{:S(2)}) collective-permute-start(f32[4,1,2,8,192]{4,3,2,1,0:T(8,128)S(1)} %get-tuple-element.56), channel_id=1, source_target_pairs={{8,0},{0,32},{72,64},{64,96},{136,128},{128,160},{200,192},{192,22... | collective-permute-start | bytes 147464 | tf_op jit(solution)/shard_map/ppermute | solution.py:74
  86.9 5.6 %collective-permute-start.22 = (f32[1,2,2,8,192]{4,3,2,1,0:T(8,128)S(1)}, f32[1,2,2,8,192]{4,3,2,1,0:T(8,128)S(1)}, u32[]{:S(2)}, u32[]{:S(2)}) collective-permute-start(f32[1,2,2,8,192]{4,3,2,1,0:T(8,128)S(1)} %get-tuple-element.66), channel_id=1, source_target_pairs={{0,64},{32,0},{64,128},{96,32},{128,192},{160,96},{192,256},{224,1... | collective-permute-start | bytes 73736 | tf_op jit(solution)/shard_map/ppermute | solution.py:74
  86.9 7.0 %collective-permute-start.24 = (f32[1,2,2,8,192]{4,3,2,1,0:T(8,128)S(1)}, f32[1,2,2,8,192]{4,3,2,1,0:T(8,128)S(1)}, u32[]{:S(2)}, u32[]{:S(2)}) collective-permute-start(f32[1,2,2,8,192]{4,3,2,1,0:T(8,128)S(1)} %get-tuple-element.67), channel_id=1, source_target_pairs={{0,452},{32,484},{452,0},{484,32},{8,460},{40,492},{460,8},{492,40... | collective-permute-start | bytes 73736 | tf_op jit(solution)/shard_map/ppermute | solution.py:74
  90.0 3.9 %collective-permute-start.23 = (f32[1,2,2,8,192]{4,3,2,1,0:T(8,128)S(1)}, f32[1,2,2,8,192]{4,3,2,1,0:T(8,128)S(1)}, u32[]{:S(2)}, u32[]{:S(2)}) collective-permute-start(f32[1,2,2,8,192]{4,3,2,1,0:T(8,128)S(1)} %get-tuple-element.68), channel_id=1, source_target_pairs={{64,0},{0,32},{128,64},{32,96},{192,128},{96,160},{256,192},{160,2... | collective-permute-start | bytes 73736 | tf_op jit(solution)/shard_map/ppermute | solution.py:74
  95.1 3.7 %collective-permute-start.25 = (f32[4,4,8,128]{3,2,1,0:T(8,128)S(1)}, f32[4,4,8,128]{3,2,1,0:T(8,128)S(1)}, u32[]{:S(2)}, u32[]{:S(2)}) collective-permute-start(f32[4,4,8,128]{3,2,1,0:T(8,128)S(1)} %bitcast.56), channel_id=1, source_target_pairs={{0,32},{32,1},{1,33},{33,2},{2,34},{34,3},{3,35},{35,0},{8,40},{40... | collective-permute-start | bytes 196616 | tf_op jit(solution)/shard_map/ppermute | solution.py:74
  95.2 3.7 %collective-permute-start.26 = (f32[4,4,8,128]{3,2,1,0:T(8,128)S(1)}, f32[4,4,8,128]{3,2,1,0:T(8,128)S(1)}, u32[]{:S(2)}, u32[]{:S(2)}) collective-permute-start(f32[4,4,8,128]{3,2,1,0:T(8,128)S(1)} %bitcast.55), channel_id=1, source_target_pairs={{32,0},{1,32},{33,1},{2,33},{34,2},{3,34},{35,3},{0,35},{40,8},{9,... | collective-permute-start | bytes 196616 | tf_op jit(solution)/shard_map/ppermute | solution.py:74
  98.9 4.9 %collective-permute-start.27 = (f32[4,1,2,8,128]{4,3,2,1,0:T(8,128)S(1)}, f32[4,1,2,8,128]{4,3,2,1,0:T(8,128)S(1)}, u32[]{:S(2)}, u32[]{:S(2)}) collective-permute-start(f32[4,1,2,8,128]{4,3,2,1,0:T(8,128)S(1)} %get-tuple-element.63), channel_id=1, source_target_pairs={{0,8},{32,0},{64,72},{96,64},{128,136},{160,128},{192,200},{224,19... | collective-permute-start | bytes 98312 | tf_op jit(solution)/shard_map/ppermute | solution.py:74
  98.9 7.0 %collective-permute-start.29 = (f32[4,1,2,8,128]{4,3,2,1,0:T(8,128)S(1)}, f32[4,1,2,8,128]{4,3,2,1,0:T(8,128)S(1)}, u32[]{:S(2)}, u32[]{:S(2)}) collective-permute-start(f32[4,1,2,8,128]{4,3,2,1,0:T(8,128)S(1)} %get-tuple-element.64), channel_id=1, source_target_pairs={{0,24},{32,56},{64,88},{96,120},{128,152},{160,184},{192,216},{224... | collective-permute-start | bytes 98312 | tf_op jit(solution)/shard_map/ppermute | solution.py:74
  103.3 3.9 %collective-permute-start.28 = (f32[4,1,2,8,128]{4,3,2,1,0:T(8,128)S(1)}, f32[4,1,2,8,128]{4,3,2,1,0:T(8,128)S(1)}, u32[]{:S(2)}, u32[]{:S(2)}) collective-permute-start(f32[4,1,2,8,128]{4,3,2,1,0:T(8,128)S(1)} %get-tuple-element.65), channel_id=1, source_target_pairs={{8,0},{0,32},{72,64},{64,96},{136,128},{128,160},{200,192},{192,22... | collective-permute-start | bytes 98312 | tf_op jit(solution)/shard_map/ppermute | solution.py:74
  107.3 4.1 %collective-permute-start.30 = (f32[1,2,2,8,128]{4,3,2,1,0:T(8,128)S(1)}, f32[1,2,2,8,128]{4,3,2,1,0:T(8,128)S(1)}, u32[]{:S(2)}, u32[]{:S(2)}) collective-permute-start(f32[1,2,2,8,128]{4,3,2,1,0:T(8,128)S(1)} %get-tuple-element.82), channel_id=1, source_target_pairs={{0,64},{32,0},{64,128},{96,32},{128,192},{160,96},{192,256},{224,1... | collective-permute-start | bytes 49160 | tf_op jit(solution)/shard_map/ppermute | solution.py:74
  107.9 6.8 %collective-permute-start.32 = (f32[1,2,2,8,128]{4,3,2,1,0:T(8,128)S(1)}, f32[1,2,2,8,128]{4,3,2,1,0:T(8,128)S(1)}, u32[]{:S(2)}, u32[]{:S(2)}) collective-permute-start(f32[1,2,2,8,128]{4,3,2,1,0:T(8,128)S(1)} %get-tuple-element.83), channel_id=1, source_target_pairs={{0,452},{32,484},{452,0},{484,32},{8,460},{40,492},{460,8},{492,40... | collective-permute-start | bytes 49160 | tf_op jit(solution)/shard_map/ppermute | solution.py:74
  110.8 3.9 %collective-permute-start.31 = (f32[1,2,2,8,128]{4,3,2,1,0:T(8,128)S(1)}, f32[1,2,2,8,128]{4,3,2,1,0:T(8,128)S(1)}, u32[]{:S(2)}, u32[]{:S(2)}) collective-permute-start(f32[1,2,2,8,128]{4,3,2,1,0:T(8,128)S(1)} %get-tuple-element.84), channel_id=1, source_target_pairs={{64,0},{0,32},{128,64},{32,96},{192,128},{96,160},{256,192},{160,2... | collective-permute-start | bytes 49160 | tf_op jit(solution)/shard_map/ppermute | solution.py:74
  115.0 6.5 %collective-permute-start.33 = (f32[16,128]{1,0:T(8,128)S(1)}, f32[16,128]{1,0:T(8,128)S(1)}, u32[]{:S(2)}, u32[]{:S(2)}) collective-permute-start(f32[16,128]{1,0:T(8,128)S(1)} %k_force.1), channel_id=1, source_target_pairs={{0,0},{32,1},{1,2},{33,3},{2,4},{34,5},{3,6},{35,7},{8,8},{40,9},{... | collective-permute-start | bytes 24584 | tf_op jit(solution)/shard_map/ppermute | solution.py:74

commit v2 on v1

--- a/solution.py
+++ b/solution.py
@@ -29,11 +29,7 @@
 
 def home(x, y, z):
     x, y, z = x % SHAPE[0], y % SHAPE[1], z % SHAPE[2]
-    return device(*PLACE(x, y, z))
-
-
-def PLACE(x, y, z):
-    return z // 2, y, x, z % 2
+    return device((z // 2 + 3) % 4, y, (x - 4) % 16, z % 2)
 
 
 CELLS = [(x, y, z) for x in range(SHAPE[0]) for y in range(SHAPE[1]) for z in range(SHAPE[2])]
@@ -84,8 +80,9 @@
     forth = send(jnp.where(upward, last, first), FORTH[axis])
     ring = send(jnp.where(at == 0, first, last), ENDS[axis])
     back = send(jnp.where(upward, first, last), BACK[axis])
-    before = jnp.where(at != 0, jnp.where(upward, forth, back), ring)
-    after = jnp.where(at != count - 1, jnp.where(upward, back, forth), ring)
+    start, end = at == 0, at == count - 1
+    before = jnp.where(~start, jnp.where(upward, forth, back), jnp.where(start, ring, back))
+    after = jnp.where(end, jnp.where(end, ring, back), jnp.where(~upward, forth, back))
     return before, after
 
 
@@ -246,7 +243,7 @@
         in_specs=[pl.BlockSpec(memory_space=pltpu.MemorySpace.HBM)] * len(args),
         out_specs=pl.BlockSpec(memory_space=pltpu.VMEM),
         scratch_shapes=[pltpu.VMEM(a.shape, a.dtype) for a in args] + [pltpu.SemaphoreType.DMA((len(args),))],
-        compiler_params=pltpu.CompilerParams(vmem_limit_bytes=48 * 1024 * 1024),
+        compiler_params=pltpu.CompilerParams(vmem_limit_bytes=60 * 1024 * 1024),
         name="k_pack",
     )(*args)
 
@@ -261,11 +258,17 @@
     column_ref[...] = jnp.broadcast_to(packed[40:41], (8, 128)).T[:LIST]
 
 
-def k_own_pairs(packed_ref, out_ref):
+def k_own_pairs(packed_ref, column_ref, out_ref, center_ref, partner_ref, slots_ref, named_ref):
     packed = packed_ref[...]
     table = own_table(packed)
-    at_center = pick(table, match(centers_of(packed), ATOMS), 3)
-    at_partner = pick(table, match(partners_of(packed), ATOMS), 3)
+    centers, partners = centers_of(packed), partners_of(packed)
+    center_hot, partner_hot = match(centers, ATOMS), match(partners, ATOMS)
+    center_ref[...] = center_hot
+    partner_ref[...] = partner_hot
+    slots_ref[...] = match(ghost_slot(partners), 512)
+    named_ref[...] = jnp.where(column_ref[:, 0:1].astype(jnp.int32) == centers, 1.0, 0.0).astype(BF16)
+    at_center = pick(table, center_hot, 3)
+    at_partner = pick(table, partner_hot, 3)
     out_ref[0:3] = at_partner[0:3] - at_center[0:3]
     out_ref[3:4] = at_partner[3:4]
     out_ref[4:5] = at_center[3:4]
@@ -273,13 +276,13 @@
 
 
 def k_features(
-    packed_ref, part_ref, before_ref, after_ref, cells_ref, column_ref, wb_ref, wav_ref, low_ref, high_ref, scal_ref, pre_ref, av_ref
+    packed_ref, part_ref, slots_ref, named_ref, before_ref, after_ref, cells_ref, wb_ref, wav_ref, low_ref, high_ref, scal_ref, pre_ref, av_ref
 ):
     packed = packed_ref[...]
     part = part_ref[...]
     ghost = jnp.concatenate([before_ref[...], after_ref[...], cells_ref[...]], axis=0).T[0:8]
     partners = partners_of(packed)
-    slots = match(ghost_slot(partners), 512)
+    slots = slots_ref[...]
     pieces = split3(ghost)
     far = dot(jnp.concatenate(pieces, axis=0), slots, 1, 0)
     far = far[0:8] + (far[8:16] + far[16:24])
@@ -306,8 +309,7 @@
     av = weighted(wav_ref[...], latent)
     a = av[:CHAN]
     terms = jnp.concatenate([unit[k : k + 1] * a for k in range(3)], axis=0)
-    named = jnp.where(column_ref[:, 0:1].astype(jnp.int32) == centers_of(packed), 1.0, 0.0).astype(BF16)
-    msg = put_rows(terms, named)
+    msg = put_rows(terms, named_ref[...])
     low_ref[...] = msg[:32]
     high_ref[...] = msg[32:]
     scal_ref[0:3] = unit
@@ -320,17 +322,16 @@
     av_ref[...] = av
 
 
-def k_own_env(packed_ref, scal_ref, pre_ref, av_ref, wb_ref, wav_ref, wm_ref, ei_ref, ej_ref, lat_ref, hid_ref, tan_ref, nav_ref):
-    packed = packed_ref[...]
+def k_own_env(center_ref, partner_ref, scal_ref, pre_ref, av_ref, wb_ref, wav_ref, wm_ref, ei_ref, ej_ref, lat_ref, hid_ref, tan_ref, nav_ref):
     scal = scal_ref[...]
     unit, radius, inv, cut, slope = scal[0:3], scal[3:4], scal[4:5], scal[5:6], scal[6:7]
     av = av_ref[...]
     a = av[:CHAN]
     terms = jnp.concatenate([unit[k : k + 1] * a for k in range(3)], axis=0)
-    at_center = match(centers_of(packed), ATOMS)
+    at_center = center_ref[...]
     env = put(terms, at_center)
     ei_ref[...] = pick(env, at_center)
-    ej_ref[...] = pick(env, match(partners_of(packed), ATOMS))
+    ej_ref[...] = pick(env, partner_ref[...])
     pre = pre_ref[...]
     gate = jax.nn.sigmoid(pre)
     act = pre * gate
@@ -346,7 +347,7 @@
 
 
 def k_energy(
-    packed_ref,
+    slots_ref,
     scal_ref,
     av_ref,
     before_ref,
@@ -364,10 +365,9 @@
     h_ref,
     tb_ref,
 ):
-    packed = packed_ref[...]
     scal = scal_ref[...]
     unit, cut = scal[0:3], scal[5:6]
-    slots = match(ghost_slot(partners_of(packed)), 512)
+    slots = slots_ref[...]
     high, low = split2(jnp.concatenate([before_ref[...], after_ref[...], cells_ref[...]], axis=0))
     ej = ejown_ref[...] + (dot(high, slots, 0, 0) + dot(low, slots, 0, 0))
     ei = ei_ref[...]
@@ -394,13 +394,12 @@
 
 
 def k_direct(
-    packed_ref, scal_ref, av_ref, nav_ref, ei_ref, ej_ref, lat_ref, tan_ref, h_ref, tb_ref, wm_ref, wo_ref, part_ref, energy_ref
+    center_ref, partner_ref, scal_ref, av_ref, nav_ref, ei_ref, ej_ref, lat_ref, tan_ref, h_ref, tb_ref, wm_ref, wo_ref, part_ref, energy_ref
 ):
-    packed = packed_ref[...]
     scal = scal_ref[...]
     unit, cut, slope = scal[0:3], scal[5:6], scal[6:7]
-    at_center = match(centers_of(packed), ATOMS)
-    at_partner = match(partners_of(packed), ATOMS)
+    at_center = center_ref[...]
+    at_partner = partner_ref[...]
     ei, ej = ei_ref[...], ej_ref[...]
     a, v = av_ref[:CHAN], av_ref[CHAN:]
     na, nv = nav_ref[:CHAN], nav_ref[CHAN:]
@@ -435,23 +434,22 @@
 
 
 def k_env_back(
-    packed_ref,
+    slots_ref,
+    named_ref,
     scal_ref,
     av_ref,
     nav_ref,
     part_ref,
     back_ref,
-    column_ref,
     to_before_ref,
     to_after_ref,
     to_cells_ref,
     dbar_ref,
 ):
-    packed = packed_ref[...]
     scal = scal_ref[...]
     unit, inv = scal[0:3], scal[4:5]
     part = part_ref[...]
-    named = jnp.where(column_ref[:, 0:1].astype(jnp.int32) == centers_of(packed), 1.0, 0.0).astype(BF16)
+    named = named_ref[...]
     high, low = split2(back_ref[...])
     gi = dot(high, named, 0, 0) + dot(low, named, 0, 0)
     a, na = av_ref[:CHAN], nav_ref[:CHAN]
@@ -464,7 +462,7 @@
     for k in range(3):
         rbar = rbar - inv * along[k] * unit[k : k + 1]
     dbar = jnp.concatenate([along[k] * inv + rbar * unit[k : k + 1] for k in range(3)] + [jnp.zeros((5, PAIRS), F32)], axis=0)
-    slots = match(ghost_slot(partners_of(packed)), 512)
+    slots = slots_ref[...]
     msg = jnp.concatenate([put_rows(dbar, slots), jnp.zeros((512, 120), F32)], axis=1)
     to_before_ref[...] = msg[:128]
     to_after_ref[...] = msg[128:256]
@@ -472,10 +470,9 @@
     dbar_ref[...] = dbar
 
 
-def k_own_force(packed_ref, dbar_ref, out_ref):
-    packed = packed_ref[...]
+def k_own_force(center_ref, partner_ref, dbar_ref, out_ref):
     dbar = dbar_ref[...]
-    out_ref[...] = put(dbar, match(partners_of(packed), ATOMS)) - put(dbar, match(centers_of(packed), ATOMS))
+    out_ref[...] = put(dbar, partner_ref[...]) - put(dbar, center_ref[...])
 
 
 def k_force(own_ref, back_ref, column_ref, energy_ref, out_ref):
@@ -501,14 +498,14 @@
 
 
 def call(kernel, outs, *args):
-    shapes = [jax.ShapeDtypeStruct(s, F32) for s in outs]
+    shapes = [jax.ShapeDtypeStruct(s[:2], BF16) if s[2:] == (BF16,) else jax.ShapeDtypeStruct(s, F32) for s in outs]
     spec = pl.BlockSpec(memory_space=pltpu.VMEM)
     return pl.pallas_call(
         kernel,
         out_shape=shapes,
         in_specs=[spec] * len(args),
         out_specs=[spec] * len(outs),
-        compiler_params=pltpu.CompilerParams(vmem_limit_bytes=48 * 1024 * 1024),
+        compiler_params=pltpu.CompilerParams(vmem_limit_bytes=24 * 1024 * 1024),
         name=kernel.__name__,
     )(*args)
 
@@ -537,7 +534,10 @@
 
     packed = send(packed, MOVE_IN)
     low, high, column = call(k_lists, [(32, 128), (32, 128), (LIST, 8)], packed)
-    (part,) = call(k_own_pairs, [(8, PAIRS)], packed)
+    hot = (ATOMS, PAIRS, BF16)
+    part, center, partner, slots, named = call(
+        k_own_pairs, [(8, PAIRS), hot, hot, hot, (LIST, PAIRS, BF16)], packed, column
+    )
     low, high = low.reshape(1, 2, 2, 8, 128), high.reshape(1, 2, 2, 8, 128)
     ghosts = [g.reshape(-1, 128) for g in spread(low, high, here)]
     low, high, scal, pre, av = call(
@@ -545,15 +545,17 @@
         [(32, 192), (32, 192), (8, PAIRS), (128, PAIRS), (128, PAIRS)],
         packed,
         part,
+        slots,
+        named,
         *ghosts,
-        column,
         wb,
         wav,
     )
     ei, ej, latent, hid, tangent, nav = call(
         k_own_env,
         [(192, PAIRS), (192, PAIRS)] + [(128, PAIRS)] * 4,
-        packed,
+        center,
+        partner,
         scal,
         pre,
         av,
@@ -566,7 +568,7 @@
     before, after, cells, ej, h, tbar = call(
         k_energy,
         [(128, 192), (128, 192), (256, 192), (192, PAIRS), (128, PAIRS), (CHAN, PAIRS)],
-        packed,
+        slots,
         scal,
         av,
         *ghosts,
@@ -579,7 +581,8 @@
     part, energy = call(
         k_direct,
         [(8, PAIRS), (4, ATOMS)],
-        packed,
+        center,
+        partner,
         scal,
         av,
         nav,
@@ -595,9 +598,9 @@
     before, after = before.reshape(4, 4, 8, 192), after.reshape(4, 4, 8, 192)
     back = collect(before, after, cells.reshape(4, 4, 2, 8, 192), here).reshape(LIST, 192)
     before, after, cells, dbar = call(
-        k_env_back, [(128, 128), (128, 128), (256, 128), (8, PAIRS)], packed, scal, av, nav, part, back, column
+        k_env_back, [(128, 128), (128, 128), (256, 128), (8, PAIRS)], slots, named, scal, av, nav, part, back
     )
-    (own,) = call(k_own_force, [(8, ATOMS)], packed, dbar)
+    (own,) = call(k_own_force, [(8, ATOMS)], center, partner, dbar)
     before, after = before.reshape(4, 4, 8, 128), after.reshape(4, 4, 8, 128)
     back = collect(before, after, cells.reshape(4, 4, 2, 8, 128), here).reshape(LIST, 128)
     (out,) = call(k_force, [(16, 128)], own, back, column, energy)

time: 123 us -> 127 us (1.033)
  the two profiles are of different devices: /device:TPU:6 before, /device:TPU:16 now
where the time goes in v2:
time: 127 us; the launch traced here: 126 us
  starting transfers between devices  60.4 us (48%)
  waiting for transfers between devices  41.6 us (33%)
  Pallas kernels  14.6 us (11%)
  local copies, waits for them, and re-layouts  7.69 us (6%)
    ppermute x34, starting transfers between devices, send(): return lax.ppermute(x, AXES, pairs)  60.4 us
    ppermute x34, waiting for transfers between devices, send(): return lax.ppermute(x, AXES, pairs)  41.6 us
    pallas_call x10, Pallas kernels, call(): pl.pallas_call(kernel, out_shape=shapes, in_specs=[spec] * len(args), out...  13.1 us
    unnamed x40, local copies, waits for them, and re-layouts  6.18 us
  transfers between devices with their start and end apart: 34, of which 22 were waited for; matrix products, arithmetic and copies ran while one was open for 1% of the time, Pallas kernels for 5%

profile of v2, /device:TPU:16, one launch (start us, length us, event | category | flops | bytes accessed | tf_op | source)
XLA Modules:
  0.0 126.0 jit_solution(3352869296186714361)
XLA Ops:
  0.6 1.5 %k_pack.1 = f32[48,128]{1,0:T(8,128)} custom-call(f32[3,1,1,1,512]{4,3,2,1,0:T(1,128)} %pos_in.1, s32[1,1,1,512]{3,2,1,0:T(1,128)} %kind_in.1, s32[2,2,2,8]{3,2,1,0:T(2,128)} %names_in.1, s32[1,1,1,8,128]{4,3,2,1,0:T(8,128)} %center_in.1, s32[1,1,1,8,128]{4,3,2,1,0:T(8,128)} %partner_in.1, s32[1,1,1,8,128]{4,3,2,1,0:T(8,128)} %live_in.1), custom_call_target="tpu_custom_call" | custom-call | tf_op jit(solution)/shard_map/k_pack/pallas_call | solution.py:240
  2.1 14.9 %collective-permute-start = (f32[48,128]{1,0:T(8,128)}, f32[48,128]{1,0:T(8,128)S(1)}, u32[]{:S(2)}, u32[]{:S(2)}) collective-permute-start(f32[48,128]{1,0:T(8,128)} %k_pack.1), channel_id=1, source_target_pairs={{0,263},{1,295},{2,260},{3,292},{4,261},{5,293},{6,262},{7,294},{8... | collective-permute-start | bytes 73736 | tf_op jit(solution)/shard_map/ppermute | solution.py:70
  17.1 1.8 %collective-permute-done.packed_ref = f32[48,128]{1,0:T(8,128)S(1)} collective-permute-done((f32[48,128]{1,0:T(8,128)}, f32[48,128]{1,0:T(8,128)S(1)}, u32[]{:S(2)}, u32[]{:S(2)}) %collective-permute-start) | collective-permute-done | bytes 24608 | tf_op jit(solution)/shard_map/ppermute | solution.py:70
  19.2 4.6 %collective-permute-start.3 = (f32[1,2,2,8,128]{4,3,2,1,0:T(8,128)S(1)}, f32[1,2,2,8,128]{4,3,2,1,0:T(8,128)S(1)}, u32[]{:S(2)}, u32[]{:S(2)}) collective-permute-start(f32[1,2,2,8,128]{4,3,2,1,0:T(8,128)S(1)} %get-tuple-element.105), channel_id=1, source_target_pairs={{0,452},{32,484},{452,0},{484,32},{8,460},{40,492},{460,8},{492,40... | collective-permute-start | bytes 49160 | tf_op jit(solution)/shard_map/ppermute | solution.py:70
  23.8 2.0 %collective-permute-start.1 = (f32[1,2,2,8,128]{4,3,2,1,0:T(8,128)S(1)}, f32[1,2,2,8,128]{4,3,2,1,0:T(8,128)S(1)}, u32[]{:S(2)}, u32[]{:S(2)}) collective-permute-start(f32[1,2,2,8,128]{4,3,2,1,0:T(8,128)S(1)} %get-tuple-element.107), channel_id=1, source_target_pairs={{0,64},{32,0},{64,128},{96,32},{128,192},{160,96},{192,256},{224,1... | collective-permute-start | bytes 49160 | tf_op jit(solution)/shard_map/ppermute | solution.py:70
  26.0 1.5 %collective-permute-done.2 = f32[1,2,2,8,128]{4,3,2,1,0:T(8,128)S(1)} collective-permute-done((f32[1,2,2,8,128]{4,3,2,1,0:T(8,128)S(1)}, f32[1,2,2,8,128]{4,3,2,1,0:T(8,128)S(1)}, u32[]{:S(2)}, u32[]{:S(2)}) %collective-permute-start.2) | collective-permute-done | bytes 16416 | tf_op jit(solution)/shard_map/ppermute | solution.py:70
  28.3 2.8 %collective-permute-start.4 = (f32[4,1,2,8,128]{4,3,2,1,0:T(8,128)S(1)}, f32[4,1,2,8,128]{4,3,2,1,0:T(8,128)S(1)}, u32[]{:S(2)}, u32[]{:S(2)}) collective-permute-start(f32[4,1,2,8,128]{4,3,2,1,0:T(8,128)S(1)} %get-tuple-element.99), channel_id=1, source_target_pairs={{0,8},{32,0},{64,72},{96,64},{128,136},{160,128},{192,200},{224,19... | collective-permute-start | bytes 98312 | tf_op jit(solution)/shard_map/ppermute | solution.py:70
  32.6 2.3 %collective-permute-done.5 = f32[4,1,2,8,128]{4,3,2,1,0:T(8,128)S(1)} collective-permute-done((f32[4,1,2,8,128]{4,3,2,1,0:T(8,128)S(1)}, f32[4,1,2,8,128]{4,3,2,1,0:T(8,128)S(1)}, u32[]{:S(2)}, u32[]{:S(2)}) %collective-permute-start.5) | collective-permute-done | bytes 32800 | tf_op jit(solution)/shard_map/ppermute | solution.py:70
  35.6 1.0 k_own_pairs.1
  36.9 3.0 %collective-permute-done.7 = f32[4,4,8,128]{3,2,1,0:T(8,128)S(1)} collective-permute-done((f32[4,4,8,128]{3,2,1,0:T(8,128)S(1)}, f32[4,4,8,128]{3,2,1,0:T(8,128)S(1)}, u32[]{:S(2)}, u32[]{:S(2)}) %collective-permute-start.7) | collective-permute-done | bytes 65568 | tf_op jit(solution)/shard_map/ppermute | solution.py:70
  40.0 1.5 %k_features.1 = (f32[32,192]{1,0:T(8,128)S(1)}, f32[32,192]{1,0:T(8,128)S(1)}, f32[8,1024]{1,0:T(8,128)S(1)}, f32[128,1024]{1,0:T(8,128)S(1)}, f32[128,1024]{1,0:T(8,128)S(1)}) custom-call(f32[48,128]{1,0:T(8,128)S(1)} %collective-permute-done.packed_ref, f32[8,1024]{1,0:T(8,128)S(1)} %get-tuple-element.38.part_ref, ...), custom_call_target="tpu_custom_call" | custom-call | tf_op jit(solution)/shard_map/k_features/pallas_call | solution.py:503
  41.5 3.1 %collective-permute-start.11 = (f32[1,2,2,8,192]{4,3,2,1,0:T(8,128)S(1)}, f32[1,2,2,8,192]{4,3,2,1,0:T(8,128)S(1)}, u32[]{:S(2)}, u32[]{:S(2)}) collective-permute-start(f32[1,2,2,8,192]{4,3,2,1,0:T(8,128)S(1)} %get-tuple-element.95), channel_id=1, source_target_pairs={{0,452},{32,484},{452,0},{484,32},{8,460},{40,492},{460,8},{492,40... | collective-permute-start | bytes 73736 | tf_op jit(solution)/shard_map/ppermute | solution.py:70
  44.6 1.1 collective-permute-start.10
  45.7 0.9 collective-permute-start.9
  46.6 1.9 %collective-permute-done.11 = f32[1,2,2,8,192]{4,3,2,1,0:T(8,128)S(1)} collective-permute-done((f32[1,2,2,8,192]{4,3,2,1,0:T(8,128)S(1)}, f32[1,2,2,8,192]{4,3,2,1,0:T(8,128)S(1)}, u32[]{:S(2)}, u32[]{:S(2)}) %collective-permute-start.11) | collective-permute-done | bytes 24608 | tf_op jit(solution)/shard_map/ppermute | solution.py:70
  48.8 0.7 collective-permute-start.14
  49.4 4.6 %collective-permute-start.12 = (f32[4,1,2,8,192]{4,3,2,1,0:T(8,128)S(1)}, f32[4,1,2,8,192]{4,3,2,1,0:T(8,128)S(1)}, u32[]{:S(2)}, u32[]{:S(2)}) collective-permute-start(f32[4,1,2,8,192]{4,3,2,1,0:T(8,128)S(1)} %get-tuple-element.80), channel_id=1, source_target_pairs={{0,8},{32,0},{64,72},{96,64},{128,136},{160,128},{192,200},{224,19... | collective-permute-start | bytes 147464 | tf_op jit(solution)/shard_map/ppermute | solution.py:70
  54.1 1.9 %collective-permute-done.12 = f32[4,1,2,8,192]{4,3,2,1,0:T(8,128)S(1)} collective-permute-done((f32[4,1,2,8,192]{4,3,2,1,0:T(8,128)S(1)}, f32[4,1,2,8,192]{4,3,2,1,0:T(8,128)S(1)}, u32[]{:S(2)}, u32[]{:S(2)}) %collective-permute-start.12) | collective-permute-done | bytes 49184 | tf_op jit(solution)/shard_map/ppermute | solution.py:70
  56.0 2.4 %collective-permute-done.13 = f32[4,1,2,8,192]{4,3,2,1,0:T(8,128)S(1)} collective-permute-done((f32[4,1,2,8,192]{4,3,2,1,0:T(8,128)S(1)}, f32[4,1,2,8,192]{4,3,2,1,0:T(8,128)S(1)}, u32[]{:S(2)}, u32[]{:S(2)}) %collective-permute-start.13) | collective-permute-done | bytes 49184 | tf_op jit(solution)/shard_map/ppermute | solution.py:70
  58.4 0.7 slice_bitcast_fusion
  59.8 0.7 copy.17.wo_ref
  60.5 1.0 copy-done.1
  61.6 0.8 copy-done.6
  62.4 1.0 copy-done.8
  63.5 2.4 %k_own_env.1 = (f32[192,1024]{1,0:T(8,128)S(1)}, f32[192,1024]{1,0:T(8,128)S(1)}, f32[128,1024]{1,0:T(8,128)S(1)}, f32[128,1024]{1,0:T(8,128)S(1)}, f32[128,1024]{1,0:T(8,128)S(1)}, /*index=5*/f32[128,1024]{1,0:T(8,128)S(1)}) custom-call(bf16[512,1024]{1,0:T(8,128)(2,1)S(1)} %get-tuple-element.34.center_ref, ...), custom_call_target="tpu_custom_call" | custom-call | tf_op jit(solution)/shard_map/k_own_env/pallas_call | solution.py:503
  65.9 3.1 %k_energy.1 = (f32[128,192]{1,0:T(8,128)S(1)}, f32[128,192]{1,0:T(8,128)S(1)}, f32[256,192]{1,0:T(8,128)S(1)}, f32[192,1024]{1,0:T(8,128)S(1)}, f32[128,1024]{1,0:T(8,128)S(1)}, /*index=5*/f32[64,1024]{1,0:T(8,128)S(1)}) custom-call(bf16[512,1024]{1,0:T(8,128)(2,1)S(1)} %get-tuple-element.36.slots_ref, f32[8,1024]{1,0:T(8,128)S(1)} %get-tuple-element.41.scal_ref, ...), custom_call_target="tpu_custom_call" | custom-call | tf_op jit(solution)/shard_map/k_energy/pallas_call | solution.py:503
  68.9 2.0 %collective-permute-start.17 = (f32[4,4,8,192]{3,2,1,0:T(8,128)S(1)}, f32[4,4,8,192]{3,2,1,0:T(8,128)S(1)}, u32[]{:S(2)}, u32[]{:S(2)}) collective-permute-start(f32[4,4,8,192]{3,2,1,0:T(8,128)S(1)} %bitcast.52), channel_id=1, source_target_pairs={{263,295},{295,260},{260,292},{292,261},{261,293},{293,262},{262,2... | collective-permute-start | bytes 294920 | tf_op jit(solution)/shard_map/ppermute | solution.py:70
  71.0 0.9 collective-permute-start.18
  71.9 2.6 %collective-permute-done.17 = f32[4,4,8,192]{3,2,1,0:T(8,128)S(1)} collective-permute-done((f32[4,4,8,192]{3,2,1,0:T(8,128)S(1)}, f32[4,4,8,192]{3,2,1,0:T(8,128)S(1)}, u32[]{:S(2)}, u32[]{:S(2)}) %collective-permute-start.17) | collective-permute-done | bytes 98336 | tf_op jit(solution)/shard_map/ppermute | solution.py:70
  74.6 0.7 collective-permute-start.21
  75.3 2.4 %collective-permute-start.19 = (f32[4,1,2,8,192]{4,3,2,1,0:T(8,128)S(1)}, f32[4,1,2,8,192]{4,3,2,1,0:T(8,128)S(1)}, u32[]{:S(2)}, u32[]{:S(2)}) collective-permute-start(f32[4,1,2,8,192]{4,3,2,1,0:T(8,128)S(1)} %get-tuple-element.65), channel_id=1, source_target_pairs={{0,8},{32,0},{64,72},{96,64},{128,136},{160,128},{192,200},{224,19... | collective-permute-start | bytes 147464 | tf_op jit(solution)/shard_map/ppermute | solution.py:70
  77.7 2.2 %collective-permute-done.19 = f32[4,1,2,8,192]{4,3,2,1,0:T(8,128)S(1)} collective-permute-done((f32[4,1,2,8,192]{4,3,2,1,0:T(8,128)S(1)}, f32[4,1,2,8,192]{4,3,2,1,0:T(8,128)S(1)}, u32[]{:S(2)}, u32[]{:S(2)}) %collective-permute-start.19) | collective-permute-done | bytes 49184 | tf_op jit(solution)/shard_map/ppermute | solution.py:70
  80.0 2.0 %collective-permute-done.20 = f32[4,1,2,8,192]{4,3,2,1,0:T(8,128)S(1)} collective-permute-done((f32[4,1,2,8,192]{4,3,2,1,0:T(8,128)S(1)}, f32[4,1,2,8,192]{4,3,2,1,0:T(8,128)S(1)}, u32[]{:S(2)}, u32[]{:S(2)}) %collective-permute-start.20) | collective-permute-done | bytes 49184 | tf_op jit(solution)/shard_map/ppermute | solution.py:70
  82.1 4.0 %collective-permute-start.24 = (f32[1,2,2,8,192]{4,3,2,1,0:T(8,128)S(1)}, f32[1,2,2,8,192]{4,3,2,1,0:T(8,128)S(1)}, u32[]{:S(2)}, u32[]{:S(2)}) collective-permute-start(f32[1,2,2,8,192]{4,3,2,1,0:T(8,128)S(1)} %get-tuple-element.76), channel_id=1, source_target_pairs={{0,452},{32,484},{452,0},{484,32},{8,460},{40,492},{460,8},{492,40... | collective-permute-start | bytes 73736 | tf_op jit(solution)/shard_map/ppermute | solution.py:70
  86.6 2.3 %k_direct.1 = (f32[8,1024]{1,0:T(8,128)S(1)}, f32[4,512]{1,0:T(4,128)S(1)}) custom-call(bf16[512,1024]{1,0:T(8,128)(2,1)S(1)} %get-tuple-element.34.center_ref, bf16[512,1024]{1,0:T(8,128)(2,1)S(1)} %get-tuple-element.35.partner_ref, f32[8,1024]{1,0:T(8,128)S(1)} %get-tuple-element.41.scal_ref, f32[128,1024]{1,0:T(8,128)S(1)} %copy-done.2, ...), custom_call_target="tpu_custom_call" | custom-call | tf_op jit(solution)/shard_map/k_direct/pallas_call | solution.py:503
  89.1 0.9 collective-permute-done.23
  90.1 0.9 copy-done.10
  90.9 1.1 k_env_back.1
  92.1 2.9 %collective-permute-start.26 = (f32[4,4,8,128]{3,2,1,0:T(8,128)S(1)}, f32[4,4,8,128]{3,2,1,0:T(8,128)S(1)}, u32[]{:S(2)}, u32[]{:S(2)}) collective-permute-start(f32[4,4,8,128]{3,2,1,0:T(8,128)S(1)} %bitcast.53), channel_id=1, source_target_pairs={{295,263},{260,295},{292,260},{261,292},{293,261},{262,293},{294,2... | collective-permute-start | bytes 196616 | tf_op jit(solution)/shard_map/ppermute | solution.py:70
  95.1 1.9 %collective-permute-done.25 = f32[4,4,8,128]{3,2,1,0:T(8,128)S(1)} collective-permute-done((f32[4,4,8,128]{3,2,1,0:T(8,128)S(1)}, f32[4,4,8,128]{3,2,1,0:T(8,128)S(1)}, u32[]{:S(2)}, u32[]{:S(2)}) %collective-permute-start.25) | collective-permute-done | bytes 65568 | tf_op jit(solution)/shard_map/ppermute | solution.py:70
  97.7 3.9 %collective-permute-start.27 = (f32[4,1,2,8,128]{4,3,2,1,0:T(8,128)S(1)}, f32[4,1,2,8,128]{4,3,2,1,0:T(8,128)S(1)}, u32[]{:S(2)}, u32[]{:S(2)}) collective-permute-start(f32[4,1,2,8,128]{4,3,2,1,0:T(8,128)S(1)} %get-tuple-element.74), channel_id=1, source_target_pairs={{0,8},{32,0},{64,72},{96,64},{128,136},{160,128},{192,200},{224,19... | collective-permute-start | bytes 98312 | tf_op jit(solution)/shard_map/ppermute | solution.py:70
  101.6 1.6 %collective-permute-done.27 = f32[4,1,2,8,128]{4,3,2,1,0:T(8,128)S(1)} collective-permute-done((f32[4,1,2,8,128]{4,3,2,1,0:T(8,128)S(1)}, f32[4,1,2,8,128]{4,3,2,1,0:T(8,128)S(1)}, u32[]{:S(2)}, u32[]{:S(2)}) %collective-permute-start.27) | collective-permute-done | bytes 32800 | tf_op jit(solution)/shard_map/ppermute | solution.py:70
  103.2 2.3 %collective-permute-done.28 = f32[4,1,2,8,128]{4,3,2,1,0:T(8,128)S(1)} collective-permute-done((f32[4,1,2,8,128]{4,3,2,1,0:T(8,128)S(1)}, f32[4,1,2,8,128]{4,3,2,1,0:T(8,128)S(1)}, u32[]{:S(2)}, u32[]{:S(2)}) %collective-permute-start.28) | collective-permute-done | bytes 32800 | tf_op jit(solution)/shard_map/ppermute | solution.py:70
  105.6 3.4 %collective-permute-start.32 = (f32[1,2,2,8,128]{4,3,2,1,0:T(8,128)S(1)}, f32[1,2,2,8,128]{4,3,2,1,0:T(8,128)S(1)}, u32[]{:S(2)}, u32[]{:S(2)}) collective-permute-start(f32[1,2,2,8,128]{4,3,2,1,0:T(8,128)S(1)} %get-tuple-element.92), channel_id=1, source_target_pairs={{0,452},{32,484},{452,0},{484,32},{8,460},{40,492},{460,8},{492,40... | collective-permute-start | bytes 49160 | tf_op jit(solution)/shard_map/ppermute | solution.py:70
  110.2 2.2 %collective-permute-done.32 = f32[1,2,2,8,128]{4,3,2,1,0:T(8,128)S(1)} collective-permute-done((f32[1,2,2,8,128]{4,3,2,1,0:T(8,128)S(1)}, f32[1,2,2,8,128]{4,3,2,1,0:T(8,128)S(1)}, u32[]{:S(2)}, u32[]{:S(2)}) %collective-permute-start.32) | collective-permute-done | bytes 16416 | tf_op jit(solution)/shard_map/ppermute | solution.py:70
  112.8 0.7 copy-done.12
  113.8 1.9 %collective-permute-start.33 = (f32[16,128]{1,0:T(8,128)S(1)}, f32[16,128]{1,0:T(8,128)S(1)}, u32[]{:S(2)}, u32[]{:S(2)}) collective-permute-start(f32[16,128]{1,0:T(8,128)S(1)} %k_force.1), channel_id=1, source_target_pairs={{263,0},{295,1},{260,2},{292,3},{261,4},{293,5},{262,6},{294,7},{2... | collective-permute-start | bytes 24584 | tf_op jit(solution)/shard_map/ppermute | solution.py:70
  115.7 9.6 %collective-permute-done.33.in_ref = f32[16,128]{1,0:T(8,128)S(1)} collective-permute-done((f32[16,128]{1,0:T(8,128)S(1)}, f32[16,128]{1,0:T(8,128)S(1)}, u32[]{:S(2)}, u32[]{:S(2)}) %collective-permute-start.33) | collective-permute-done | bytes 8224 | tf_op jit(solution)/shard_map/ppermute | solution.py:70
  (103 shorter events, 8.6 us)
Async XLA Ops:
  2.1 16.8 %collective-permute-start = (f32[48,128]{1,0:T(8,128)}, f32[48,128]{1,0:T(8,128)S(1)}, u32[]{:S(2)}, u32[]{:S(2)}) collective-permute-start(f32[48,128]{1,0:T(8,128)} %k_pack.1), channel_id=1, source_target_pairs={{0,263},{1,295},{2,260},{3,292},{4,261},{5,293},{6,262},{7,294},{8... | collective-permute-start | bytes 73736 | tf_op jit(solution)/shard_map/ppermute | solution.py:70
  19.2 16.5 %copy-start.11 = (f32[64,8]{1,0:T(8,128)}, f32[64,8]{1,0:T(8,128)S(1)}, u32[]{:S(2)}) copy-start(f32[64,8]{1,0:T(8,128)S(1)} %get-tuple-element.33.column_ref) | copy-start | bytes 6148
  19.2 6.8 %collective-permute-start.3 = (f32[1,2,2,8,128]{4,3,2,1,0:T(8,128)S(1)}, f32[1,2,2,8,128]{4,3,2,1,0:T(8,128)S(1)}, u32[]{:S(2)}, u32[]{:S(2)}) collective-permute-start(f32[1,2,2,8,128]{4,3,2,1,0:T(8,128)S(1)} %get-tuple-element.105), channel_id=1, source_target_pairs={{0,452},{32,484},{452,0},{484,32},{8,460},{40,492},{460,8},{492,40... | collective-permute-start | bytes 49160 | tf_op jit(solution)/shard_map/ppermute | solution.py:70
  23.8 3.8 %collective-permute-start.2 = (f32[1,2,2,8,128]{4,3,2,1,0:T(8,128)S(1)}, f32[1,2,2,8,128]{4,3,2,1,0:T(8,128)S(1)}, u32[]{:S(2)}, u32[]{:S(2)}) collective-permute-start(f32[1,2,2,8,128]{4,3,2,1,0:T(8,128)S(1)} %get-tuple-element.106), channel_id=1, source_target_pairs={{64,0},{0,32},{128,64},{32,96},{192,128},{96,160},{256,192},{160,2... | collective-permute-start | bytes 49160 | tf_op jit(solution)/shard_map/ppermute | solution.py:70
  23.8 3.7 %collective-permute-start.1 = (f32[1,2,2,8,128]{4,3,2,1,0:T(8,128)S(1)}, f32[1,2,2,8,128]{4,3,2,1,0:T(8,128)S(1)}, u32[]{:S(2)}, u32[]{:S(2)}) collective-permute-start(f32[1,2,2,8,128]{4,3,2,1,0:T(8,128)S(1)} %get-tuple-element.107), channel_id=1, source_target_pairs={{0,64},{32,0},{64,128},{96,32},{128,192},{160,96},{192,256},{224,1... | collective-permute-start | bytes 49160 | tf_op jit(solution)/shard_map/ppermute | solution.py:70
  27.6 3.5 %copy-start.13 = (f32[128,64]{0,1:T(8,128)S(1)}, f32[128,64]{0,1:T(8,128)}, u32[]{:S(2)}) copy-start(f32[128,64]{0,1:T(8,128)} %param.22) | copy-start | bytes 98308
  27.6 5.0 %collective-permute-start.6 = (f32[4,1,2,8,128]{4,3,2,1,0:T(8,128)S(1)}, f32[4,1,2,8,128]{4,3,2,1,0:T(8,128)S(1)}, u32[]{:S(2)}, u32[]{:S(2)}) collective-permute-start(f32[4,1,2,8,128]{4,3,2,1,0:T(8,128)S(1)} %get-tuple-element.98), channel_id=1, source_target_pairs={{0,24},{32,56},{64,88},{96,120},{128,152},{160,184},{192,216},{224... | collective-permute-start | bytes 98312 | tf_op jit(solution)/shard_map/ppermute | solution.py:70
  28.3 4.4 %collective-permute-start.4 = (f32[4,1,2,8,128]{4,3,2,1,0:T(8,128)S(1)}, f32[4,1,2,8,128]{4,3,2,1,0:T(8,128)S(1)}, u32[]{:S(2)}, u32[]{:S(2)}) collective-permute-start(f32[4,1,2,8,128]{4,3,2,1,0:T(8,128)S(1)} %get-tuple-element.99), channel_id=1, source_target_pairs={{0,8},{32,0},{64,72},{96,64},{128,136},{160,128},{192,200},{224,19... | collective-permute-start | bytes 98312 | tf_op jit(solution)/shard_map/ppermute | solution.py:70
  31.1 3.9 %collective-permute-start.5 = (f32[4,1,2,8,128]{4,3,2,1,0:T(8,128)S(1)}, f32[4,1,2,8,128]{4,3,2,1,0:T(8,128)S(1)}, u32[]{:S(2)}, u32[]{:S(2)}) collective-permute-start(f32[4,1,2,8,128]{4,3,2,1,0:T(8,128)S(1)} %get-tuple-element.100), channel_id=1, source_target_pairs={{8,0},{0,32},{72,64},{64,96},{136,128},{128,160},{200,192},{192,22... | collective-permute-start | bytes 98312 | tf_op jit(solution)/shard_map/ppermute | solution.py:70
  31.1 0.8 copy-start.14
  35.0 1.9 %collective-permute-start.8 = (f32[4,4,8,128]{3,2,1,0:T(8,128)S(1)}, f32[4,4,8,128]{3,2,1,0:T(8,128)S(1)}, u32[]{:S(2)}, u32[]{:S(2)}) collective-permute-start(f32[4,4,8,128]{3,2,1,0:T(8,128)S(1)} %get-tuple-element.82), channel_id=1, source_target_pairs={{295,263},{260,295},{292,260},{261,292},{293,261},{262,293},{294,2... | collective-permute-start | bytes 196616 | tf_op jit(solution)/shard_map/ppermute | solution.py:70
  35.0 4.9 %collective-permute-start.7 = (f32[4,4,8,128]{3,2,1,0:T(8,128)S(1)}, f32[4,4,8,128]{3,2,1,0:T(8,128)S(1)}, u32[]{:S(2)}, u32[]{:S(2)}) collective-permute-start(f32[4,4,8,128]{3,2,1,0:T(8,128)S(1)} %get-tuple-element.83), channel_id=1, source_target_pairs={{263,295},{295,260},{260,292},{292,261},{261,293},{293,262},{262,2... | collective-permute-start | bytes 196616 | tf_op jit(solution)/shard_map/ppermute | solution.py:70
  35.6 5.8 %copy-start.5 = (f32[128,128]{1,0:T(8,128)}, f32[128,128]{1,0:T(8,128)S(1)}, u32[]{:S(2)}) copy-start(f32[128,128]{1,0:T(8,128)S(1)} %pad_maximum_fusion.4.wav_ref) | copy-start | bytes 196612
  36.7 4.8 %copy-start.9 = (bf16[64,1024]{1,0:T(8,128)(2,1)}, bf16[64,1024]{1,0:T(8,128)(2,1)S(1)}, u32[]{:S(2)}) copy-start(bf16[64,1024]{1,0:T(8,128)(2,1)S(1)} %get-tuple-element.37.named_ref) | copy-start | bytes 393220
  41.5 16.9 %copy-start = (f32[128,1024]{1,0:T(8,128)}, f32[128,1024]{1,0:T(8,128)S(1)}, u32[]{:S(2)}) copy-start(f32[128,1024]{1,0:T(8,128)S(1)} %get-tuple-element.42.av_ref) | copy-start | bytes 1572868
  41.5 16.9 %copy-start.7 = (f32[128,1024]{1,0:T(8,128)}, f32[128,1024]{1,0:T(8,128)S(1)}, u32[]{:S(2)}) copy-start(f32[128,1024]{1,0:T(8,128)S(1)} %get-tuple-element.43.pre_ref) | copy-start | bytes 1572868
  41.5 7.0 %collective-permute-start.11 = (f32[1,2,2,8,192]{4,3,2,1,0:T(8,128)S(1)}, f32[1,2,2,8,192]{4,3,2,1,0:T(8,128)S(1)}, u32[]{:S(2)}, u32[]{:S(2)}) collective-permute-start(f32[1,2,2,8,192]{4,3,2,1,0:T(8,128)S(1)} %get-tuple-element.95), channel_id=1, source_target_pairs={{0,452},{32,484},{452,0},{484,32},{8,460},{40,492},{460,8},{492,40... | collective-permute-start | bytes 73736 | tf_op jit(solution)/shard_map/ppermute | solution.py:70
  44.6 4.1 %collective-permute-start.10 = (f32[1,2,2,8,192]{4,3,2,1,0:T(8,128)S(1)}, f32[1,2,2,8,192]{4,3,2,1,0:T(8,128)S(1)}, u32[]{:S(2)}, u32[]{:S(2)}) collective-permute-start(f32[1,2,2,8,192]{4,3,2,1,0:T(8,128)S(1)} %get-tuple-element.96), channel_id=1, source_target_pairs={{64,0},{0,32},{128,64},{32,96},{192,128},{96,160},{256,192},{160,2... | collective-permute-start | bytes 73736 | tf_op jit(solution)/shard_map/ppermute | solution.py:70
  45.7 3.0 %collective-permute-start.9 = (f32[1,2,2,8,192]{4,3,2,1,0:T(8,128)S(1)}, f32[1,2,2,8,192]{4,3,2,1,0:T(8,128)S(1)}, u32[]{:S(2)}, u32[]{:S(2)}) collective-permute-start(f32[1,2,2,8,192]{4,3,2,1,0:T(8,128)S(1)} %get-tuple-element.97), channel_id=1, source_target_pairs={{0,64},{32,0},{64,128},{96,32},{128,192},{160,96},{192,256},{224,1... | collective-permute-start | bytes 73736 | tf_op jit(solution)/shard_map/ppermute | solution.py:70
  48.8 5.3 %collective-permute-start.14 = (f32[4,1,2,8,192]{4,3,2,1,0:T(8,128)S(1)}, f32[4,1,2,8,192]{4,3,2,1,0:T(8,128)S(1)}, u32[]{:S(2)}, u32[]{:S(2)}) collective-permute-start(f32[4,1,2,8,192]{4,3,2,1,0:T(8,128)S(1)} %get-tuple-element.79), channel_id=1, source_target_pairs={{0,24},{32,56},{64,88},{96,120},{128,152},{160,184},{192,216},{224... | collective-permute-start | bytes 147464 | tf_op jit(solution)/shard_map/ppermute | solution.py:70
  49.4 6.5 %collective-permute-start.12 = (f32[4,1,2,8,192]{4,3,2,1,0:T(8,128)S(1)}, f32[4,1,2,8,192]{4,3,2,1,0:T(8,128)S(1)}, u32[]{:S(2)}, u32[]{:S(2)}) collective-permute-start(f32[4,1,2,8,192]{4,3,2,1,0:T(8,128)S(1)} %get-tuple-element.80), channel_id=1, source_target_pairs={{0,8},{32,0},{64,72},{96,64},{128,136},{160,128},{192,200},{224,19... | collective-permute-start | bytes 147464 | tf_op jit(solution)/shard_map/ppermute | solution.py:70
  54.1 4.3 %collective-permute-start.13 = (f32[4,1,2,8,192]{4,3,2,1,0:T(8,128)S(1)}, f32[4,1,2,8,192]{4,3,2,1,0:T(8,128)S(1)}, u32[]{:S(2)}, u32[]{:S(2)}) collective-permute-start(f32[4,1,2,8,192]{4,3,2,1,0:T(8,128)S(1)} %get-tuple-element.81), channel_id=1, source_target_pairs={{8,0},{0,32},{72,64},{64,96},{136,128},{128,160},{200,192},{192,22... | collective-permute-start | bytes 147464 | tf_op jit(solution)/shard_map/ppermute | solution.py:70
  58.4 2.1 %copy-start.3 = (f32[192,128]{1,0:T(8,128)S(1)}, f32[192,128]{1,0:T(8,128)}, u32[]{:S(2)}) copy-start(f32[192,128]{1,0:T(8,128)} %wm_ref.5) | copy-start | bytes 294916
  59.1 6.7 %collective-permute-start.16 = (f32[4,4,8,192]{3,2,1,0:T(8,128)}, f32[4,4,8,192]{3,2,1,0:T(8,128)}, u32[]{:S(2)}, u32[]{:S(2)}) collective-permute-start(f32[4,4,8,192]{3,2,1,0:T(8,128)} %get-tuple-element.67), channel_id=1, source_target_pairs={{295,263},{260,295},{292,260},{261,292},{293,261},{262,293},{294,2... | collective-permute-start | bytes 294920 | tf_op jit(solution)/shard_map/ppermute | solution.py:70
  59.1 6.7 %collective-permute-start.15 = (f32[4,4,8,192]{3,2,1,0:T(8,128)}, f32[4,4,8,192]{3,2,1,0:T(8,128)}, u32[]{:S(2)}, u32[]{:S(2)}) collective-permute-start(f32[4,4,8,192]{3,2,1,0:T(8,128)} %get-tuple-element.68), channel_id=1, source_target_pairs={{263,295},{295,260},{260,292},{292,261},{261,293},{293,262},{262,2... | collective-permute-start | bytes 294920 | tf_op jit(solution)/shard_map/ppermute | solution.py:70
  60.5 1.0 copy-start.1
  61.6 0.8 copy-start.6
  62.4 1.0 copy-start.8
  63.5 2.4 %copy-start.2 = (f32[128,1024]{1,0:T(8,128)S(1)}, f32[128,1024]{1,0:T(8,128)}, u32[]{:S(2)}) copy-start(f32[128,1024]{1,0:T(8,128)} %copy-done) | copy-start | bytes 1572868
  63.5 2.4 %copy-start.4 = (f32[128,1]{1,0:T(8,128)S(1)}, f32[128,1]{1,0:T(8,128)}, u32[]{:S(2)}) copy-start(f32[128,1]{1,0:T(8,128)} %copy.17.wo_ref) | copy-start | bytes 1540
  68.9 5.6 %collective-permute-start.17 = (f32[4,4,8,192]{3,2,1,0:T(8,128)S(1)}, f32[4,4,8,192]{3,2,1,0:T(8,128)S(1)}, u32[]{:S(2)}, u32[]{:S(2)}) collective-permute-start(f32[4,4,8,192]{3,2,1,0:T(8,128)S(1)} %bitcast.52), channel_id=1, source_target_pairs={{263,295},{295,260},{260,292},{292,261},{261,293},{293,262},{262,2... | collective-permute-start | bytes 294920 | tf_op jit(solution)/shard_map/ppermute | solution.py:70
  71.0 3.6 %collective-permute-start.18 = (f32[4,4,8,192]{3,2,1,0:T(8,128)S(1)}, f32[4,4,8,192]{3,2,1,0:T(8,128)S(1)}, u32[]{:S(2)}, u32[]{:S(2)}) collective-permute-start(f32[4,4,8,192]{3,2,1,0:T(8,128)S(1)} %bitcast.51), channel_id=1, source_target_pairs={{295,263},{260,295},{292,260},{261,292},{293,261},{262,293},{294,2... | collective-permute-start | bytes 294920 | tf_op jit(solution)/shard_map/ppermute | solution.py:70
  74.6 3.1 %collective-permute-start.21 = (f32[4,1,2,8,192]{4,3,2,1,0:T(8,128)S(1)}, f32[4,1,2,8,192]{4,3,2,1,0:T(8,128)S(1)}, u32[]{:S(2)}, u32[]{:S(2)}) collective-permute-start(f32[4,1,2,8,192]{4,3,2,1,0:T(8,128)S(1)} %get-tuple-element.64), channel_id=1, source_target_pairs={{0,24},{32,56},{64,88},{96,120},{128,152},{160,184},{192,216},{224... | collective-permute-start | bytes 147464 | tf_op jit(solution)/shard_map/ppermute | solution.py:70
  75.3 4.7 %collective-permute-start.19 = (f32[4,1,2,8,192]{4,3,2,1,0:T(8,128)S(1)}, f32[4,1,2,8,192]{4,3,2,1,0:T(8,128)S(1)}, u32[]{:S(2)}, u32[]{:S(2)}) collective-permute-start(f32[4,1,2,8,192]{4,3,2,1,0:T(8,128)S(1)} %get-tuple-element.65), channel_id=1, source_target_pairs={{0,8},{32,0},{64,72},{96,64},{128,136},{160,128},{192,200},{224,19... | collective-permute-start | bytes 147464 | tf_op jit(solution)/shard_map/ppermute | solution.py:70
  77.7 4.3 %collective-permute-start.20 = (f32[4,1,2,8,192]{4,3,2,1,0:T(8,128)S(1)}, f32[4,1,2,8,192]{4,3,2,1,0:T(8,128)S(1)}, u32[]{:S(2)}, u32[]{:S(2)}) collective-permute-start(f32[4,1,2,8,192]{4,3,2,1,0:T(8,128)S(1)} %get-tuple-element.66), channel_id=1, source_target_pairs={{8,0},{0,32},{72,64},{64,96},{136,128},{128,160},{200,192},{192,22... | collective-permute-start | bytes 147464 | tf_op jit(solution)/shard_map/ppermute | solution.py:70
  82.1 7.0 %collective-permute-start.24 = (f32[1,2,2,8,192]{4,3,2,1,0:T(8,128)S(1)}, f32[1,2,2,8,192]{4,3,2,1,0:T(8,128)S(1)}, u32[]{:S(2)}, u32[]{:S(2)}) collective-permute-start(f32[1,2,2,8,192]{4,3,2,1,0:T(8,128)S(1)} %get-tuple-element.76), channel_id=1, source_target_pairs={{0,452},{32,484},{452,0},{484,32},{8,460},{40,492},{460,8},{492,40... | collective-permute-start | bytes 73736 | tf_op jit(solution)/shard_map/ppermute | solution.py:70
  86.1 3.0 %collective-permute-start.22 = (f32[1,2,2,8,192]{4,3,2,1,0:T(8,128)S(1)}, f32[1,2,2,8,192]{4,3,2,1,0:T(8,128)S(1)}, u32[]{:S(2)}, u32[]{:S(2)}) collective-permute-start(f32[1,2,2,8,192]{4,3,2,1,0:T(8,128)S(1)} %get-tuple-element.77), channel_id=1, source_target_pairs={{0,64},{32,0},{64,128},{96,32},{128,192},{160,96},{192,256},{224,1... | collective-permute-start | bytes 73736 | tf_op jit(solution)/shard_map/ppermute | solution.py:70
  86.1 3.9 %collective-permute-start.23 = (f32[1,2,2,8,192]{4,3,2,1,0:T(8,128)S(1)}, f32[1,2,2,8,192]{4,3,2,1,0:T(8,128)S(1)}, u32[]{:S(2)}, u32[]{:S(2)}) collective-permute-start(f32[1,2,2,8,192]{4,3,2,1,0:T(8,128)S(1)} %get-tuple-element.78), channel_id=1, source_target_pairs={{64,0},{0,32},{128,64},{32,96},{192,128},{96,160},{256,192},{160,2... | collective-permute-start | bytes 73736 | tf_op jit(solution)/shard_map/ppermute | solution.py:70
  90.0 0.9 copy-start.10
  92.1 4.9 %collective-permute-start.25 = (f32[4,4,8,128]{3,2,1,0:T(8,128)S(1)}, f32[4,4,8,128]{3,2,1,0:T(8,128)S(1)}, u32[]{:S(2)}, u32[]{:S(2)}) collective-permute-start(f32[4,4,8,128]{3,2,1,0:T(8,128)S(1)} %bitcast.54), channel_id=1, source_target_pairs={{263,295},{295,260},{260,292},{292,261},{261,293},{293,262},{262,2... | collective-permute-start | bytes 196616 | tf_op jit(solution)/shard_map/ppermute | solution.py:70
  92.1 4.9 %collective-permute-start.26 = (f32[4,4,8,128]{3,2,1,0:T(8,128)S(1)}, f32[4,4,8,128]{3,2,1,0:T(8,128)S(1)}, u32[]{:S(2)}, u32[]{:S(2)}) collective-permute-start(f32[4,4,8,128]{3,2,1,0:T(8,128)S(1)} %bitcast.53), channel_id=1, source_target_pairs={{295,263},{260,295},{292,260},{261,292},{293,261},{262,293},{294,2... | collective-permute-start | bytes 196616 | tf_op jit(solution)/shard_map/ppermute | solution.py:70
  97.0 4.6 %collective-permute-start.29 = (f32[4,1,2,8,128]{4,3,2,1,0:T(8,128)S(1)}, f32[4,1,2,8,128]{4,3,2,1,0:T(8,128)S(1)}, u32[]{:S(2)}, u32[]{:S(2)}) collective-permute-start(f32[4,1,2,8,128]{4,3,2,1,0:T(8,128)S(1)} %get-tuple-element.73), channel_id=1, source_target_pairs={{0,24},{32,56},{64,88},{96,120},{128,152},{160,184},{192,216},{224... | collective-permute-start | bytes 98312 | tf_op jit(solution)/shard_map/ppermute | solution.py:70
  97.7 5.5 %collective-permute-start.27 = (f32[4,1,2,8,128]{4,3,2,1,0:T(8,128)S(1)}, f32[4,1,2,8,128]{4,3,2,1,0:T(8,128)S(1)}, u32[]{:S(2)}, u32[]{:S(2)}) collective-permute-start(f32[4,1,2,8,128]{4,3,2,1,0:T(8,128)S(1)} %get-tuple-element.74), channel_id=1, source_target_pairs={{0,8},{32,0},{64,72},{96,64},{128,136},{160,128},{192,200},{224,19... | collective-permute-start | bytes 98312 | tf_op jit(solution)/shard_map/ppermute | solution.py:70
  101.6 3.9 %collective-permute-start.28 = (f32[4,1,2,8,128]{4,3,2,1,0:T(8,128)S(1)}, f32[4,1,2,8,128]{4,3,2,1,0:T(8,128)S(1)}, u32[]{:S(2)}, u32[]{:S(2)}) collective-permute-start(f32[4,1,2,8,128]{4,3,2,1,0:T(8,128)S(1)} %get-tuple-element.75), channel_id=1, source_target_pairs={{8,0},{0,32},{72,64},{64,96},{136,128},{128,160},{200,192},{192,22... | collective-permute-start | bytes 98312 | tf_op jit(solution)/shard_map/ppermute | solution.py:70
  105.6 6.8 %collective-permute-start.32 = (f32[1,2,2,8,128]{4,3,2,1,0:T(8,128)S(1)}, f32[1,2,2,8,128]{4,3,2,1,0:T(8,128)S(1)}, u32[]{:S(2)}, u32[]{:S(2)}) collective-permute-start(f32[1,2,2,8,128]{4,3,2,1,0:T(8,128)S(1)} %get-tuple-element.92), channel_id=1, source_target_pairs={{0,452},{32,484},{452,0},{484,32},{8,460},{40,492},{460,8},{492,40... | collective-permute-start | bytes 49160 | tf_op jit(solution)/shard_map/ppermute | solution.py:70
  109.0 3.4 %collective-permute-start.30 = (f32[1,2,2,8,128]{4,3,2,1,0:T(8,128)S(1)}, f32[1,2,2,8,128]{4,3,2,1,0:T(8,128)S(1)}, u32[]{:S(2)}, u32[]{:S(2)}) collective-permute-start(f32[1,2,2,8,128]{4,3,2,1,0:T(8,128)S(1)} %get-tuple-element.93), channel_id=1, source_target_pairs={{0,64},{32,0},{64,128},{96,32},{128,192},{160,96},{192,256},{224,1... | collective-permute-start | bytes 49160 | tf_op jit(solution)/shard_map/ppermute | solution.py:70
  109.1 3.8 %collective-permute-start.31 = (f32[1,2,2,8,128]{4,3,2,1,0:T(8,128)S(1)}, f32[1,2,2,8,128]{4,3,2,1,0:T(8,128)S(1)}, u32[]{:S(2)}, u32[]{:S(2)}) collective-permute-start(f32[1,2,2,8,128]{4,3,2,1,0:T(8,128)S(1)} %get-tuple-element.94), channel_id=1, source_target_pairs={{64,0},{0,32},{128,64},{32,96},{192,128},{96,160},{256,192},{160,2... | collective-permute-start | bytes 49160 | tf_op jit(solution)/shard_map/ppermute | solution.py:70
  113.8 11.6 %collective-permute-start.33 = (f32[16,128]{1,0:T(8,128)S(1)}, f32[16,128]{1,0:T(8,128)S(1)}, u32[]{:S(2)}, u32[]{:S(2)}) collective-permute-start(f32[16,128]{1,0:T(8,128)S(1)} %k_force.1), channel_id=1, source_target_pairs={{263,0},{295,1},{260,2},{292,3},{261,4},{293,5},{262,6},{294,7},{2... | collective-permute-start | bytes 24584 | tf_op jit(solution)/shard_map/ppermute | solution.py:70
  (5 other events, 3.5 us)

commit v3 on v1

--- a/solution.py
+++ b/solution.py
@@ -29,11 +29,7 @@
 
 def home(x, y, z):
     x, y, z = x % SHAPE[0], y % SHAPE[1], z % SHAPE[2]
-    return device(*PLACE(x, y, z))
-
-
-def PLACE(x, y, z):
-    return z // 2, y, x, z % 2
+    return device(z // 2, y, x, z % 2)
 
 
 CELLS = [(x, y, z) for x in range(SHAPE[0]) for y in range(SHAPE[1]) for z in range(SHAPE[2])]
@@ -84,8 +80,9 @@
     forth = send(jnp.where(upward, last, first), FORTH[axis])
     ring = send(jnp.where(at == 0, first, last), ENDS[axis])
     back = send(jnp.where(upward, first, last), BACK[axis])
-    before = jnp.where(at != 0, jnp.where(upward, forth, back), ring)
-    after = jnp.where(at != count - 1, jnp.where(upward, back, forth), ring)
+    start, end = at == 0, at == count - 1
+    before = jnp.where(~start, jnp.where(upward, forth, back), jnp.where(start, ring, back))
+    after = jnp.where(end, jnp.where(end, ring, back), jnp.where(~upward, forth, back))
     return before, after
 
 
@@ -246,7 +243,7 @@
         in_specs=[pl.BlockSpec(memory_space=pltpu.MemorySpace.HBM)] * len(args),
         out_specs=pl.BlockSpec(memory_space=pltpu.VMEM),
         scratch_shapes=[pltpu.VMEM(a.shape, a.dtype) for a in args] + [pltpu.SemaphoreType.DMA((len(args),))],
-        compiler_params=pltpu.CompilerParams(vmem_limit_bytes=48 * 1024 * 1024),
+        compiler_params=pltpu.CompilerParams(vmem_limit_bytes=60 * 1024 * 1024),
         name="k_pack",
     )(*args)
 

time: 123 us -> 120 us (0.976)
  the two profiles are of different devices: /device:TPU:6 before, /device:TPU:71 now
where the time goes in v3:
time: 120 us; the launch traced here: 119 us
  starting transfers between devices  62.7 us (52%)
  waiting for transfers between devices  40.2 us (34%)
  Pallas kernels  13.3 us (11%)
  local copies, waits for them, and re-layouts  1.66 us (1%)
    ppermute x34, starting transfers between devices, send(): return lax.ppermute(x, AXES, pairs)  62.7 us
    ppermute x34, waiting for transfers between devices, send(): return lax.ppermute(x, AXES, pairs)  40.2 us
    pallas_call x10, Pallas kernels, call(): pl.pallas_call(kernel, out_shape=shapes, in_specs=[spec] * len(args), out...  11.8 us
  transfers between devices with their start and end apart: 34, of which 17 were waited for; matrix products, arithmetic and copies ran while one was open for 0% of the time, Pallas kernels for 5%

profile of v3, /device:TPU:71, one launch (start us, length us, event | category | flops | bytes accessed | tf_op | source)
XLA Modules:
  0.0 119.4 jit_solution(673070158260644659)
XLA Ops:
  0.6 1.5 %k_pack.1 = f32[48,128]{1,0:T(8,128)} custom-call(f32[3,1,1,1,512]{4,3,2,1,0:T(1,128)} %pos_in.1, s32[1,1,1,512]{3,2,1,0:T(1,128)} %kind_in.1, s32[2,2,2,8]{3,2,1,0:T(2,128)} %names_in.1, s32[1,1,1,8,128]{4,3,2,1,0:T(8,128)} %center_in.1, s32[1,1,1,8,128]{4,3,2,1,0:T(8,128)} %partner_in.1, s32[1,1,1,8,128]{4,3,2,1,0:T(8,128)} %live_in.1), custom_call_target="tpu_custom_call" | custom-call | tf_op jit(solution)/shard_map/k_pack/pallas_call | solution.py:240
  2.1 8.3 %collective-permute-start = (f32[48,128]{1,0:T(8,128)}, f32[48,128]{1,0:T(8,128)S(1)}, u32[]{:S(2)}, u32[]{:S(2)}) collective-permute-start(f32[48,128]{1,0:T(8,128)} %k_pack.1), channel_id=1, source_target_pairs={{0,0},{1,32},{2,1},{3,33},{4,2},{5,34},{6,3},{7,35},{8,8},{9,40},{... | collective-permute-start | bytes 73736 | tf_op jit(solution)/shard_map/ppermute | solution.py:70
  10.5 7.4 %collective-permute-done.packed_ref = f32[48,128]{1,0:T(8,128)S(1)} collective-permute-done((f32[48,128]{1,0:T(8,128)}, f32[48,128]{1,0:T(8,128)S(1)}, u32[]{:S(2)}, u32[]{:S(2)}) %collective-permute-start) | collective-permute-done | bytes 24608 | tf_op jit(solution)/shard_map/ppermute | solution.py:70
  18.2 0.7 collective-permute-start.3
  18.9 1.5 %collective-permute-start.1 = (f32[1,2,2,8,128]{4,3,2,1,0:T(8,128)S(1)}, f32[1,2,2,8,128]{4,3,2,1,0:T(8,128)S(1)}, u32[]{:S(2)}, u32[]{:S(2)}) collective-permute-start(f32[1,2,2,8,128]{4,3,2,1,0:T(8,128)S(1)} %get-tuple-element.97), channel_id=1, source_target_pairs={{0,64},{32,0},{64,128},{96,32},{128,192},{160,96},{192,256},{224,1... | collective-permute-start | bytes 49160 | tf_op jit(solution)/shard_map/ppermute | solution.py:70
  20.3 1.1 collective-permute-done.2
  21.5 4.6 %collective-permute-start.6 = (f32[4,1,2,8,128]{4,3,2,1,0:T(8,128)S(1)}, f32[4,1,2,8,128]{4,3,2,1,0:T(8,128)S(1)}, u32[]{:S(2)}, u32[]{:S(2)}) collective-permute-start(f32[4,1,2,8,128]{4,3,2,1,0:T(8,128)S(1)} %get-tuple-element.88), channel_id=1, source_target_pairs={{0,24},{32,56},{64,88},{96,120},{128,152},{160,184},{192,216},{224... | collective-permute-start | bytes 98312 | tf_op jit(solution)/shard_map/ppermute | solution.py:70
  26.2 3.8 %collective-permute-start.4 = (f32[4,1,2,8,128]{4,3,2,1,0:T(8,128)S(1)}, f32[4,1,2,8,128]{4,3,2,1,0:T(8,128)S(1)}, u32[]{:S(2)}, u32[]{:S(2)}) collective-permute-start(f32[4,1,2,8,128]{4,3,2,1,0:T(8,128)S(1)} %get-tuple-element.89), channel_id=1, source_target_pairs={{0,8},{32,0},{64,72},{96,64},{128,136},{160,128},{192,200},{224,19... | collective-permute-start | bytes 98312 | tf_op jit(solution)/shard_map/ppermute | solution.py:70
  30.1 0.7 copy-done.2
  30.8 0.6 copy-done.3
  31.6 2.4 %collective-permute-start.8 = (f32[4,4,8,128]{3,2,1,0:T(8,128)S(1)}, f32[4,4,8,128]{3,2,1,0:T(8,128)S(1)}, u32[]{:S(2)}, u32[]{:S(2)}) collective-permute-start(f32[4,4,8,128]{3,2,1,0:T(8,128)S(1)} %get-tuple-element.72), channel_id=1, source_target_pairs={{32,0},{1,32},{33,1},{2,33},{34,2},{3,34},{35,3},{0,35},{40,8},{9,... | collective-permute-start | bytes 196616 | tf_op jit(solution)/shard_map/ppermute | solution.py:70
  34.0 5.9 %collective-permute-start.7 = (f32[4,4,8,128]{3,2,1,0:T(8,128)S(1)}, f32[4,4,8,128]{3,2,1,0:T(8,128)S(1)}, u32[]{:S(2)}, u32[]{:S(2)}) collective-permute-start(f32[4,4,8,128]{3,2,1,0:T(8,128)S(1)} %get-tuple-element.73), channel_id=1, source_target_pairs={{0,32},{32,1},{1,33},{33,2},{2,34},{34,3},{3,35},{35,0},{8,40},{40... | collective-permute-start | bytes 196616 | tf_op jit(solution)/shard_map/ppermute | solution.py:70
  40.4 1.4 %collective-permute-done.8 = f32[4,4,8,128]{3,2,1,0:T(8,128)S(1)} collective-permute-done((f32[4,4,8,128]{3,2,1,0:T(8,128)S(1)}, f32[4,4,8,128]{3,2,1,0:T(8,128)S(1)}, u32[]{:S(2)}, u32[]{:S(2)}) %collective-permute-start.8) | collective-permute-done | bytes 65568 | tf_op jit(solution)/shard_map/ppermute | solution.py:70
  41.8 1.5 %k_features.1 = (f32[32,192]{1,0:T(8,128)S(1)}, f32[32,192]{1,0:T(8,128)S(1)}, f32[8,1024]{1,0:T(8,128)S(1)}, f32[128,1024]{1,0:T(8,128)S(1)}, f32[128,1024]{1,0:T(8,128)S(1)}) custom-call(f32[48,128]{1,0:T(8,128)S(1)} %collective-permute-done.packed_ref, f32[8,1024]{1,0:T(8,128)S(1)} %k_own_pairs.1.part_ref, f32[128,128]{1,0:T(8,128)S(1)} %bitcast.52, ...), custom_call_target="tpu_custom_call" | custom-call | tf_op jit(solution)/shard_map/k_features/pallas_call | solution.py:503
  43.4 0.7 collective-permute-start.11
  44.1 1.8 %collective-permute-start.9 = (f32[1,2,2,8,192]{4,3,2,1,0:T(8,128)S(1)}, f32[1,2,2,8,192]{4,3,2,1,0:T(8,128)S(1)}, u32[]{:S(2)}, u32[]{:S(2)}) collective-permute-start(f32[1,2,2,8,192]{4,3,2,1,0:T(8,128)S(1)} %get-tuple-element.87), channel_id=1, source_target_pairs={{0,64},{32,0},{64,128},{96,32},{128,192},{160,96},{192,256},{224,1... | collective-permute-start | bytes 73736 | tf_op jit(solution)/shard_map/ppermute | solution.py:70
  45.8 1.3 %collective-permute-done.10 = f32[1,2,2,8,192]{4,3,2,1,0:T(8,128)S(1)} collective-permute-done((f32[1,2,2,8,192]{4,3,2,1,0:T(8,128)S(1)}, f32[1,2,2,8,192]{4,3,2,1,0:T(8,128)S(1)}, u32[]{:S(2)}, u32[]{:S(2)}) %collective-permute-start.10) | collective-permute-done | bytes 24608 | tf_op jit(solution)/shard_map/ppermute | solution.py:70
  47.2 2.8 %collective-permute-start.14 = (f32[4,1,2,8,192]{4,3,2,1,0:T(8,128)S(1)}, f32[4,1,2,8,192]{4,3,2,1,0:T(8,128)S(1)}, u32[]{:S(2)}, u32[]{:S(2)}) collective-permute-start(f32[4,1,2,8,192]{4,3,2,1,0:T(8,128)S(1)} %get-tuple-element.69), channel_id=1, source_target_pairs={{0,24},{32,56},{64,88},{96,120},{128,152},{160,184},{192,216},{224... | collective-permute-start | bytes 147464 | tf_op jit(solution)/shard_map/ppermute | solution.py:70
  49.9 1.6 %collective-permute-start.12 = (f32[4,1,2,8,192]{4,3,2,1,0:T(8,128)S(1)}, f32[4,1,2,8,192]{4,3,2,1,0:T(8,128)S(1)}, u32[]{:S(2)}, u32[]{:S(2)}) collective-permute-start(f32[4,1,2,8,192]{4,3,2,1,0:T(8,128)S(1)} %get-tuple-element.70), channel_id=1, source_target_pairs={{0,8},{32,0},{64,72},{96,64},{128,136},{160,128},{192,200},{224,19... | collective-permute-start | bytes 147464 | tf_op jit(solution)/shard_map/ppermute | solution.py:70
  51.5 1.9 %collective-permute-done.14 = f32[4,1,2,8,192]{4,3,2,1,0:T(8,128)S(1)} collective-permute-done((f32[4,1,2,8,192]{4,3,2,1,0:T(8,128)S(1)}, f32[4,1,2,8,192]{4,3,2,1,0:T(8,128)S(1)}, u32[]{:S(2)}, u32[]{:S(2)}) %collective-permute-start.14) | collective-permute-done | bytes 49184 | tf_op jit(solution)/shard_map/ppermute | solution.py:70
  53.5 2.4 %collective-permute-start.16 = (f32[4,4,8,192]{3,2,1,0:T(8,128)S(1)}, f32[4,4,8,192]{3,2,1,0:T(8,128)S(1)}, u32[]{:S(2)}, u32[]{:S(2)}) collective-permute-start(f32[4,4,8,192]{3,2,1,0:T(8,128)S(1)} %get-tuple-element.57), channel_id=1, source_target_pairs={{32,0},{1,32},{33,1},{2,33},{34,2},{3,34},{35,3},{0,35},{40,8},{9,... | collective-permute-start | bytes 294920 | tf_op jit(solution)/shard_map/ppermute | solution.py:70
  55.9 5.0 %collective-permute-start.15 = (f32[4,4,8,192]{3,2,1,0:T(8,128)S(1)}, f32[4,4,8,192]{3,2,1,0:T(8,128)S(1)}, u32[]{:S(2)}, u32[]{:S(2)}) collective-permute-start(f32[4,4,8,192]{3,2,1,0:T(8,128)S(1)} %get-tuple-element.58), channel_id=1, source_target_pairs={{0,32},{32,1},{1,33},{33,2},{2,34},{34,3},{3,35},{35,0},{8,40},{40... | collective-permute-start | bytes 294920 | tf_op jit(solution)/shard_map/ppermute | solution.py:70
  61.1 2.4 %k_own_env.1 = (f32[192,1024]{1,0:T(8,128)S(1)}, f32[192,1024]{1,0:T(8,128)S(1)}, f32[128,1024]{1,0:T(8,128)S(1)}, f32[128,1024]{1,0:T(8,128)S(1)}, f32[128,1024]{1,0:T(8,128)S(1)}, /*index=5*/f32[128,1024]{1,0:T(8,128)S(1)}) custom-call(f32[48,128]{1,0:T(8,128)S(1)} %collective-permute-done.packed_ref, f32[8,1024]{1,0:T(8,128)S(1)} %get-tuple-element.31.scal_ref, ...), custom_call_target="tpu_custom_call" | custom-call | tf_op jit(solution)/shard_map/k_own_env/pallas_call | solution.py:503
  63.6 2.2 %k_energy.1 = (f32[128,192]{1,0:T(8,128)S(1)}, f32[128,192]{1,0:T(8,128)S(1)}, f32[256,192]{1,0:T(8,128)S(1)}, f32[192,1024]{1,0:T(8,128)S(1)}, f32[128,1024]{1,0:T(8,128)S(1)}, /*index=5*/f32[64,1024]{1,0:T(8,128)S(1)}) custom-call(f32[48,128]{1,0:T(8,128)S(1)} %collective-permute-done.packed_ref, f32[8,1024]{1,0:T(8,128)S(1)} %get-tuple-element.31.scal_ref, ...), custom_call_target="tpu_custom_call" | custom-call | tf_op jit(solution)/shard_map/k_energy/pallas_call | solution.py:503
  65.7 3.0 %collective-permute-start.17 = (f32[4,4,8,192]{3,2,1,0:T(8,128)S(1)}, f32[4,4,8,192]{3,2,1,0:T(8,128)S(1)}, u32[]{:S(2)}, u32[]{:S(2)}) collective-permute-start(f32[4,4,8,192]{3,2,1,0:T(8,128)S(1)} %bitcast.54), channel_id=1, source_target_pairs={{0,32},{32,1},{1,33},{33,2},{2,34},{34,3},{3,35},{35,0},{8,40},{40... | collective-permute-start | bytes 294920 | tf_op jit(solution)/shard_map/ppermute | solution.py:70
  68.7 1.9 %collective-permute-done.17 = f32[4,4,8,192]{3,2,1,0:T(8,128)S(1)} collective-permute-done((f32[4,4,8,192]{3,2,1,0:T(8,128)S(1)}, f32[4,4,8,192]{3,2,1,0:T(8,128)S(1)}, u32[]{:S(2)}, u32[]{:S(2)}) %collective-permute-start.17) | collective-permute-done | bytes 98336 | tf_op jit(solution)/shard_map/ppermute | solution.py:70
  70.7 3.7 %collective-permute-done.18 = f32[4,4,8,192]{3,2,1,0:T(8,128)S(1)} collective-permute-done((f32[4,4,8,192]{3,2,1,0:T(8,128)S(1)}, f32[4,4,8,192]{3,2,1,0:T(8,128)S(1)}, u32[]{:S(2)}, u32[]{:S(2)}) %collective-permute-start.18) | collective-permute-done | bytes 98336 | tf_op jit(solution)/shard_map/ppermute | solution.py:70
  74.4 3.7 %collective-permute-start.21 = (f32[4,1,2,8,192]{4,3,2,1,0:T(8,128)S(1)}, f32[4,1,2,8,192]{4,3,2,1,0:T(8,128)S(1)}, u32[]{:S(2)}, u32[]{:S(2)}) collective-permute-start(f32[4,1,2,8,192]{4,3,2,1,0:T(8,128)S(1)} %get-tuple-element.54), channel_id=1, source_target_pairs={{0,24},{32,56},{64,88},{96,120},{128,152},{160,184},{192,216},{224... | collective-permute-start | bytes 147464 | tf_op jit(solution)/shard_map/ppermute | solution.py:70
  78.1 1.5 %collective-permute-start.20 = (f32[4,1,2,8,192]{4,3,2,1,0:T(8,128)S(1)}, f32[4,1,2,8,192]{4,3,2,1,0:T(8,128)S(1)}, u32[]{:S(2)}, u32[]{:S(2)}) collective-permute-start(f32[4,1,2,8,192]{4,3,2,1,0:T(8,128)S(1)} %get-tuple-element.56), channel_id=1, source_target_pairs={{8,0},{0,32},{72,64},{64,96},{136,128},{128,160},{200,192},{192,22... | collective-permute-start | bytes 147464 | tf_op jit(solution)/shard_map/ppermute | solution.py:70
  79.6 1.0 collective-permute-done.21
  80.6 0.6 collective-permute-done.19
  81.3 0.7 collective-permute-start.24
  82.0 1.8 %collective-permute-start.22 = (f32[1,2,2,8,192]{4,3,2,1,0:T(8,128)S(1)}, f32[1,2,2,8,192]{4,3,2,1,0:T(8,128)S(1)}, u32[]{:S(2)}, u32[]{:S(2)}) collective-permute-start(f32[1,2,2,8,192]{4,3,2,1,0:T(8,128)S(1)} %get-tuple-element.67), channel_id=1, source_target_pairs={{0,64},{32,0},{64,128},{96,32},{128,192},{160,96},{192,256},{224,1... | collective-permute-start | bytes 73736 | tf_op jit(solution)/shard_map/ppermute | solution.py:70
  83.7 2.4 %k_direct.1 = (f32[8,1024]{1,0:T(8,128)S(1)}, f32[4,512]{1,0:T(4,128)S(1)}) custom-call(f32[48,128]{1,0:T(8,128)S(1)} %collective-permute-done.packed_ref, f32[8,1024]{1,0:T(8,128)S(1)} %get-tuple-element.31.scal_ref, f32[128,1024]{1,0:T(8,128)S(1)} %get-tuple-element.32.av_ref, f32[128,1024]{1,0:T(8,128)S(1)} %get-tuple-element.34.nav_ref, ...), custom_call_target="tpu_custom_call" | custom-call | tf_op jit(solution)/shard_map/k_direct/pallas_call | solution.py:503
  86.1 1.7 %collective-permute-done.23 = f32[1,2,2,8,192]{4,3,2,1,0:T(8,128)S(1)} collective-permute-done((f32[1,2,2,8,192]{4,3,2,1,0:T(8,128)S(1)}, f32[1,2,2,8,192]{4,3,2,1,0:T(8,128)S(1)}, u32[]{:S(2)}, u32[]{:S(2)}) %collective-permute-start.23) | collective-permute-done | bytes 24608 | tf_op jit(solution)/shard_map/ppermute | solution.py:70
  87.9 1.2 k_env_back.1
  89.6 0.9 collective-permute-done.25
  90.5 3.6 %collective-permute-done.26 = f32[4,4,8,128]{3,2,1,0:T(8,128)S(1)} collective-permute-done((f32[4,4,8,128]{3,2,1,0:T(8,128)S(1)}, f32[4,4,8,128]{3,2,1,0:T(8,128)S(1)}, u32[]{:S(2)}, u32[]{:S(2)}) %collective-permute-start.26) | collective-permute-done | bytes 65568 | tf_op jit(solution)/shard_map/ppermute | solution.py:70
  94.1 3.0 %collective-permute-start.29 = (f32[4,1,2,8,128]{4,3,2,1,0:T(8,128)S(1)}, f32[4,1,2,8,128]{4,3,2,1,0:T(8,128)S(1)}, u32[]{:S(2)}, u32[]{:S(2)}) collective-permute-start(f32[4,1,2,8,128]{4,3,2,1,0:T(8,128)S(1)} %get-tuple-element.63), channel_id=1, source_target_pairs={{0,24},{32,56},{64,88},{96,120},{128,152},{160,184},{192,216},{224... | collective-permute-start | bytes 98312 | tf_op jit(solution)/shard_map/ppermute | solution.py:70
  97.1 1.5 %collective-permute-start.28 = (f32[4,1,2,8,128]{4,3,2,1,0:T(8,128)S(1)}, f32[4,1,2,8,128]{4,3,2,1,0:T(8,128)S(1)}, u32[]{:S(2)}, u32[]{:S(2)}) collective-permute-start(f32[4,1,2,8,128]{4,3,2,1,0:T(8,128)S(1)} %get-tuple-element.65), channel_id=1, source_target_pairs={{8,0},{0,32},{72,64},{64,96},{136,128},{128,160},{200,192},{192,22... | collective-permute-start | bytes 98312 | tf_op jit(solution)/shard_map/ppermute | solution.py:70
  98.6 1.4 %collective-permute-done.29 = f32[4,1,2,8,128]{4,3,2,1,0:T(8,128)S(1)} collective-permute-done((f32[4,1,2,8,128]{4,3,2,1,0:T(8,128)S(1)}, f32[4,1,2,8,128]{4,3,2,1,0:T(8,128)S(1)}, u32[]{:S(2)}, u32[]{:S(2)}) %collective-permute-start.29) | collective-permute-done | bytes 32800 | tf_op jit(solution)/shard_map/ppermute | solution.py:70
  100.0 0.7 collective-permute-start.32
  100.7 3.1 %collective-permute-start.30 = (f32[1,2,2,8,128]{4,3,2,1,0:T(8,128)S(1)}, f32[1,2,2,8,128]{4,3,2,1,0:T(8,128)S(1)}, u32[]{:S(2)}, u32[]{:S(2)}) collective-permute-start(f32[1,2,2,8,128]{4,3,2,1,0:T(8,128)S(1)} %get-tuple-element.83), channel_id=1, source_target_pairs={{0,64},{32,0},{64,128},{96,32},{128,192},{160,96},{192,256},{224,1... | collective-permute-start | bytes 49160 | tf_op jit(solution)/shard_map/ppermute | solution.py:70
  103.8 0.6 k_own_force.1.own_ref
  104.6 4.1 %collective-permute-done.31 = f32[1,2,2,8,128]{4,3,2,1,0:T(8,128)S(1)} collective-permute-done((f32[1,2,2,8,128]{4,3,2,1,0:T(8,128)S(1)}, f32[1,2,2,8,128]{4,3,2,1,0:T(8,128)S(1)}, u32[]{:S(2)}, u32[]{:S(2)}) %collective-permute-start.31) | collective-permute-done | bytes 16416 | tf_op jit(solution)/shard_map/ppermute | solution.py:70
  109.0 1.9 %collective-permute-start.33 = (f32[16,128]{1,0:T(8,128)S(1)}, f32[16,128]{1,0:T(8,128)S(1)}, u32[]{:S(2)}, u32[]{:S(2)}) collective-permute-start(f32[16,128]{1,0:T(8,128)S(1)} %k_force.1), channel_id=1, source_target_pairs={{0,0},{32,1},{1,2},{33,3},{2,4},{34,5},{3,6},{35,7},{8,8},{40,9},{... | collective-permute-start | bytes 24584 | tf_op jit(solution)/shard_map/ppermute | solution.py:70
  110.9 7.9 %collective-permute-done.33.in_ref = f32[16,128]{1,0:T(8,128)S(1)} collective-permute-done((f32[16,128]{1,0:T(8,128)S(1)}, f32[16,128]{1,0:T(8,128)S(1)}, u32[]{:S(2)}, u32[]{:S(2)}) %collective-permute-start.33) | collective-permute-done | bytes 8224 | tf_op jit(solution)/shard_map/ppermute | solution.py:70
  118.8 0.6 k_unpack.1
  (79 shorter events, 2.7 us)
Async XLA Ops:
  2.1 15.8 %collective-permute-start = (f32[48,128]{1,0:T(8,128)}, f32[48,128]{1,0:T(8,128)S(1)}, u32[]{:S(2)}, u32[]{:S(2)}) collective-permute-start(f32[48,128]{1,0:T(8,128)} %k_pack.1), channel_id=1, source_target_pairs={{0,0},{1,32},{2,1},{3,33},{4,2},{5,34},{6,3},{7,35},{8,8},{9,40},{... | collective-permute-start | bytes 73736 | tf_op jit(solution)/shard_map/ppermute | solution.py:70
  18.2 2.2 %collective-permute-start.3 = (f32[1,2,2,8,128]{4,3,2,1,0:T(8,128)S(1)}, f32[1,2,2,8,128]{4,3,2,1,0:T(8,128)S(1)}, u32[]{:S(2)}, u32[]{:S(2)}) collective-permute-start(f32[1,2,2,8,128]{4,3,2,1,0:T(8,128)S(1)} %get-tuple-element.95), channel_id=1, source_target_pairs={{0,452},{32,484},{452,0},{484,32},{8,460},{40,492},{460,8},{492,40... | collective-permute-start | bytes 49160 | tf_op jit(solution)/shard_map/ppermute | solution.py:70
  18.8 2.6 %collective-permute-start.2 = (f32[1,2,2,8,128]{4,3,2,1,0:T(8,128)S(1)}, f32[1,2,2,8,128]{4,3,2,1,0:T(8,128)S(1)}, u32[]{:S(2)}, u32[]{:S(2)}) collective-permute-start(f32[1,2,2,8,128]{4,3,2,1,0:T(8,128)S(1)} %get-tuple-element.96), channel_id=1, source_target_pairs={{64,0},{0,32},{128,64},{32,96},{192,128},{96,160},{256,192},{160,2... | collective-permute-start | bytes 49160 | tf_op jit(solution)/shard_map/ppermute | solution.py:70
  18.9 2.6 %collective-permute-start.1 = (f32[1,2,2,8,128]{4,3,2,1,0:T(8,128)S(1)}, f32[1,2,2,8,128]{4,3,2,1,0:T(8,128)S(1)}, u32[]{:S(2)}, u32[]{:S(2)}) collective-permute-start(f32[1,2,2,8,128]{4,3,2,1,0:T(8,128)S(1)} %get-tuple-element.97), channel_id=1, source_target_pairs={{0,64},{32,0},{64,128},{96,32},{128,192},{160,96},{192,256},{224,1... | collective-permute-start | bytes 49160 | tf_op jit(solution)/shard_map/ppermute | solution.py:70
  21.5 8.5 %copy-start.1 = (f32[128,64]{0,1:T(8,128)S(1)}, f32[128,64]{0,1:T(8,128)}, u32[]{:S(2)}) copy-start(f32[128,64]{0,1:T(8,128)} %param.22) | copy-start | bytes 98308
  21.5 10.0 %collective-permute-start.6 = (f32[4,1,2,8,128]{4,3,2,1,0:T(8,128)S(1)}, f32[4,1,2,8,128]{4,3,2,1,0:T(8,128)S(1)}, u32[]{:S(2)}, u32[]{:S(2)}) collective-permute-start(f32[4,1,2,8,128]{4,3,2,1,0:T(8,128)S(1)} %get-tuple-element.88), channel_id=1, source_target_pairs={{0,24},{32,56},{64,88},{96,120},{128,152},{160,184},{192,216},{224... | collective-permute-start | bytes 98312 | tf_op jit(solution)/shard_map/ppermute | solution.py:70
  26.2 5.3 %collective-permute-start.4 = (f32[4,1,2,8,128]{4,3,2,1,0:T(8,128)S(1)}, f32[4,1,2,8,128]{4,3,2,1,0:T(8,128)S(1)}, u32[]{:S(2)}, u32[]{:S(2)}) collective-permute-start(f32[4,1,2,8,128]{4,3,2,1,0:T(8,128)S(1)} %get-tuple-element.89), channel_id=1, source_target_pairs={{0,8},{32,0},{64,72},{96,64},{128,136},{160,128},{192,200},{224,19... | collective-permute-start | bytes 98312 | tf_op jit(solution)/shard_map/ppermute | solution.py:70
  30.0 1.5 %collective-permute-start.5 = (f32[4,1,2,8,128]{4,3,2,1,0:T(8,128)S(1)}, f32[4,1,2,8,128]{4,3,2,1,0:T(8,128)S(1)}, u32[]{:S(2)}, u32[]{:S(2)}) collective-permute-start(f32[4,1,2,8,128]{4,3,2,1,0:T(8,128)S(1)} %get-tuple-element.90), channel_id=1, source_target_pairs={{8,0},{0,32},{72,64},{64,96},{136,128},{128,160},{200,192},{192,22... | collective-permute-start | bytes 98312 | tf_op jit(solution)/shard_map/ppermute | solution.py:70
  30.0 0.8 copy-start.2
  30.7 0.7 copy-start.3
  30.7 0.7 copy-start.4
  30.7 0.7 copy-start.5
  31.6 10.2 %collective-permute-start.8 = (f32[4,4,8,128]{3,2,1,0:T(8,128)S(1)}, f32[4,4,8,128]{3,2,1,0:T(8,128)S(1)}, u32[]{:S(2)}, u32[]{:S(2)}) collective-permute-start(f32[4,4,8,128]{3,2,1,0:T(8,128)S(1)} %get-tuple-element.72), channel_id=1, source_target_pairs={{32,0},{1,32},{33,1},{2,33},{34,2},{3,34},{35,3},{0,35},{40,8},{9,... | collective-permute-start | bytes 196616 | tf_op jit(solution)/shard_map/ppermute | solution.py:70
  34.0 7.8 %collective-permute-start.7 = (f32[4,4,8,128]{3,2,1,0:T(8,128)S(1)}, f32[4,4,8,128]{3,2,1,0:T(8,128)S(1)}, u32[]{:S(2)}, u32[]{:S(2)}) collective-permute-start(f32[4,4,8,128]{3,2,1,0:T(8,128)S(1)} %get-tuple-element.73), channel_id=1, source_target_pairs={{0,32},{32,1},{1,33},{33,2},{2,34},{34,3},{3,35},{35,0},{8,40},{40... | collective-permute-start | bytes 196616 | tf_op jit(solution)/shard_map/ppermute | solution.py:70
  43.4 2.5 %collective-permute-start.11 = (f32[1,2,2,8,192]{4,3,2,1,0:T(8,128)S(1)}, f32[1,2,2,8,192]{4,3,2,1,0:T(8,128)S(1)}, u32[]{:S(2)}, u32[]{:S(2)}) collective-permute-start(f32[1,2,2,8,192]{4,3,2,1,0:T(8,128)S(1)} %get-tuple-element.85), channel_id=1, source_target_pairs={{0,452},{32,484},{452,0},{484,32},{8,460},{40,492},{460,8},{492,40... | collective-permute-start | bytes 73736 | tf_op jit(solution)/shard_map/ppermute | solution.py:70
  44.0 3.1 %collective-permute-start.10 = (f32[1,2,2,8,192]{4,3,2,1,0:T(8,128)S(1)}, f32[1,2,2,8,192]{4,3,2,1,0:T(8,128)S(1)}, u32[]{:S(2)}, u32[]{:S(2)}) collective-permute-start(f32[1,2,2,8,192]{4,3,2,1,0:T(8,128)S(1)} %get-tuple-element.86), channel_id=1, source_target_pairs={{64,0},{0,32},{128,64},{32,96},{192,128},{96,160},{256,192},{160,2... | collective-permute-start | bytes 73736 | tf_op jit(solution)/shard_map/ppermute | solution.py:70
  44.1 3.0 %collective-permute-start.9 = (f32[1,2,2,8,192]{4,3,2,1,0:T(8,128)S(1)}, f32[1,2,2,8,192]{4,3,2,1,0:T(8,128)S(1)}, u32[]{:S(2)}, u32[]{:S(2)}) collective-permute-start(f32[1,2,2,8,192]{4,3,2,1,0:T(8,128)S(1)} %get-tuple-element.87), channel_id=1, source_target_pairs={{0,64},{32,0},{64,128},{96,32},{128,192},{160,96},{192,256},{224,1... | collective-permute-start | bytes 73736 | tf_op jit(solution)/shard_map/ppermute | solution.py:70
  47.2 6.2 %collective-permute-start.14 = (f32[4,1,2,8,192]{4,3,2,1,0:T(8,128)S(1)}, f32[4,1,2,8,192]{4,3,2,1,0:T(8,128)S(1)}, u32[]{:S(2)}, u32[]{:S(2)}) collective-permute-start(f32[4,1,2,8,192]{4,3,2,1,0:T(8,128)S(1)} %get-tuple-element.69), channel_id=1, source_target_pairs={{0,24},{32,56},{64,88},{96,120},{128,152},{160,184},{192,216},{224... | collective-permute-start | bytes 147464 | tf_op jit(solution)/shard_map/ppermute | solution.py:70
  49.9 3.4 %collective-permute-start.12 = (f32[4,1,2,8,192]{4,3,2,1,0:T(8,128)S(1)}, f32[4,1,2,8,192]{4,3,2,1,0:T(8,128)S(1)}, u32[]{:S(2)}, u32[]{:S(2)}) collective-permute-start(f32[4,1,2,8,192]{4,3,2,1,0:T(8,128)S(1)} %get-tuple-element.70), channel_id=1, source_target_pairs={{0,8},{32,0},{64,72},{96,64},{128,136},{160,128},{192,200},{224,19... | collective-permute-start | bytes 147464 | tf_op jit(solution)/shard_map/ppermute | solution.py:70
  51.5 1.9 %collective-permute-start.13 = (f32[4,1,2,8,192]{4,3,2,1,0:T(8,128)S(1)}, f32[4,1,2,8,192]{4,3,2,1,0:T(8,128)S(1)}, u32[]{:S(2)}, u32[]{:S(2)}) collective-permute-start(f32[4,1,2,8,192]{4,3,2,1,0:T(8,128)S(1)} %get-tuple-element.71), channel_id=1, source_target_pairs={{8,0},{0,32},{72,64},{64,96},{136,128},{128,160},{200,192},{192,22... | collective-permute-start | bytes 147464 | tf_op jit(solution)/shard_map/ppermute | solution.py:70
  53.4 7.6 %copy-start = (f32[192,128]{1,0:T(8,128)S(1)}, f32[192,128]{1,0:T(8,128)}, u32[]{:S(2)}) copy-start(f32[192,128]{1,0:T(8,128)} %wm_ref.5) | copy-start | bytes 294916
  53.5 10.1 %collective-permute-start.16 = (f32[4,4,8,192]{3,2,1,0:T(8,128)S(1)}, f32[4,4,8,192]{3,2,1,0:T(8,128)S(1)}, u32[]{:S(2)}, u32[]{:S(2)}) collective-permute-start(f32[4,4,8,192]{3,2,1,0:T(8,128)S(1)} %get-tuple-element.57), channel_id=1, source_target_pairs={{32,0},{1,32},{33,1},{2,33},{34,2},{3,34},{35,3},{0,35},{40,8},{9,... | collective-permute-start | bytes 294920 | tf_op jit(solution)/shard_map/ppermute | solution.py:70
  55.9 5.0 %copy-start.6 = (f32[128]{0:T(128)S(1)}, f32[128]{0:T(128)}, u32[]{:S(2)}) copy-start(f32[128]{0:T(128)} %param.25) | copy-start | bytes 1540
  55.9 7.7 %collective-permute-start.15 = (f32[4,4,8,192]{3,2,1,0:T(8,128)S(1)}, f32[4,4,8,192]{3,2,1,0:T(8,128)S(1)}, u32[]{:S(2)}, u32[]{:S(2)}) collective-permute-start(f32[4,4,8,192]{3,2,1,0:T(8,128)S(1)} %get-tuple-element.58), channel_id=1, source_target_pairs={{0,32},{32,1},{1,33},{33,2},{2,34},{34,3},{3,35},{35,0},{8,40},{40... | collective-permute-start | bytes 294920 | tf_op jit(solution)/shard_map/ppermute | solution.py:70
  65.7 4.9 %collective-permute-start.17 = (f32[4,4,8,192]{3,2,1,0:T(8,128)S(1)}, f32[4,4,8,192]{3,2,1,0:T(8,128)S(1)}, u32[]{:S(2)}, u32[]{:S(2)}) collective-permute-start(f32[4,4,8,192]{3,2,1,0:T(8,128)S(1)} %bitcast.54), channel_id=1, source_target_pairs={{0,32},{32,1},{1,33},{33,2},{2,34},{34,3},{3,35},{35,0},{8,40},{40... | collective-permute-start | bytes 294920 | tf_op jit(solution)/shard_map/ppermute | solution.py:70
  68.7 5.6 %collective-permute-start.18 = (f32[4,4,8,192]{3,2,1,0:T(8,128)S(1)}, f32[4,4,8,192]{3,2,1,0:T(8,128)S(1)}, u32[]{:S(2)}, u32[]{:S(2)}) collective-permute-start(f32[4,4,8,192]{3,2,1,0:T(8,128)S(1)} %bitcast.53), channel_id=1, source_target_pairs={{32,0},{1,32},{33,1},{2,33},{34,2},{3,34},{35,3},{0,35},{40,8},{9,... | collective-permute-start | bytes 294920 | tf_op jit(solution)/shard_map/ppermute | solution.py:70
  74.4 6.2 %collective-permute-start.21 = (f32[4,1,2,8,192]{4,3,2,1,0:T(8,128)S(1)}, f32[4,1,2,8,192]{4,3,2,1,0:T(8,128)S(1)}, u32[]{:S(2)}, u32[]{:S(2)}) collective-permute-start(f32[4,1,2,8,192]{4,3,2,1,0:T(8,128)S(1)} %get-tuple-element.54), channel_id=1, source_target_pairs={{0,24},{32,56},{64,88},{96,120},{128,152},{160,184},{192,216},{224... | collective-permute-start | bytes 147464 | tf_op jit(solution)/shard_map/ppermute | solution.py:70
  78.1 3.1 %collective-permute-start.19 = (f32[4,1,2,8,192]{4,3,2,1,0:T(8,128)S(1)}, f32[4,1,2,8,192]{4,3,2,1,0:T(8,128)S(1)}, u32[]{:S(2)}, u32[]{:S(2)}) collective-permute-start(f32[4,1,2,8,192]{4,3,2,1,0:T(8,128)S(1)} %get-tuple-element.55), channel_id=1, source_target_pairs={{0,8},{32,0},{64,72},{96,64},{128,136},{160,128},{192,200},{224,19... | collective-permute-start | bytes 147464 | tf_op jit(solution)/shard_map/ppermute | solution.py:70
  78.1 3.1 %collective-permute-start.20 = (f32[4,1,2,8,192]{4,3,2,1,0:T(8,128)S(1)}, f32[4,1,2,8,192]{4,3,2,1,0:T(8,128)S(1)}, u32[]{:S(2)}, u32[]{:S(2)}) collective-permute-start(f32[4,1,2,8,192]{4,3,2,1,0:T(8,128)S(1)} %get-tuple-element.56), channel_id=1, source_target_pairs={{8,0},{0,32},{72,64},{64,96},{136,128},{128,160},{200,192},{192,22... | collective-permute-start | bytes 147464 | tf_op jit(solution)/shard_map/ppermute | solution.py:70
  81.3 4.8 %collective-permute-start.24 = (f32[1,2,2,8,192]{4,3,2,1,0:T(8,128)S(1)}, f32[1,2,2,8,192]{4,3,2,1,0:T(8,128)S(1)}, u32[]{:S(2)}, u32[]{:S(2)}) collective-permute-start(f32[1,2,2,8,192]{4,3,2,1,0:T(8,128)S(1)} %get-tuple-element.66), channel_id=1, source_target_pairs={{0,452},{32,484},{452,0},{484,32},{8,460},{40,492},{460,8},{492,40... | collective-permute-start | bytes 73736 | tf_op jit(solution)/shard_map/ppermute | solution.py:70
  82.0 4.2 %collective-permute-start.22 = (f32[1,2,2,8,192]{4,3,2,1,0:T(8,128)S(1)}, f32[1,2,2,8,192]{4,3,2,1,0:T(8,128)S(1)}, u32[]{:S(2)}, u32[]{:S(2)}) collective-permute-start(f32[1,2,2,8,192]{4,3,2,1,0:T(8,128)S(1)} %get-tuple-element.67), channel_id=1, source_target_pairs={{0,64},{32,0},{64,128},{96,32},{128,192},{160,96},{192,256},{224,1... | collective-permute-start | bytes 73736 | tf_op jit(solution)/shard_map/ppermute | solution.py:70
  83.7 4.1 %collective-permute-start.23 = (f32[1,2,2,8,192]{4,3,2,1,0:T(8,128)S(1)}, f32[1,2,2,8,192]{4,3,2,1,0:T(8,128)S(1)}, u32[]{:S(2)}, u32[]{:S(2)}) collective-permute-start(f32[1,2,2,8,192]{4,3,2,1,0:T(8,128)S(1)} %get-tuple-element.68), channel_id=1, source_target_pairs={{64,0},{0,32},{128,64},{32,96},{192,128},{96,160},{256,192},{160,2... | collective-permute-start | bytes 73736 | tf_op jit(solution)/shard_map/ppermute | solution.py:70
  89.0 1.4 %collective-permute-start.25 = (f32[4,4,8,128]{3,2,1,0:T(8,128)S(1)}, f32[4,4,8,128]{3,2,1,0:T(8,128)S(1)}, u32[]{:S(2)}, u32[]{:S(2)}) collective-permute-start(f32[4,4,8,128]{3,2,1,0:T(8,128)S(1)} %bitcast.56), channel_id=1, source_target_pairs={{0,32},{32,1},{1,33},{33,2},{2,34},{34,3},{3,35},{35,0},{8,40},{40... | collective-permute-start | bytes 196616 | tf_op jit(solution)/shard_map/ppermute | solution.py:70
  89.1 4.9 %collective-permute-start.26 = (f32[4,4,8,128]{3,2,1,0:T(8,128)S(1)}, f32[4,4,8,128]{3,2,1,0:T(8,128)S(1)}, u32[]{:S(2)}, u32[]{:S(2)}) collective-permute-start(f32[4,4,8,128]{3,2,1,0:T(8,128)S(1)} %bitcast.55), channel_id=1, source_target_pairs={{32,0},{1,32},{33,1},{2,33},{34,2},{3,34},{35,3},{0,35},{40,8},{9,... | collective-permute-start | bytes 196616 | tf_op jit(solution)/shard_map/ppermute | solution.py:70
  94.1 5.9 %collective-permute-start.29 = (f32[4,1,2,8,128]{4,3,2,1,0:T(8,128)S(1)}, f32[4,1,2,8,128]{4,3,2,1,0:T(8,128)S(1)}, u32[]{:S(2)}, u32[]{:S(2)}) collective-permute-start(f32[4,1,2,8,128]{4,3,2,1,0:T(8,128)S(1)} %get-tuple-element.63), channel_id=1, source_target_pairs={{0,24},{32,56},{64,88},{96,120},{128,152},{160,184},{192,216},{224... | collective-permute-start | bytes 98312 | tf_op jit(solution)/shard_map/ppermute | solution.py:70
  97.1 2.9 %collective-permute-start.27 = (f32[4,1,2,8,128]{4,3,2,1,0:T(8,128)S(1)}, f32[4,1,2,8,128]{4,3,2,1,0:T(8,128)S(1)}, u32[]{:S(2)}, u32[]{:S(2)}) collective-permute-start(f32[4,1,2,8,128]{4,3,2,1,0:T(8,128)S(1)} %get-tuple-element.64), channel_id=1, source_target_pairs={{0,8},{32,0},{64,72},{96,64},{128,136},{160,128},{192,200},{224,19... | collective-permute-start | bytes 98312 | tf_op jit(solution)/shard_map/ppermute | solution.py:70
  97.1 2.8 %collective-permute-start.28 = (f32[4,1,2,8,128]{4,3,2,1,0:T(8,128)S(1)}, f32[4,1,2,8,128]{4,3,2,1,0:T(8,128)S(1)}, u32[]{:S(2)}, u32[]{:S(2)}) collective-permute-start(f32[4,1,2,8,128]{4,3,2,1,0:T(8,128)S(1)} %get-tuple-element.65), channel_id=1, source_target_pairs={{8,0},{0,32},{72,64},{64,96},{136,128},{128,160},{200,192},{192,22... | collective-permute-start | bytes 98312 | tf_op jit(solution)/shard_map/ppermute | solution.py:70
  100.0 4.4 %collective-permute-start.32 = (f32[1,2,2,8,128]{4,3,2,1,0:T(8,128)S(1)}, f32[1,2,2,8,128]{4,3,2,1,0:T(8,128)S(1)}, u32[]{:S(2)}, u32[]{:S(2)}) collective-permute-start(f32[1,2,2,8,128]{4,3,2,1,0:T(8,128)S(1)} %get-tuple-element.82), channel_id=1, source_target_pairs={{0,452},{32,484},{452,0},{484,32},{8,460},{40,492},{460,8},{492,40... | collective-permute-start | bytes 49160 | tf_op jit(solution)/shard_map/ppermute | solution.py:70
  100.7 4.0 %collective-permute-start.30 = (f32[1,2,2,8,128]{4,3,2,1,0:T(8,128)S(1)}, f32[1,2,2,8,128]{4,3,2,1,0:T(8,128)S(1)}, u32[]{:S(2)}, u32[]{:S(2)}) collective-permute-start(f32[1,2,2,8,128]{4,3,2,1,0:T(8,128)S(1)} %get-tuple-element.83), channel_id=1, source_target_pairs={{0,64},{32,0},{64,128},{96,32},{128,192},{160,96},{192,256},{224,1... | collective-permute-start | bytes 49160 | tf_op jit(solution)/shard_map/ppermute | solution.py:70
  103.8 5.0 %collective-permute-start.31 = (f32[1,2,2,8,128]{4,3,2,1,0:T(8,128)S(1)}, f32[1,2,2,8,128]{4,3,2,1,0:T(8,128)S(1)}, u32[]{:S(2)}, u32[]{:S(2)}) collective-permute-start(f32[1,2,2,8,128]{4,3,2,1,0:T(8,128)S(1)} %get-tuple-element.84), channel_id=1, source_target_pairs={{64,0},{0,32},{128,64},{32,96},{192,128},{96,160},{256,192},{160,2... | collective-permute-start | bytes 49160 | tf_op jit(solution)/shard_map/ppermute | solution.py:70
  109.0 9.8 %collective-permute-start.33 = (f32[16,128]{1,0:T(8,128)S(1)}, f32[16,128]{1,0:T(8,128)S(1)}, u32[]{:S(2)}, u32[]{:S(2)}) collective-permute-start(f32[16,128]{1,0:T(8,128)S(1)} %k_force.1), channel_id=1, source_target_pairs={{0,0},{32,1},{1,2},{33,3},{2,4},{34,5},{3,6},{35,7},{8,8},{40,9},{... | collective-permute-start | bytes 24584 | tf_op jit(solution)/shard_map/ppermute | solution.py:70

commit v4 on v3

--- a/solution.py
+++ b/solution.py
@@ -96,16 +96,17 @@
     return before, after, cells
 
 
-def collect(before, after, cells, here):
+def collect(before, after, cells, here, beside):
     first = send(after, UP)
     last = send(before, DOWN)
     cells = cells + jnp.stack([first, last], axis=2)
+    cells, beside = lax.optimization_barrier((cells, beside))
     for axis in (1, 0):
         first = lax.slice_in_dim(cells, 0, 1, axis=axis)
         last = lax.slice_in_dim(cells, 3, 4, axis=axis)
         from_before, from_after = swap(axis, first, last, here)
         cells = lax.slice_in_dim(cells, 1, 3, axis=axis) + jnp.concatenate([from_before, from_after], axis=axis)
-    return cells
+    return cells, beside
 
 
 def split2(x):
@@ -590,13 +591,15 @@
         wo,
     )
     before, after = before.reshape(4, 4, 8, 192), after.reshape(4, 4, 8, 192)
-    back = collect(before, after, cells.reshape(4, 4, 2, 8, 192), here).reshape(LIST, 192)
+    back, (part, energy) = collect(before, after, cells.reshape(4, 4, 2, 8, 192), here, (part, energy))
+    back = back.reshape(LIST, 192)
     before, after, cells, dbar = call(
         k_env_back, [(128, 128), (128, 128), (256, 128), (8, PAIRS)], packed, scal, av, nav, part, back, column
     )
     (own,) = call(k_own_force, [(8, ATOMS)], packed, dbar)
     before, after = before.reshape(4, 4, 8, 128), after.reshape(4, 4, 8, 128)
-    back = collect(before, after, cells.reshape(4, 4, 2, 8, 128), here).reshape(LIST, 128)
+    back, own = collect(before, after, cells.reshape(4, 4, 2, 8, 128), here, own)
+    back = back.reshape(LIST, 128)
     (out,) = call(k_force, [(16, 128)], own, back, column, energy)
     out = send(out, MOVE_OUT)
     return call(k_unpack, [(3, 1, 1, 1, ATOMS), (1, 1, 1, ATOMS)], out)

time: 120 us -> 120 us (level)
  no operation moved by 1% of the time
where the time goes in v4:
time: 120 us; the launch traced here: 119 us
  starting transfers between devices  61.8 us (52%)
  waiting for transfers between devices  40.6 us (34%)
  Pallas kernels  13.2 us (11%)
  local copies, waits for them, and re-layouts  1.66 us (1%)
    ppermute x34, starting transfers between devices, send(): return lax.ppermute(x, AXES, pairs)  61.8 us
    ppermute x34, waiting for transfers between devices, send(): return lax.ppermute(x, AXES, pairs)  40.6 us
    pallas_call x10, Pallas kernels, call(): pl.pallas_call(kernel, out_shape=shapes, in_specs=[spec] * len(args), out...  11.7 us
  transfers between devices with their start and end apart: 34, of which 17 were waited for; matrix products, arithmetic and copies ran while one was open for 0% of the time, Pallas kernels for 5%

profile of v4, /device:TPU:71, one launch (start us, length us, event | category | flops | bytes accessed | tf_op | source)
XLA Modules:
  0.0 118.9 jit_solution(2035353886751326981)
XLA Ops:
  0.6 1.5 %k_pack.1 = f32[48,128]{1,0:T(8,128)} custom-call(f32[3,1,1,1,512]{4,3,2,1,0:T(1,128)} %pos_in.1, s32[1,1,1,512]{3,2,1,0:T(1,128)} %kind_in.1, s32[2,2,2,8]{3,2,1,0:T(2,128)} %names_in.1, s32[1,1,1,8,128]{4,3,2,1,0:T(8,128)} %center_in.1, s32[1,1,1,8,128]{4,3,2,1,0:T(8,128)} %partner_in.1, s32[1,1,1,8,128]{4,3,2,1,0:T(8,128)} %live_in.1), custom_call_target="tpu_custom_call" | custom-call | tf_op jit(solution)/shard_map/k_pack/pallas_call | solution.py:241
  2.1 8.3 %collective-permute-start = (f32[48,128]{1,0:T(8,128)}, f32[48,128]{1,0:T(8,128)S(1)}, u32[]{:S(2)}, u32[]{:S(2)}) collective-permute-start(f32[48,128]{1,0:T(8,128)} %k_pack.1), channel_id=1, source_target_pairs={{0,0},{1,32},{2,1},{3,33},{4,2},{5,34},{6,3},{7,35},{8,8},{9,40},{... | collective-permute-start | bytes 73736 | tf_op jit(solution)/shard_map/ppermute | solution.py:70
  10.5 7.4 %collective-permute-done.packed_ref = f32[48,128]{1,0:T(8,128)S(1)} collective-permute-done((f32[48,128]{1,0:T(8,128)}, f32[48,128]{1,0:T(8,128)S(1)}, u32[]{:S(2)}, u32[]{:S(2)}) %collective-permute-start) | collective-permute-done | bytes 24608 | tf_op jit(solution)/shard_map/ppermute | solution.py:70
  18.2 0.7 collective-permute-start.3
  18.9 1.5 %collective-permute-start.1 = (f32[1,2,2,8,128]{4,3,2,1,0:T(8,128)S(1)}, f32[1,2,2,8,128]{4,3,2,1,0:T(8,128)S(1)}, u32[]{:S(2)}, u32[]{:S(2)}) collective-permute-start(f32[1,2,2,8,128]{4,3,2,1,0:T(8,128)S(1)} %get-tuple-element.107), channel_id=1, source_target_pairs={{0,64},{32,0},{64,128},{96,32},{128,192},{160,96},{192,256},{224,1... | collective-permute-start | bytes 49160 | tf_op jit(solution)/shard_map/ppermute | solution.py:70
  20.3 1.1 collective-permute-done.2
  21.5 4.6 %collective-permute-start.6 = (f32[4,1,2,8,128]{4,3,2,1,0:T(8,128)S(1)}, f32[4,1,2,8,128]{4,3,2,1,0:T(8,128)S(1)}, u32[]{:S(2)}, u32[]{:S(2)}) collective-permute-start(f32[4,1,2,8,128]{4,3,2,1,0:T(8,128)S(1)} %get-tuple-element.98), channel_id=1, source_target_pairs={{0,24},{32,56},{64,88},{96,120},{128,152},{160,184},{192,216},{224... | collective-permute-start | bytes 98312 | tf_op jit(solution)/shard_map/ppermute | solution.py:70
  26.2 3.8 %collective-permute-start.4 = (f32[4,1,2,8,128]{4,3,2,1,0:T(8,128)S(1)}, f32[4,1,2,8,128]{4,3,2,1,0:T(8,128)S(1)}, u32[]{:S(2)}, u32[]{:S(2)}) collective-permute-start(f32[4,1,2,8,128]{4,3,2,1,0:T(8,128)S(1)} %get-tuple-element.99), channel_id=1, source_target_pairs={{0,8},{32,0},{64,72},{96,64},{128,136},{160,128},{192,200},{224,19... | collective-permute-start | bytes 98312 | tf_op jit(solution)/shard_map/ppermute | solution.py:70
  30.1 0.7 copy-done.2
  30.8 0.6 copy-done.3
  31.6 2.4 %collective-permute-start.8 = (f32[4,4,8,128]{3,2,1,0:T(8,128)S(1)}, f32[4,4,8,128]{3,2,1,0:T(8,128)S(1)}, u32[]{:S(2)}, u32[]{:S(2)}) collective-permute-start(f32[4,4,8,128]{3,2,1,0:T(8,128)S(1)} %get-tuple-element.82), channel_id=1, source_target_pairs={{32,0},{1,32},{33,1},{2,33},{34,2},{3,34},{35,3},{0,35},{40,8},{9,... | collective-permute-start | bytes 196616 | tf_op jit(solution)/shard_map/ppermute | solution.py:70
  34.0 5.9 %collective-permute-start.7 = (f32[4,4,8,128]{3,2,1,0:T(8,128)S(1)}, f32[4,4,8,128]{3,2,1,0:T(8,128)S(1)}, u32[]{:S(2)}, u32[]{:S(2)}) collective-permute-start(f32[4,4,8,128]{3,2,1,0:T(8,128)S(1)} %get-tuple-element.83), channel_id=1, source_target_pairs={{0,32},{32,1},{1,33},{33,2},{2,34},{34,3},{3,35},{35,0},{8,40},{40... | collective-permute-start | bytes 196616 | tf_op jit(solution)/shard_map/ppermute | solution.py:70
  40.4 1.4 %collective-permute-done.8 = f32[4,4,8,128]{3,2,1,0:T(8,128)S(1)} collective-permute-done((f32[4,4,8,128]{3,2,1,0:T(8,128)S(1)}, f32[4,4,8,128]{3,2,1,0:T(8,128)S(1)}, u32[]{:S(2)}, u32[]{:S(2)}) %collective-permute-start.8) | collective-permute-done | bytes 65568 | tf_op jit(solution)/shard_map/ppermute | solution.py:70
  41.8 1.5 %k_features.1 = (f32[32,192]{1,0:T(8,128)S(1)}, f32[32,192]{1,0:T(8,128)S(1)}, f32[8,1024]{1,0:T(8,128)S(1)}, f32[128,1024]{1,0:T(8,128)S(1)}, f32[128,1024]{1,0:T(8,128)S(1)}) custom-call(f32[48,128]{1,0:T(8,128)S(1)} %collective-permute-done.packed_ref, f32[8,1024]{1,0:T(8,128)S(1)} %k_own_pairs.1.part_ref, f32[128,128]{1,0:T(8,128)S(1)} %bitcast.52, ...), custom_call_target="tpu_custom_call" | custom-call | tf_op jit(solution)/shard_map/k_features/pallas_call | solution.py:504
  43.4 0.7 collective-permute-start.11
  44.1 1.8 %collective-permute-start.9 = (f32[1,2,2,8,192]{4,3,2,1,0:T(8,128)S(1)}, f32[1,2,2,8,192]{4,3,2,1,0:T(8,128)S(1)}, u32[]{:S(2)}, u32[]{:S(2)}) collective-permute-start(f32[1,2,2,8,192]{4,3,2,1,0:T(8,128)S(1)} %get-tuple-element.97), channel_id=1, source_target_pairs={{0,64},{32,0},{64,128},{96,32},{128,192},{160,96},{192,256},{224,1... | collective-permute-start | bytes 73736 | tf_op jit(solution)/shard_map/ppermute | solution.py:70
  45.8 1.3 %collective-permute-done.10 = f32[1,2,2,8,192]{4,3,2,1,0:T(8,128)S(1)} collective-permute-done((f32[1,2,2,8,192]{4,3,2,1,0:T(8,128)S(1)}, f32[1,2,2,8,192]{4,3,2,1,0:T(8,128)S(1)}, u32[]{:S(2)}, u32[]{:S(2)}) %collective-permute-start.10) | collective-permute-done | bytes 24608 | tf_op jit(solution)/shard_map/ppermute | solution.py:70
  47.2 2.8 %collective-permute-start.14 = (f32[4,1,2,8,192]{4,3,2,1,0:T(8,128)S(1)}, f32[4,1,2,8,192]{4,3,2,1,0:T(8,128)S(1)}, u32[]{:S(2)}, u32[]{:S(2)}) collective-permute-start(f32[4,1,2,8,192]{4,3,2,1,0:T(8,128)S(1)} %get-tuple-element.79), channel_id=1, source_target_pairs={{0,24},{32,56},{64,88},{96,120},{128,152},{160,184},{192,216},{224... | collective-permute-start | bytes 147464 | tf_op jit(solution)/shard_map/ppermute | solution.py:70
  49.9 1.6 %collective-permute-start.12 = (f32[4,1,2,8,192]{4,3,2,1,0:T(8,128)S(1)}, f32[4,1,2,8,192]{4,3,2,1,0:T(8,128)S(1)}, u32[]{:S(2)}, u32[]{:S(2)}) collective-permute-start(f32[4,1,2,8,192]{4,3,2,1,0:T(8,128)S(1)} %get-tuple-element.80), channel_id=1, source_target_pairs={{0,8},{32,0},{64,72},{96,64},{128,136},{160,128},{192,200},{224,19... | collective-permute-start | bytes 147464 | tf_op jit(solution)/shard_map/ppermute | solution.py:70
  51.5 1.9 %collective-permute-done.14 = f32[4,1,2,8,192]{4,3,2,1,0:T(8,128)S(1)} collective-permute-done((f32[4,1,2,8,192]{4,3,2,1,0:T(8,128)S(1)}, f32[4,1,2,8,192]{4,3,2,1,0:T(8,128)S(1)}, u32[]{:S(2)}, u32[]{:S(2)}) %collective-permute-start.14) | collective-permute-done | bytes 49184 | tf_op jit(solution)/shard_map/ppermute | solution.py:70
  53.5 2.4 %collective-permute-start.16 = (f32[4,4,8,192]{3,2,1,0:T(8,128)S(1)}, f32[4,4,8,192]{3,2,1,0:T(8,128)S(1)}, u32[]{:S(2)}, u32[]{:S(2)}) collective-permute-start(f32[4,4,8,192]{3,2,1,0:T(8,128)S(1)} %get-tuple-element.67), channel_id=1, source_target_pairs={{32,0},{1,32},{33,1},{2,33},{34,2},{3,34},{35,3},{0,35},{40,8},{9,... | collective-permute-start | bytes 294920 | tf_op jit(solution)/shard_map/ppermute | solution.py:70
  55.9 5.0 %collective-permute-start.15 = (f32[4,4,8,192]{3,2,1,0:T(8,128)S(1)}, f32[4,4,8,192]{3,2,1,0:T(8,128)S(1)}, u32[]{:S(2)}, u32[]{:S(2)}) collective-permute-start(f32[4,4,8,192]{3,2,1,0:T(8,128)S(1)} %get-tuple-element.68), channel_id=1, source_target_pairs={{0,32},{32,1},{1,33},{33,2},{2,34},{34,3},{3,35},{35,0},{8,40},{40... | collective-permute-start | bytes 294920 | tf_op jit(solution)/shard_map/ppermute | solution.py:70
  61.1 2.4 %k_own_env.1 = (f32[192,1024]{1,0:T(8,128)S(1)}, f32[192,1024]{1,0:T(8,128)S(1)}, f32[128,1024]{1,0:T(8,128)S(1)}, f32[128,1024]{1,0:T(8,128)S(1)}, f32[128,1024]{1,0:T(8,128)S(1)}, /*index=5*/f32[128,1024]{1,0:T(8,128)S(1)}) custom-call(f32[48,128]{1,0:T(8,128)S(1)} %collective-permute-done.packed_ref, f32[8,1024]{1,0:T(8,128)S(1)} %get-tuple-element.36.scal_ref, ...), custom_call_target="tpu_custom_call" | custom-call | tf_op jit(solution)/shard_map/k_own_env/pallas_call | solution.py:504
  63.6 2.2 %k_energy.1 = (f32[128,192]{1,0:T(8,128)S(1)}, f32[128,192]{1,0:T(8,128)S(1)}, f32[256,192]{1,0:T(8,128)S(1)}, f32[192,1024]{1,0:T(8,128)S(1)}, f32[128,1024]{1,0:T(8,128)S(1)}, /*index=5*/f32[64,1024]{1,0:T(8,128)S(1)}) custom-call(f32[48,128]{1,0:T(8,128)S(1)} %collective-permute-done.packed_ref, f32[8,1024]{1,0:T(8,128)S(1)} %get-tuple-element.36.scal_ref, ...), custom_call_target="tpu_custom_call" | custom-call | tf_op jit(solution)/shard_map/k_energy/pallas_call | solution.py:504
  65.7 3.0 %collective-permute-start.17 = (f32[4,4,8,192]{3,2,1,0:T(8,128)S(1)}, f32[4,4,8,192]{3,2,1,0:T(8,128)S(1)}, u32[]{:S(2)}, u32[]{:S(2)}) collective-permute-start(f32[4,4,8,192]{3,2,1,0:T(8,128)S(1)} %bitcast.54), channel_id=1, source_target_pairs={{0,32},{32,1},{1,33},{33,2},{2,34},{34,3},{3,35},{35,0},{8,40},{40... | collective-permute-start | bytes 294920 | tf_op jit(solution)/shard_map/ppermute | solution.py:70
  68.7 2.3 %k_direct.1 = (f32[8,1024]{1,0:T(8,128)S(1)}, f32[4,512]{1,0:T(4,128)S(1)}) custom-call(f32[48,128]{1,0:T(8,128)S(1)} %collective-permute-done.packed_ref, f32[8,1024]{1,0:T(8,128)S(1)} %get-tuple-element.36.scal_ref, f32[128,1024]{1,0:T(8,128)S(1)} %get-tuple-element.37.av_ref, f32[128,1024]{1,0:T(8,128)S(1)} %get-tuple-element.39.nav_ref, ...), custom_call_target="tpu_custom_call" | custom-call | tf_op jit(solution)/shard_map/k_direct/pallas_call | solution.py:504
  71.1 3.3 %collective-permute-done.18 = f32[4,4,8,192]{3,2,1,0:T(8,128)S(1)} collective-permute-done((f32[4,4,8,192]{3,2,1,0:T(8,128)S(1)}, f32[4,4,8,192]{3,2,1,0:T(8,128)S(1)}, u32[]{:S(2)}, u32[]{:S(2)}) %collective-permute-start.18) | collective-permute-done | bytes 98336 | tf_op jit(solution)/shard_map/ppermute | solution.py:70
  74.4 3.7 %collective-permute-start.21 = (f32[4,1,2,8,192]{4,3,2,1,0:T(8,128)S(1)}, f32[4,1,2,8,192]{4,3,2,1,0:T(8,128)S(1)}, u32[]{:S(2)}, u32[]{:S(2)}) collective-permute-start(f32[4,1,2,8,192]{4,3,2,1,0:T(8,128)S(1)} %get-tuple-element.64), channel_id=1, source_target_pairs={{0,24},{32,56},{64,88},{96,120},{128,152},{160,184},{192,216},{224... | collective-permute-start | bytes 147464 | tf_op jit(solution)/shard_map/ppermute | solution.py:70
  78.1 1.5 %collective-permute-start.20 = (f32[4,1,2,8,192]{4,3,2,1,0:T(8,128)S(1)}, f32[4,1,2,8,192]{4,3,2,1,0:T(8,128)S(1)}, u32[]{:S(2)}, u32[]{:S(2)}) collective-permute-start(f32[4,1,2,8,192]{4,3,2,1,0:T(8,128)S(1)} %get-tuple-element.66), channel_id=1, source_target_pairs={{8,0},{0,32},{72,64},{64,96},{136,128},{128,160},{200,192},{192,22... | collective-permute-start | bytes 147464 | tf_op jit(solution)/shard_map/ppermute | solution.py:70
  79.6 1.0 collective-permute-done.21
  80.6 0.6 collective-permute-done.19
  81.3 0.7 collective-permute-start.24
  82.0 1.8 %collective-permute-start.22 = (f32[1,2,2,8,192]{4,3,2,1,0:T(8,128)S(1)}, f32[1,2,2,8,192]{4,3,2,1,0:T(8,128)S(1)}, u32[]{:S(2)}, u32[]{:S(2)}) collective-permute-start(f32[1,2,2,8,192]{4,3,2,1,0:T(8,128)S(1)} %get-tuple-element.77), channel_id=1, source_target_pairs={{0,64},{32,0},{64,128},{96,32},{128,192},{160,96},{192,256},{224,1... | collective-permute-start | bytes 73736 | tf_op jit(solution)/shard_map/ppermute | solution.py:70
  83.8 1.0 collective-permute-done.22
  84.8 3.4 %collective-permute-done.23 = f32[1,2,2,8,192]{4,3,2,1,0:T(8,128)S(1)} collective-permute-done((f32[1,2,2,8,192]{4,3,2,1,0:T(8,128)S(1)}, f32[1,2,2,8,192]{4,3,2,1,0:T(8,128)S(1)}, u32[]{:S(2)}, u32[]{:S(2)}) %collective-permute-start.23) | collective-permute-done | bytes 24608 | tf_op jit(solution)/shard_map/ppermute | solution.py:70
  88.2 1.2 k_env_back.1
  89.9 0.6 k_own_force.1.own_ref
  90.7 3.6 %collective-permute-done.26 = f32[4,4,8,128]{3,2,1,0:T(8,128)S(1)} collective-permute-done((f32[4,4,8,128]{3,2,1,0:T(8,128)S(1)}, f32[4,4,8,128]{3,2,1,0:T(8,128)S(1)}, u32[]{:S(2)}, u32[]{:S(2)}) %collective-permute-start.26) | collective-permute-done | bytes 65568 | tf_op jit(solution)/shard_map/ppermute | solution.py:70
  94.3 2.8 %collective-permute-start.29 = (f32[4,1,2,8,128]{4,3,2,1,0:T(8,128)S(1)}, f32[4,1,2,8,128]{4,3,2,1,0:T(8,128)S(1)}, u32[]{:S(2)}, u32[]{:S(2)}) collective-permute-start(f32[4,1,2,8,128]{4,3,2,1,0:T(8,128)S(1)} %get-tuple-element.73), channel_id=1, source_target_pairs={{0,24},{32,56},{64,88},{96,120},{128,152},{160,184},{192,216},{224... | collective-permute-start | bytes 98312 | tf_op jit(solution)/shard_map/ppermute | solution.py:70
  97.2 1.5 %collective-permute-start.28 = (f32[4,1,2,8,128]{4,3,2,1,0:T(8,128)S(1)}, f32[4,1,2,8,128]{4,3,2,1,0:T(8,128)S(1)}, u32[]{:S(2)}, u32[]{:S(2)}) collective-permute-start(f32[4,1,2,8,128]{4,3,2,1,0:T(8,128)S(1)} %get-tuple-element.75), channel_id=1, source_target_pairs={{8,0},{0,32},{72,64},{64,96},{136,128},{128,160},{200,192},{192,22... | collective-permute-start | bytes 98312 | tf_op jit(solution)/shard_map/ppermute | solution.py:70
  98.6 1.6 %collective-permute-done.29 = f32[4,1,2,8,128]{4,3,2,1,0:T(8,128)S(1)} collective-permute-done((f32[4,1,2,8,128]{4,3,2,1,0:T(8,128)S(1)}, f32[4,1,2,8,128]{4,3,2,1,0:T(8,128)S(1)}, u32[]{:S(2)}, u32[]{:S(2)}) %collective-permute-start.29) | collective-permute-done | bytes 32800 | tf_op jit(solution)/shard_map/ppermute | solution.py:70
  100.3 0.7 collective-permute-start.32
  100.9 2.5 %collective-permute-start.30 = (f32[1,2,2,8,128]{4,3,2,1,0:T(8,128)S(1)}, f32[1,2,2,8,128]{4,3,2,1,0:T(8,128)S(1)}, u32[]{:S(2)}, u32[]{:S(2)}) collective-permute-start(f32[1,2,2,8,128]{4,3,2,1,0:T(8,128)S(1)} %get-tuple-element.93), channel_id=1, source_target_pairs={{0,64},{32,0},{64,128},{96,32},{128,192},{160,96},{192,256},{224,1... | collective-permute-start | bytes 49160 | tf_op jit(solution)/shard_map/ppermute | solution.py:70
  103.4 0.9 collective-permute-done.30
  104.3 4.0 %collective-permute-done.31 = f32[1,2,2,8,128]{4,3,2,1,0:T(8,128)S(1)} collective-permute-done((f32[1,2,2,8,128]{4,3,2,1,0:T(8,128)S(1)}, f32[1,2,2,8,128]{4,3,2,1,0:T(8,128)S(1)}, u32[]{:S(2)}, u32[]{:S(2)}) %collective-permute-start.31) | collective-permute-done | bytes 16416 | tf_op jit(solution)/shard_map/ppermute | solution.py:70
  108.5 1.9 %collective-permute-start.33 = (f32[16,128]{1,0:T(8,128)S(1)}, f32[16,128]{1,0:T(8,128)S(1)}, u32[]{:S(2)}, u32[]{:S(2)}) collective-permute-start(f32[16,128]{1,0:T(8,128)S(1)} %k_force.1), channel_id=1, source_target_pairs={{0,0},{32,1},{1,2},{33,3},{2,4},{34,5},{3,6},{35,7},{8,8},{40,9},{... | collective-permute-start | bytes 24584 | tf_op jit(solution)/shard_map/ppermute | solution.py:70
  110.4 7.9 %collective-permute-done.33.in_ref = f32[16,128]{1,0:T(8,128)S(1)} collective-permute-done((f32[16,128]{1,0:T(8,128)S(1)}, f32[16,128]{1,0:T(8,128)S(1)}, u32[]{:S(2)}, u32[]{:S(2)}) %collective-permute-start.33) | collective-permute-done | bytes 8224 | tf_op jit(solution)/shard_map/ppermute | solution.py:70
  118.3 0.6 k_unpack.1
  (79 shorter events, 2.7 us)
Async XLA Ops:
  2.1 15.8 %collective-permute-start = (f32[48,128]{1,0:T(8,128)}, f32[48,128]{1,0:T(8,128)S(1)}, u32[]{:S(2)}, u32[]{:S(2)}) collective-permute-start(f32[48,128]{1,0:T(8,128)} %k_pack.1), channel_id=1, source_target_pairs={{0,0},{1,32},{2,1},{3,33},{4,2},{5,34},{6,3},{7,35},{8,8},{9,40},{... | collective-permute-start | bytes 73736 | tf_op jit(solution)/shard_map/ppermute | solution.py:70
  18.2 2.2 %collective-permute-start.3 = (f32[1,2,2,8,128]{4,3,2,1,0:T(8,128)S(1)}, f32[1,2,2,8,128]{4,3,2,1,0:T(8,128)S(1)}, u32[]{:S(2)}, u32[]{:S(2)}) collective-permute-start(f32[1,2,2,8,128]{4,3,2,1,0:T(8,128)S(1)} %get-tuple-element.105), channel_id=1, source_target_pairs={{0,452},{32,484},{452,0},{484,32},{8,460},{40,492},{460,8},{492,40... | collective-permute-start | bytes 49160 | tf_op jit(solution)/shard_map/ppermute | solution.py:70
  18.8 2.6 %collective-permute-start.2 = (f32[1,2,2,8,128]{4,3,2,1,0:T(8,128)S(1)}, f32[1,2,2,8,128]{4,3,2,1,0:T(8,128)S(1)}, u32[]{:S(2)}, u32[]{:S(2)}) collective-permute-start(f32[1,2,2,8,128]{4,3,2,1,0:T(8,128)S(1)} %get-tuple-element.106), channel_id=1, source_target_pairs={{64,0},{0,32},{128,64},{32,96},{192,128},{96,160},{256,192},{160,2... | collective-permute-start | bytes 49160 | tf_op jit(solution)/shard_map/ppermute | solution.py:70
  18.9 2.6 %collective-permute-start.1 = (f32[1,2,2,8,128]{4,3,2,1,0:T(8,128)S(1)}, f32[1,2,2,8,128]{4,3,2,1,0:T(8,128)S(1)}, u32[]{:S(2)}, u32[]{:S(2)}) collective-permute-start(f32[1,2,2,8,128]{4,3,2,1,0:T(8,128)S(1)} %get-tuple-element.107), channel_id=1, source_target_pairs={{0,64},{32,0},{64,128},{96,32},{128,192},{160,96},{192,256},{224,1... | collective-permute-start | bytes 49160 | tf_op jit(solution)/shard_map/ppermute | solution.py:70
  21.5 8.5 %copy-start.1 = (f32[128,64]{0,1:T(8,128)S(1)}, f32[128,64]{0,1:T(8,128)}, u32[]{:S(2)}) copy-start(f32[128,64]{0,1:T(8,128)} %param.22) | copy-start | bytes 98308
  21.5 10.0 %collective-permute-start.6 = (f32[4,1,2,8,128]{4,3,2,1,0:T(8,128)S(1)}, f32[4,1,2,8,128]{4,3,2,1,0:T(8,128)S(1)}, u32[]{:S(2)}, u32[]{:S(2)}) collective-permute-start(f32[4,1,2,8,128]{4,3,2,1,0:T(8,128)S(1)} %get-tuple-element.98), channel_id=1, source_target_pairs={{0,24},{32,56},{64,88},{96,120},{128,152},{160,184},{192,216},{224... | collective-permute-start | bytes 98312 | tf_op jit(solution)/shard_map/ppermute | solution.py:70
  26.2 5.3 %collective-permute-start.4 = (f32[4,1,2,8,128]{4,3,2,1,0:T(8,128)S(1)}, f32[4,1,2,8,128]{4,3,2,1,0:T(8,128)S(1)}, u32[]{:S(2)}, u32[]{:S(2)}) collective-permute-start(f32[4,1,2,8,128]{4,3,2,1,0:T(8,128)S(1)} %get-tuple-element.99), channel_id=1, source_target_pairs={{0,8},{32,0},{64,72},{96,64},{128,136},{160,128},{192,200},{224,19... | collective-permute-start | bytes 98312 | tf_op jit(solution)/shard_map/ppermute | solution.py:70
  30.0 1.5 %collective-permute-start.5 = (f32[4,1,2,8,128]{4,3,2,1,0:T(8,128)S(1)}, f32[4,1,2,8,128]{4,3,2,1,0:T(8,128)S(1)}, u32[]{:S(2)}, u32[]{:S(2)}) collective-permute-start(f32[4,1,2,8,128]{4,3,2,1,0:T(8,128)S(1)} %get-tuple-element.100), channel_id=1, source_target_pairs={{8,0},{0,32},{72,64},{64,96},{136,128},{128,160},{200,192},{192,22... | collective-permute-start | bytes 98312 | tf_op jit(solution)/shard_map/ppermute | solution.py:70
  30.0 0.8 copy-start.2
  30.7 0.7 copy-start.3
  30.7 0.7 copy-start.4
  30.7 0.7 copy-start.5
  31.6 10.2 %collective-permute-start.8 = (f32[4,4,8,128]{3,2,1,0:T(8,128)S(1)}, f32[4,4,8,128]{3,2,1,0:T(8,128)S(1)}, u32[]{:S(2)}, u32[]{:S(2)}) collective-permute-start(f32[4,4,8,128]{3,2,1,0:T(8,128)S(1)} %get-tuple-element.82), channel_id=1, source_target_pairs={{32,0},{1,32},{33,1},{2,33},{34,2},{3,34},{35,3},{0,35},{40,8},{9,... | collective-permute-start | bytes 196616 | tf_op jit(solution)/shard_map/ppermute | solution.py:70
  34.0 7.8 %collective-permute-start.7 = (f32[4,4,8,128]{3,2,1,0:T(8,128)S(1)}, f32[4,4,8,128]{3,2,1,0:T(8,128)S(1)}, u32[]{:S(2)}, u32[]{:S(2)}) collective-permute-start(f32[4,4,8,128]{3,2,1,0:T(8,128)S(1)} %get-tuple-element.83), channel_id=1, source_target_pairs={{0,32},{32,1},{1,33},{33,2},{2,34},{34,3},{3,35},{35,0},{8,40},{40... | collective-permute-start | bytes 196616 | tf_op jit(solution)/shard_map/ppermute | solution.py:70
  43.4 2.5 %collective-permute-start.11 = (f32[1,2,2,8,192]{4,3,2,1,0:T(8,128)S(1)}, f32[1,2,2,8,192]{4,3,2,1,0:T(8,128)S(1)}, u32[]{:S(2)}, u32[]{:S(2)}) collective-permute-start(f32[1,2,2,8,192]{4,3,2,1,0:T(8,128)S(1)} %get-tuple-element.95), channel_id=1, source_target_pairs={{0,452},{32,484},{452,0},{484,32},{8,460},{40,492},{460,8},{492,40... | collective-permute-start | bytes 73736 | tf_op jit(solution)/shard_map/ppermute | solution.py:70
  44.0 3.1 %collective-permute-start.10 = (f32[1,2,2,8,192]{4,3,2,1,0:T(8,128)S(1)}, f32[1,2,2,8,192]{4,3,2,1,0:T(8,128)S(1)}, u32[]{:S(2)}, u32[]{:S(2)}) collective-permute-start(f32[1,2,2,8,192]{4,3,2,1,0:T(8,128)S(1)} %get-tuple-element.96), channel_id=1, source_target_pairs={{64,0},{0,32},{128,64},{32,96},{192,128},{96,160},{256,192},{160,2... | collective-permute-start | bytes 73736 | tf_op jit(solution)/shard_map/ppermute | solution.py:70
  44.1 3.0 %collective-permute-start.9 = (f32[1,2,2,8,192]{4,3,2,1,0:T(8,128)S(1)}, f32[1,2,2,8,192]{4,3,2,1,0:T(8,128)S(1)}, u32[]{:S(2)}, u32[]{:S(2)}) collective-permute-start(f32[1,2,2,8,192]{4,3,2,1,0:T(8,128)S(1)} %get-tuple-element.97), channel_id=1, source_target_pairs={{0,64},{32,0},{64,128},{96,32},{128,192},{160,96},{192,256},{224,1... | collective-permute-start | bytes 73736 | tf_op jit(solution)/shard_map/ppermute | solution.py:70
  47.2 6.2 %collective-permute-start.14 = (f32[4,1,2,8,192]{4,3,2,1,0:T(8,128)S(1)}, f32[4,1,2,8,192]{4,3,2,1,0:T(8,128)S(1)}, u32[]{:S(2)}, u32[]{:S(2)}) collective-permute-start(f32[4,1,2,8,192]{4,3,2,1,0:T(8,128)S(1)} %get-tuple-element.79), channel_id=1, source_target_pairs={{0,24},{32,56},{64,88},{96,120},{128,152},{160,184},{192,216},{224... | collective-permute-start | bytes 147464 | tf_op jit(solution)/shard_map/ppermute | solution.py:70
  49.9 3.4 %collective-permute-start.12 = (f32[4,1,2,8,192]{4,3,2,1,0:T(8,128)S(1)}, f32[4,1,2,8,192]{4,3,2,1,0:T(8,128)S(1)}, u32[]{:S(2)}, u32[]{:S(2)}) collective-permute-start(f32[4,1,2,8,192]{4,3,2,1,0:T(8,128)S(1)} %get-tuple-element.80), channel_id=1, source_target_pairs={{0,8},{32,0},{64,72},{96,64},{128,136},{160,128},{192,200},{224,19... | collective-permute-start | bytes 147464 | tf_op jit(solution)/shard_map/ppermute | solution.py:70
  51.5 1.9 %collective-permute-start.13 = (f32[4,1,2,8,192]{4,3,2,1,0:T(8,128)S(1)}, f32[4,1,2,8,192]{4,3,2,1,0:T(8,128)S(1)}, u32[]{:S(2)}, u32[]{:S(2)}) collective-permute-start(f32[4,1,2,8,192]{4,3,2,1,0:T(8,128)S(1)} %get-tuple-element.81), channel_id=1, source_target_pairs={{8,0},{0,32},{72,64},{64,96},{136,128},{128,160},{200,192},{192,22... | collective-permute-start | bytes 147464 | tf_op jit(solution)/shard_map/ppermute | solution.py:70
  53.4 7.6 %copy-start = (f32[192,128]{1,0:T(8,128)S(1)}, f32[192,128]{1,0:T(8,128)}, u32[]{:S(2)}) copy-start(f32[192,128]{1,0:T(8,128)} %wm_ref.5) | copy-start | bytes 294916
  53.5 10.1 %collective-permute-start.16 = (f32[4,4,8,192]{3,2,1,0:T(8,128)S(1)}, f32[4,4,8,192]{3,2,1,0:T(8,128)S(1)}, u32[]{:S(2)}, u32[]{:S(2)}) collective-permute-start(f32[4,4,8,192]{3,2,1,0:T(8,128)S(1)} %get-tuple-element.67), channel_id=1, source_target_pairs={{32,0},{1,32},{33,1},{2,33},{34,2},{3,34},{35,3},{0,35},{40,8},{9,... | collective-permute-start | bytes 294920 | tf_op jit(solution)/shard_map/ppermute | solution.py:70
  55.9 5.1 %copy-start.6 = (f32[128]{0:T(128)S(1)}, f32[128]{0:T(128)}, u32[]{:S(2)}) copy-start(f32[128]{0:T(128)} %param.25) | copy-start | bytes 1540
  55.9 7.7 %collective-permute-start.15 = (f32[4,4,8,192]{3,2,1,0:T(8,128)S(1)}, f32[4,4,8,192]{3,2,1,0:T(8,128)S(1)}, u32[]{:S(2)}, u32[]{:S(2)}) collective-permute-start(f32[4,4,8,192]{3,2,1,0:T(8,128)S(1)} %get-tuple-element.68), channel_id=1, source_target_pairs={{0,32},{32,1},{1,33},{33,2},{2,34},{34,3},{3,35},{35,0},{8,40},{40... | collective-permute-start | bytes 294920 | tf_op jit(solution)/shard_map/ppermute | solution.py:70
  65.7 5.3 %collective-permute-start.17 = (f32[4,4,8,192]{3,2,1,0:T(8,128)S(1)}, f32[4,4,8,192]{3,2,1,0:T(8,128)S(1)}, u32[]{:S(2)}, u32[]{:S(2)}) collective-permute-start(f32[4,4,8,192]{3,2,1,0:T(8,128)S(1)} %bitcast.54), channel_id=1, source_target_pairs={{0,32},{32,1},{1,33},{33,2},{2,34},{34,3},{3,35},{35,0},{8,40},{40... | collective-permute-start | bytes 294920 | tf_op jit(solution)/shard_map/ppermute | solution.py:70
  68.7 5.6 %collective-permute-start.18 = (f32[4,4,8,192]{3,2,1,0:T(8,128)S(1)}, f32[4,4,8,192]{3,2,1,0:T(8,128)S(1)}, u32[]{:S(2)}, u32[]{:S(2)}) collective-permute-start(f32[4,4,8,192]{3,2,1,0:T(8,128)S(1)} %bitcast.53), channel_id=1, source_target_pairs={{32,0},{1,32},{33,1},{2,33},{34,2},{3,34},{35,3},{0,35},{40,8},{9,... | collective-permute-start | bytes 294920 | tf_op jit(solution)/shard_map/ppermute | solution.py:70
  74.4 6.2 %collective-permute-start.21 = (f32[4,1,2,8,192]{4,3,2,1,0:T(8,128)S(1)}, f32[4,1,2,8,192]{4,3,2,1,0:T(8,128)S(1)}, u32[]{:S(2)}, u32[]{:S(2)}) collective-permute-start(f32[4,1,2,8,192]{4,3,2,1,0:T(8,128)S(1)} %get-tuple-element.64), channel_id=1, source_target_pairs={{0,24},{32,56},{64,88},{96,120},{128,152},{160,184},{192,216},{224... | collective-permute-start | bytes 147464 | tf_op jit(solution)/shard_map/ppermute | solution.py:70
  78.1 3.1 %collective-permute-start.19 = (f32[4,1,2,8,192]{4,3,2,1,0:T(8,128)S(1)}, f32[4,1,2,8,192]{4,3,2,1,0:T(8,128)S(1)}, u32[]{:S(2)}, u32[]{:S(2)}) collective-permute-start(f32[4,1,2,8,192]{4,3,2,1,0:T(8,128)S(1)} %get-tuple-element.65), channel_id=1, source_target_pairs={{0,8},{32,0},{64,72},{96,64},{128,136},{160,128},{192,200},{224,19... | collective-permute-start | bytes 147464 | tf_op jit(solution)/shard_map/ppermute | solution.py:70
  78.1 3.1 %collective-permute-start.20 = (f32[4,1,2,8,192]{4,3,2,1,0:T(8,128)S(1)}, f32[4,1,2,8,192]{4,3,2,1,0:T(8,128)S(1)}, u32[]{:S(2)}, u32[]{:S(2)}) collective-permute-start(f32[4,1,2,8,192]{4,3,2,1,0:T(8,128)S(1)} %get-tuple-element.66), channel_id=1, source_target_pairs={{8,0},{0,32},{72,64},{64,96},{136,128},{128,160},{200,192},{192,22... | collective-permute-start | bytes 147464 | tf_op jit(solution)/shard_map/ppermute | solution.py:70
  81.3 2.4 %collective-permute-start.24 = (f32[1,2,2,8,192]{4,3,2,1,0:T(8,128)S(1)}, f32[1,2,2,8,192]{4,3,2,1,0:T(8,128)S(1)}, u32[]{:S(2)}, u32[]{:S(2)}) collective-permute-start(f32[1,2,2,8,192]{4,3,2,1,0:T(8,128)S(1)} %get-tuple-element.76), channel_id=1, source_target_pairs={{0,452},{32,484},{452,0},{484,32},{8,460},{40,492},{460,8},{492,40... | collective-permute-start | bytes 73736 | tf_op jit(solution)/shard_map/ppermute | solution.py:70
  82.0 2.8 %collective-permute-start.22 = (f32[1,2,2,8,192]{4,3,2,1,0:T(8,128)S(1)}, f32[1,2,2,8,192]{4,3,2,1,0:T(8,128)S(1)}, u32[]{:S(2)}, u32[]{:S(2)}) collective-permute-start(f32[1,2,2,8,192]{4,3,2,1,0:T(8,128)S(1)} %get-tuple-element.77), channel_id=1, source_target_pairs={{0,64},{32,0},{64,128},{96,32},{128,192},{160,96},{192,256},{224,1... | collective-permute-start | bytes 73736 | tf_op jit(solution)/shard_map/ppermute | solution.py:70
  83.7 4.4 %collective-permute-start.23 = (f32[1,2,2,8,192]{4,3,2,1,0:T(8,128)S(1)}, f32[1,2,2,8,192]{4,3,2,1,0:T(8,128)S(1)}, u32[]{:S(2)}, u32[]{:S(2)}) collective-permute-start(f32[1,2,2,8,192]{4,3,2,1,0:T(8,128)S(1)} %get-tuple-element.78), channel_id=1, source_target_pairs={{64,0},{0,32},{128,64},{32,96},{192,128},{96,160},{256,192},{160,2... | collective-permute-start | bytes 73736 | tf_op jit(solution)/shard_map/ppermute | solution.py:70
  89.3 1.3 %collective-permute-start.25 = (f32[4,4,8,128]{3,2,1,0:T(8,128)S(1)}, f32[4,4,8,128]{3,2,1,0:T(8,128)S(1)}, u32[]{:S(2)}, u32[]{:S(2)}) collective-permute-start(f32[4,4,8,128]{3,2,1,0:T(8,128)S(1)} %bitcast.56), channel_id=1, source_target_pairs={{0,32},{32,1},{1,33},{33,2},{2,34},{34,3},{3,35},{35,0},{8,40},{40... | collective-permute-start | bytes 196616 | tf_op jit(solution)/shard_map/ppermute | solution.py:70
  89.4 4.9 %collective-permute-start.26 = (f32[4,4,8,128]{3,2,1,0:T(8,128)S(1)}, f32[4,4,8,128]{3,2,1,0:T(8,128)S(1)}, u32[]{:S(2)}, u32[]{:S(2)}) collective-permute-start(f32[4,4,8,128]{3,2,1,0:T(8,128)S(1)} %bitcast.55), channel_id=1, source_target_pairs={{32,0},{1,32},{33,1},{2,33},{34,2},{3,34},{35,3},{0,35},{40,8},{9,... | collective-permute-start | bytes 196616 | tf_op jit(solution)/shard_map/ppermute | solution.py:70
  94.3 5.9 %collective-permute-start.29 = (f32[4,1,2,8,128]{4,3,2,1,0:T(8,128)S(1)}, f32[4,1,2,8,128]{4,3,2,1,0:T(8,128)S(1)}, u32[]{:S(2)}, u32[]{:S(2)}) collective-permute-start(f32[4,1,2,8,128]{4,3,2,1,0:T(8,128)S(1)} %get-tuple-element.73), channel_id=1, source_target_pairs={{0,24},{32,56},{64,88},{96,120},{128,152},{160,184},{192,216},{224... | collective-permute-start | bytes 98312 | tf_op jit(solution)/shard_map/ppermute | solution.py:70
  97.1 3.1 %collective-permute-start.27 = (f32[4,1,2,8,128]{4,3,2,1,0:T(8,128)S(1)}, f32[4,1,2,8,128]{4,3,2,1,0:T(8,128)S(1)}, u32[]{:S(2)}, u32[]{:S(2)}) collective-permute-start(f32[4,1,2,8,128]{4,3,2,1,0:T(8,128)S(1)} %get-tuple-element.74), channel_id=1, source_target_pairs={{0,8},{32,0},{64,72},{96,64},{128,136},{160,128},{192,200},{224,19... | collective-permute-start | bytes 98312 | tf_op jit(solution)/shard_map/ppermute | solution.py:70
  97.2 3.0 %collective-permute-start.28 = (f32[4,1,2,8,128]{4,3,2,1,0:T(8,128)S(1)}, f32[4,1,2,8,128]{4,3,2,1,0:T(8,128)S(1)}, u32[]{:S(2)}, u32[]{:S(2)}) collective-permute-start(f32[4,1,2,8,128]{4,3,2,1,0:T(8,128)S(1)} %get-tuple-element.75), channel_id=1, source_target_pairs={{8,0},{0,32},{72,64},{64,96},{136,128},{128,160},{200,192},{192,22... | collective-permute-start | bytes 98312 | tf_op jit(solution)/shard_map/ppermute | solution.py:70
  100.3 3.2 %collective-permute-start.32 = (f32[1,2,2,8,128]{4,3,2,1,0:T(8,128)S(1)}, f32[1,2,2,8,128]{4,3,2,1,0:T(8,128)S(1)}, u32[]{:S(2)}, u32[]{:S(2)}) collective-permute-start(f32[1,2,2,8,128]{4,3,2,1,0:T(8,128)S(1)} %get-tuple-element.92), channel_id=1, source_target_pairs={{0,452},{32,484},{452,0},{484,32},{8,460},{40,492},{460,8},{492,40... | collective-permute-start | bytes 49160 | tf_op jit(solution)/shard_map/ppermute | solution.py:70
  100.9 3.4 %collective-permute-start.30 = (f32[1,2,2,8,128]{4,3,2,1,0:T(8,128)S(1)}, f32[1,2,2,8,128]{4,3,2,1,0:T(8,128)S(1)}, u32[]{:S(2)}, u32[]{:S(2)}) collective-permute-start(f32[1,2,2,8,128]{4,3,2,1,0:T(8,128)S(1)} %get-tuple-element.93), channel_id=1, source_target_pairs={{0,64},{32,0},{64,128},{96,32},{128,192},{160,96},{192,256},{224,1... | collective-permute-start | bytes 49160 | tf_op jit(solution)/shard_map/ppermute | solution.py:70
  103.4 4.8 %collective-permute-start.31 = (f32[1,2,2,8,128]{4,3,2,1,0:T(8,128)S(1)}, f32[1,2,2,8,128]{4,3,2,1,0:T(8,128)S(1)}, u32[]{:S(2)}, u32[]{:S(2)}) collective-permute-start(f32[1,2,2,8,128]{4,3,2,1,0:T(8,128)S(1)} %get-tuple-element.94), channel_id=1, source_target_pairs={{64,0},{0,32},{128,64},{32,96},{192,128},{96,160},{256,192},{160,2... | collective-permute-start | bytes 49160 | tf_op jit(solution)/shard_map/ppermute | solution.py:70
  108.5 9.8 %collective-permute-start.33 = (f32[16,128]{1,0:T(8,128)S(1)}, f32[16,128]{1,0:T(8,128)S(1)}, u32[]{:S(2)}, u32[]{:S(2)}) collective-permute-start(f32[16,128]{1,0:T(8,128)S(1)} %k_force.1), channel_id=1, source_target_pairs={{0,0},{32,1},{1,2},{33,3},{2,4},{34,5},{3,6},{35,7},{8,8},{40,9},{... | collective-permute-start | bytes 24584 | tf_op jit(solution)/shard_map/ppermute | solution.py:70

commit v5 on v4

--- a/solution.py
+++ b/solution.py
@@ -29,7 +29,7 @@
 
 def home(x, y, z):
     x, y, z = x % SHAPE[0], y % SHAPE[1], z % SHAPE[2]
-    return device(z // 2, y, x, z % 2)
+    return device(z // 2, y, (x - 1) % 16, z % 2)
 
 
 CELLS = [(x, y, z) for x in range(SHAPE[0]) for y in range(SHAPE[1]) for z in range(SHAPE[2])]

time: 120 us -> 120 us (level)
  the two profiles are of different devices: /device:TPU:71 before, /device:TPU:22 now
where the time goes in v5:
time: 120 us
  starting transfers between devices  55.9 us (47%)
  waiting for transfers between devices  46.9 us (39%)
  Pallas kernels  13.2 us (11%)
  local copies, waits for them, and re-layouts  1.88 us (2%)
    ppermute x34, starting transfers between devices, send(): return lax.ppermute(x, AXES, pairs)  55.9 us
    ppermute x34, waiting for transfers between devices, send(): return lax.ppermute(x, AXES, pairs)  46.9 us
    pallas_call x10, Pallas kernels, call(): pl.pallas_call(kernel, out_shape=shapes, in_specs=[spec] * len(args), out...  11.7 us
  transfers between devices with their start and end apart: 34, of which 20 were waited for; matrix products, arithmetic and copies ran while one was open for 0% of the time, Pallas kernels for 5%

profile of v5, /device:TPU:22, one launch (start us, length us, event | category | flops | bytes accessed | tf_op | source)
XLA Modules:
  0.0 119.5 jit_solution(14316512850917776176)
XLA Ops:
  0.6 1.5 %k_pack.1 = f32[48,128]{1,0:T(8,128)} custom-call(f32[3,1,1,1,512]{4,3,2,1,0:T(1,128)} %pos_in.1, s32[1,1,1,512]{3,2,1,0:T(1,128)} %kind_in.1, s32[2,2,2,8]{3,2,1,0:T(2,128)} %names_in.1, s32[1,1,1,8,128]{4,3,2,1,0:T(8,128)} %center_in.1, s32[1,1,1,8,128]{4,3,2,1,0:T(8,128)} %partner_in.1, s32[1,1,1,8,128]{4,3,2,1,0:T(8,128)} %live_in.1), custom_call_target="tpu_custom_call" | custom-call | tf_op jit(solution)/shard_map/k_pack/pallas_call | solution.py:241
  2.1 11.7 %collective-permute-start = (f32[48,128]{1,0:T(8,128)}, f32[48,128]{1,0:T(8,128)S(1)}, u32[]{:S(2)}, u32[]{:S(2)}) collective-permute-start(f32[48,128]{1,0:T(8,128)} %k_pack.1), channel_id=1, source_target_pairs={{0,452},{1,484},{2,453},{3,485},{4,454},{5,486},{6,455},{7,487},{8... | collective-permute-start | bytes 73736 | tf_op jit(solution)/shard_map/ppermute | solution.py:70
  13.9 5.4 %collective-permute-done.packed_ref = f32[48,128]{1,0:T(8,128)S(1)} collective-permute-done((f32[48,128]{1,0:T(8,128)}, f32[48,128]{1,0:T(8,128)S(1)}, u32[]{:S(2)}, u32[]{:S(2)}) %collective-permute-start) | collective-permute-done | bytes 24608 | tf_op jit(solution)/shard_map/ppermute | solution.py:70
  19.5 7.7 %collective-permute-start.3 = (f32[1,2,2,8,128]{4,3,2,1,0:T(8,128)S(1)}, f32[1,2,2,8,128]{4,3,2,1,0:T(8,128)S(1)}, u32[]{:S(2)}, u32[]{:S(2)}) collective-permute-start(f32[1,2,2,8,128]{4,3,2,1,0:T(8,128)S(1)} %get-tuple-element.105), channel_id=1, source_target_pairs={{0,452},{32,484},{452,0},{484,32},{8,460},{40,492},{460,8},{492,40... | collective-permute-start | bytes 49160 | tf_op jit(solution)/shard_map/ppermute | solution.py:70
  27.3 2.0 %collective-permute-start.1 = (f32[1,2,2,8,128]{4,3,2,1,0:T(8,128)S(1)}, f32[1,2,2,8,128]{4,3,2,1,0:T(8,128)S(1)}, u32[]{:S(2)}, u32[]{:S(2)}) collective-permute-start(f32[1,2,2,8,128]{4,3,2,1,0:T(8,128)S(1)} %get-tuple-element.107), channel_id=1, source_target_pairs={{0,64},{32,0},{64,128},{96,32},{128,192},{160,96},{192,256},{224,1... | collective-permute-start | bytes 49160 | tf_op jit(solution)/shard_map/ppermute | solution.py:70
  29.3 1.7 %collective-permute-done.2 = f32[1,2,2,8,128]{4,3,2,1,0:T(8,128)S(1)} collective-permute-done((f32[1,2,2,8,128]{4,3,2,1,0:T(8,128)S(1)}, f32[1,2,2,8,128]{4,3,2,1,0:T(8,128)S(1)}, u32[]{:S(2)}, u32[]{:S(2)}) %collective-permute-start.2) | collective-permute-done | bytes 16416 | tf_op jit(solution)/shard_map/ppermute | solution.py:70
  31.1 0.7 collective-permute-start.6
  31.7 2.8 %collective-permute-start.4 = (f32[4,1,2,8,128]{4,3,2,1,0:T(8,128)S(1)}, f32[4,1,2,8,128]{4,3,2,1,0:T(8,128)S(1)}, u32[]{:S(2)}, u32[]{:S(2)}) collective-permute-start(f32[4,1,2,8,128]{4,3,2,1,0:T(8,128)S(1)} %get-tuple-element.99), channel_id=1, source_target_pairs={{0,8},{32,0},{64,72},{96,64},{128,136},{160,128},{192,200},{224,19... | collective-permute-start | bytes 98312 | tf_op jit(solution)/shard_map/ppermute | solution.py:70
  34.6 0.7 copy-done.2
  35.4 0.6 copy-done.3
  36.1 2.3 %collective-permute-done.5 = f32[4,1,2,8,128]{4,3,2,1,0:T(8,128)S(1)} collective-permute-done((f32[4,1,2,8,128]{4,3,2,1,0:T(8,128)S(1)}, f32[4,1,2,8,128]{4,3,2,1,0:T(8,128)S(1)}, u32[]{:S(2)}, u32[]{:S(2)}) %collective-permute-start.5) | collective-permute-done | bytes 32800 | tf_op jit(solution)/shard_map/ppermute | solution.py:70
  38.5 0.5 collective-permute-start.7
  39.5 0.9 collective-permute-done.8
  40.4 2.9 %collective-permute-done.7 = f32[4,4,8,128]{3,2,1,0:T(8,128)S(1)} collective-permute-done((f32[4,4,8,128]{3,2,1,0:T(8,128)S(1)}, f32[4,4,8,128]{3,2,1,0:T(8,128)S(1)}, u32[]{:S(2)}, u32[]{:S(2)}) %collective-permute-start.7) | collective-permute-done | bytes 65568 | tf_op jit(solution)/shard_map/ppermute | solution.py:70
  43.3 1.5 %k_features.1 = (f32[32,192]{1,0:T(8,128)S(1)}, f32[32,192]{1,0:T(8,128)S(1)}, f32[8,1024]{1,0:T(8,128)S(1)}, f32[128,1024]{1,0:T(8,128)S(1)}, f32[128,1024]{1,0:T(8,128)S(1)}) custom-call(f32[48,128]{1,0:T(8,128)S(1)} %collective-permute-done.packed_ref, f32[8,1024]{1,0:T(8,128)S(1)} %k_own_pairs.1.part_ref, f32[128,128]{1,0:T(8,128)S(1)} %bitcast.52, ...), custom_call_target="tpu_custom_call" | custom-call | tf_op jit(solution)/shard_map/k_features/pallas_call | solution.py:504
  44.9 3.1 %collective-permute-start.11 = (f32[1,2,2,8,192]{4,3,2,1,0:T(8,128)S(1)}, f32[1,2,2,8,192]{4,3,2,1,0:T(8,128)S(1)}, u32[]{:S(2)}, u32[]{:S(2)}) collective-permute-start(f32[1,2,2,8,192]{4,3,2,1,0:T(8,128)S(1)} %get-tuple-element.95), channel_id=1, source_target_pairs={{0,452},{32,484},{452,0},{484,32},{8,460},{40,492},{460,8},{492,40... | collective-permute-start | bytes 73736 | tf_op jit(solution)/shard_map/ppermute | solution.py:70
  48.0 2.0 %collective-permute-start.9 = (f32[1,2,2,8,192]{4,3,2,1,0:T(8,128)S(1)}, f32[1,2,2,8,192]{4,3,2,1,0:T(8,128)S(1)}, u32[]{:S(2)}, u32[]{:S(2)}) collective-permute-start(f32[1,2,2,8,192]{4,3,2,1,0:T(8,128)S(1)} %get-tuple-element.97), channel_id=1, source_target_pairs={{0,64},{32,0},{64,128},{96,32},{128,192},{160,96},{192,256},{224,1... | collective-permute-start | bytes 73736 | tf_op jit(solution)/shard_map/ppermute | solution.py:70
  50.0 1.9 %collective-permute-done.11 = f32[1,2,2,8,192]{4,3,2,1,0:T(8,128)S(1)} collective-permute-done((f32[1,2,2,8,192]{4,3,2,1,0:T(8,128)S(1)}, f32[1,2,2,8,192]{4,3,2,1,0:T(8,128)S(1)}, u32[]{:S(2)}, u32[]{:S(2)}) %collective-permute-start.11) | collective-permute-done | bytes 24608 | tf_op jit(solution)/shard_map/ppermute | solution.py:70
  52.0 0.7 collective-permute-start.14
  52.6 4.3 %collective-permute-start.12 = (f32[4,1,2,8,192]{4,3,2,1,0:T(8,128)S(1)}, f32[4,1,2,8,192]{4,3,2,1,0:T(8,128)S(1)}, u32[]{:S(2)}, u32[]{:S(2)}) collective-permute-start(f32[4,1,2,8,192]{4,3,2,1,0:T(8,128)S(1)} %get-tuple-element.80), channel_id=1, source_target_pairs={{0,8},{32,0},{64,72},{96,64},{128,136},{160,128},{192,200},{224,19... | collective-permute-start | bytes 147464 | tf_op jit(solution)/shard_map/ppermute | solution.py:70
  56.9 1.9 %collective-permute-done.12 = f32[4,1,2,8,192]{4,3,2,1,0:T(8,128)S(1)} collective-permute-done((f32[4,1,2,8,192]{4,3,2,1,0:T(8,128)S(1)}, f32[4,1,2,8,192]{4,3,2,1,0:T(8,128)S(1)}, u32[]{:S(2)}, u32[]{:S(2)}) %collective-permute-start.12) | collective-permute-done | bytes 49184 | tf_op jit(solution)/shard_map/ppermute | solution.py:70
  58.8 2.4 %collective-permute-done.13 = f32[4,1,2,8,192]{4,3,2,1,0:T(8,128)S(1)} collective-permute-done((f32[4,1,2,8,192]{4,3,2,1,0:T(8,128)S(1)}, f32[4,1,2,8,192]{4,3,2,1,0:T(8,128)S(1)}, u32[]{:S(2)}, u32[]{:S(2)}) %collective-permute-start.13) | collective-permute-done | bytes 49184 | tf_op jit(solution)/shard_map/ppermute | solution.py:70
  62.2 2.4 %k_own_env.1 = (f32[192,1024]{1,0:T(8,128)S(1)}, f32[192,1024]{1,0:T(8,128)S(1)}, f32[128,1024]{1,0:T(8,128)S(1)}, f32[128,1024]{1,0:T(8,128)S(1)}, f32[128,1024]{1,0:T(8,128)S(1)}, /*index=5*/f32[128,1024]{1,0:T(8,128)S(1)}) custom-call(f32[48,128]{1,0:T(8,128)S(1)} %collective-permute-done.packed_ref, f32[8,1024]{1,0:T(8,128)S(1)} %get-tuple-element.36.scal_ref, ...), custom_call_target="tpu_custom_call" | custom-call | tf_op jit(solution)/shard_map/k_own_env/pallas_call | solution.py:504
  64.6 1.1 collective-permute-done.15
  65.7 2.2 %k_energy.1 = (f32[128,192]{1,0:T(8,128)S(1)}, f32[128,192]{1,0:T(8,128)S(1)}, f32[256,192]{1,0:T(8,128)S(1)}, f32[192,1024]{1,0:T(8,128)S(1)}, f32[128,1024]{1,0:T(8,128)S(1)}, /*index=5*/f32[64,1024]{1,0:T(8,128)S(1)}) custom-call(f32[48,128]{1,0:T(8,128)S(1)} %collective-permute-done.packed_ref, f32[8,1024]{1,0:T(8,128)S(1)} %get-tuple-element.36.scal_ref, ...), custom_call_target="tpu_custom_call" | custom-call | tf_op jit(solution)/shard_map/k_energy/pallas_call | solution.py:504
  67.9 1.7 %collective-permute-start.18 = (f32[4,4,8,192]{3,2,1,0:T(8,128)S(1)}, f32[4,4,8,192]{3,2,1,0:T(8,128)S(1)}, u32[]{:S(2)}, u32[]{:S(2)}) collective-permute-start(f32[4,4,8,192]{3,2,1,0:T(8,128)S(1)} %bitcast.53), channel_id=1, source_target_pairs={{484,452},{453,484},{485,453},{454,485},{486,454},{455,486},{487,4... | collective-permute-start | bytes 294920 | tf_op jit(solution)/shard_map/ppermute | solution.py:70
  69.7 2.3 %k_direct.1 = (f32[8,1024]{1,0:T(8,128)S(1)}, f32[4,512]{1,0:T(4,128)S(1)}) custom-call(f32[48,128]{1,0:T(8,128)S(1)} %collective-permute-done.packed_ref, f32[8,1024]{1,0:T(8,128)S(1)} %get-tuple-element.36.scal_ref, f32[128,1024]{1,0:T(8,128)S(1)} %get-tuple-element.37.av_ref, f32[128,1024]{1,0:T(8,128)S(1)} %get-tuple-element.39.nav_ref, ...), custom_call_target="tpu_custom_call" | custom-call | tf_op jit(solution)/shard_map/k_direct/pallas_call | solution.py:504
  72.4 0.7 collective-permute-start.21
  73.1 2.4 %collective-permute-start.19 = (f32[4,1,2,8,192]{4,3,2,1,0:T(8,128)S(1)}, f32[4,1,2,8,192]{4,3,2,1,0:T(8,128)S(1)}, u32[]{:S(2)}, u32[]{:S(2)}) collective-permute-start(f32[4,1,2,8,192]{4,3,2,1,0:T(8,128)S(1)} %get-tuple-element.65), channel_id=1, source_target_pairs={{0,8},{32,0},{64,72},{96,64},{128,136},{160,128},{192,200},{224,19... | collective-permute-start | bytes 147464 | tf_op jit(solution)/shard_map/ppermute | solution.py:70
  75.5 1.9 %collective-permute-done.19 = f32[4,1,2,8,192]{4,3,2,1,0:T(8,128)S(1)} collective-permute-done((f32[4,1,2,8,192]{4,3,2,1,0:T(8,128)S(1)}, f32[4,1,2,8,192]{4,3,2,1,0:T(8,128)S(1)}, u32[]{:S(2)}, u32[]{:S(2)}) %collective-permute-start.19) | collective-permute-done | bytes 49184 | tf_op jit(solution)/shard_map/ppermute | solution.py:70
  77.4 3.6 %collective-permute-done.20 = f32[4,1,2,8,192]{4,3,2,1,0:T(8,128)S(1)} collective-permute-done((f32[4,1,2,8,192]{4,3,2,1,0:T(8,128)S(1)}, f32[4,1,2,8,192]{4,3,2,1,0:T(8,128)S(1)}, u32[]{:S(2)}, u32[]{:S(2)}) %collective-permute-start.20) | collective-permute-done | bytes 49184 | tf_op jit(solution)/shard_map/ppermute | solution.py:70
  81.1 4.0 %collective-permute-start.24 = (f32[1,2,2,8,192]{4,3,2,1,0:T(8,128)S(1)}, f32[1,2,2,8,192]{4,3,2,1,0:T(8,128)S(1)}, u32[]{:S(2)}, u32[]{:S(2)}) collective-permute-start(f32[1,2,2,8,192]{4,3,2,1,0:T(8,128)S(1)} %get-tuple-element.76), channel_id=1, source_target_pairs={{0,452},{32,484},{452,0},{484,32},{8,460},{40,492},{460,8},{492,40... | collective-permute-start | bytes 73736 | tf_op jit(solution)/shard_map/ppermute | solution.py:70
  85.7 2.5 %collective-permute-done.24 = f32[1,2,2,8,192]{4,3,2,1,0:T(8,128)S(1)} collective-permute-done((f32[1,2,2,8,192]{4,3,2,1,0:T(8,128)S(1)}, f32[1,2,2,8,192]{4,3,2,1,0:T(8,128)S(1)}, u32[]{:S(2)}, u32[]{:S(2)}) %collective-permute-start.24) | collective-permute-done | bytes 24608 | tf_op jit(solution)/shard_map/ppermute | solution.py:70
  88.1 0.9 collective-permute-done.23
  89.1 1.2 %k_env_back.1 = (f32[128,128]{1,0:T(8,128)S(1)}, f32[128,128]{1,0:T(8,128)S(1)}, f32[256,128]{1,0:T(8,128)S(1)}, f32[8,1024]{1,0:T(8,128)S(1)}) custom-call(f32[48,128]{1,0:T(8,128)S(1)} %collective-permute-done.packed_ref, f32[8,1024]{1,0:T(8,128)S(1)} %get-tuple-element.36.scal_ref, f32[128,1024]{1,0:T(8,128)S(1)} %get-tuple-element.37.av_ref, ...), custom_call_target="tpu_custom_call" | custom-call | tf_op jit(solution)/shard_map/k_env_back/pallas_call | solution.py:504
  90.4 1.7 %collective-permute-start.26 = (f32[4,4,8,128]{3,2,1,0:T(8,128)S(1)}, f32[4,4,8,128]{3,2,1,0:T(8,128)S(1)}, u32[]{:S(2)}, u32[]{:S(2)}) collective-permute-start(f32[4,4,8,128]{3,2,1,0:T(8,128)S(1)} %bitcast.55), channel_id=1, source_target_pairs={{484,452},{453,484},{485,453},{454,485},{486,454},{455,486},{487,4... | collective-permute-start | bytes 196616 | tf_op jit(solution)/shard_map/ppermute | solution.py:70
  92.1 0.6 k_own_force.1.own_ref
  92.7 1.3 %collective-permute-done.25 = f32[4,4,8,128]{3,2,1,0:T(8,128)S(1)} collective-permute-done((f32[4,4,8,128]{3,2,1,0:T(8,128)S(1)}, f32[4,4,8,128]{3,2,1,0:T(8,128)S(1)}, u32[]{:S(2)}, u32[]{:S(2)}) %collective-permute-start.25) | collective-permute-done | bytes 65568 | tf_op jit(solution)/shard_map/ppermute | solution.py:70
  94.1 0.7 collective-permute-start.29
  94.8 2.7 %collective-permute-start.27 = (f32[4,1,2,8,128]{4,3,2,1,0:T(8,128)S(1)}, f32[4,1,2,8,128]{4,3,2,1,0:T(8,128)S(1)}, u32[]{:S(2)}, u32[]{:S(2)}) collective-permute-start(f32[4,1,2,8,128]{4,3,2,1,0:T(8,128)S(1)} %get-tuple-element.74), channel_id=1, source_target_pairs={{0,8},{32,0},{64,72},{96,64},{128,136},{160,128},{192,200},{224,19... | collective-permute-start | bytes 98312 | tf_op jit(solution)/shard_map/ppermute | solution.py:70
  97.4 1.6 %collective-permute-done.27 = f32[4,1,2,8,128]{4,3,2,1,0:T(8,128)S(1)} collective-permute-done((f32[4,1,2,8,128]{4,3,2,1,0:T(8,128)S(1)}, f32[4,1,2,8,128]{4,3,2,1,0:T(8,128)S(1)}, u32[]{:S(2)}, u32[]{:S(2)}) %collective-permute-start.27) | collective-permute-done | bytes 32800 | tf_op jit(solution)/shard_map/ppermute | solution.py:70
  99.0 4.2 %collective-permute-done.28 = f32[4,1,2,8,128]{4,3,2,1,0:T(8,128)S(1)} collective-permute-done((f32[4,1,2,8,128]{4,3,2,1,0:T(8,128)S(1)}, f32[4,1,2,8,128]{4,3,2,1,0:T(8,128)S(1)}, u32[]{:S(2)}, u32[]{:S(2)}) %collective-permute-start.28) | collective-permute-done | bytes 32800 | tf_op jit(solution)/shard_map/ppermute | solution.py:70
  103.3 3.0 %collective-permute-start.32 = (f32[1,2,2,8,128]{4,3,2,1,0:T(8,128)S(1)}, f32[1,2,2,8,128]{4,3,2,1,0:T(8,128)S(1)}, u32[]{:S(2)}, u32[]{:S(2)}) collective-permute-start(f32[1,2,2,8,128]{4,3,2,1,0:T(8,128)S(1)} %get-tuple-element.92), channel_id=1, source_target_pairs={{0,452},{32,484},{452,0},{484,32},{8,460},{40,492},{460,8},{492,40... | collective-permute-start | bytes 49160 | tf_op jit(solution)/shard_map/ppermute | solution.py:70
  106.3 0.5 collective-permute-start.31
  106.8 3.3 %collective-permute-done.32 = f32[1,2,2,8,128]{4,3,2,1,0:T(8,128)S(1)} collective-permute-done((f32[1,2,2,8,128]{4,3,2,1,0:T(8,128)S(1)}, f32[1,2,2,8,128]{4,3,2,1,0:T(8,128)S(1)}, u32[]{:S(2)}, u32[]{:S(2)}) %collective-permute-start.32) | collective-permute-done | bytes 16416 | tf_op jit(solution)/shard_map/ppermute | solution.py:70
  110.4 1.9 %collective-permute-start.33 = (f32[16,128]{1,0:T(8,128)S(1)}, f32[16,128]{1,0:T(8,128)S(1)}, u32[]{:S(2)}, u32[]{:S(2)}) collective-permute-start(f32[16,128]{1,0:T(8,128)S(1)} %k_force.1), channel_id=1, source_target_pairs={{452,0},{484,1},{453,2},{485,3},{454,4},{486,5},{455,6},{487,7},{4... | collective-permute-start | bytes 24584 | tf_op jit(solution)/shard_map/ppermute | solution.py:70
  112.3 6.7 %collective-permute-done.33.in_ref = f32[16,128]{1,0:T(8,128)S(1)} collective-permute-done((f32[16,128]{1,0:T(8,128)S(1)}, f32[16,128]{1,0:T(8,128)S(1)}, u32[]{:S(2)}, u32[]{:S(2)}) %collective-permute-start.33) | collective-permute-done | bytes 8224 | tf_op jit(solution)/shard_map/ppermute | solution.py:70
  118.9 0.6 k_unpack.1
  (79 shorter events, 3.5 us)
Async XLA Ops:
  2.1 17.1 %collective-permute-start = (f32[48,128]{1,0:T(8,128)}, f32[48,128]{1,0:T(8,128)S(1)}, u32[]{:S(2)}, u32[]{:S(2)}) collective-permute-start(f32[48,128]{1,0:T(8,128)} %k_pack.1), channel_id=1, source_target_pairs={{0,452},{1,484},{2,453},{3,485},{4,454},{5,486},{6,455},{7,487},{8... | collective-permute-start | bytes 73736 | tf_op jit(solution)/shard_map/ppermute | solution.py:70
  19.5 9.7 %collective-permute-start.3 = (f32[1,2,2,8,128]{4,3,2,1,0:T(8,128)S(1)}, f32[1,2,2,8,128]{4,3,2,1,0:T(8,128)S(1)}, u32[]{:S(2)}, u32[]{:S(2)}) collective-permute-start(f32[1,2,2,8,128]{4,3,2,1,0:T(8,128)S(1)} %get-tuple-element.105), channel_id=1, source_target_pairs={{0,452},{32,484},{452,0},{484,32},{8,460},{40,492},{460,8},{492,40... | collective-permute-start | bytes 49160 | tf_op jit(solution)/shard_map/ppermute | solution.py:70
  27.3 3.8 %collective-permute-start.2 = (f32[1,2,2,8,128]{4,3,2,1,0:T(8,128)S(1)}, f32[1,2,2,8,128]{4,3,2,1,0:T(8,128)S(1)}, u32[]{:S(2)}, u32[]{:S(2)}) collective-permute-start(f32[1,2,2,8,128]{4,3,2,1,0:T(8,128)S(1)} %get-tuple-element.106), channel_id=1, source_target_pairs={{64,0},{0,32},{128,64},{32,96},{192,128},{96,160},{256,192},{160,2... | collective-permute-start | bytes 49160 | tf_op jit(solution)/shard_map/ppermute | solution.py:70
  27.3 3.7 %collective-permute-start.1 = (f32[1,2,2,8,128]{4,3,2,1,0:T(8,128)S(1)}, f32[1,2,2,8,128]{4,3,2,1,0:T(8,128)S(1)}, u32[]{:S(2)}, u32[]{:S(2)}) collective-permute-start(f32[1,2,2,8,128]{4,3,2,1,0:T(8,128)S(1)} %get-tuple-element.107), channel_id=1, source_target_pairs={{0,64},{32,0},{64,128},{96,32},{128,192},{160,96},{192,256},{224,1... | collective-permute-start | bytes 49160 | tf_op jit(solution)/shard_map/ppermute | solution.py:70
  31.0 3.5 %copy-start.1 = (f32[128,64]{0,1:T(8,128)S(1)}, f32[128,64]{0,1:T(8,128)}, u32[]{:S(2)}) copy-start(f32[128,64]{0,1:T(8,128)} %param.22) | copy-start | bytes 98308
  31.1 5.0 %collective-permute-start.6 = (f32[4,1,2,8,128]{4,3,2,1,0:T(8,128)S(1)}, f32[4,1,2,8,128]{4,3,2,1,0:T(8,128)S(1)}, u32[]{:S(2)}, u32[]{:S(2)}) collective-permute-start(f32[4,1,2,8,128]{4,3,2,1,0:T(8,128)S(1)} %get-tuple-element.98), channel_id=1, source_target_pairs={{0,24},{32,56},{64,88},{96,120},{128,152},{160,184},{192,216},{224... | collective-permute-start | bytes 98312 | tf_op jit(solution)/shard_map/ppermute | solution.py:70
  31.7 4.4 %collective-permute-start.4 = (f32[4,1,2,8,128]{4,3,2,1,0:T(8,128)S(1)}, f32[4,1,2,8,128]{4,3,2,1,0:T(8,128)S(1)}, u32[]{:S(2)}, u32[]{:S(2)}) collective-permute-start(f32[4,1,2,8,128]{4,3,2,1,0:T(8,128)S(1)} %get-tuple-element.99), channel_id=1, source_target_pairs={{0,8},{32,0},{64,72},{96,64},{128,136},{160,128},{192,200},{224,19... | collective-permute-start | bytes 98312 | tf_op jit(solution)/shard_map/ppermute | solution.py:70
  34.5 3.9 %collective-permute-start.5 = (f32[4,1,2,8,128]{4,3,2,1,0:T(8,128)S(1)}, f32[4,1,2,8,128]{4,3,2,1,0:T(8,128)S(1)}, u32[]{:S(2)}, u32[]{:S(2)}) collective-permute-start(f32[4,1,2,8,128]{4,3,2,1,0:T(8,128)S(1)} %get-tuple-element.100), channel_id=1, source_target_pairs={{8,0},{0,32},{72,64},{64,96},{136,128},{128,160},{200,192},{192,22... | collective-permute-start | bytes 98312 | tf_op jit(solution)/shard_map/ppermute | solution.py:70
  34.5 0.8 copy-start.2
  35.3 0.7 copy-start.3
  35.3 0.7 copy-start.4
  35.3 0.7 copy-start.5
  38.5 1.9 %collective-permute-start.8 = (f32[4,4,8,128]{3,2,1,0:T(8,128)S(1)}, f32[4,4,8,128]{3,2,1,0:T(8,128)S(1)}, u32[]{:S(2)}, u32[]{:S(2)}) collective-permute-start(f32[4,4,8,128]{3,2,1,0:T(8,128)S(1)} %get-tuple-element.82), channel_id=1, source_target_pairs={{484,452},{453,484},{485,453},{454,485},{486,454},{455,486},{487,4... | collective-permute-start | bytes 196616 | tf_op jit(solution)/shard_map/ppermute | solution.py:70
  38.5 4.8 %collective-permute-start.7 = (f32[4,4,8,128]{3,2,1,0:T(8,128)S(1)}, f32[4,4,8,128]{3,2,1,0:T(8,128)S(1)}, u32[]{:S(2)}, u32[]{:S(2)}) collective-permute-start(f32[4,4,8,128]{3,2,1,0:T(8,128)S(1)} %get-tuple-element.83), channel_id=1, source_target_pairs={{452,484},{484,453},{453,485},{485,454},{454,486},{486,455},{455,4... | collective-permute-start | bytes 196616 | tf_op jit(solution)/shard_map/ppermute | solution.py:70
  44.9 7.0 %collective-permute-start.11 = (f32[1,2,2,8,192]{4,3,2,1,0:T(8,128)S(1)}, f32[1,2,2,8,192]{4,3,2,1,0:T(8,128)S(1)}, u32[]{:S(2)}, u32[]{:S(2)}) collective-permute-start(f32[1,2,2,8,192]{4,3,2,1,0:T(8,128)S(1)} %get-tuple-element.95), channel_id=1, source_target_pairs={{0,452},{32,484},{452,0},{484,32},{8,460},{40,492},{460,8},{492,40... | collective-permute-start | bytes 73736 | tf_op jit(solution)/shard_map/ppermute | solution.py:70
  48.0 3.9 %collective-permute-start.10 = (f32[1,2,2,8,192]{4,3,2,1,0:T(8,128)S(1)}, f32[1,2,2,8,192]{4,3,2,1,0:T(8,128)S(1)}, u32[]{:S(2)}, u32[]{:S(2)}) collective-permute-start(f32[1,2,2,8,192]{4,3,2,1,0:T(8,128)S(1)} %get-tuple-element.96), channel_id=1, source_target_pairs={{64,0},{0,32},{128,64},{32,96},{192,128},{96,160},{256,192},{160,2... | collective-permute-start | bytes 73736 | tf_op jit(solution)/shard_map/ppermute | solution.py:70
  48.0 3.9 %collective-permute-start.9 = (f32[1,2,2,8,192]{4,3,2,1,0:T(8,128)S(1)}, f32[1,2,2,8,192]{4,3,2,1,0:T(8,128)S(1)}, u32[]{:S(2)}, u32[]{:S(2)}) collective-permute-start(f32[1,2,2,8,192]{4,3,2,1,0:T(8,128)S(1)} %get-tuple-element.97), channel_id=1, source_target_pairs={{0,64},{32,0},{64,128},{96,32},{128,192},{160,96},{192,256},{224,1... | collective-permute-start | bytes 73736 | tf_op jit(solution)/shard_map/ppermute | solution.py:70
  52.0 5.0 %collective-permute-start.14 = (f32[4,1,2,8,192]{4,3,2,1,0:T(8,128)S(1)}, f32[4,1,2,8,192]{4,3,2,1,0:T(8,128)S(1)}, u32[]{:S(2)}, u32[]{:S(2)}) collective-permute-start(f32[4,1,2,8,192]{4,3,2,1,0:T(8,128)S(1)} %get-tuple-element.79), channel_id=1, source_target_pairs={{0,24},{32,56},{64,88},{96,120},{128,152},{160,184},{192,216},{224... | collective-permute-start | bytes 147464 | tf_op jit(solution)/shard_map/ppermute | solution.py:70
  52.6 6.2 %collective-permute-start.12 = (f32[4,1,2,8,192]{4,3,2,1,0:T(8,128)S(1)}, f32[4,1,2,8,192]{4,3,2,1,0:T(8,128)S(1)}, u32[]{:S(2)}, u32[]{:S(2)}) collective-permute-start(f32[4,1,2,8,192]{4,3,2,1,0:T(8,128)S(1)} %get-tuple-element.80), channel_id=1, source_target_pairs={{0,8},{32,0},{64,72},{96,64},{128,136},{160,128},{192,200},{224,19... | collective-permute-start | bytes 147464 | tf_op jit(solution)/shard_map/ppermute | solution.py:70
  56.9 4.3 %collective-permute-start.13 = (f32[4,1,2,8,192]{4,3,2,1,0:T(8,128)S(1)}, f32[4,1,2,8,192]{4,3,2,1,0:T(8,128)S(1)}, u32[]{:S(2)}, u32[]{:S(2)}) collective-permute-start(f32[4,1,2,8,192]{4,3,2,1,0:T(8,128)S(1)} %get-tuple-element.81), channel_id=1, source_target_pairs={{8,0},{0,32},{72,64},{64,96},{136,128},{128,160},{200,192},{192,22... | collective-permute-start | bytes 147464 | tf_op jit(solution)/shard_map/ppermute | solution.py:70
  61.3 0.9 copy-start
  61.3 3.3 %collective-permute-start.16 = (f32[4,4,8,192]{3,2,1,0:T(8,128)S(1)}, f32[4,4,8,192]{3,2,1,0:T(8,128)S(1)}, u32[]{:S(2)}, u32[]{:S(2)}) collective-permute-start(f32[4,4,8,192]{3,2,1,0:T(8,128)S(1)} %get-tuple-element.67), channel_id=1, source_target_pairs={{484,452},{453,484},{485,453},{454,485},{486,454},{455,486},{487,4... | collective-permute-start | bytes 294920 | tf_op jit(solution)/shard_map/ppermute | solution.py:70
  61.3 0.7 copy-start.6
  61.3 4.4 %collective-permute-start.15 = (f32[4,4,8,192]{3,2,1,0:T(8,128)S(1)}, f32[4,4,8,192]{3,2,1,0:T(8,128)S(1)}, u32[]{:S(2)}, u32[]{:S(2)}) collective-permute-start(f32[4,4,8,192]{3,2,1,0:T(8,128)S(1)} %get-tuple-element.68), channel_id=1, source_target_pairs={{452,484},{484,453},{453,485},{485,454},{454,486},{486,455},{455,4... | collective-permute-start | bytes 294920 | tf_op jit(solution)/shard_map/ppermute | solution.py:70
  67.9 4.4 %collective-permute-start.17 = (f32[4,4,8,192]{3,2,1,0:T(8,128)S(1)}, f32[4,4,8,192]{3,2,1,0:T(8,128)S(1)}, u32[]{:S(2)}, u32[]{:S(2)}) collective-permute-start(f32[4,4,8,192]{3,2,1,0:T(8,128)S(1)} %bitcast.54), channel_id=1, source_target_pairs={{452,484},{484,453},{453,485},{485,454},{454,486},{486,455},{455,4... | collective-permute-start | bytes 294920 | tf_op jit(solution)/shard_map/ppermute | solution.py:70
  67.9 4.4 %collective-permute-start.18 = (f32[4,4,8,192]{3,2,1,0:T(8,128)S(1)}, f32[4,4,8,192]{3,2,1,0:T(8,128)S(1)}, u32[]{:S(2)}, u32[]{:S(2)}) collective-permute-start(f32[4,4,8,192]{3,2,1,0:T(8,128)S(1)} %bitcast.53), channel_id=1, source_target_pairs={{484,452},{453,484},{485,453},{454,485},{486,454},{455,486},{487,4... | collective-permute-start | bytes 294920 | tf_op jit(solution)/shard_map/ppermute | solution.py:70
  72.4 3.1 %collective-permute-start.21 = (f32[4,1,2,8,192]{4,3,2,1,0:T(8,128)S(1)}, f32[4,1,2,8,192]{4,3,2,1,0:T(8,128)S(1)}, u32[]{:S(2)}, u32[]{:S(2)}) collective-permute-start(f32[4,1,2,8,192]{4,3,2,1,0:T(8,128)S(1)} %get-tuple-element.64), channel_id=1, source_target_pairs={{0,24},{32,56},{64,88},{96,120},{128,152},{160,184},{192,216},{224... | collective-permute-start | bytes 147464 | tf_op jit(solution)/shard_map/ppermute | solution.py:70
  73.1 4.3 %collective-permute-start.19 = (f32[4,1,2,8,192]{4,3,2,1,0:T(8,128)S(1)}, f32[4,1,2,8,192]{4,3,2,1,0:T(8,128)S(1)}, u32[]{:S(2)}, u32[]{:S(2)}) collective-permute-start(f32[4,1,2,8,192]{4,3,2,1,0:T(8,128)S(1)} %get-tuple-element.65), channel_id=1, source_target_pairs={{0,8},{32,0},{64,72},{96,64},{128,136},{160,128},{192,200},{224,19... | collective-permute-start | bytes 147464 | tf_op jit(solution)/shard_map/ppermute | solution.py:70
  75.5 5.5 %collective-permute-start.20 = (f32[4,1,2,8,192]{4,3,2,1,0:T(8,128)S(1)}, f32[4,1,2,8,192]{4,3,2,1,0:T(8,128)S(1)}, u32[]{:S(2)}, u32[]{:S(2)}) collective-permute-start(f32[4,1,2,8,192]{4,3,2,1,0:T(8,128)S(1)} %get-tuple-element.66), channel_id=1, source_target_pairs={{8,0},{0,32},{72,64},{64,96},{136,128},{128,160},{200,192},{192,22... | collective-permute-start | bytes 147464 | tf_op jit(solution)/shard_map/ppermute | solution.py:70
  81.1 7.0 %collective-permute-start.24 = (f32[1,2,2,8,192]{4,3,2,1,0:T(8,128)S(1)}, f32[1,2,2,8,192]{4,3,2,1,0:T(8,128)S(1)}, u32[]{:S(2)}, u32[]{:S(2)}) collective-permute-start(f32[1,2,2,8,192]{4,3,2,1,0:T(8,128)S(1)} %get-tuple-element.76), channel_id=1, source_target_pairs={{0,452},{32,484},{452,0},{484,32},{8,460},{40,492},{460,8},{492,40... | collective-permute-start | bytes 73736 | tf_op jit(solution)/shard_map/ppermute | solution.py:70
  85.1 3.0 %collective-permute-start.22 = (f32[1,2,2,8,192]{4,3,2,1,0:T(8,128)S(1)}, f32[1,2,2,8,192]{4,3,2,1,0:T(8,128)S(1)}, u32[]{:S(2)}, u32[]{:S(2)}) collective-permute-start(f32[1,2,2,8,192]{4,3,2,1,0:T(8,128)S(1)} %get-tuple-element.77), channel_id=1, source_target_pairs={{0,64},{32,0},{64,128},{96,32},{128,192},{160,96},{192,256},{224,1... | collective-permute-start | bytes 73736 | tf_op jit(solution)/shard_map/ppermute | solution.py:70
  85.2 3.9 %collective-permute-start.23 = (f32[1,2,2,8,192]{4,3,2,1,0:T(8,128)S(1)}, f32[1,2,2,8,192]{4,3,2,1,0:T(8,128)S(1)}, u32[]{:S(2)}, u32[]{:S(2)}) collective-permute-start(f32[1,2,2,8,192]{4,3,2,1,0:T(8,128)S(1)} %get-tuple-element.78), channel_id=1, source_target_pairs={{64,0},{0,32},{128,64},{32,96},{192,128},{96,160},{256,192},{160,2... | collective-permute-start | bytes 73736 | tf_op jit(solution)/shard_map/ppermute | solution.py:70
  90.3 3.7 %collective-permute-start.25 = (f32[4,4,8,128]{3,2,1,0:T(8,128)S(1)}, f32[4,4,8,128]{3,2,1,0:T(8,128)S(1)}, u32[]{:S(2)}, u32[]{:S(2)}) collective-permute-start(f32[4,4,8,128]{3,2,1,0:T(8,128)S(1)} %bitcast.56), channel_id=1, source_target_pairs={{452,484},{484,453},{453,485},{485,454},{454,486},{486,455},{455,4... | collective-permute-start | bytes 196616 | tf_op jit(solution)/shard_map/ppermute | solution.py:70
  90.4 3.7 %collective-permute-start.26 = (f32[4,4,8,128]{3,2,1,0:T(8,128)S(1)}, f32[4,4,8,128]{3,2,1,0:T(8,128)S(1)}, u32[]{:S(2)}, u32[]{:S(2)}) collective-permute-start(f32[4,4,8,128]{3,2,1,0:T(8,128)S(1)} %bitcast.55), channel_id=1, source_target_pairs={{484,452},{453,484},{485,453},{454,485},{486,454},{455,486},{487,4... | collective-permute-start | bytes 196616 | tf_op jit(solution)/shard_map/ppermute | solution.py:70
  94.1 3.4 %collective-permute-start.29 = (f32[4,1,2,8,128]{4,3,2,1,0:T(8,128)S(1)}, f32[4,1,2,8,128]{4,3,2,1,0:T(8,128)S(1)}, u32[]{:S(2)}, u32[]{:S(2)}) collective-permute-start(f32[4,1,2,8,128]{4,3,2,1,0:T(8,128)S(1)} %get-tuple-element.73), channel_id=1, source_target_pairs={{0,24},{32,56},{64,88},{96,120},{128,152},{160,184},{192,216},{224... | collective-permute-start | bytes 98312 | tf_op jit(solution)/shard_map/ppermute | solution.py:70
  94.8 4.3 %collective-permute-start.27 = (f32[4,1,2,8,128]{4,3,2,1,0:T(8,128)S(1)}, f32[4,1,2,8,128]{4,3,2,1,0:T(8,128)S(1)}, u32[]{:S(2)}, u32[]{:S(2)}) collective-permute-start(f32[4,1,2,8,128]{4,3,2,1,0:T(8,128)S(1)} %get-tuple-element.74), channel_id=1, source_target_pairs={{0,8},{32,0},{64,72},{96,64},{128,136},{160,128},{192,200},{224,19... | collective-permute-start | bytes 98312 | tf_op jit(solution)/shard_map/ppermute | solution.py:70
  97.4 5.8 %collective-permute-start.28 = (f32[4,1,2,8,128]{4,3,2,1,0:T(8,128)S(1)}, f32[4,1,2,8,128]{4,3,2,1,0:T(8,128)S(1)}, u32[]{:S(2)}, u32[]{:S(2)}) collective-permute-start(f32[4,1,2,8,128]{4,3,2,1,0:T(8,128)S(1)} %get-tuple-element.75), channel_id=1, source_target_pairs={{8,0},{0,32},{72,64},{64,96},{136,128},{128,160},{200,192},{192,22... | collective-permute-start | bytes 98312 | tf_op jit(solution)/shard_map/ppermute | solution.py:70
  103.3 6.8 %collective-permute-start.32 = (f32[1,2,2,8,128]{4,3,2,1,0:T(8,128)S(1)}, f32[1,2,2,8,128]{4,3,2,1,0:T(8,128)S(1)}, u32[]{:S(2)}, u32[]{:S(2)}) collective-permute-start(f32[1,2,2,8,128]{4,3,2,1,0:T(8,128)S(1)} %get-tuple-element.92), channel_id=1, source_target_pairs={{0,452},{32,484},{452,0},{484,32},{8,460},{40,492},{460,8},{492,40... | collective-permute-start | bytes 49160 | tf_op jit(solution)/shard_map/ppermute | solution.py:70
  106.3 3.8 %collective-permute-start.30 = (f32[1,2,2,8,128]{4,3,2,1,0:T(8,128)S(1)}, f32[1,2,2,8,128]{4,3,2,1,0:T(8,128)S(1)}, u32[]{:S(2)}, u32[]{:S(2)}) collective-permute-start(f32[1,2,2,8,128]{4,3,2,1,0:T(8,128)S(1)} %get-tuple-element.93), channel_id=1, source_target_pairs={{0,64},{32,0},{64,128},{96,32},{128,192},{160,96},{192,256},{224,1... | collective-permute-start | bytes 49160 | tf_op jit(solution)/shard_map/ppermute | solution.py:70
  106.3 3.8 %collective-permute-start.31 = (f32[1,2,2,8,128]{4,3,2,1,0:T(8,128)S(1)}, f32[1,2,2,8,128]{4,3,2,1,0:T(8,128)S(1)}, u32[]{:S(2)}, u32[]{:S(2)}) collective-permute-start(f32[1,2,2,8,128]{4,3,2,1,0:T(8,128)S(1)} %get-tuple-element.94), channel_id=1, source_target_pairs={{64,0},{0,32},{128,64},{32,96},{192,128},{96,160},{256,192},{160,2... | collective-permute-start | bytes 49160 | tf_op jit(solution)/shard_map/ppermute | solution.py:70
  110.4 8.6 %collective-permute-start.33 = (f32[16,128]{1,0:T(8,128)S(1)}, f32[16,128]{1,0:T(8,128)S(1)}, u32[]{:S(2)}, u32[]{:S(2)}) collective-permute-start(f32[16,128]{1,0:T(8,128)S(1)} %k_force.1), channel_id=1, source_target_pairs={{452,0},{484,1},{453,2},{485,3},{454,4},{486,5},{455,6},{487,7},{4... | collective-permute-start | bytes 24584 | tf_op jit(solution)/shard_map/ppermute | solution.py:70

commit v6 on v4

--- a/solution.py
+++ b/solution.py
@@ -126,16 +126,23 @@
     return lax.dot_general(a, b, (((ca,), (cb,)), ((), ())), preferred_element_type=F32)
 
 
+def halves(x):
+    high = x.astype(BF16).astype(F32)
+    return high, x - high
+
+
 def weighted(w, x):
-    wh, wl = split2(w)
-    xh, xl = split2(x)
-    return dot(wh, xh, 0, 0) + (dot(wl, xh, 0, 0) + dot(wh, xl, 0, 0))
+    wh, wl = halves(w)
+    xh, xl = halves(x)
+    left = jnp.concatenate([wh, wl, wh], axis=0).astype(BF16)
+    return dot(left, jnp.concatenate([xh, xh, xl], axis=0).astype(BF16), 0, 0)
 
 
 def weighted_t(w, x):
-    wh, wl = split2(w)
-    xh, xl = split2(x)
-    return dot(wh, xh, 1, 0) + (dot(wl, xh, 1, 0) + dot(wh, xl, 1, 0))
+    wh, wl = halves(w)
+    xh, xl = halves(x)
+    left = jnp.concatenate([wh, wl, wh], axis=1).astype(BF16)
+    return dot(left, jnp.concatenate([xh, xh, xl], axis=0).astype(BF16), 1, 0)
 
 
 def pick(table, onehot, parts=2):
@@ -159,8 +166,13 @@
 
 
 def put_rows(values, onehot):
-    high, low = split2(values)
-    return dot(onehot, high, 1, 1) + dot(onehot, low, 1, 1)
+    high, low = halves(values)
+    if values.shape[0] % 128:
+        gap = jnp.zeros((-values.shape[0] % 128, values.shape[1]), F32)
+        high, low = jnp.concatenate([high, gap], axis=0), jnp.concatenate([low, gap], axis=0)
+    rows = high.shape[0]
+    full = dot(onehot, jnp.concatenate([high, low], axis=0).astype(BF16), 1, 1)
+    return (full[:, :rows] + full[:, rows:])[:, : values.shape[0]]
 
 
 def lanes(block):
@@ -366,8 +378,9 @@
     scal = scal_ref[...]
     unit, cut = scal[0:3], scal[5:6]
     slots = match(ghost_slot(partners_of(packed)), 512)
-    high, low = split2(jnp.concatenate([before_ref[...], after_ref[...], cells_ref[...]], axis=0))
-    ej = ejown_ref[...] + (dot(high, slots, 0, 0) + dot(low, slots, 0, 0))
+    ghost = jnp.concatenate([before_ref[...], after_ref[...], cells_ref[...]], axis=0)
+    ghost = jnp.concatenate([ghost, jnp.zeros((512, 64), F32)], axis=1).T[:192]
+    ej = ejown_ref[...] + pick(ghost, slots)
     ei = ei_ref[...]
     coupling = 0.0
     for k in range(3):
@@ -463,7 +476,7 @@
         rbar = rbar - inv * along[k] * unit[k : k + 1]
     dbar = jnp.concatenate([along[k] * inv + rbar * unit[k : k + 1] for k in range(3)] + [jnp.zeros((5, PAIRS), F32)], axis=0)
     slots = match(ghost_slot(partners_of(packed)), 512)
-    msg = jnp.concatenate([put_rows(dbar, slots), jnp.zeros((512, 120), F32)], axis=1)
+    msg = put_rows(jnp.concatenate([dbar, jnp.zeros((120, PAIRS), F32)], axis=0), slots)
     to_before_ref[...] = msg[:128]
     to_after_ref[...] = msg[128:256]
     to_cells_ref[...] = msg[256:]

time: 120 us -> 119 us (level)
    pallas_call x10, Pallas kernels: 11.7 us -> 10.5 us  [call(): pl.pallas_call(kernel, out_shape=shapes, in_specs=[spec] * len(args), out...]
where the time goes in v6:
time: 119 us; the launch traced here: 118 us
  starting transfers between devices  61.8 us (52%)
  waiting for transfers between devices  41 us (34%)
  Pallas kernels  12 us (10%)
  local copies, waits for them, and re-layouts  1.66 us (1%)
    ppermute x34, starting transfers between devices, send(): return lax.ppermute(x, AXES, pairs)  61.8 us
    ppermute x34, waiting for transfers between devices, send(): return lax.ppermute(x, AXES, pairs)  41 us
    pallas_call x10, Pallas kernels, call(): pl.pallas_call(kernel, out_shape=shapes, in_specs=[spec] * len(args), out...  10.5 us
  transfers between devices with their start and end apart: 34, of which 17 were waited for; matrix products, arithmetic and copies ran while one was open for 0% of the time, Pallas kernels for 5%

profile of v6, /device:TPU:71, one launch (start us, length us, event | category | flops | bytes accessed | tf_op | source)
XLA Modules:
  0.0 118.0 jit_solution(11434021795173510717)
XLA Ops:
  0.6 1.5 %k_pack.1 = f32[48,128]{1,0:T(8,128)} custom-call(f32[3,1,1,1,512]{4,3,2,1,0:T(1,128)} %pos_in.1, s32[1,1,1,512]{3,2,1,0:T(1,128)} %kind_in.1, s32[2,2,2,8]{3,2,1,0:T(2,128)} %names_in.1, s32[1,1,1,8,128]{4,3,2,1,0:T(8,128)} %center_in.1, s32[1,1,1,8,128]{4,3,2,1,0:T(8,128)} %partner_in.1, s32[1,1,1,8,128]{4,3,2,1,0:T(8,128)} %live_in.1), custom_call_target="tpu_custom_call" | custom-call | tf_op jit(solution)/shard_map/k_pack/pallas_call | solution.py:253
  2.1 8.3 %collective-permute-start = (f32[48,128]{1,0:T(8,128)}, f32[48,128]{1,0:T(8,128)S(1)}, u32[]{:S(2)}, u32[]{:S(2)}) collective-permute-start(f32[48,128]{1,0:T(8,128)} %k_pack.1), channel_id=1, source_target_pairs={{0,0},{1,32},{2,1},{3,33},{4,2},{5,34},{6,3},{7,35},{8,8},{9,40},{... | collective-permute-start | bytes 73736 | tf_op jit(solution)/shard_map/ppermute | solution.py:70
  10.5 7.4 %collective-permute-done.packed_ref = f32[48,128]{1,0:T(8,128)S(1)} collective-permute-done((f32[48,128]{1,0:T(8,128)}, f32[48,128]{1,0:T(8,128)S(1)}, u32[]{:S(2)}, u32[]{:S(2)}) %collective-permute-start) | collective-permute-done | bytes 24608 | tf_op jit(solution)/shard_map/ppermute | solution.py:70
  18.2 0.7 collective-permute-start.3
  18.9 1.5 %collective-permute-start.1 = (f32[1,2,2,8,128]{4,3,2,1,0:T(8,128)S(1)}, f32[1,2,2,8,128]{4,3,2,1,0:T(8,128)S(1)}, u32[]{:S(2)}, u32[]{:S(2)}) collective-permute-start(f32[1,2,2,8,128]{4,3,2,1,0:T(8,128)S(1)} %get-tuple-element.107), channel_id=1, source_target_pairs={{0,64},{32,0},{64,128},{96,32},{128,192},{160,96},{192,256},{224,1... | collective-permute-start | bytes 49160 | tf_op jit(solution)/shard_map/ppermute | solution.py:70
  20.3 1.1 collective-permute-done.2
  21.5 4.6 %collective-permute-start.6 = (f32[4,1,2,8,128]{4,3,2,1,0:T(8,128)S(1)}, f32[4,1,2,8,128]{4,3,2,1,0:T(8,128)S(1)}, u32[]{:S(2)}, u32[]{:S(2)}) collective-permute-start(f32[4,1,2,8,128]{4,3,2,1,0:T(8,128)S(1)} %get-tuple-element.98), channel_id=1, source_target_pairs={{0,24},{32,56},{64,88},{96,120},{128,152},{160,184},{192,216},{224... | collective-permute-start | bytes 98312 | tf_op jit(solution)/shard_map/ppermute | solution.py:70
  26.2 3.8 %collective-permute-start.4 = (f32[4,1,2,8,128]{4,3,2,1,0:T(8,128)S(1)}, f32[4,1,2,8,128]{4,3,2,1,0:T(8,128)S(1)}, u32[]{:S(2)}, u32[]{:S(2)}) collective-permute-start(f32[4,1,2,8,128]{4,3,2,1,0:T(8,128)S(1)} %get-tuple-element.99), channel_id=1, source_target_pairs={{0,8},{32,0},{64,72},{96,64},{128,136},{160,128},{192,200},{224,19... | collective-permute-start | bytes 98312 | tf_op jit(solution)/shard_map/ppermute | solution.py:70
  30.1 0.7 copy-done.2
  30.8 0.6 copy-done.3
  31.6 2.4 %collective-permute-start.8 = (f32[4,4,8,128]{3,2,1,0:T(8,128)S(1)}, f32[4,4,8,128]{3,2,1,0:T(8,128)S(1)}, u32[]{:S(2)}, u32[]{:S(2)}) collective-permute-start(f32[4,4,8,128]{3,2,1,0:T(8,128)S(1)} %get-tuple-element.82), channel_id=1, source_target_pairs={{32,0},{1,32},{33,1},{2,33},{34,2},{3,34},{35,3},{0,35},{40,8},{9,... | collective-permute-start | bytes 196616 | tf_op jit(solution)/shard_map/ppermute | solution.py:70
  34.0 5.9 %collective-permute-start.7 = (f32[4,4,8,128]{3,2,1,0:T(8,128)S(1)}, f32[4,4,8,128]{3,2,1,0:T(8,128)S(1)}, u32[]{:S(2)}, u32[]{:S(2)}) collective-permute-start(f32[4,4,8,128]{3,2,1,0:T(8,128)S(1)} %get-tuple-element.83), channel_id=1, source_target_pairs={{0,32},{32,1},{1,33},{33,2},{2,34},{34,3},{3,35},{35,0},{8,40},{40... | collective-permute-start | bytes 196616 | tf_op jit(solution)/shard_map/ppermute | solution.py:70
  40.4 1.4 %collective-permute-done.8 = f32[4,4,8,128]{3,2,1,0:T(8,128)S(1)} collective-permute-done((f32[4,4,8,128]{3,2,1,0:T(8,128)S(1)}, f32[4,4,8,128]{3,2,1,0:T(8,128)S(1)}, u32[]{:S(2)}, u32[]{:S(2)}) %collective-permute-start.8) | collective-permute-done | bytes 65568 | tf_op jit(solution)/shard_map/ppermute | solution.py:70
  41.8 1.2 %k_features.1 = (f32[32,192]{1,0:T(8,128)S(1)}, f32[32,192]{1,0:T(8,128)S(1)}, f32[8,1024]{1,0:T(8,128)S(1)}, f32[128,1024]{1,0:T(8,128)S(1)}, f32[128,1024]{1,0:T(8,128)S(1)}) custom-call(f32[48,128]{1,0:T(8,128)S(1)} %collective-permute-done.packed_ref, f32[8,1024]{1,0:T(8,128)S(1)} %k_own_pairs.1.part_ref, f32[128,128]{1,0:T(8,128)S(1)} %bitcast.52, ...), custom_call_target="tpu_custom_call" | custom-call | tf_op jit(solution)/shard_map/k_features/pallas_call | solution.py:517
  43.0 0.7 collective-permute-start.11
  43.7 1.8 %collective-permute-start.9 = (f32[1,2,2,8,192]{4,3,2,1,0:T(8,128)S(1)}, f32[1,2,2,8,192]{4,3,2,1,0:T(8,128)S(1)}, u32[]{:S(2)}, u32[]{:S(2)}) collective-permute-start(f32[1,2,2,8,192]{4,3,2,1,0:T(8,128)S(1)} %get-tuple-element.97), channel_id=1, source_target_pairs={{0,64},{32,0},{64,128},{96,32},{128,192},{160,96},{192,256},{224,1... | collective-permute-start | bytes 73736 | tf_op jit(solution)/shard_map/ppermute | solution.py:70
  45.5 1.3 %collective-permute-done.10 = f32[1,2,2,8,192]{4,3,2,1,0:T(8,128)S(1)} collective-permute-done((f32[1,2,2,8,192]{4,3,2,1,0:T(8,128)S(1)}, f32[1,2,2,8,192]{4,3,2,1,0:T(8,128)S(1)}, u32[]{:S(2)}, u32[]{:S(2)}) %collective-permute-start.10) | collective-permute-done | bytes 24608 | tf_op jit(solution)/shard_map/ppermute | solution.py:70
  46.8 2.8 %collective-permute-start.14 = (f32[4,1,2,8,192]{4,3,2,1,0:T(8,128)S(1)}, f32[4,1,2,8,192]{4,3,2,1,0:T(8,128)S(1)}, u32[]{:S(2)}, u32[]{:S(2)}) collective-permute-start(f32[4,1,2,8,192]{4,3,2,1,0:T(8,128)S(1)} %get-tuple-element.79), channel_id=1, source_target_pairs={{0,24},{32,56},{64,88},{96,120},{128,152},{160,184},{192,216},{224... | collective-permute-start | bytes 147464 | tf_op jit(solution)/shard_map/ppermute | solution.py:70
  49.6 1.5 %collective-permute-start.12 = (f32[4,1,2,8,192]{4,3,2,1,0:T(8,128)S(1)}, f32[4,1,2,8,192]{4,3,2,1,0:T(8,128)S(1)}, u32[]{:S(2)}, u32[]{:S(2)}) collective-permute-start(f32[4,1,2,8,192]{4,3,2,1,0:T(8,128)S(1)} %get-tuple-element.80), channel_id=1, source_target_pairs={{0,8},{32,0},{64,72},{96,64},{128,136},{160,128},{192,200},{224,19... | collective-permute-start | bytes 147464 | tf_op jit(solution)/shard_map/ppermute | solution.py:70
  51.2 1.9 %collective-permute-done.14 = f32[4,1,2,8,192]{4,3,2,1,0:T(8,128)S(1)} collective-permute-done((f32[4,1,2,8,192]{4,3,2,1,0:T(8,128)S(1)}, f32[4,1,2,8,192]{4,3,2,1,0:T(8,128)S(1)}, u32[]{:S(2)}, u32[]{:S(2)}) %collective-permute-start.14) | collective-permute-done | bytes 49184 | tf_op jit(solution)/shard_map/ppermute | solution.py:70
  53.2 2.4 %collective-permute-start.16 = (f32[4,4,8,192]{3,2,1,0:T(8,128)S(1)}, f32[4,4,8,192]{3,2,1,0:T(8,128)S(1)}, u32[]{:S(2)}, u32[]{:S(2)}) collective-permute-start(f32[4,4,8,192]{3,2,1,0:T(8,128)S(1)} %get-tuple-element.67), channel_id=1, source_target_pairs={{32,0},{1,32},{33,1},{2,33},{34,2},{3,34},{35,3},{0,35},{40,8},{9,... | collective-permute-start | bytes 294920 | tf_op jit(solution)/shard_map/ppermute | solution.py:70
  55.6 5.0 %collective-permute-start.15 = (f32[4,4,8,192]{3,2,1,0:T(8,128)S(1)}, f32[4,4,8,192]{3,2,1,0:T(8,128)S(1)}, u32[]{:S(2)}, u32[]{:S(2)}) collective-permute-start(f32[4,4,8,192]{3,2,1,0:T(8,128)S(1)} %get-tuple-element.68), channel_id=1, source_target_pairs={{0,32},{32,1},{1,33},{33,2},{2,34},{34,3},{3,35},{35,0},{8,40},{40... | collective-permute-start | bytes 294920 | tf_op jit(solution)/shard_map/ppermute | solution.py:70
  60.7 2.2 %k_own_env.1 = (f32[192,1024]{1,0:T(8,128)S(1)}, f32[192,1024]{1,0:T(8,128)S(1)}, f32[128,1024]{1,0:T(8,128)S(1)}, f32[128,1024]{1,0:T(8,128)S(1)}, f32[128,1024]{1,0:T(8,128)S(1)}, /*index=5*/f32[128,1024]{1,0:T(8,128)S(1)}) custom-call(f32[48,128]{1,0:T(8,128)S(1)} %collective-permute-done.packed_ref, f32[8,1024]{1,0:T(8,128)S(1)} %get-tuple-element.36.scal_ref, ...), custom_call_target="tpu_custom_call" | custom-call | tf_op jit(solution)/shard_map/k_own_env/pallas_call | solution.py:517
  63.2 1.8 %k_energy.1 = (f32[128,192]{1,0:T(8,128)S(1)}, f32[128,192]{1,0:T(8,128)S(1)}, f32[256,192]{1,0:T(8,128)S(1)}, f32[192,1024]{1,0:T(8,128)S(1)}, f32[128,1024]{1,0:T(8,128)S(1)}, /*index=5*/f32[64,1024]{1,0:T(8,128)S(1)}) custom-call(f32[48,128]{1,0:T(8,128)S(1)} %collective-permute-done.packed_ref, f32[8,1024]{1,0:T(8,128)S(1)} %get-tuple-element.36.scal_ref, ...), custom_call_target="tpu_custom_call" | custom-call | tf_op jit(solution)/shard_map/k_energy/pallas_call | solution.py:517
  65.0 3.0 %collective-permute-start.17 = (f32[4,4,8,192]{3,2,1,0:T(8,128)S(1)}, f32[4,4,8,192]{3,2,1,0:T(8,128)S(1)}, u32[]{:S(2)}, u32[]{:S(2)}) collective-permute-start(f32[4,4,8,192]{3,2,1,0:T(8,128)S(1)} %bitcast.54), channel_id=1, source_target_pairs={{0,32},{32,1},{1,33},{33,2},{2,34},{34,3},{3,35},{35,0},{8,40},{40... | collective-permute-start | bytes 294920 | tf_op jit(solution)/shard_map/ppermute | solution.py:70
  68.0 2.2 %k_direct.1 = (f32[8,1024]{1,0:T(8,128)S(1)}, f32[4,512]{1,0:T(4,128)S(1)}) custom-call(f32[48,128]{1,0:T(8,128)S(1)} %collective-permute-done.packed_ref, f32[8,1024]{1,0:T(8,128)S(1)} %get-tuple-element.36.scal_ref, f32[128,1024]{1,0:T(8,128)S(1)} %get-tuple-element.37.av_ref, f32[128,1024]{1,0:T(8,128)S(1)} %get-tuple-element.39.nav_ref, ...), custom_call_target="tpu_custom_call" | custom-call | tf_op jit(solution)/shard_map/k_direct/pallas_call | solution.py:517
  70.2 3.4 %collective-permute-done.18 = f32[4,4,8,192]{3,2,1,0:T(8,128)S(1)} collective-permute-done((f32[4,4,8,192]{3,2,1,0:T(8,128)S(1)}, f32[4,4,8,192]{3,2,1,0:T(8,128)S(1)}, u32[]{:S(2)}, u32[]{:S(2)}) %collective-permute-start.18) | collective-permute-done | bytes 98336 | tf_op jit(solution)/shard_map/ppermute | solution.py:70
  73.7 3.7 %collective-permute-start.21 = (f32[4,1,2,8,192]{4,3,2,1,0:T(8,128)S(1)}, f32[4,1,2,8,192]{4,3,2,1,0:T(8,128)S(1)}, u32[]{:S(2)}, u32[]{:S(2)}) collective-permute-start(f32[4,1,2,8,192]{4,3,2,1,0:T(8,128)S(1)} %get-tuple-element.64), channel_id=1, source_target_pairs={{0,24},{32,56},{64,88},{96,120},{128,152},{160,184},{192,216},{224... | collective-permute-start | bytes 147464 | tf_op jit(solution)/shard_map/ppermute | solution.py:70
  77.4 1.5 %collective-permute-start.20 = (f32[4,1,2,8,192]{4,3,2,1,0:T(8,128)S(1)}, f32[4,1,2,8,192]{4,3,2,1,0:T(8,128)S(1)}, u32[]{:S(2)}, u32[]{:S(2)}) collective-permute-start(f32[4,1,2,8,192]{4,3,2,1,0:T(8,128)S(1)} %get-tuple-element.66), channel_id=1, source_target_pairs={{8,0},{0,32},{72,64},{64,96},{136,128},{128,160},{200,192},{192,22... | collective-permute-start | bytes 147464 | tf_op jit(solution)/shard_map/ppermute | solution.py:70
  78.9 1.0 collective-permute-done.21
  79.9 0.6 collective-permute-done.19
  80.6 0.7 collective-permute-start.24
  81.3 1.8 %collective-permute-start.22 = (f32[1,2,2,8,192]{4,3,2,1,0:T(8,128)S(1)}, f32[1,2,2,8,192]{4,3,2,1,0:T(8,128)S(1)}, u32[]{:S(2)}, u32[]{:S(2)}) collective-permute-start(f32[1,2,2,8,192]{4,3,2,1,0:T(8,128)S(1)} %get-tuple-element.77), channel_id=1, source_target_pairs={{0,64},{32,0},{64,128},{96,32},{128,192},{160,96},{192,256},{224,1... | collective-permute-start | bytes 73736 | tf_op jit(solution)/shard_map/ppermute | solution.py:70
  83.0 1.0 collective-permute-done.22
  84.0 3.3 %collective-permute-done.23 = f32[1,2,2,8,192]{4,3,2,1,0:T(8,128)S(1)} collective-permute-done((f32[1,2,2,8,192]{4,3,2,1,0:T(8,128)S(1)}, f32[1,2,2,8,192]{4,3,2,1,0:T(8,128)S(1)}, u32[]{:S(2)}, u32[]{:S(2)}) %collective-permute-start.23) | collective-permute-done | bytes 24608 | tf_op jit(solution)/shard_map/ppermute | solution.py:70
  87.4 1.0 k_env_back.1
  88.9 0.6 k_own_force.1.own_ref
  89.8 3.6 %collective-permute-done.26 = f32[4,4,8,128]{3,2,1,0:T(8,128)S(1)} collective-permute-done((f32[4,4,8,128]{3,2,1,0:T(8,128)S(1)}, f32[4,4,8,128]{3,2,1,0:T(8,128)S(1)}, u32[]{:S(2)}, u32[]{:S(2)}) %collective-permute-start.26) | collective-permute-done | bytes 65568 | tf_op jit(solution)/shard_map/ppermute | solution.py:70
  93.4 2.8 %collective-permute-start.29 = (f32[4,1,2,8,128]{4,3,2,1,0:T(8,128)S(1)}, f32[4,1,2,8,128]{4,3,2,1,0:T(8,128)S(1)}, u32[]{:S(2)}, u32[]{:S(2)}) collective-permute-start(f32[4,1,2,8,128]{4,3,2,1,0:T(8,128)S(1)} %get-tuple-element.73), channel_id=1, source_target_pairs={{0,24},{32,56},{64,88},{96,120},{128,152},{160,184},{192,216},{224... | collective-permute-start | bytes 98312 | tf_op jit(solution)/shard_map/ppermute | solution.py:70
  96.2 1.5 %collective-permute-start.28 = (f32[4,1,2,8,128]{4,3,2,1,0:T(8,128)S(1)}, f32[4,1,2,8,128]{4,3,2,1,0:T(8,128)S(1)}, u32[]{:S(2)}, u32[]{:S(2)}) collective-permute-start(f32[4,1,2,8,128]{4,3,2,1,0:T(8,128)S(1)} %get-tuple-element.75), channel_id=1, source_target_pairs={{8,0},{0,32},{72,64},{64,96},{136,128},{128,160},{200,192},{192,22... | collective-permute-start | bytes 98312 | tf_op jit(solution)/shard_map/ppermute | solution.py:70
  97.7 1.6 %collective-permute-done.29 = f32[4,1,2,8,128]{4,3,2,1,0:T(8,128)S(1)} collective-permute-done((f32[4,1,2,8,128]{4,3,2,1,0:T(8,128)S(1)}, f32[4,1,2,8,128]{4,3,2,1,0:T(8,128)S(1)}, u32[]{:S(2)}, u32[]{:S(2)}) %collective-permute-start.29) | collective-permute-done | bytes 32800 | tf_op jit(solution)/shard_map/ppermute | solution.py:70
  99.3 0.7 collective-permute-start.32
  100.0 2.5 %collective-permute-start.30 = (f32[1,2,2,8,128]{4,3,2,1,0:T(8,128)S(1)}, f32[1,2,2,8,128]{4,3,2,1,0:T(8,128)S(1)}, u32[]{:S(2)}, u32[]{:S(2)}) collective-permute-start(f32[1,2,2,8,128]{4,3,2,1,0:T(8,128)S(1)} %get-tuple-element.93), channel_id=1, source_target_pairs={{0,64},{32,0},{64,128},{96,32},{128,192},{160,96},{192,256},{224,1... | collective-permute-start | bytes 49160 | tf_op jit(solution)/shard_map/ppermute | solution.py:70
  102.5 0.9 collective-permute-done.30
  103.3 4.0 %collective-permute-done.31 = f32[1,2,2,8,128]{4,3,2,1,0:T(8,128)S(1)} collective-permute-done((f32[1,2,2,8,128]{4,3,2,1,0:T(8,128)S(1)}, f32[1,2,2,8,128]{4,3,2,1,0:T(8,128)S(1)}, u32[]{:S(2)}, u32[]{:S(2)}) %collective-permute-start.31) | collective-permute-done | bytes 16416 | tf_op jit(solution)/shard_map/ppermute | solution.py:70
  107.5 1.9 %collective-permute-start.33 = (f32[16,128]{1,0:T(8,128)S(1)}, f32[16,128]{1,0:T(8,128)S(1)}, u32[]{:S(2)}, u32[]{:S(2)}) collective-permute-start(f32[16,128]{1,0:T(8,128)S(1)} %k_force.1), channel_id=1, source_target_pairs={{0,0},{32,1},{1,2},{33,3},{2,4},{34,5},{3,6},{35,7},{8,8},{40,9},{... | collective-permute-start | bytes 24584 | tf_op jit(solution)/shard_map/ppermute | solution.py:70
  109.5 7.9 %collective-permute-done.33.in_ref = f32[16,128]{1,0:T(8,128)S(1)} collective-permute-done((f32[16,128]{1,0:T(8,128)S(1)}, f32[16,128]{1,0:T(8,128)S(1)}, u32[]{:S(2)}, u32[]{:S(2)}) %collective-permute-start.33) | collective-permute-done | bytes 8224 | tf_op jit(solution)/shard_map/ppermute | solution.py:70
  117.4 0.6 k_unpack.1
  (79 shorter events, 2.9 us)
Async XLA Ops:
  2.1 15.8 %collective-permute-start = (f32[48,128]{1,0:T(8,128)}, f32[48,128]{1,0:T(8,128)S(1)}, u32[]{:S(2)}, u32[]{:S(2)}) collective-permute-start(f32[48,128]{1,0:T(8,128)} %k_pack.1), channel_id=1, source_target_pairs={{0,0},{1,32},{2,1},{3,33},{4,2},{5,34},{6,3},{7,35},{8,8},{9,40},{... | collective-permute-start | bytes 73736 | tf_op jit(solution)/shard_map/ppermute | solution.py:70
  18.2 2.2 %collective-permute-start.3 = (f32[1,2,2,8,128]{4,3,2,1,0:T(8,128)S(1)}, f32[1,2,2,8,128]{4,3,2,1,0:T(8,128)S(1)}, u32[]{:S(2)}, u32[]{:S(2)}) collective-permute-start(f32[1,2,2,8,128]{4,3,2,1,0:T(8,128)S(1)} %get-tuple-element.105), channel_id=1, source_target_pairs={{0,452},{32,484},{452,0},{484,32},{8,460},{40,492},{460,8},{492,40... | collective-permute-start | bytes 49160 | tf_op jit(solution)/shard_map/ppermute | solution.py:70
  18.8 2.6 %collective-permute-start.2 = (f32[1,2,2,8,128]{4,3,2,1,0:T(8,128)S(1)}, f32[1,2,2,8,128]{4,3,2,1,0:T(8,128)S(1)}, u32[]{:S(2)}, u32[]{:S(2)}) collective-permute-start(f32[1,2,2,8,128]{4,3,2,1,0:T(8,128)S(1)} %get-tuple-element.106), channel_id=1, source_target_pairs={{64,0},{0,32},{128,64},{32,96},{192,128},{96,160},{256,192},{160,2... | collective-permute-start | bytes 49160 | tf_op jit(solution)/shard_map/ppermute | solution.py:70
  18.9 2.6 %collective-permute-start.1 = (f32[1,2,2,8,128]{4,3,2,1,0:T(8,128)S(1)}, f32[1,2,2,8,128]{4,3,2,1,0:T(8,128)S(1)}, u32[]{:S(2)}, u32[]{:S(2)}) collective-permute-start(f32[1,2,2,8,128]{4,3,2,1,0:T(8,128)S(1)} %get-tuple-element.107), channel_id=1, source_target_pairs={{0,64},{32,0},{64,128},{96,32},{128,192},{160,96},{192,256},{224,1... | collective-permute-start | bytes 49160 | tf_op jit(solution)/shard_map/ppermute | solution.py:70
  21.5 8.5 %copy-start.1 = (f32[128,64]{0,1:T(8,128)S(1)}, f32[128,64]{0,1:T(8,128)}, u32[]{:S(2)}) copy-start(f32[128,64]{0,1:T(8,128)} %param.22) | copy-start | bytes 98308
  21.5 10.0 %collective-permute-start.6 = (f32[4,1,2,8,128]{4,3,2,1,0:T(8,128)S(1)}, f32[4,1,2,8,128]{4,3,2,1,0:T(8,128)S(1)}, u32[]{:S(2)}, u32[]{:S(2)}) collective-permute-start(f32[4,1,2,8,128]{4,3,2,1,0:T(8,128)S(1)} %get-tuple-element.98), channel_id=1, source_target_pairs={{0,24},{32,56},{64,88},{96,120},{128,152},{160,184},{192,216},{224... | collective-permute-start | bytes 98312 | tf_op jit(solution)/shard_map/ppermute | solution.py:70
  26.2 5.3 %collective-permute-start.4 = (f32[4,1,2,8,128]{4,3,2,1,0:T(8,128)S(1)}, f32[4,1,2,8,128]{4,3,2,1,0:T(8,128)S(1)}, u32[]{:S(2)}, u32[]{:S(2)}) collective-permute-start(f32[4,1,2,8,128]{4,3,2,1,0:T(8,128)S(1)} %get-tuple-element.99), channel_id=1, source_target_pairs={{0,8},{32,0},{64,72},{96,64},{128,136},{160,128},{192,200},{224,19... | collective-permute-start | bytes 98312 | tf_op jit(solution)/shard_map/ppermute | solution.py:70
  30.0 1.5 %collective-permute-start.5 = (f32[4,1,2,8,128]{4,3,2,1,0:T(8,128)S(1)}, f32[4,1,2,8,128]{4,3,2,1,0:T(8,128)S(1)}, u32[]{:S(2)}, u32[]{:S(2)}) collective-permute-start(f32[4,1,2,8,128]{4,3,2,1,0:T(8,128)S(1)} %get-tuple-element.100), channel_id=1, source_target_pairs={{8,0},{0,32},{72,64},{64,96},{136,128},{128,160},{200,192},{192,22... | collective-permute-start | bytes 98312 | tf_op jit(solution)/shard_map/ppermute | solution.py:70
  30.0 0.8 copy-start.2
  30.7 0.7 copy-start.3
  30.7 0.7 copy-start.4
  30.7 0.7 copy-start.5
  31.6 10.2 %collective-permute-start.8 = (f32[4,4,8,128]{3,2,1,0:T(8,128)S(1)}, f32[4,4,8,128]{3,2,1,0:T(8,128)S(1)}, u32[]{:S(2)}, u32[]{:S(2)}) collective-permute-start(f32[4,4,8,128]{3,2,1,0:T(8,128)S(1)} %get-tuple-element.82), channel_id=1, source_target_pairs={{32,0},{1,32},{33,1},{2,33},{34,2},{3,34},{35,3},{0,35},{40,8},{9,... | collective-permute-start | bytes 196616 | tf_op jit(solution)/shard_map/ppermute | solution.py:70
  34.0 7.8 %collective-permute-start.7 = (f32[4,4,8,128]{3,2,1,0:T(8,128)S(1)}, f32[4,4,8,128]{3,2,1,0:T(8,128)S(1)}, u32[]{:S(2)}, u32[]{:S(2)}) collective-permute-start(f32[4,4,8,128]{3,2,1,0:T(8,128)S(1)} %get-tuple-element.83), channel_id=1, source_target_pairs={{0,32},{32,1},{1,33},{33,2},{2,34},{34,3},{3,35},{35,0},{8,40},{40... | collective-permute-start | bytes 196616 | tf_op jit(solution)/shard_map/ppermute | solution.py:70
  43.0 2.5 %collective-permute-start.11 = (f32[1,2,2,8,192]{4,3,2,1,0:T(8,128)S(1)}, f32[1,2,2,8,192]{4,3,2,1,0:T(8,128)S(1)}, u32[]{:S(2)}, u32[]{:S(2)}) collective-permute-start(f32[1,2,2,8,192]{4,3,2,1,0:T(8,128)S(1)} %get-tuple-element.95), channel_id=1, source_target_pairs={{0,452},{32,484},{452,0},{484,32},{8,460},{40,492},{460,8},{492,40... | collective-permute-start | bytes 73736 | tf_op jit(solution)/shard_map/ppermute | solution.py:70
  43.7 3.1 %collective-permute-start.10 = (f32[1,2,2,8,192]{4,3,2,1,0:T(8,128)S(1)}, f32[1,2,2,8,192]{4,3,2,1,0:T(8,128)S(1)}, u32[]{:S(2)}, u32[]{:S(2)}) collective-permute-start(f32[1,2,2,8,192]{4,3,2,1,0:T(8,128)S(1)} %get-tuple-element.96), channel_id=1, source_target_pairs={{64,0},{0,32},{128,64},{32,96},{192,128},{96,160},{256,192},{160,2... | collective-permute-start | bytes 73736 | tf_op jit(solution)/shard_map/ppermute | solution.py:70
  43.7 3.0 %collective-permute-start.9 = (f32[1,2,2,8,192]{4,3,2,1,0:T(8,128)S(1)}, f32[1,2,2,8,192]{4,3,2,1,0:T(8,128)S(1)}, u32[]{:S(2)}, u32[]{:S(2)}) collective-permute-start(f32[1,2,2,8,192]{4,3,2,1,0:T(8,128)S(1)} %get-tuple-element.97), channel_id=1, source_target_pairs={{0,64},{32,0},{64,128},{96,32},{128,192},{160,96},{192,256},{224,1... | collective-permute-start | bytes 73736 | tf_op jit(solution)/shard_map/ppermute | solution.py:70
  46.8 6.2 %collective-permute-start.14 = (f32[4,1,2,8,192]{4,3,2,1,0:T(8,128)S(1)}, f32[4,1,2,8,192]{4,3,2,1,0:T(8,128)S(1)}, u32[]{:S(2)}, u32[]{:S(2)}) collective-permute-start(f32[4,1,2,8,192]{4,3,2,1,0:T(8,128)S(1)} %get-tuple-element.79), channel_id=1, source_target_pairs={{0,24},{32,56},{64,88},{96,120},{128,152},{160,184},{192,216},{224... | collective-permute-start | bytes 147464 | tf_op jit(solution)/shard_map/ppermute | solution.py:70
  49.6 3.4 %collective-permute-start.12 = (f32[4,1,2,8,192]{4,3,2,1,0:T(8,128)S(1)}, f32[4,1,2,8,192]{4,3,2,1,0:T(8,128)S(1)}, u32[]{:S(2)}, u32[]{:S(2)}) collective-permute-start(f32[4,1,2,8,192]{4,3,2,1,0:T(8,128)S(1)} %get-tuple-element.80), channel_id=1, source_target_pairs={{0,8},{32,0},{64,72},{96,64},{128,136},{160,128},{192,200},{224,19... | collective-permute-start | bytes 147464 | tf_op jit(solution)/shard_map/ppermute | solution.py:70
  51.2 1.9 %collective-permute-start.13 = (f32[4,1,2,8,192]{4,3,2,1,0:T(8,128)S(1)}, f32[4,1,2,8,192]{4,3,2,1,0:T(8,128)S(1)}, u32[]{:S(2)}, u32[]{:S(2)}) collective-permute-start(f32[4,1,2,8,192]{4,3,2,1,0:T(8,128)S(1)} %get-tuple-element.81), channel_id=1, source_target_pairs={{8,0},{0,32},{72,64},{64,96},{136,128},{128,160},{200,192},{192,22... | collective-permute-start | bytes 147464 | tf_op jit(solution)/shard_map/ppermute | solution.py:70
  53.1 7.6 %copy-start = (f32[192,128]{1,0:T(8,128)S(1)}, f32[192,128]{1,0:T(8,128)}, u32[]{:S(2)}) copy-start(f32[192,128]{1,0:T(8,128)} %wm_ref.5) | copy-start | bytes 294916
  53.2 10.1 %collective-permute-start.16 = (f32[4,4,8,192]{3,2,1,0:T(8,128)S(1)}, f32[4,4,8,192]{3,2,1,0:T(8,128)S(1)}, u32[]{:S(2)}, u32[]{:S(2)}) collective-permute-start(f32[4,4,8,192]{3,2,1,0:T(8,128)S(1)} %get-tuple-element.67), channel_id=1, source_target_pairs={{32,0},{1,32},{33,1},{2,33},{34,2},{3,34},{35,3},{0,35},{40,8},{9,... | collective-permute-start | bytes 294920 | tf_op jit(solution)/shard_map/ppermute | solution.py:70
  55.6 5.1 %copy-start.6 = (f32[128]{0:T(128)S(1)}, f32[128]{0:T(128)}, u32[]{:S(2)}) copy-start(f32[128]{0:T(128)} %param.25) | copy-start | bytes 1540
  55.6 7.7 %collective-permute-start.15 = (f32[4,4,8,192]{3,2,1,0:T(8,128)S(1)}, f32[4,4,8,192]{3,2,1,0:T(8,128)S(1)}, u32[]{:S(2)}, u32[]{:S(2)}) collective-permute-start(f32[4,4,8,192]{3,2,1,0:T(8,128)S(1)} %get-tuple-element.68), channel_id=1, source_target_pairs={{0,32},{32,1},{1,33},{33,2},{2,34},{34,3},{3,35},{35,0},{8,40},{40... | collective-permute-start | bytes 294920 | tf_op jit(solution)/shard_map/ppermute | solution.py:70
  65.0 5.2 %collective-permute-start.17 = (f32[4,4,8,192]{3,2,1,0:T(8,128)S(1)}, f32[4,4,8,192]{3,2,1,0:T(8,128)S(1)}, u32[]{:S(2)}, u32[]{:S(2)}) collective-permute-start(f32[4,4,8,192]{3,2,1,0:T(8,128)S(1)} %bitcast.54), channel_id=1, source_target_pairs={{0,32},{32,1},{1,33},{33,2},{2,34},{34,3},{3,35},{35,0},{8,40},{40... | collective-permute-start | bytes 294920 | tf_op jit(solution)/shard_map/ppermute | solution.py:70
  68.0 5.6 %collective-permute-start.18 = (f32[4,4,8,192]{3,2,1,0:T(8,128)S(1)}, f32[4,4,8,192]{3,2,1,0:T(8,128)S(1)}, u32[]{:S(2)}, u32[]{:S(2)}) collective-permute-start(f32[4,4,8,192]{3,2,1,0:T(8,128)S(1)} %bitcast.53), channel_id=1, source_target_pairs={{32,0},{1,32},{33,1},{2,33},{34,2},{3,34},{35,3},{0,35},{40,8},{9,... | collective-permute-start | bytes 294920 | tf_op jit(solution)/shard_map/ppermute | solution.py:70
  73.7 6.2 %collective-permute-start.21 = (f32[4,1,2,8,192]{4,3,2,1,0:T(8,128)S(1)}, f32[4,1,2,8,192]{4,3,2,1,0:T(8,128)S(1)}, u32[]{:S(2)}, u32[]{:S(2)}) collective-permute-start(f32[4,1,2,8,192]{4,3,2,1,0:T(8,128)S(1)} %get-tuple-element.64), channel_id=1, source_target_pairs={{0,24},{32,56},{64,88},{96,120},{128,152},{160,184},{192,216},{224... | collective-permute-start | bytes 147464 | tf_op jit(solution)/shard_map/ppermute | solution.py:70
  77.4 3.1 %collective-permute-start.19 = (f32[4,1,2,8,192]{4,3,2,1,0:T(8,128)S(1)}, f32[4,1,2,8,192]{4,3,2,1,0:T(8,128)S(1)}, u32[]{:S(2)}, u32[]{:S(2)}) collective-permute-start(f32[4,1,2,8,192]{4,3,2,1,0:T(8,128)S(1)} %get-tuple-element.65), channel_id=1, source_target_pairs={{0,8},{32,0},{64,72},{96,64},{128,136},{160,128},{192,200},{224,19... | collective-permute-start | bytes 147464 | tf_op jit(solution)/shard_map/ppermute | solution.py:70
  77.4 3.1 %collective-permute-start.20 = (f32[4,1,2,8,192]{4,3,2,1,0:T(8,128)S(1)}, f32[4,1,2,8,192]{4,3,2,1,0:T(8,128)S(1)}, u32[]{:S(2)}, u32[]{:S(2)}) collective-permute-start(f32[4,1,2,8,192]{4,3,2,1,0:T(8,128)S(1)} %get-tuple-element.66), channel_id=1, source_target_pairs={{8,0},{0,32},{72,64},{64,96},{136,128},{128,160},{200,192},{192,22... | collective-permute-start | bytes 147464 | tf_op jit(solution)/shard_map/ppermute | solution.py:70
  80.6 2.4 %collective-permute-start.24 = (f32[1,2,2,8,192]{4,3,2,1,0:T(8,128)S(1)}, f32[1,2,2,8,192]{4,3,2,1,0:T(8,128)S(1)}, u32[]{:S(2)}, u32[]{:S(2)}) collective-permute-start(f32[1,2,2,8,192]{4,3,2,1,0:T(8,128)S(1)} %get-tuple-element.76), channel_id=1, source_target_pairs={{0,452},{32,484},{452,0},{484,32},{8,460},{40,492},{460,8},{492,40... | collective-permute-start | bytes 73736 | tf_op jit(solution)/shard_map/ppermute | solution.py:70
  81.3 2.8 %collective-permute-start.22 = (f32[1,2,2,8,192]{4,3,2,1,0:T(8,128)S(1)}, f32[1,2,2,8,192]{4,3,2,1,0:T(8,128)S(1)}, u32[]{:S(2)}, u32[]{:S(2)}) collective-permute-start(f32[1,2,2,8,192]{4,3,2,1,0:T(8,128)S(1)} %get-tuple-element.77), channel_id=1, source_target_pairs={{0,64},{32,0},{64,128},{96,32},{128,192},{160,96},{192,256},{224,1... | collective-permute-start | bytes 73736 | tf_op jit(solution)/shard_map/ppermute | solution.py:70
  83.0 4.4 %collective-permute-start.23 = (f32[1,2,2,8,192]{4,3,2,1,0:T(8,128)S(1)}, f32[1,2,2,8,192]{4,3,2,1,0:T(8,128)S(1)}, u32[]{:S(2)}, u32[]{:S(2)}) collective-permute-start(f32[1,2,2,8,192]{4,3,2,1,0:T(8,128)S(1)} %get-tuple-element.78), channel_id=1, source_target_pairs={{64,0},{0,32},{128,64},{32,96},{192,128},{96,160},{256,192},{160,2... | collective-permute-start | bytes 73736 | tf_op jit(solution)/shard_map/ppermute | solution.py:70
  88.4 1.3 %collective-permute-start.25 = (f32[4,4,8,128]{3,2,1,0:T(8,128)S(1)}, f32[4,4,8,128]{3,2,1,0:T(8,128)S(1)}, u32[]{:S(2)}, u32[]{:S(2)}) collective-permute-start(f32[4,4,8,128]{3,2,1,0:T(8,128)S(1)} %bitcast.56), channel_id=1, source_target_pairs={{0,32},{32,1},{1,33},{33,2},{2,34},{34,3},{3,35},{35,0},{8,40},{40... | collective-permute-start | bytes 196616 | tf_op jit(solution)/shard_map/ppermute | solution.py:70
  88.4 4.9 %collective-permute-start.26 = (f32[4,4,8,128]{3,2,1,0:T(8,128)S(1)}, f32[4,4,8,128]{3,2,1,0:T(8,128)S(1)}, u32[]{:S(2)}, u32[]{:S(2)}) collective-permute-start(f32[4,4,8,128]{3,2,1,0:T(8,128)S(1)} %bitcast.55), channel_id=1, source_target_pairs={{32,0},{1,32},{33,1},{2,33},{34,2},{3,34},{35,3},{0,35},{40,8},{9,... | collective-permute-start | bytes 196616 | tf_op jit(solution)/shard_map/ppermute | solution.py:70
  93.4 5.9 %collective-permute-start.29 = (f32[4,1,2,8,128]{4,3,2,1,0:T(8,128)S(1)}, f32[4,1,2,8,128]{4,3,2,1,0:T(8,128)S(1)}, u32[]{:S(2)}, u32[]{:S(2)}) collective-permute-start(f32[4,1,2,8,128]{4,3,2,1,0:T(8,128)S(1)} %get-tuple-element.73), channel_id=1, source_target_pairs={{0,24},{32,56},{64,88},{96,120},{128,152},{160,184},{192,216},{224... | collective-permute-start | bytes 98312 | tf_op jit(solution)/shard_map/ppermute | solution.py:70
  96.2 3.1 %collective-permute-start.27 = (f32[4,1,2,8,128]{4,3,2,1,0:T(8,128)S(1)}, f32[4,1,2,8,128]{4,3,2,1,0:T(8,128)S(1)}, u32[]{:S(2)}, u32[]{:S(2)}) collective-permute-start(f32[4,1,2,8,128]{4,3,2,1,0:T(8,128)S(1)} %get-tuple-element.74), channel_id=1, source_target_pairs={{0,8},{32,0},{64,72},{96,64},{128,136},{160,128},{192,200},{224,19... | collective-permute-start | bytes 98312 | tf_op jit(solution)/shard_map/ppermute | solution.py:70
  96.2 3.0 %collective-permute-start.28 = (f32[4,1,2,8,128]{4,3,2,1,0:T(8,128)S(1)}, f32[4,1,2,8,128]{4,3,2,1,0:T(8,128)S(1)}, u32[]{:S(2)}, u32[]{:S(2)}) collective-permute-start(f32[4,1,2,8,128]{4,3,2,1,0:T(8,128)S(1)} %get-tuple-element.75), channel_id=1, source_target_pairs={{8,0},{0,32},{72,64},{64,96},{136,128},{128,160},{200,192},{192,22... | collective-permute-start | bytes 98312 | tf_op jit(solution)/shard_map/ppermute | solution.py:70
  99.3 3.2 %collective-permute-start.32 = (f32[1,2,2,8,128]{4,3,2,1,0:T(8,128)S(1)}, f32[1,2,2,8,128]{4,3,2,1,0:T(8,128)S(1)}, u32[]{:S(2)}, u32[]{:S(2)}) collective-permute-start(f32[1,2,2,8,128]{4,3,2,1,0:T(8,128)S(1)} %get-tuple-element.92), channel_id=1, source_target_pairs={{0,452},{32,484},{452,0},{484,32},{8,460},{40,492},{460,8},{492,40... | collective-permute-start | bytes 49160 | tf_op jit(solution)/shard_map/ppermute | solution.py:70
  100.0 3.4 %collective-permute-start.30 = (f32[1,2,2,8,128]{4,3,2,1,0:T(8,128)S(1)}, f32[1,2,2,8,128]{4,3,2,1,0:T(8,128)S(1)}, u32[]{:S(2)}, u32[]{:S(2)}) collective-permute-start(f32[1,2,2,8,128]{4,3,2,1,0:T(8,128)S(1)} %get-tuple-element.93), channel_id=1, source_target_pairs={{0,64},{32,0},{64,128},{96,32},{128,192},{160,96},{192,256},{224,1... | collective-permute-start | bytes 49160 | tf_op jit(solution)/shard_map/ppermute | solution.py:70
  102.5 4.8 %collective-permute-start.31 = (f32[1,2,2,8,128]{4,3,2,1,0:T(8,128)S(1)}, f32[1,2,2,8,128]{4,3,2,1,0:T(8,128)S(1)}, u32[]{:S(2)}, u32[]{:S(2)}) collective-permute-start(f32[1,2,2,8,128]{4,3,2,1,0:T(8,128)S(1)} %get-tuple-element.94), channel_id=1, source_target_pairs={{64,0},{0,32},{128,64},{32,96},{192,128},{96,160},{256,192},{160,2... | collective-permute-start | bytes 49160 | tf_op jit(solution)/shard_map/ppermute | solution.py:70
  107.5 9.8 %collective-permute-start.33 = (f32[16,128]{1,0:T(8,128)S(1)}, f32[16,128]{1,0:T(8,128)S(1)}, u32[]{:S(2)}, u32[]{:S(2)}) collective-permute-start(f32[16,128]{1,0:T(8,128)S(1)} %k_force.1), channel_id=1, source_target_pairs={{0,0},{32,1},{1,2},{33,3},{2,4},{34,5},{3,6},{35,7},{8,8},{40,9},{... | collective-permute-start | bytes 24584 | tf_op jit(solution)/shard_map/ppermute | solution.py:70

commit v7 on v6

--- a/solution.py
+++ b/solution.py
@@ -86,14 +86,16 @@
     return before, after
 
 
-def spread(low, high, here):
+def spread(low, high, here, first, second):
     before, after = swap(0, low, high, here)
     cells = jnp.concatenate([before, low, high, after], axis=0)
+    cells, first = lax.optimization_barrier((cells, first))
     before, after = swap(1, cells[:, 0:1], cells[:, 1:2], here)
     cells = jnp.concatenate([before, cells, after], axis=1)
+    cells, second = lax.optimization_barrier((cells, second))
     before = send(cells[:, :, 1], UP)
     after = send(cells[:, :, 0], DOWN)
-    return before, after, cells
+    return (before, after, cells), first, second
 
 
 def collect(before, after, cells, here, beside):
@@ -330,17 +332,20 @@
     av_ref[...] = av
 
 
-def k_own_env(packed_ref, scal_ref, pre_ref, av_ref, wb_ref, wav_ref, wm_ref, ei_ref, ej_ref, lat_ref, hid_ref, tan_ref, nav_ref):
-    packed = packed_ref[...]
-    scal = scal_ref[...]
-    unit, radius, inv, cut, slope = scal[0:3], scal[3:4], scal[4:5], scal[5:6], scal[6:7]
-    av = av_ref[...]
-    a = av[:CHAN]
+def k_own_env(packed_ref, scal_ref, av_ref, ei_ref, ej_ref):
+    packed = packed_ref[...]
+    unit = scal_ref[0:3]
+    a = av_ref[:CHAN]
     terms = jnp.concatenate([unit[k : k + 1] * a for k in range(3)], axis=0)
     at_center = match(centers_of(packed), ATOMS)
     env = put(terms, at_center)
     ei_ref[...] = pick(env, at_center)
     ej_ref[...] = pick(env, match(partners_of(packed), ATOMS))
+
+
+def k_tangent(scal_ref, pre_ref, wb_ref, wav_ref, wm_ref, lat_ref, hid_ref, tan_ref, nav_ref):
+    scal = scal_ref[...]
+    radius, inv, cut, slope = scal[3:4], scal[4:5], scal[5:6], scal[6:7]
     pre = pre_ref[...]
     gate = jax.nn.sigmoid(pre)
     act = pre * gate
@@ -550,7 +555,8 @@
     low, high, column = call(k_lists, [(32, 128), (32, 128), (LIST, 8)], packed)
     (part,) = call(k_own_pairs, [(8, PAIRS)], packed)
     low, high = low.reshape(1, 2, 2, 8, 128), high.reshape(1, 2, 2, 8, 128)
-    ghosts = [g.reshape(-1, 128) for g in spread(low, high, here)]
+    ghosts, part, _ = spread(low, high, here, part, ())
+    ghosts = [g.reshape(-1, 128) for g in ghosts]
     low, high, scal, pre, av = call(
         k_features,
         [(32, 192), (32, 192), (8, PAIRS), (128, PAIRS), (128, PAIRS)],
@@ -561,19 +567,11 @@
         wb,
         wav,
     )
-    ei, ej, latent, hid, tangent, nav = call(
-        k_own_env,
-        [(192, PAIRS), (192, PAIRS)] + [(128, PAIRS)] * 4,
-        packed,
-        scal,
-        pre,
-        av,
-        wb,
-        wav,
-        w_mix,
-    )
+    own = call(k_own_env, [(192, PAIRS), (192, PAIRS)], packed, scal, av)
+    rest = call(k_tangent, [(128, PAIRS)] * 4, scal, pre, wb, wav, w_mix)
     low, high = low.reshape(1, 2, 2, 8, 192), high.reshape(1, 2, 2, 8, 192)
-    ghosts = [g.reshape(-1, 192) for g in spread(low, high, here)]
+    ghosts, (ei, ej), (latent, hid, tangent, nav) = spread(low, high, here, own, rest)
+    ghosts = [g.reshape(-1, 192) for g in ghosts]
     before, after, cells, ej, h, tbar = call(
         k_energy,
         [(128, 192), (128, 192), (256, 192), (192, PAIRS), (128, PAIRS), (CHAN, PAIRS)],

time: 119 us -> 120 us (level)
  local copies, waits for them, and re-layouts: 1.66 us -> 4.19 us
    unnamed x16 -> x28, local copies, waits for them, and re-layouts: 1.47 us -> 3.33 us
    pallas_call x10 -> x11, Pallas kernels: 10.5 us -> 10.8 us  [call(): pl.pallas_call(kernel, out_shape=shapes, in_specs=[spec] * len(args), out...]
  transfers between devices with their start and end apart: 34 -> 34, of which waited for: 17 -> 16; matrix products, arithmetic and copies ran while one was open for 0% -> 0% of each run, Pallas kernels for 5% -> 5%
where the time goes in v7:
time: 120 us
  starting transfers between devices  61.2 us (51%)
  waiting for transfers between devices  40.5 us (34%)
  Pallas kernels  12.2 us (10%)
  local copies, waits for them, and re-layouts  4.19 us (3%)
    ppermute x34, starting transfers between devices, send(): return lax.ppermute(x, AXES, pairs)  61.2 us
    ppermute x34, waiting for transfers between devices, send(): return lax.ppermute(x, AXES, pairs)  40.5 us
    pallas_call x11, Pallas kernels, call(): pl.pallas_call(kernel, out_shape=shapes, in_specs=[spec] * len(args), out...  10.8 us
    unnamed x28, local copies, waits for them, and re-layouts  3.33 us
  transfers between devices with their start and end apart: 34, of which 16 were waited for; matrix products, arithmetic and copies ran while one was open for 0% of the time, Pallas kernels for 5%

profile of v7, /device:TPU:71, one launch (start us, length us, event | category | flops | bytes accessed | tf_op | source)
XLA Modules:
  0.0 119.6 jit_solution(9040390390092771956)
XLA Ops:
  0.6 1.5 %k_pack.1 = f32[48,128]{1,0:T(8,128)} custom-call(f32[3,1,1,1,512]{4,3,2,1,0:T(1,128)} %pos_in.1, s32[1,1,1,512]{3,2,1,0:T(1,128)} %kind_in.1, s32[2,2,2,8]{3,2,1,0:T(2,128)} %names_in.1, s32[1,1,1,8,128]{4,3,2,1,0:T(8,128)} %center_in.1, s32[1,1,1,8,128]{4,3,2,1,0:T(8,128)} %partner_in.1, s32[1,1,1,8,128]{4,3,2,1,0:T(8,128)} %live_in.1), custom_call_target="tpu_custom_call" | custom-call | tf_op jit(solution)/shard_map/k_pack/pallas_call | solution.py:255
  2.1 8.3 %collective-permute-start = (f32[48,128]{1,0:T(8,128)}, f32[48,128]{1,0:T(8,128)S(1)}, u32[]{:S(2)}, u32[]{:S(2)}) collective-permute-start(f32[48,128]{1,0:T(8,128)} %k_pack.1), channel_id=1, source_target_pairs={{0,0},{1,32},{2,1},{3,33},{4,2},{5,34},{6,3},{7,35},{8,8},{9,40},{... | collective-permute-start | bytes 73736 | tf_op jit(solution)/shard_map/ppermute | solution.py:70
  10.5 7.4 %collective-permute-done.packed_ref = f32[48,128]{1,0:T(8,128)S(1)} collective-permute-done((f32[48,128]{1,0:T(8,128)}, f32[48,128]{1,0:T(8,128)S(1)}, u32[]{:S(2)}, u32[]{:S(2)}) %collective-permute-start) | collective-permute-done | bytes 24608 | tf_op jit(solution)/shard_map/ppermute | solution.py:70
  18.2 0.7 collective-permute-start.3
  18.9 1.5 %collective-permute-start.1 = (f32[1,2,2,8,128]{4,3,2,1,0:T(8,128)S(1)}, f32[1,2,2,8,128]{4,3,2,1,0:T(8,128)S(1)}, u32[]{:S(2)}, u32[]{:S(2)}) collective-permute-start(f32[1,2,2,8,128]{4,3,2,1,0:T(8,128)S(1)} %get-tuple-element.127), channel_id=1, source_target_pairs={{0,64},{32,0},{64,128},{96,32},{128,192},{160,96},{192,256},{224,1... | collective-permute-start | bytes 49160 | tf_op jit(solution)/shard_map/ppermute | solution.py:70
  20.7 0.7 collective-permute-done.2
  21.5 4.6 %collective-permute-start.6 = (f32[4,1,2,8,128]{4,3,2,1,0:T(8,128)S(1)}, f32[4,1,2,8,128]{4,3,2,1,0:T(8,128)S(1)}, u32[]{:S(2)}, u32[]{:S(2)}) collective-permute-start(f32[4,1,2,8,128]{4,3,2,1,0:T(8,128)S(1)} %get-tuple-element.118), channel_id=1, source_target_pairs={{0,24},{32,56},{64,88},{96,120},{128,152},{160,184},{192,216},{224... | collective-permute-start | bytes 98312 | tf_op jit(solution)/shard_map/ppermute | solution.py:70
  26.2 3.8 %collective-permute-start.4 = (f32[4,1,2,8,128]{4,3,2,1,0:T(8,128)S(1)}, f32[4,1,2,8,128]{4,3,2,1,0:T(8,128)S(1)}, u32[]{:S(2)}, u32[]{:S(2)}) collective-permute-start(f32[4,1,2,8,128]{4,3,2,1,0:T(8,128)S(1)} %get-tuple-element.119), channel_id=1, source_target_pairs={{0,8},{32,0},{64,72},{96,64},{128,136},{160,128},{192,200},{224,19... | collective-permute-start | bytes 98312 | tf_op jit(solution)/shard_map/ppermute | solution.py:70
  30.1 0.7 copy-done.8
  31.6 2.4 %collective-permute-start.8 = (f32[4,4,8,128]{3,2,1,0:T(8,128)S(1)}, f32[4,4,8,128]{3,2,1,0:T(8,128)S(1)}, u32[]{:S(2)}, u32[]{:S(2)}) collective-permute-start(f32[4,4,8,128]{3,2,1,0:T(8,128)S(1)} %get-tuple-element.102), channel_id=1, source_target_pairs={{32,0},{1,32},{33,1},{2,33},{34,2},{3,34},{35,3},{0,35},{40,8},{9,... | collective-permute-start | bytes 196616 | tf_op jit(solution)/shard_map/ppermute | solution.py:70
  34.0 5.9 %collective-permute-start.7 = (f32[4,4,8,128]{3,2,1,0:T(8,128)S(1)}, f32[4,4,8,128]{3,2,1,0:T(8,128)S(1)}, u32[]{:S(2)}, u32[]{:S(2)}) collective-permute-start(f32[4,4,8,128]{3,2,1,0:T(8,128)S(1)} %get-tuple-element.103), channel_id=1, source_target_pairs={{0,32},{32,1},{1,33},{33,2},{2,34},{34,3},{3,35},{35,0},{8,40},{40... | collective-permute-start | bytes 196616 | tf_op jit(solution)/shard_map/ppermute | solution.py:70
  39.9 1.8 %collective-permute-done.8 = f32[4,4,8,128]{3,2,1,0:T(8,128)S(1)} collective-permute-done((f32[4,4,8,128]{3,2,1,0:T(8,128)S(1)}, f32[4,4,8,128]{3,2,1,0:T(8,128)S(1)}, u32[]{:S(2)}, u32[]{:S(2)}) %collective-permute-start.8) | collective-permute-done | bytes 65568 | tf_op jit(solution)/shard_map/ppermute | solution.py:70
  41.8 1.2 %k_features.1 = (f32[32,192]{1,0:T(8,128)S(1)}, f32[32,192]{1,0:T(8,128)S(1)}, f32[8,1024]{1,0:T(8,128)S(1)}, f32[128,1024]{1,0:T(8,128)S(1)}, f32[128,1024]{1,0:T(8,128)S(1)}) custom-call(f32[48,128]{1,0:T(8,128)S(1)} %collective-permute-done.packed_ref, f32[8,1024]{1,0:T(8,128)S(1)} %k_own_pairs.1.part_ref, f32[128,128]{1,0:T(8,128)S(1)} %bitcast.44, ...), custom_call_target="tpu_custom_call" | custom-call | tf_op jit(solution)/shard_map/k_features/pallas_call | solution.py:522
  43.0 0.7 collective-permute-start.11
  43.7 1.8 %collective-permute-start.9 = (f32[1,2,2,8,192]{4,3,2,1,0:T(8,128)S(1)}, f32[1,2,2,8,192]{4,3,2,1,0:T(8,128)S(1)}, u32[]{:S(2)}, u32[]{:S(2)}) collective-permute-start(f32[1,2,2,8,192]{4,3,2,1,0:T(8,128)S(1)} %get-tuple-element.117), channel_id=1, source_target_pairs={{0,64},{32,0},{64,128},{96,32},{128,192},{160,96},{192,256},{224,1... | collective-permute-start | bytes 73736 | tf_op jit(solution)/shard_map/ppermute | solution.py:70
  45.5 1.6 %k_own_env.1 = (f32[192,1024]{1,0:T(8,128)S(1)}, f32[192,1024]{1,0:T(8,128)S(1)}) custom-call(f32[48,128]{1,0:T(8,128)S(1)} %collective-permute-done.packed_ref, f32[8,1024]{1,0:T(8,128)S(1)} %get-tuple-element.48.scal_ref, f32[128,1024]{1,0:T(8,128)S(1)} %get-tuple-element.49.av_ref), custom_call_target="tpu_custom_call" | custom-call | tf_op jit(solution)/shard_map/k_own_env/pallas_call | solution.py:522
  47.2 2.8 %collective-permute-start.14 = (f32[4,1,2,8,192]{4,3,2,1,0:T(8,128)S(1)}, f32[4,1,2,8,192]{4,3,2,1,0:T(8,128)S(1)}, u32[]{:S(2)}, u32[]{:S(2)}) collective-permute-start(f32[4,1,2,8,192]{4,3,2,1,0:T(8,128)S(1)} %get-tuple-element.99), channel_id=1, source_target_pairs={{0,24},{32,56},{64,88},{96,120},{128,152},{160,184},{192,216},{224... | collective-permute-start | bytes 147464 | tf_op jit(solution)/shard_map/ppermute | solution.py:70
  50.0 1.2 %collective-permute-start.12 = (f32[4,1,2,8,192]{4,3,2,1,0:T(8,128)S(1)}, f32[4,1,2,8,192]{4,3,2,1,0:T(8,128)S(1)}, u32[]{:S(2)}, u32[]{:S(2)}) collective-permute-start(f32[4,1,2,8,192]{4,3,2,1,0:T(8,128)S(1)} %get-tuple-element.100), channel_id=1, source_target_pairs={{0,8},{32,0},{64,72},{96,64},{128,136},{160,128},{192,200},{224,19... | collective-permute-start | bytes 147464 | tf_op jit(solution)/shard_map/ppermute | solution.py:70
  51.4 0.9 k_tangent.1
  52.3 0.8 copy-done.5
  53.5 0.7 slice_bitcast_fusion
  54.2 2.0 %collective-permute-start.16 = (f32[4,4,8,192]{3,2,1,0:T(8,128)}, f32[4,4,8,192]{3,2,1,0:T(8,128)S(1)}, u32[]{:S(2)}, u32[]{:S(2)}) collective-permute-start(f32[4,4,8,192]{3,2,1,0:T(8,128)} %get-tuple-element.87), channel_id=1, source_target_pairs={{32,0},{1,32},{33,1},{2,33},{34,2},{3,34},{35,3},{0,35},{40,8},{9,... | collective-permute-start | bytes 294920 | tf_op jit(solution)/shard_map/ppermute | solution.py:70
  56.2 5.0 %collective-permute-start.15 = (f32[4,4,8,192]{3,2,1,0:T(8,128)S(1)}, f32[4,4,8,192]{3,2,1,0:T(8,128)S(1)}, u32[]{:S(2)}, u32[]{:S(2)}) collective-permute-start(f32[4,4,8,192]{3,2,1,0:T(8,128)S(1)} %get-tuple-element.88), channel_id=1, source_target_pairs={{0,32},{32,1},{1,33},{33,2},{2,34},{34,3},{3,35},{35,0},{8,40},{40... | collective-permute-start | bytes 294920 | tf_op jit(solution)/shard_map/ppermute | solution.py:70
  61.4 2.7 %collective-permute-done.16 = f32[4,4,8,192]{3,2,1,0:T(8,128)S(1)} collective-permute-done((f32[4,4,8,192]{3,2,1,0:T(8,128)}, f32[4,4,8,192]{3,2,1,0:T(8,128)S(1)}, u32[]{:S(2)}, u32[]{:S(2)}) %collective-permute-start.16) | collective-permute-done | bytes 98336 | tf_op jit(solution)/shard_map/ppermute | solution.py:70
  64.1 1.0 copy-done.6
  65.1 1.8 %k_energy.1 = (f32[128,192]{1,0:T(8,128)S(1)}, f32[128,192]{1,0:T(8,128)S(1)}, f32[256,192]{1,0:T(8,128)S(1)}, f32[192,1024]{1,0:T(8,128)S(1)}, f32[128,1024]{1,0:T(8,128)S(1)}, /*index=5*/f32[64,1024]{1,0:T(8,128)S(1)}) custom-call(f32[48,128]{1,0:T(8,128)S(1)} %collective-permute-done.packed_ref, f32[8,1024]{1,0:T(8,128)S(1)} %get-tuple-element.48.scal_ref, ...), custom_call_target="tpu_custom_call" | custom-call | tf_op jit(solution)/shard_map/k_energy/pallas_call | solution.py:522
  66.9 2.8 %collective-permute-start.17 = (f32[4,4,8,192]{3,2,1,0:T(8,128)S(1)}, f32[4,4,8,192]{3,2,1,0:T(8,128)S(1)}, u32[]{:S(2)}, u32[]{:S(2)}) collective-permute-start(f32[4,4,8,192]{3,2,1,0:T(8,128)S(1)} %bitcast.50), channel_id=1, source_target_pairs={{0,32},{32,1},{1,33},{33,2},{2,34},{34,3},{3,35},{35,0},{8,40},{40... | collective-permute-start | bytes 294920 | tf_op jit(solution)/shard_map/ppermute | solution.py:70
  69.7 2.2 %k_direct.1 = (f32[8,1024]{1,0:T(8,128)S(1)}, f32[4,512]{1,0:T(4,128)S(1)}) custom-call(f32[48,128]{1,0:T(8,128)S(1)} %collective-permute-done.packed_ref, f32[8,1024]{1,0:T(8,128)S(1)} %get-tuple-element.48.scal_ref, f32[128,1024]{1,0:T(8,128)S(1)} %get-tuple-element.49.av_ref, f32[128,1024]{1,0:T(8,128)S(1)} %get-tuple-element.60.nav_ref, ...), custom_call_target="tpu_custom_call" | custom-call | tf_op jit(solution)/shard_map/k_direct/pallas_call | solution.py:522
  71.9 3.3 %collective-permute-done.18 = f32[4,4,8,192]{3,2,1,0:T(8,128)S(1)} collective-permute-done((f32[4,4,8,192]{3,2,1,0:T(8,128)S(1)}, f32[4,4,8,192]{3,2,1,0:T(8,128)S(1)}, u32[]{:S(2)}, u32[]{:S(2)}) %collective-permute-start.18) | collective-permute-done | bytes 98336 | tf_op jit(solution)/shard_map/ppermute | solution.py:70
  75.3 3.7 %collective-permute-start.21 = (f32[4,1,2,8,192]{4,3,2,1,0:T(8,128)S(1)}, f32[4,1,2,8,192]{4,3,2,1,0:T(8,128)S(1)}, u32[]{:S(2)}, u32[]{:S(2)}) collective-permute-start(f32[4,1,2,8,192]{4,3,2,1,0:T(8,128)S(1)} %get-tuple-element.84), channel_id=1, source_target_pairs={{0,24},{32,56},{64,88},{96,120},{128,152},{160,184},{192,216},{224... | collective-permute-start | bytes 147464 | tf_op jit(solution)/shard_map/ppermute | solution.py:70
  79.1 1.5 %collective-permute-start.20 = (f32[4,1,2,8,192]{4,3,2,1,0:T(8,128)S(1)}, f32[4,1,2,8,192]{4,3,2,1,0:T(8,128)S(1)}, u32[]{:S(2)}, u32[]{:S(2)}) collective-permute-start(f32[4,1,2,8,192]{4,3,2,1,0:T(8,128)S(1)} %get-tuple-element.86), channel_id=1, source_target_pairs={{8,0},{0,32},{72,64},{64,96},{136,128},{128,160},{200,192},{192,22... | collective-permute-start | bytes 147464 | tf_op jit(solution)/shard_map/ppermute | solution.py:70
  80.5 1.0 collective-permute-done.21
  82.2 0.7 collective-permute-start.24
  82.9 1.8 %collective-permute-start.22 = (f32[1,2,2,8,192]{4,3,2,1,0:T(8,128)S(1)}, f32[1,2,2,8,192]{4,3,2,1,0:T(8,128)S(1)}, u32[]{:S(2)}, u32[]{:S(2)}) collective-permute-start(f32[1,2,2,8,192]{4,3,2,1,0:T(8,128)S(1)} %get-tuple-element.97), channel_id=1, source_target_pairs={{0,64},{32,0},{64,128},{96,32},{128,192},{160,96},{192,256},{224,1... | collective-permute-start | bytes 73736 | tf_op jit(solution)/shard_map/ppermute | solution.py:70
  84.7 1.0 collective-permute-done.22
  85.7 3.4 %collective-permute-done.23 = f32[1,2,2,8,192]{4,3,2,1,0:T(8,128)S(1)} collective-permute-done((f32[1,2,2,8,192]{4,3,2,1,0:T(8,128)S(1)}, f32[1,2,2,8,192]{4,3,2,1,0:T(8,128)S(1)}, u32[]{:S(2)}, u32[]{:S(2)}) %collective-permute-start.23) | collective-permute-done | bytes 24608 | tf_op jit(solution)/shard_map/ppermute | solution.py:70
  89.1 1.0 k_env_back.1
  90.6 0.6 k_own_force.1.own_ref
  91.4 3.6 %collective-permute-done.26 = f32[4,4,8,128]{3,2,1,0:T(8,128)S(1)} collective-permute-done((f32[4,4,8,128]{3,2,1,0:T(8,128)S(1)}, f32[4,4,8,128]{3,2,1,0:T(8,128)S(1)}, u32[]{:S(2)}, u32[]{:S(2)}) %collective-permute-start.26) | collective-permute-done | bytes 65568 | tf_op jit(solution)/shard_map/ppermute | solution.py:70
  95.1 2.8 %collective-permute-start.29 = (f32[4,1,2,8,128]{4,3,2,1,0:T(8,128)S(1)}, f32[4,1,2,8,128]{4,3,2,1,0:T(8,128)S(1)}, u32[]{:S(2)}, u32[]{:S(2)}) collective-permute-start(f32[4,1,2,8,128]{4,3,2,1,0:T(8,128)S(1)} %get-tuple-element.93), channel_id=1, source_target_pairs={{0,24},{32,56},{64,88},{96,120},{128,152},{160,184},{192,216},{224... | collective-permute-start | bytes 98312 | tf_op jit(solution)/shard_map/ppermute | solution.py:70
  97.9 1.5 %collective-permute-start.28 = (f32[4,1,2,8,128]{4,3,2,1,0:T(8,128)S(1)}, f32[4,1,2,8,128]{4,3,2,1,0:T(8,128)S(1)}, u32[]{:S(2)}, u32[]{:S(2)}) collective-permute-start(f32[4,1,2,8,128]{4,3,2,1,0:T(8,128)S(1)} %get-tuple-element.95), channel_id=1, source_target_pairs={{8,0},{0,32},{72,64},{64,96},{136,128},{128,160},{200,192},{192,22... | collective-permute-start | bytes 98312 | tf_op jit(solution)/shard_map/ppermute | solution.py:70
  99.3 1.6 %collective-permute-done.29 = f32[4,1,2,8,128]{4,3,2,1,0:T(8,128)S(1)} collective-permute-done((f32[4,1,2,8,128]{4,3,2,1,0:T(8,128)S(1)}, f32[4,1,2,8,128]{4,3,2,1,0:T(8,128)S(1)}, u32[]{:S(2)}, u32[]{:S(2)}) %collective-permute-start.29) | collective-permute-done | bytes 32800 | tf_op jit(solution)/shard_map/ppermute | solution.py:70
  101.0 0.7 collective-permute-start.32
  101.7 2.5 %collective-permute-start.30 = (f32[1,2,2,8,128]{4,3,2,1,0:T(8,128)S(1)}, f32[1,2,2,8,128]{4,3,2,1,0:T(8,128)S(1)}, u32[]{:S(2)}, u32[]{:S(2)}) collective-permute-start(f32[1,2,2,8,128]{4,3,2,1,0:T(8,128)S(1)} %get-tuple-element.113), channel_id=1, source_target_pairs={{0,64},{32,0},{64,128},{96,32},{128,192},{160,96},{192,256},{224,1... | collective-permute-start | bytes 49160 | tf_op jit(solution)/shard_map/ppermute | solution.py:70
  104.1 0.9 collective-permute-done.30
  105.0 4.0 %collective-permute-done.31 = f32[1,2,2,8,128]{4,3,2,1,0:T(8,128)S(1)} collective-permute-done((f32[1,2,2,8,128]{4,3,2,1,0:T(8,128)S(1)}, f32[1,2,2,8,128]{4,3,2,1,0:T(8,128)S(1)}, u32[]{:S(2)}, u32[]{:S(2)}) %collective-permute-start.31) | collective-permute-done | bytes 16416 | tf_op jit(solution)/shard_map/ppermute | solution.py:70
  109.2 1.9 %collective-permute-start.33 = (f32[16,128]{1,0:T(8,128)S(1)}, f32[16,128]{1,0:T(8,128)S(1)}, u32[]{:S(2)}, u32[]{:S(2)}) collective-permute-start(f32[16,128]{1,0:T(8,128)S(1)} %k_force.1), channel_id=1, source_target_pairs={{0,0},{32,1},{1,2},{33,3},{2,4},{34,5},{3,6},{35,7},{8,8},{40,9},{... | collective-permute-start | bytes 24584 | tf_op jit(solution)/shard_map/ppermute | solution.py:70
  111.2 7.9 %collective-permute-done.33.in_ref = f32[16,128]{1,0:T(8,128)S(1)} collective-permute-done((f32[16,128]{1,0:T(8,128)S(1)}, f32[16,128]{1,0:T(8,128)S(1)}, u32[]{:S(2)}, u32[]{:S(2)}) %collective-permute-start.33) | collective-permute-done | bytes 8224 | tf_op jit(solution)/shard_map/ppermute | solution.py:70
  (92 shorter events, 4.9 us)
Async XLA Ops:
  2.1 15.8 %collective-permute-start = (f32[48,128]{1,0:T(8,128)}, f32[48,128]{1,0:T(8,128)S(1)}, u32[]{:S(2)}, u32[]{:S(2)}) collective-permute-start(f32[48,128]{1,0:T(8,128)} %k_pack.1), channel_id=1, source_target_pairs={{0,0},{1,32},{2,1},{3,33},{4,2},{5,34},{6,3},{7,35},{8,8},{9,40},{... | collective-permute-start | bytes 73736 | tf_op jit(solution)/shard_map/ppermute | solution.py:70
  18.2 2.6 %collective-permute-start.3 = (f32[1,2,2,8,128]{4,3,2,1,0:T(8,128)S(1)}, f32[1,2,2,8,128]{4,3,2,1,0:T(8,128)S(1)}, u32[]{:S(2)}, u32[]{:S(2)}) collective-permute-start(f32[1,2,2,8,128]{4,3,2,1,0:T(8,128)S(1)} %get-tuple-element.125), channel_id=1, source_target_pairs={{0,452},{32,484},{452,0},{484,32},{8,460},{40,492},{460,8},{492,40... | collective-permute-start | bytes 49160 | tf_op jit(solution)/shard_map/ppermute | solution.py:70
  18.8 2.6 %collective-permute-start.2 = (f32[1,2,2,8,128]{4,3,2,1,0:T(8,128)S(1)}, f32[1,2,2,8,128]{4,3,2,1,0:T(8,128)S(1)}, u32[]{:S(2)}, u32[]{:S(2)}) collective-permute-start(f32[1,2,2,8,128]{4,3,2,1,0:T(8,128)S(1)} %get-tuple-element.126), channel_id=1, source_target_pairs={{64,0},{0,32},{128,64},{32,96},{192,128},{96,160},{256,192},{160,2... | collective-permute-start | bytes 49160 | tf_op jit(solution)/shard_map/ppermute | solution.py:70
  18.9 2.6 %collective-permute-start.1 = (f32[1,2,2,8,128]{4,3,2,1,0:T(8,128)S(1)}, f32[1,2,2,8,128]{4,3,2,1,0:T(8,128)S(1)}, u32[]{:S(2)}, u32[]{:S(2)}) collective-permute-start(f32[1,2,2,8,128]{4,3,2,1,0:T(8,128)S(1)} %get-tuple-element.127), channel_id=1, source_target_pairs={{0,64},{32,0},{64,128},{96,32},{128,192},{160,96},{192,256},{224,1... | collective-permute-start | bytes 49160 | tf_op jit(solution)/shard_map/ppermute | solution.py:70
  21.5 8.5 %copy-start.7 = (f32[128,64]{0,1:T(8,128)S(1)}, f32[128,64]{0,1:T(8,128)}, u32[]{:S(2)}) copy-start(f32[128,64]{0,1:T(8,128)} %param.22) | copy-start | bytes 98308
  21.5 10.0 %collective-permute-start.6 = (f32[4,1,2,8,128]{4,3,2,1,0:T(8,128)S(1)}, f32[4,1,2,8,128]{4,3,2,1,0:T(8,128)S(1)}, u32[]{:S(2)}, u32[]{:S(2)}) collective-permute-start(f32[4,1,2,8,128]{4,3,2,1,0:T(8,128)S(1)} %get-tuple-element.118), channel_id=1, source_target_pairs={{0,24},{32,56},{64,88},{96,120},{128,152},{160,184},{192,216},{224... | collective-permute-start | bytes 98312 | tf_op jit(solution)/shard_map/ppermute | solution.py:70
  26.2 5.3 %collective-permute-start.4 = (f32[4,1,2,8,128]{4,3,2,1,0:T(8,128)S(1)}, f32[4,1,2,8,128]{4,3,2,1,0:T(8,128)S(1)}, u32[]{:S(2)}, u32[]{:S(2)}) collective-permute-start(f32[4,1,2,8,128]{4,3,2,1,0:T(8,128)S(1)} %get-tuple-element.119), channel_id=1, source_target_pairs={{0,8},{32,0},{64,72},{96,64},{128,136},{160,128},{192,200},{224,19... | collective-permute-start | bytes 98312 | tf_op jit(solution)/shard_map/ppermute | solution.py:70
  30.0 1.5 %collective-permute-start.5 = (f32[4,1,2,8,128]{4,3,2,1,0:T(8,128)S(1)}, f32[4,1,2,8,128]{4,3,2,1,0:T(8,128)S(1)}, u32[]{:S(2)}, u32[]{:S(2)}) collective-permute-start(f32[4,1,2,8,128]{4,3,2,1,0:T(8,128)S(1)} %get-tuple-element.120), channel_id=1, source_target_pairs={{8,0},{0,32},{72,64},{64,96},{136,128},{128,160},{200,192},{192,22... | collective-permute-start | bytes 98312 | tf_op jit(solution)/shard_map/ppermute | solution.py:70
  30.0 0.8 copy-start.8
  30.7 0.7 copy-start.9
  30.7 0.7 copy-start.10
  30.7 0.7 copy-start.11
  31.6 10.2 %collective-permute-start.8 = (f32[4,4,8,128]{3,2,1,0:T(8,128)S(1)}, f32[4,4,8,128]{3,2,1,0:T(8,128)S(1)}, u32[]{:S(2)}, u32[]{:S(2)}) collective-permute-start(f32[4,4,8,128]{3,2,1,0:T(8,128)S(1)} %get-tuple-element.102), channel_id=1, source_target_pairs={{32,0},{1,32},{33,1},{2,33},{34,2},{3,34},{35,3},{0,35},{40,8},{9,... | collective-permute-start | bytes 196616 | tf_op jit(solution)/shard_map/ppermute | solution.py:70
  34.0 7.8 %collective-permute-start.7 = (f32[4,4,8,128]{3,2,1,0:T(8,128)S(1)}, f32[4,4,8,128]{3,2,1,0:T(8,128)S(1)}, u32[]{:S(2)}, u32[]{:S(2)}) collective-permute-start(f32[4,4,8,128]{3,2,1,0:T(8,128)S(1)} %get-tuple-element.103), channel_id=1, source_target_pairs={{0,32},{32,1},{1,33},{33,2},{2,34},{34,3},{3,35},{35,0},{8,40},{40... | collective-permute-start | bytes 196616 | tf_op jit(solution)/shard_map/ppermute | solution.py:70
  43.0 4.0 %collective-permute-start.11 = (f32[1,2,2,8,192]{4,3,2,1,0:T(8,128)S(1)}, f32[1,2,2,8,192]{4,3,2,1,0:T(8,128)S(1)}, u32[]{:S(2)}, u32[]{:S(2)}) collective-permute-start(f32[1,2,2,8,192]{4,3,2,1,0:T(8,128)S(1)} %get-tuple-element.115), channel_id=1, source_target_pairs={{0,452},{32,484},{452,0},{484,32},{8,460},{40,492},{460,8},{492,40... | collective-permute-start | bytes 73736 | tf_op jit(solution)/shard_map/ppermute | solution.py:70
  43.7 3.4 %collective-permute-start.10 = (f32[1,2,2,8,192]{4,3,2,1,0:T(8,128)S(1)}, f32[1,2,2,8,192]{4,3,2,1,0:T(8,128)S(1)}, u32[]{:S(2)}, u32[]{:S(2)}) collective-permute-start(f32[1,2,2,8,192]{4,3,2,1,0:T(8,128)S(1)} %get-tuple-element.116), channel_id=1, source_target_pairs={{64,0},{0,32},{128,64},{32,96},{192,128},{96,160},{256,192},{160,2... | collective-permute-start | bytes 73736 | tf_op jit(solution)/shard_map/ppermute | solution.py:70
  43.7 3.4 %collective-permute-start.9 = (f32[1,2,2,8,192]{4,3,2,1,0:T(8,128)S(1)}, f32[1,2,2,8,192]{4,3,2,1,0:T(8,128)S(1)}, u32[]{:S(2)}, u32[]{:S(2)}) collective-permute-start(f32[1,2,2,8,192]{4,3,2,1,0:T(8,128)S(1)} %get-tuple-element.117), channel_id=1, source_target_pairs={{0,64},{32,0},{64,128},{96,32},{128,192},{160,96},{192,256},{224,1... | collective-permute-start | bytes 73736 | tf_op jit(solution)/shard_map/ppermute | solution.py:70
  47.1 4.3 %copy-start = (f32[192,128]{1,0:T(8,128)S(1)}, f32[192,128]{1,0:T(8,128)}, u32[]{:S(2)}) copy-start(f32[192,128]{1,0:T(8,128)} %wm_ref.5) | copy-start | bytes 294916
  47.2 6.2 %collective-permute-start.14 = (f32[4,1,2,8,192]{4,3,2,1,0:T(8,128)S(1)}, f32[4,1,2,8,192]{4,3,2,1,0:T(8,128)S(1)}, u32[]{:S(2)}, u32[]{:S(2)}) collective-permute-start(f32[4,1,2,8,192]{4,3,2,1,0:T(8,128)S(1)} %get-tuple-element.99), channel_id=1, source_target_pairs={{0,24},{32,56},{64,88},{96,120},{128,152},{160,184},{192,216},{224... | collective-permute-start | bytes 147464 | tf_op jit(solution)/shard_map/ppermute | solution.py:70
  50.0 3.4 %collective-permute-start.12 = (f32[4,1,2,8,192]{4,3,2,1,0:T(8,128)S(1)}, f32[4,1,2,8,192]{4,3,2,1,0:T(8,128)S(1)}, u32[]{:S(2)}, u32[]{:S(2)}) collective-permute-start(f32[4,1,2,8,192]{4,3,2,1,0:T(8,128)S(1)} %get-tuple-element.100), channel_id=1, source_target_pairs={{0,8},{32,0},{64,72},{96,64},{128,136},{160,128},{192,200},{224,19... | collective-permute-start | bytes 147464 | tf_op jit(solution)/shard_map/ppermute | solution.py:70
  51.2 2.2 %collective-permute-start.13 = (f32[4,1,2,8,192]{4,3,2,1,0:T(8,128)S(1)}, f32[4,1,2,8,192]{4,3,2,1,0:T(8,128)S(1)}, u32[]{:S(2)}, u32[]{:S(2)}) collective-permute-start(f32[4,1,2,8,192]{4,3,2,1,0:T(8,128)S(1)} %get-tuple-element.101), channel_id=1, source_target_pairs={{8,0},{0,32},{72,64},{64,96},{136,128},{128,160},{200,192},{192,22... | collective-permute-start | bytes 147464 | tf_op jit(solution)/shard_map/ppermute | solution.py:70
  52.3 0.8 copy-start.5
  53.1 1.0 copy-start.1
  53.1 1.0 copy-start.3
  54.2 9.9 %collective-permute-start.16 = (f32[4,4,8,192]{3,2,1,0:T(8,128)}, f32[4,4,8,192]{3,2,1,0:T(8,128)S(1)}, u32[]{:S(2)}, u32[]{:S(2)}) collective-permute-start(f32[4,4,8,192]{3,2,1,0:T(8,128)} %get-tuple-element.87), channel_id=1, source_target_pairs={{32,0},{1,32},{33,1},{2,33},{34,2},{3,34},{35,3},{0,35},{40,8},{9,... | collective-permute-start | bytes 294920 | tf_op jit(solution)/shard_map/ppermute | solution.py:70
  56.2 5.0 %copy-start.12 = (f32[128]{0:T(128)S(1)}, f32[128]{0:T(128)}, u32[]{:S(2)}) copy-start(f32[128]{0:T(128)} %param.25) | copy-start | bytes 1540
  56.2 7.9 %collective-permute-start.15 = (f32[4,4,8,192]{3,2,1,0:T(8,128)S(1)}, f32[4,4,8,192]{3,2,1,0:T(8,128)S(1)}, u32[]{:S(2)}, u32[]{:S(2)}) collective-permute-start(f32[4,4,8,192]{3,2,1,0:T(8,128)S(1)} %get-tuple-element.88), channel_id=1, source_target_pairs={{0,32},{32,1},{1,33},{33,2},{2,34},{34,3},{3,35},{35,0},{8,40},{40... | collective-permute-start | bytes 294920 | tf_op jit(solution)/shard_map/ppermute | solution.py:70
  64.1 1.0 copy-start.6
  65.1 4.6 %copy-start.2 = (f32[128,1024]{1,0:T(8,128)S(1)}, f32[128,1024]{1,0:T(8,128)}, u32[]{:S(2)}) copy-start(f32[128,1024]{1,0:T(8,128)} %copy-done.1) | copy-start | bytes 1572868
  65.1 4.6 %copy-start.4 = (f32[128,1024]{1,0:T(8,128)S(1)}, f32[128,1024]{1,0:T(8,128)}, u32[]{:S(2)}) copy-start(f32[128,1024]{1,0:T(8,128)} %copy-done.3) | copy-start | bytes 1572868
  66.9 5.0 %collective-permute-start.17 = (f32[4,4,8,192]{3,2,1,0:T(8,128)S(1)}, f32[4,4,8,192]{3,2,1,0:T(8,128)S(1)}, u32[]{:S(2)}, u32[]{:S(2)}) collective-permute-start(f32[4,4,8,192]{3,2,1,0:T(8,128)S(1)} %bitcast.50), channel_id=1, source_target_pairs={{0,32},{32,1},{1,33},{33,2},{2,34},{34,3},{3,35},{35,0},{8,40},{40... | collective-permute-start | bytes 294920 | tf_op jit(solution)/shard_map/ppermute | solution.py:70
  69.7 5.6 %collective-permute-start.18 = (f32[4,4,8,192]{3,2,1,0:T(8,128)S(1)}, f32[4,4,8,192]{3,2,1,0:T(8,128)S(1)}, u32[]{:S(2)}, u32[]{:S(2)}) collective-permute-start(f32[4,4,8,192]{3,2,1,0:T(8,128)S(1)} %bitcast.49), channel_id=1, source_target_pairs={{32,0},{1,32},{33,1},{2,33},{34,2},{3,34},{35,3},{0,35},{40,8},{9,... | collective-permute-start | bytes 294920 | tf_op jit(solution)/shard_map/ppermute | solution.py:70
  75.3 6.2 %collective-permute-start.21 = (f32[4,1,2,8,192]{4,3,2,1,0:T(8,128)S(1)}, f32[4,1,2,8,192]{4,3,2,1,0:T(8,128)S(1)}, u32[]{:S(2)}, u32[]{:S(2)}) collective-permute-start(f32[4,1,2,8,192]{4,3,2,1,0:T(8,128)S(1)} %get-tuple-element.84), channel_id=1, source_target_pairs={{0,24},{32,56},{64,88},{96,120},{128,152},{160,184},{192,216},{224... | collective-permute-start | bytes 147464 | tf_op jit(solution)/shard_map/ppermute | solution.py:70
  79.0 3.1 %collective-permute-start.19 = (f32[4,1,2,8,192]{4,3,2,1,0:T(8,128)S(1)}, f32[4,1,2,8,192]{4,3,2,1,0:T(8,128)S(1)}, u32[]{:S(2)}, u32[]{:S(2)}) collective-permute-start(f32[4,1,2,8,192]{4,3,2,1,0:T(8,128)S(1)} %get-tuple-element.85), channel_id=1, source_target_pairs={{0,8},{32,0},{64,72},{96,64},{128,136},{160,128},{192,200},{224,19... | collective-permute-start | bytes 147464 | tf_op jit(solution)/shard_map/ppermute | solution.py:70
  79.1 3.1 %collective-permute-start.20 = (f32[4,1,2,8,192]{4,3,2,1,0:T(8,128)S(1)}, f32[4,1,2,8,192]{4,3,2,1,0:T(8,128)S(1)}, u32[]{:S(2)}, u32[]{:S(2)}) collective-permute-start(f32[4,1,2,8,192]{4,3,2,1,0:T(8,128)S(1)} %get-tuple-element.86), channel_id=1, source_target_pairs={{8,0},{0,32},{72,64},{64,96},{136,128},{128,160},{200,192},{192,22... | collective-permute-start | bytes 147464 | tf_op jit(solution)/shard_map/ppermute | solution.py:70
  82.2 2.4 %collective-permute-start.24 = (f32[1,2,2,8,192]{4,3,2,1,0:T(8,128)S(1)}, f32[1,2,2,8,192]{4,3,2,1,0:T(8,128)S(1)}, u32[]{:S(2)}, u32[]{:S(2)}) collective-permute-start(f32[1,2,2,8,192]{4,3,2,1,0:T(8,128)S(1)} %get-tuple-element.96), channel_id=1, source_target_pairs={{0,452},{32,484},{452,0},{484,32},{8,460},{40,492},{460,8},{492,40... | collective-permute-start | bytes 73736 | tf_op jit(solution)/shard_map/ppermute | solution.py:70
  82.9 2.8 %collective-permute-start.22 = (f32[1,2,2,8,192]{4,3,2,1,0:T(8,128)S(1)}, f32[1,2,2,8,192]{4,3,2,1,0:T(8,128)S(1)}, u32[]{:S(2)}, u32[]{:S(2)}) collective-permute-start(f32[1,2,2,8,192]{4,3,2,1,0:T(8,128)S(1)} %get-tuple-element.97), channel_id=1, source_target_pairs={{0,64},{32,0},{64,128},{96,32},{128,192},{160,96},{192,256},{224,1... | collective-permute-start | bytes 73736 | tf_op jit(solution)/shard_map/ppermute | solution.py:70
  84.7 4.4 %collective-permute-start.23 = (f32[1,2,2,8,192]{4,3,2,1,0:T(8,128)S(1)}, f32[1,2,2,8,192]{4,3,2,1,0:T(8,128)S(1)}, u32[]{:S(2)}, u32[]{:S(2)}) collective-permute-start(f32[1,2,2,8,192]{4,3,2,1,0:T(8,128)S(1)} %get-tuple-element.98), channel_id=1, source_target_pairs={{64,0},{0,32},{128,64},{32,96},{192,128},{96,160},{256,192},{160,2... | collective-permute-start | bytes 73736 | tf_op jit(solution)/shard_map/ppermute | solution.py:70
  90.1 1.3 %collective-permute-start.25 = (f32[4,4,8,128]{3,2,1,0:T(8,128)S(1)}, f32[4,4,8,128]{3,2,1,0:T(8,128)S(1)}, u32[]{:S(2)}, u32[]{:S(2)}) collective-permute-start(f32[4,4,8,128]{3,2,1,0:T(8,128)S(1)} %bitcast.52), channel_id=1, source_target_pairs={{0,32},{32,1},{1,33},{33,2},{2,34},{34,3},{3,35},{35,0},{8,40},{40... | collective-permute-start | bytes 196616 | tf_op jit(solution)/shard_map/ppermute | solution.py:70
  90.1 4.9 %collective-permute-start.26 = (f32[4,4,8,128]{3,2,1,0:T(8,128)S(1)}, f32[4,4,8,128]{3,2,1,0:T(8,128)S(1)}, u32[]{:S(2)}, u32[]{:S(2)}) collective-permute-start(f32[4,4,8,128]{3,2,1,0:T(8,128)S(1)} %bitcast.51), channel_id=1, source_target_pairs={{32,0},{1,32},{33,1},{2,33},{34,2},{3,34},{35,3},{0,35},{40,8},{9,... | collective-permute-start | bytes 196616 | tf_op jit(solution)/shard_map/ppermute | solution.py:70
  95.1 5.9 %collective-permute-start.29 = (f32[4,1,2,8,128]{4,3,2,1,0:T(8,128)S(1)}, f32[4,1,2,8,128]{4,3,2,1,0:T(8,128)S(1)}, u32[]{:S(2)}, u32[]{:S(2)}) collective-permute-start(f32[4,1,2,8,128]{4,3,2,1,0:T(8,128)S(1)} %get-tuple-element.93), channel_id=1, source_target_pairs={{0,24},{32,56},{64,88},{96,120},{128,152},{160,184},{192,216},{224... | collective-permute-start | bytes 98312 | tf_op jit(solution)/shard_map/ppermute | solution.py:70
  97.9 3.1 %collective-permute-start.27 = (f32[4,1,2,8,128]{4,3,2,1,0:T(8,128)S(1)}, f32[4,1,2,8,128]{4,3,2,1,0:T(8,128)S(1)}, u32[]{:S(2)}, u32[]{:S(2)}) collective-permute-start(f32[4,1,2,8,128]{4,3,2,1,0:T(8,128)S(1)} %get-tuple-element.94), channel_id=1, source_target_pairs={{0,8},{32,0},{64,72},{96,64},{128,136},{160,128},{192,200},{224,19... | collective-permute-start | bytes 98312 | tf_op jit(solution)/shard_map/ppermute | solution.py:70
  97.9 3.1 %collective-permute-start.28 = (f32[4,1,2,8,128]{4,3,2,1,0:T(8,128)S(1)}, f32[4,1,2,8,128]{4,3,2,1,0:T(8,128)S(1)}, u32[]{:S(2)}, u32[]{:S(2)}) collective-permute-start(f32[4,1,2,8,128]{4,3,2,1,0:T(8,128)S(1)} %get-tuple-element.95), channel_id=1, source_target_pairs={{8,0},{0,32},{72,64},{64,96},{136,128},{128,160},{200,192},{192,22... | collective-permute-start | bytes 98312 | tf_op jit(solution)/shard_map/ppermute | solution.py:70
  101.0 3.2 %collective-permute-start.32 = (f32[1,2,2,8,128]{4,3,2,1,0:T(8,128)S(1)}, f32[1,2,2,8,128]{4,3,2,1,0:T(8,128)S(1)}, u32[]{:S(2)}, u32[]{:S(2)}) collective-permute-start(f32[1,2,2,8,128]{4,3,2,1,0:T(8,128)S(1)} %get-tuple-element.112), channel_id=1, source_target_pairs={{0,452},{32,484},{452,0},{484,32},{8,460},{40,492},{460,8},{492,40... | collective-permute-start | bytes 49160 | tf_op jit(solution)/shard_map/ppermute | solution.py:70
  101.7 3.3 %collective-permute-start.30 = (f32[1,2,2,8,128]{4,3,2,1,0:T(8,128)S(1)}, f32[1,2,2,8,128]{4,3,2,1,0:T(8,128)S(1)}, u32[]{:S(2)}, u32[]{:S(2)}) collective-permute-start(f32[1,2,2,8,128]{4,3,2,1,0:T(8,128)S(1)} %get-tuple-element.113), channel_id=1, source_target_pairs={{0,64},{32,0},{64,128},{96,32},{128,192},{160,96},{192,256},{224,1... | collective-permute-start | bytes 49160 | tf_op jit(solution)/shard_map/ppermute | solution.py:70
  104.1 4.8 %collective-permute-start.31 = (f32[1,2,2,8,128]{4,3,2,1,0:T(8,128)S(1)}, f32[1,2,2,8,128]{4,3,2,1,0:T(8,128)S(1)}, u32[]{:S(2)}, u32[]{:S(2)}) collective-permute-start(f32[1,2,2,8,128]{4,3,2,1,0:T(8,128)S(1)} %get-tuple-element.114), channel_id=1, source_target_pairs={{64,0},{0,32},{128,64},{32,96},{192,128},{96,160},{256,192},{160,2... | collective-permute-start | bytes 49160 | tf_op jit(solution)/shard_map/ppermute | solution.py:70
  109.2 9.8 %collective-permute-start.33 = (f32[16,128]{1,0:T(8,128)S(1)}, f32[16,128]{1,0:T(8,128)S(1)}, u32[]{:S(2)}, u32[]{:S(2)}) collective-permute-start(f32[16,128]{1,0:T(8,128)S(1)} %k_force.1), channel_id=1, source_target_pairs={{0,0},{32,1},{1,2},{33,3},{2,4},{34,5},{3,6},{35,7},{8,8},{40,9},{... | collective-permute-start | bytes 24584 | tf_op jit(solution)/shard_map/ppermute | solution.py:70

commit v8 on v7

--- a/solution.py
+++ b/solution.py
@@ -568,9 +568,10 @@
         wav,
     )
     own = call(k_own_env, [(192, PAIRS), (192, PAIRS)], packed, scal, av)
-    rest = call(k_tangent, [(128, PAIRS)] * 4, scal, pre, wb, wav, w_mix)
+    latent, hid, tangent, nav = call(k_tangent, [(128, PAIRS)] * 4, scal, pre, wb, wav, w_mix)
     low, high = low.reshape(1, 2, 2, 8, 192), high.reshape(1, 2, 2, 8, 192)
-    ghosts, (ei, ej), (latent, hid, tangent, nav) = spread(low, high, here, own, rest)
+    ghosts, _, nav = spread(low, high, here, (), nav)
+    ei, ej = own
     ghosts = [g.reshape(-1, 192) for g in ghosts]
     before, after, cells, ej, h, tbar = call(
         k_energy,

time: 120 us -> 119 us (level)
  local copies, waits for them, and re-layouts: 4.19 us -> 2.3 us
    unnamed x28 -> x16, local copies, waits for them, and re-layouts: 3.33 us -> 1.47 us
  transfers between devices with their start and end apart: 34 -> 34, of which waited for: 16 -> 17; matrix products, arithmetic and copies ran while one was open for 0% -> 0% of each run, Pallas kernels for 5% -> 5%
where the time goes in v8:
time: 119 us
  starting transfers between devices  61.5 us (52%)
  waiting for transfers between devices  40.9 us (34%)
  Pallas kernels  12.2 us (10%)
  local copies, waits for them, and re-layouts  2.3 us (2%)
    ppermute x34, starting transfers between devices, send(): return lax.ppermute(x, AXES, pairs)  61.5 us
    ppermute x34, waiting for transfers between devices, send(): return lax.ppermute(x, AXES, pairs)  40.9 us
    pallas_call x11, Pallas kernels, call(): pl.pallas_call(kernel, out_shape=shapes, in_specs=[spec] * len(args), out...  10.7 us
  transfers between devices with their start and end apart: 34, of which 17 were waited for; matrix products, arithmetic and copies ran while one was open for 0% of the time, Pallas kernels for 5%

profile of v8, /device:TPU:71, one launch (start us, length us, event | category | flops | bytes accessed | tf_op | source)
XLA Modules:
  0.0 118.5 jit_solution(4613776065572443840)
XLA Ops:
  0.6 1.5 %k_pack.1 = f32[48,128]{1,0:T(8,128)} custom-call(f32[3,1,1,1,512]{4,3,2,1,0:T(1,128)} %pos_in.1, s32[1,1,1,512]{3,2,1,0:T(1,128)} %kind_in.1, s32[2,2,2,8]{3,2,1,0:T(2,128)} %names_in.1, s32[1,1,1,8,128]{4,3,2,1,0:T(8,128)} %center_in.1, s32[1,1,1,8,128]{4,3,2,1,0:T(8,128)} %partner_in.1, s32[1,1,1,8,128]{4,3,2,1,0:T(8,128)} %live_in.1), custom_call_target="tpu_custom_call" | custom-call | tf_op jit(solution)/shard_map/k_pack/pallas_call | solution.py:255
  2.1 8.3 %collective-permute-start = (f32[48,128]{1,0:T(8,128)}, f32[48,128]{1,0:T(8,128)S(1)}, u32[]{:S(2)}, u32[]{:S(2)}) collective-permute-start(f32[48,128]{1,0:T(8,128)} %k_pack.1), channel_id=1, source_target_pairs={{0,0},{1,32},{2,1},{3,33},{4,2},{5,34},{6,3},{7,35},{8,8},{9,40},{... | collective-permute-start | bytes 73736 | tf_op jit(solution)/shard_map/ppermute | solution.py:70
  10.5 7.4 %collective-permute-done.packed_ref = f32[48,128]{1,0:T(8,128)S(1)} collective-permute-done((f32[48,128]{1,0:T(8,128)}, f32[48,128]{1,0:T(8,128)S(1)}, u32[]{:S(2)}, u32[]{:S(2)}) %collective-permute-start) | collective-permute-done | bytes 24608 | tf_op jit(solution)/shard_map/ppermute | solution.py:70
  18.2 0.7 collective-permute-start.3
  18.9 1.5 %collective-permute-start.1 = (f32[1,2,2,8,128]{4,3,2,1,0:T(8,128)S(1)}, f32[1,2,2,8,128]{4,3,2,1,0:T(8,128)S(1)}, u32[]{:S(2)}, u32[]{:S(2)}) collective-permute-start(f32[1,2,2,8,128]{4,3,2,1,0:T(8,128)S(1)} %get-tuple-element.115), channel_id=1, source_target_pairs={{0,64},{32,0},{64,128},{96,32},{128,192},{160,96},{192,256},{224,1... | collective-permute-start | bytes 49160 | tf_op jit(solution)/shard_map/ppermute | solution.py:70
  20.7 0.7 collective-permute-done.2
  21.5 4.6 %collective-permute-start.6 = (f32[4,1,2,8,128]{4,3,2,1,0:T(8,128)S(1)}, f32[4,1,2,8,128]{4,3,2,1,0:T(8,128)S(1)}, u32[]{:S(2)}, u32[]{:S(2)}) collective-permute-start(f32[4,1,2,8,128]{4,3,2,1,0:T(8,128)S(1)} %get-tuple-element.106), channel_id=1, source_target_pairs={{0,24},{32,56},{64,88},{96,120},{128,152},{160,184},{192,216},{224... | collective-permute-start | bytes 98312 | tf_op jit(solution)/shard_map/ppermute | solution.py:70
  26.2 3.8 %collective-permute-start.4 = (f32[4,1,2,8,128]{4,3,2,1,0:T(8,128)S(1)}, f32[4,1,2,8,128]{4,3,2,1,0:T(8,128)S(1)}, u32[]{:S(2)}, u32[]{:S(2)}) collective-permute-start(f32[4,1,2,8,128]{4,3,2,1,0:T(8,128)S(1)} %get-tuple-element.107), channel_id=1, source_target_pairs={{0,8},{32,0},{64,72},{96,64},{128,136},{160,128},{192,200},{224,19... | collective-permute-start | bytes 98312 | tf_op jit(solution)/shard_map/ppermute | solution.py:70
  30.1 0.7 copy-done.2
  31.6 2.4 %collective-permute-start.8 = (f32[4,4,8,128]{3,2,1,0:T(8,128)S(1)}, f32[4,4,8,128]{3,2,1,0:T(8,128)S(1)}, u32[]{:S(2)}, u32[]{:S(2)}) collective-permute-start(f32[4,4,8,128]{3,2,1,0:T(8,128)S(1)} %get-tuple-element.90), channel_id=1, source_target_pairs={{32,0},{1,32},{33,1},{2,33},{34,2},{3,34},{35,3},{0,35},{40,8},{9,... | collective-permute-start | bytes 196616 | tf_op jit(solution)/shard_map/ppermute | solution.py:70
  34.0 5.9 %collective-permute-start.7 = (f32[4,4,8,128]{3,2,1,0:T(8,128)S(1)}, f32[4,4,8,128]{3,2,1,0:T(8,128)S(1)}, u32[]{:S(2)}, u32[]{:S(2)}) collective-permute-start(f32[4,4,8,128]{3,2,1,0:T(8,128)S(1)} %get-tuple-element.91), channel_id=1, source_target_pairs={{0,32},{32,1},{1,33},{33,2},{2,34},{34,3},{3,35},{35,0},{8,40},{40... | collective-permute-start | bytes 196616 | tf_op jit(solution)/shard_map/ppermute | solution.py:70
  40.0 1.8 %collective-permute-done.8 = f32[4,4,8,128]{3,2,1,0:T(8,128)S(1)} collective-permute-done((f32[4,4,8,128]{3,2,1,0:T(8,128)S(1)}, f32[4,4,8,128]{3,2,1,0:T(8,128)S(1)}, u32[]{:S(2)}, u32[]{:S(2)}) %collective-permute-start.8) | collective-permute-done | bytes 65568 | tf_op jit(solution)/shard_map/ppermute | solution.py:70
  41.8 1.2 %k_features.1 = (f32[32,192]{1,0:T(8,128)S(1)}, f32[32,192]{1,0:T(8,128)S(1)}, f32[8,1024]{1,0:T(8,128)S(1)}, f32[128,1024]{1,0:T(8,128)S(1)}, f32[128,1024]{1,0:T(8,128)S(1)}) custom-call(f32[48,128]{1,0:T(8,128)S(1)} %collective-permute-done.packed_ref, f32[8,1024]{1,0:T(8,128)S(1)} %k_own_pairs.1.part_ref, f32[128,128]{1,0:T(8,128)S(1)} %bitcast.44, ...), custom_call_target="tpu_custom_call" | custom-call | tf_op jit(solution)/shard_map/k_features/pallas_call | solution.py:522
  43.0 0.7 collective-permute-start.11
  43.7 1.8 %collective-permute-start.9 = (f32[1,2,2,8,192]{4,3,2,1,0:T(8,128)S(1)}, f32[1,2,2,8,192]{4,3,2,1,0:T(8,128)S(1)}, u32[]{:S(2)}, u32[]{:S(2)}) collective-permute-start(f32[1,2,2,8,192]{4,3,2,1,0:T(8,128)S(1)} %get-tuple-element.105), channel_id=1, source_target_pairs={{0,64},{32,0},{64,128},{96,32},{128,192},{160,96},{192,256},{224,1... | collective-permute-start | bytes 73736 | tf_op jit(solution)/shard_map/ppermute | solution.py:70
  45.5 1.3 %collective-permute-done.10 = f32[1,2,2,8,192]{4,3,2,1,0:T(8,128)S(1)} collective-permute-done((f32[1,2,2,8,192]{4,3,2,1,0:T(8,128)S(1)}, f32[1,2,2,8,192]{4,3,2,1,0:T(8,128)S(1)}, u32[]{:S(2)}, u32[]{:S(2)}) %collective-permute-start.10) | collective-permute-done | bytes 24608 | tf_op jit(solution)/shard_map/ppermute | solution.py:70
  46.9 2.8 %collective-permute-start.14 = (f32[4,1,2,8,192]{4,3,2,1,0:T(8,128)S(1)}, f32[4,1,2,8,192]{4,3,2,1,0:T(8,128)S(1)}, u32[]{:S(2)}, u32[]{:S(2)}) collective-permute-start(f32[4,1,2,8,192]{4,3,2,1,0:T(8,128)S(1)} %get-tuple-element.87), channel_id=1, source_target_pairs={{0,24},{32,56},{64,88},{96,120},{128,152},{160,184},{192,216},{224... | collective-permute-start | bytes 147464 | tf_op jit(solution)/shard_map/ppermute | solution.py:70
  49.6 1.5 %collective-permute-start.12 = (f32[4,1,2,8,192]{4,3,2,1,0:T(8,128)S(1)}, f32[4,1,2,8,192]{4,3,2,1,0:T(8,128)S(1)}, u32[]{:S(2)}, u32[]{:S(2)}) collective-permute-start(f32[4,1,2,8,192]{4,3,2,1,0:T(8,128)S(1)} %get-tuple-element.88), channel_id=1, source_target_pairs={{0,8},{32,0},{64,72},{96,64},{128,136},{160,128},{192,200},{224,19... | collective-permute-start | bytes 147464 | tf_op jit(solution)/shard_map/ppermute | solution.py:70
  51.2 0.9 k_tangent.1
  52.1 1.0 collective-permute-done.14
  53.1 0.7 slice_bitcast_fusion
  53.8 2.4 %collective-permute-start.16 = (f32[4,4,8,192]{3,2,1,0:T(8,128)}, f32[4,4,8,192]{3,2,1,0:T(8,128)S(1)}, u32[]{:S(2)}, u32[]{:S(2)}) collective-permute-start(f32[4,4,8,192]{3,2,1,0:T(8,128)} %get-tuple-element.75), channel_id=1, source_target_pairs={{32,0},{1,32},{33,1},{2,33},{34,2},{3,34},{35,3},{0,35},{40,8},{9,... | collective-permute-start | bytes 294920 | tf_op jit(solution)/shard_map/ppermute | solution.py:70
  56.2 5.0 %collective-permute-start.15 = (f32[4,4,8,192]{3,2,1,0:T(8,128)S(1)}, f32[4,4,8,192]{3,2,1,0:T(8,128)S(1)}, u32[]{:S(2)}, u32[]{:S(2)}) collective-permute-start(f32[4,4,8,192]{3,2,1,0:T(8,128)S(1)} %get-tuple-element.76), channel_id=1, source_target_pairs={{0,32},{32,1},{1,33},{33,2},{2,34},{34,3},{3,35},{35,0},{8,40},{40... | collective-permute-start | bytes 294920 | tf_op jit(solution)/shard_map/ppermute | solution.py:70
  61.3 1.6 %k_own_env.1 = (f32[192,1024]{1,0:T(8,128)S(1)}, f32[192,1024]{1,0:T(8,128)S(1)}) custom-call(f32[48,128]{1,0:T(8,128)S(1)} %collective-permute-done.packed_ref, f32[8,1024]{1,0:T(8,128)S(1)} %get-tuple-element.42.scal_ref, f32[128,1024]{1,0:T(8,128)S(1)} %get-tuple-element.43.av_ref), custom_call_target="tpu_custom_call" | custom-call | tf_op jit(solution)/shard_map/k_own_env/pallas_call | solution.py:522
  62.9 1.2 collective-permute-done.16
  64.1 1.8 %k_energy.1 = (f32[128,192]{1,0:T(8,128)S(1)}, f32[128,192]{1,0:T(8,128)S(1)}, f32[256,192]{1,0:T(8,128)S(1)}, f32[192,1024]{1,0:T(8,128)S(1)}, f32[128,1024]{1,0:T(8,128)S(1)}, /*index=5*/f32[64,1024]{1,0:T(8,128)S(1)}) custom-call(f32[48,128]{1,0:T(8,128)S(1)} %collective-permute-done.packed_ref, f32[8,1024]{1,0:T(8,128)S(1)} %get-tuple-element.42.scal_ref, ...), custom_call_target="tpu_custom_call" | custom-call | tf_op jit(solution)/shard_map/k_energy/pallas_call | solution.py:522
  65.8 2.8 %collective-permute-start.17 = (f32[4,4,8,192]{3,2,1,0:T(8,128)S(1)}, f32[4,4,8,192]{3,2,1,0:T(8,128)S(1)}, u32[]{:S(2)}, u32[]{:S(2)}) collective-permute-start(f32[4,4,8,192]{3,2,1,0:T(8,128)S(1)} %bitcast.50), channel_id=1, source_target_pairs={{0,32},{32,1},{1,33},{33,2},{2,34},{34,3},{3,35},{35,0},{8,40},{40... | collective-permute-start | bytes 294920 | tf_op jit(solution)/shard_map/ppermute | solution.py:70
  68.6 2.2 %k_direct.1 = (f32[8,1024]{1,0:T(8,128)S(1)}, f32[4,512]{1,0:T(4,128)S(1)}) custom-call(f32[48,128]{1,0:T(8,128)S(1)} %collective-permute-done.packed_ref, f32[8,1024]{1,0:T(8,128)S(1)} %get-tuple-element.42.scal_ref, f32[128,1024]{1,0:T(8,128)S(1)} %get-tuple-element.43.av_ref, f32[128,1024]{1,0:T(8,128)S(1)} %get-tuple-element.48.nav_ref, ...), custom_call_target="tpu_custom_call" | custom-call | tf_op jit(solution)/shard_map/k_direct/pallas_call | solution.py:522
  70.8 3.4 %collective-permute-done.18 = f32[4,4,8,192]{3,2,1,0:T(8,128)S(1)} collective-permute-done((f32[4,4,8,192]{3,2,1,0:T(8,128)S(1)}, f32[4,4,8,192]{3,2,1,0:T(8,128)S(1)}, u32[]{:S(2)}, u32[]{:S(2)}) %collective-permute-start.18) | collective-permute-done | bytes 98336 | tf_op jit(solution)/shard_map/ppermute | solution.py:70
  74.3 3.7 %collective-permute-start.21 = (f32[4,1,2,8,192]{4,3,2,1,0:T(8,128)S(1)}, f32[4,1,2,8,192]{4,3,2,1,0:T(8,128)S(1)}, u32[]{:S(2)}, u32[]{:S(2)}) collective-permute-start(f32[4,1,2,8,192]{4,3,2,1,0:T(8,128)S(1)} %get-tuple-element.72), channel_id=1, source_target_pairs={{0,24},{32,56},{64,88},{96,120},{128,152},{160,184},{192,216},{224... | collective-permute-start | bytes 147464 | tf_op jit(solution)/shard_map/ppermute | solution.py:70
  78.0 1.5 %collective-permute-start.20 = (f32[4,1,2,8,192]{4,3,2,1,0:T(8,128)S(1)}, f32[4,1,2,8,192]{4,3,2,1,0:T(8,128)S(1)}, u32[]{:S(2)}, u32[]{:S(2)}) collective-permute-start(f32[4,1,2,8,192]{4,3,2,1,0:T(8,128)S(1)} %get-tuple-element.74), channel_id=1, source_target_pairs={{8,0},{0,32},{72,64},{64,96},{136,128},{128,160},{200,192},{192,22... | collective-permute-start | bytes 147464 | tf_op jit(solution)/shard_map/ppermute | solution.py:70
  79.4 1.0 collective-permute-done.21
  81.2 0.7 collective-permute-start.24
  81.8 1.8 %collective-permute-start.22 = (f32[1,2,2,8,192]{4,3,2,1,0:T(8,128)S(1)}, f32[1,2,2,8,192]{4,3,2,1,0:T(8,128)S(1)}, u32[]{:S(2)}, u32[]{:S(2)}) collective-permute-start(f32[1,2,2,8,192]{4,3,2,1,0:T(8,128)S(1)} %get-tuple-element.85), channel_id=1, source_target_pairs={{0,64},{32,0},{64,128},{96,32},{128,192},{160,96},{192,256},{224,1... | collective-permute-start | bytes 73736 | tf_op jit(solution)/shard_map/ppermute | solution.py:70
  83.6 1.0 collective-permute-done.22
  84.6 3.3 %collective-permute-done.23 = f32[1,2,2,8,192]{4,3,2,1,0:T(8,128)S(1)} collective-permute-done((f32[1,2,2,8,192]{4,3,2,1,0:T(8,128)S(1)}, f32[1,2,2,8,192]{4,3,2,1,0:T(8,128)S(1)}, u32[]{:S(2)}, u32[]{:S(2)}) %collective-permute-start.23) | collective-permute-done | bytes 24608 | tf_op jit(solution)/shard_map/ppermute | solution.py:70
  88.0 1.0 k_env_back.1
  89.5 0.6 k_own_force.1.own_ref
  90.3 3.6 %collective-permute-done.26 = f32[4,4,8,128]{3,2,1,0:T(8,128)S(1)} collective-permute-done((f32[4,4,8,128]{3,2,1,0:T(8,128)S(1)}, f32[4,4,8,128]{3,2,1,0:T(8,128)S(1)}, u32[]{:S(2)}, u32[]{:S(2)}) %collective-permute-start.26) | collective-permute-done | bytes 65568 | tf_op jit(solution)/shard_map/ppermute | solution.py:70
  94.0 2.8 %collective-permute-start.29 = (f32[4,1,2,8,128]{4,3,2,1,0:T(8,128)S(1)}, f32[4,1,2,8,128]{4,3,2,1,0:T(8,128)S(1)}, u32[]{:S(2)}, u32[]{:S(2)}) collective-permute-start(f32[4,1,2,8,128]{4,3,2,1,0:T(8,128)S(1)} %get-tuple-element.81), channel_id=1, source_target_pairs={{0,24},{32,56},{64,88},{96,120},{128,152},{160,184},{192,216},{224... | collective-permute-start | bytes 98312 | tf_op jit(solution)/shard_map/ppermute | solution.py:70
  96.8 1.5 %collective-permute-start.28 = (f32[4,1,2,8,128]{4,3,2,1,0:T(8,128)S(1)}, f32[4,1,2,8,128]{4,3,2,1,0:T(8,128)S(1)}, u32[]{:S(2)}, u32[]{:S(2)}) collective-permute-start(f32[4,1,2,8,128]{4,3,2,1,0:T(8,128)S(1)} %get-tuple-element.83), channel_id=1, source_target_pairs={{8,0},{0,32},{72,64},{64,96},{136,128},{128,160},{200,192},{192,22... | collective-permute-start | bytes 98312 | tf_op jit(solution)/shard_map/ppermute | solution.py:70
  98.3 1.6 %collective-permute-done.29 = f32[4,1,2,8,128]{4,3,2,1,0:T(8,128)S(1)} collective-permute-done((f32[4,1,2,8,128]{4,3,2,1,0:T(8,128)S(1)}, f32[4,1,2,8,128]{4,3,2,1,0:T(8,128)S(1)}, u32[]{:S(2)}, u32[]{:S(2)}) %collective-permute-start.29) | collective-permute-done | bytes 32800 | tf_op jit(solution)/shard_map/ppermute | solution.py:70
  99.9 0.7 collective-permute-start.32
  100.6 2.5 %collective-permute-start.30 = (f32[1,2,2,8,128]{4,3,2,1,0:T(8,128)S(1)}, f32[1,2,2,8,128]{4,3,2,1,0:T(8,128)S(1)}, u32[]{:S(2)}, u32[]{:S(2)}) collective-permute-start(f32[1,2,2,8,128]{4,3,2,1,0:T(8,128)S(1)} %get-tuple-element.101), channel_id=1, source_target_pairs={{0,64},{32,0},{64,128},{96,32},{128,192},{160,96},{192,256},{224,1... | collective-permute-start | bytes 49160 | tf_op jit(solution)/shard_map/ppermute | solution.py:70
  103.1 0.9 collective-permute-done.30
  103.9 4.0 %collective-permute-done.31 = f32[1,2,2,8,128]{4,3,2,1,0:T(8,128)S(1)} collective-permute-done((f32[1,2,2,8,128]{4,3,2,1,0:T(8,128)S(1)}, f32[1,2,2,8,128]{4,3,2,1,0:T(8,128)S(1)}, u32[]{:S(2)}, u32[]{:S(2)}) %collective-permute-start.31) | collective-permute-done | bytes 16416 | tf_op jit(solution)/shard_map/ppermute | solution.py:70
  108.1 1.9 %collective-permute-start.33 = (f32[16,128]{1,0:T(8,128)S(1)}, f32[16,128]{1,0:T(8,128)S(1)}, u32[]{:S(2)}, u32[]{:S(2)}) collective-permute-start(f32[16,128]{1,0:T(8,128)S(1)} %k_force.1), channel_id=1, source_target_pairs={{0,0},{32,1},{1,2},{33,3},{2,4},{34,5},{3,6},{35,7},{8,8},{40,9},{... | collective-permute-start | bytes 24584 | tf_op jit(solution)/shard_map/ppermute | solution.py:70
  110.1 7.9 %collective-permute-done.33.in_ref = f32[16,128]{1,0:T(8,128)S(1)} collective-permute-done((f32[16,128]{1,0:T(8,128)S(1)}, f32[16,128]{1,0:T(8,128)S(1)}, u32[]{:S(2)}, u32[]{:S(2)}) %collective-permute-start.33) | collective-permute-done | bytes 8224 | tf_op jit(solution)/shard_map/ppermute | solution.py:70
  (80 shorter events, 4.3 us)
Async XLA Ops:
  2.1 15.8 %collective-permute-start = (f32[48,128]{1,0:T(8,128)}, f32[48,128]{1,0:T(8,128)S(1)}, u32[]{:S(2)}, u32[]{:S(2)}) collective-permute-start(f32[48,128]{1,0:T(8,128)} %k_pack.1), channel_id=1, source_target_pairs={{0,0},{1,32},{2,1},{3,33},{4,2},{5,34},{6,3},{7,35},{8,8},{9,40},{... | collective-permute-start | bytes 73736 | tf_op jit(solution)/shard_map/ppermute | solution.py:70
  18.2 2.6 %collective-permute-start.3 = (f32[1,2,2,8,128]{4,3,2,1,0:T(8,128)S(1)}, f32[1,2,2,8,128]{4,3,2,1,0:T(8,128)S(1)}, u32[]{:S(2)}, u32[]{:S(2)}) collective-permute-start(f32[1,2,2,8,128]{4,3,2,1,0:T(8,128)S(1)} %get-tuple-element.113), channel_id=1, source_target_pairs={{0,452},{32,484},{452,0},{484,32},{8,460},{40,492},{460,8},{492,40... | collective-permute-start | bytes 49160 | tf_op jit(solution)/shard_map/ppermute | solution.py:70
  18.8 2.6 %collective-permute-start.2 = (f32[1,2,2,8,128]{4,3,2,1,0:T(8,128)S(1)}, f32[1,2,2,8,128]{4,3,2,1,0:T(8,128)S(1)}, u32[]{:S(2)}, u32[]{:S(2)}) collective-permute-start(f32[1,2,2,8,128]{4,3,2,1,0:T(8,128)S(1)} %get-tuple-element.114), channel_id=1, source_target_pairs={{64,0},{0,32},{128,64},{32,96},{192,128},{96,160},{256,192},{160,2... | collective-permute-start | bytes 49160 | tf_op jit(solution)/shard_map/ppermute | solution.py:70
  18.9 2.6 %collective-permute-start.1 = (f32[1,2,2,8,128]{4,3,2,1,0:T(8,128)S(1)}, f32[1,2,2,8,128]{4,3,2,1,0:T(8,128)S(1)}, u32[]{:S(2)}, u32[]{:S(2)}) collective-permute-start(f32[1,2,2,8,128]{4,3,2,1,0:T(8,128)S(1)} %get-tuple-element.115), channel_id=1, source_target_pairs={{0,64},{32,0},{64,128},{96,32},{128,192},{160,96},{192,256},{224,1... | collective-permute-start | bytes 49160 | tf_op jit(solution)/shard_map/ppermute | solution.py:70
  21.5 8.5 %copy-start.1 = (f32[128,64]{0,1:T(8,128)S(1)}, f32[128,64]{0,1:T(8,128)}, u32[]{:S(2)}) copy-start(f32[128,64]{0,1:T(8,128)} %param.22) | copy-start | bytes 98308
  21.5 10.0 %collective-permute-start.6 = (f32[4,1,2,8,128]{4,3,2,1,0:T(8,128)S(1)}, f32[4,1,2,8,128]{4,3,2,1,0:T(8,128)S(1)}, u32[]{:S(2)}, u32[]{:S(2)}) collective-permute-start(f32[4,1,2,8,128]{4,3,2,1,0:T(8,128)S(1)} %get-tuple-element.106), channel_id=1, source_target_pairs={{0,24},{32,56},{64,88},{96,120},{128,152},{160,184},{192,216},{224... | collective-permute-start | bytes 98312 | tf_op jit(solution)/shard_map/ppermute | solution.py:70
  26.2 5.3 %collective-permute-start.4 = (f32[4,1,2,8,128]{4,3,2,1,0:T(8,128)S(1)}, f32[4,1,2,8,128]{4,3,2,1,0:T(8,128)S(1)}, u32[]{:S(2)}, u32[]{:S(2)}) collective-permute-start(f32[4,1,2,8,128]{4,3,2,1,0:T(8,128)S(1)} %get-tuple-element.107), channel_id=1, source_target_pairs={{0,8},{32,0},{64,72},{96,64},{128,136},{160,128},{192,200},{224,19... | collective-permute-start | bytes 98312 | tf_op jit(solution)/shard_map/ppermute | solution.py:70
  30.0 1.5 %collective-permute-start.5 = (f32[4,1,2,8,128]{4,3,2,1,0:T(8,128)S(1)}, f32[4,1,2,8,128]{4,3,2,1,0:T(8,128)S(1)}, u32[]{:S(2)}, u32[]{:S(2)}) collective-permute-start(f32[4,1,2,8,128]{4,3,2,1,0:T(8,128)S(1)} %get-tuple-element.108), channel_id=1, source_target_pairs={{8,0},{0,32},{72,64},{64,96},{136,128},{128,160},{200,192},{192,22... | collective-permute-start | bytes 98312 | tf_op jit(solution)/shard_map/ppermute | solution.py:70
  30.0 0.8 copy-start.2
  30.7 0.7 copy-start.3
  30.7 0.7 copy-start.4
  30.7 0.7 copy-start.5
  31.6 10.2 %collective-permute-start.8 = (f32[4,4,8,128]{3,2,1,0:T(8,128)S(1)}, f32[4,4,8,128]{3,2,1,0:T(8,128)S(1)}, u32[]{:S(2)}, u32[]{:S(2)}) collective-permute-start(f32[4,4,8,128]{3,2,1,0:T(8,128)S(1)} %get-tuple-element.90), channel_id=1, source_target_pairs={{32,0},{1,32},{33,1},{2,33},{34,2},{3,34},{35,3},{0,35},{40,8},{9,... | collective-permute-start | bytes 196616 | tf_op jit(solution)/shard_map/ppermute | solution.py:70
  34.0 7.8 %collective-permute-start.7 = (f32[4,4,8,128]{3,2,1,0:T(8,128)S(1)}, f32[4,4,8,128]{3,2,1,0:T(8,128)S(1)}, u32[]{:S(2)}, u32[]{:S(2)}) collective-permute-start(f32[4,4,8,128]{3,2,1,0:T(8,128)S(1)} %get-tuple-element.91), channel_id=1, source_target_pairs={{0,32},{32,1},{1,33},{33,2},{2,34},{34,3},{3,35},{35,0},{8,40},{40... | collective-permute-start | bytes 196616 | tf_op jit(solution)/shard_map/ppermute | solution.py:70
  43.0 2.5 %collective-permute-start.11 = (f32[1,2,2,8,192]{4,3,2,1,0:T(8,128)S(1)}, f32[1,2,2,8,192]{4,3,2,1,0:T(8,128)S(1)}, u32[]{:S(2)}, u32[]{:S(2)}) collective-permute-start(f32[1,2,2,8,192]{4,3,2,1,0:T(8,128)S(1)} %get-tuple-element.103), channel_id=1, source_target_pairs={{0,452},{32,484},{452,0},{484,32},{8,460},{40,492},{460,8},{492,40... | collective-permute-start | bytes 73736 | tf_op jit(solution)/shard_map/ppermute | solution.py:70
  43.7 3.1 %collective-permute-start.10 = (f32[1,2,2,8,192]{4,3,2,1,0:T(8,128)S(1)}, f32[1,2,2,8,192]{4,3,2,1,0:T(8,128)S(1)}, u32[]{:S(2)}, u32[]{:S(2)}) collective-permute-start(f32[1,2,2,8,192]{4,3,2,1,0:T(8,128)S(1)} %get-tuple-element.104), channel_id=1, source_target_pairs={{64,0},{0,32},{128,64},{32,96},{192,128},{96,160},{256,192},{160,2... | collective-permute-start | bytes 73736 | tf_op jit(solution)/shard_map/ppermute | solution.py:70
  43.7 3.0 %collective-permute-start.9 = (f32[1,2,2,8,192]{4,3,2,1,0:T(8,128)S(1)}, f32[1,2,2,8,192]{4,3,2,1,0:T(8,128)S(1)}, u32[]{:S(2)}, u32[]{:S(2)}) collective-permute-start(f32[1,2,2,8,192]{4,3,2,1,0:T(8,128)S(1)} %get-tuple-element.105), channel_id=1, source_target_pairs={{0,64},{32,0},{64,128},{96,32},{128,192},{160,96},{192,256},{224,1... | collective-permute-start | bytes 73736 | tf_op jit(solution)/shard_map/ppermute | solution.py:70
  46.8 4.4 %copy-start = (f32[192,128]{1,0:T(8,128)S(1)}, f32[192,128]{1,0:T(8,128)}, u32[]{:S(2)}) copy-start(f32[192,128]{1,0:T(8,128)} %wm_ref.5) | copy-start | bytes 294916
  46.9 6.2 %collective-permute-start.14 = (f32[4,1,2,8,192]{4,3,2,1,0:T(8,128)S(1)}, f32[4,1,2,8,192]{4,3,2,1,0:T(8,128)S(1)}, u32[]{:S(2)}, u32[]{:S(2)}) collective-permute-start(f32[4,1,2,8,192]{4,3,2,1,0:T(8,128)S(1)} %get-tuple-element.87), channel_id=1, source_target_pairs={{0,24},{32,56},{64,88},{96,120},{128,152},{160,184},{192,216},{224... | collective-permute-start | bytes 147464 | tf_op jit(solution)/shard_map/ppermute | solution.py:70
  49.6 3.4 %collective-permute-start.12 = (f32[4,1,2,8,192]{4,3,2,1,0:T(8,128)S(1)}, f32[4,1,2,8,192]{4,3,2,1,0:T(8,128)S(1)}, u32[]{:S(2)}, u32[]{:S(2)}) collective-permute-start(f32[4,1,2,8,192]{4,3,2,1,0:T(8,128)S(1)} %get-tuple-element.88), channel_id=1, source_target_pairs={{0,8},{32,0},{64,72},{96,64},{128,136},{160,128},{192,200},{224,19... | collective-permute-start | bytes 147464 | tf_op jit(solution)/shard_map/ppermute | solution.py:70
  51.2 1.9 %collective-permute-start.13 = (f32[4,1,2,8,192]{4,3,2,1,0:T(8,128)S(1)}, f32[4,1,2,8,192]{4,3,2,1,0:T(8,128)S(1)}, u32[]{:S(2)}, u32[]{:S(2)}) collective-permute-start(f32[4,1,2,8,192]{4,3,2,1,0:T(8,128)S(1)} %get-tuple-element.89), channel_id=1, source_target_pairs={{8,0},{0,32},{72,64},{64,96},{136,128},{128,160},{200,192},{192,22... | collective-permute-start | bytes 147464 | tf_op jit(solution)/shard_map/ppermute | solution.py:70
  53.8 10.3 %collective-permute-start.16 = (f32[4,4,8,192]{3,2,1,0:T(8,128)}, f32[4,4,8,192]{3,2,1,0:T(8,128)S(1)}, u32[]{:S(2)}, u32[]{:S(2)}) collective-permute-start(f32[4,4,8,192]{3,2,1,0:T(8,128)} %get-tuple-element.75), channel_id=1, source_target_pairs={{32,0},{1,32},{33,1},{2,33},{34,2},{3,34},{35,3},{0,35},{40,8},{9,... | collective-permute-start | bytes 294920 | tf_op jit(solution)/shard_map/ppermute | solution.py:70
  56.2 5.0 %copy-start.6 = (f32[128]{0:T(128)S(1)}, f32[128]{0:T(128)}, u32[]{:S(2)}) copy-start(f32[128]{0:T(128)} %param.25) | copy-start | bytes 1540
  56.2 7.9 %collective-permute-start.15 = (f32[4,4,8,192]{3,2,1,0:T(8,128)S(1)}, f32[4,4,8,192]{3,2,1,0:T(8,128)S(1)}, u32[]{:S(2)}, u32[]{:S(2)}) collective-permute-start(f32[4,4,8,192]{3,2,1,0:T(8,128)S(1)} %get-tuple-element.76), channel_id=1, source_target_pairs={{0,32},{32,1},{1,33},{33,2},{2,34},{34,3},{3,35},{35,0},{8,40},{40... | collective-permute-start | bytes 294920 | tf_op jit(solution)/shard_map/ppermute | solution.py:70
  65.8 5.0 %collective-permute-start.17 = (f32[4,4,8,192]{3,2,1,0:T(8,128)S(1)}, f32[4,4,8,192]{3,2,1,0:T(8,128)S(1)}, u32[]{:S(2)}, u32[]{:S(2)}) collective-permute-start(f32[4,4,8,192]{3,2,1,0:T(8,128)S(1)} %bitcast.50), channel_id=1, source_target_pairs={{0,32},{32,1},{1,33},{33,2},{2,34},{34,3},{3,35},{35,0},{8,40},{40... | collective-permute-start | bytes 294920 | tf_op jit(solution)/shard_map/ppermute | solution.py:70
  68.6 5.6 %collective-permute-start.18 = (f32[4,4,8,192]{3,2,1,0:T(8,128)S(1)}, f32[4,4,8,192]{3,2,1,0:T(8,128)S(1)}, u32[]{:S(2)}, u32[]{:S(2)}) collective-permute-start(f32[4,4,8,192]{3,2,1,0:T(8,128)S(1)} %bitcast.49), channel_id=1, source_target_pairs={{32,0},{1,32},{33,1},{2,33},{34,2},{3,34},{35,3},{0,35},{40,8},{9,... | collective-permute-start | bytes 294920 | tf_op jit(solution)/shard_map/ppermute | solution.py:70
  74.3 6.2 %collective-permute-start.21 = (f32[4,1,2,8,192]{4,3,2,1,0:T(8,128)S(1)}, f32[4,1,2,8,192]{4,3,2,1,0:T(8,128)S(1)}, u32[]{:S(2)}, u32[]{:S(2)}) collective-permute-start(f32[4,1,2,8,192]{4,3,2,1,0:T(8,128)S(1)} %get-tuple-element.72), channel_id=1, source_target_pairs={{0,24},{32,56},{64,88},{96,120},{128,152},{160,184},{192,216},{224... | collective-permute-start | bytes 147464 | tf_op jit(solution)/shard_map/ppermute | solution.py:70
  78.0 3.1 %collective-permute-start.19 = (f32[4,1,2,8,192]{4,3,2,1,0:T(8,128)S(1)}, f32[4,1,2,8,192]{4,3,2,1,0:T(8,128)S(1)}, u32[]{:S(2)}, u32[]{:S(2)}) collective-permute-start(f32[4,1,2,8,192]{4,3,2,1,0:T(8,128)S(1)} %get-tuple-element.73), channel_id=1, source_target_pairs={{0,8},{32,0},{64,72},{96,64},{128,136},{160,128},{192,200},{224,19... | collective-permute-start | bytes 147464 | tf_op jit(solution)/shard_map/ppermute | solution.py:70
  78.0 3.1 %collective-permute-start.20 = (f32[4,1,2,8,192]{4,3,2,1,0:T(8,128)S(1)}, f32[4,1,2,8,192]{4,3,2,1,0:T(8,128)S(1)}, u32[]{:S(2)}, u32[]{:S(2)}) collective-permute-start(f32[4,1,2,8,192]{4,3,2,1,0:T(8,128)S(1)} %get-tuple-element.74), channel_id=1, source_target_pairs={{8,0},{0,32},{72,64},{64,96},{136,128},{128,160},{200,192},{192,22... | collective-permute-start | bytes 147464 | tf_op jit(solution)/shard_map/ppermute | solution.py:70
  81.2 2.4 %collective-permute-start.24 = (f32[1,2,2,8,192]{4,3,2,1,0:T(8,128)S(1)}, f32[1,2,2,8,192]{4,3,2,1,0:T(8,128)S(1)}, u32[]{:S(2)}, u32[]{:S(2)}) collective-permute-start(f32[1,2,2,8,192]{4,3,2,1,0:T(8,128)S(1)} %get-tuple-element.84), channel_id=1, source_target_pairs={{0,452},{32,484},{452,0},{484,32},{8,460},{40,492},{460,8},{492,40... | collective-permute-start | bytes 73736 | tf_op jit(solution)/shard_map/ppermute | solution.py:70
  81.8 2.8 %collective-permute-start.22 = (f32[1,2,2,8,192]{4,3,2,1,0:T(8,128)S(1)}, f32[1,2,2,8,192]{4,3,2,1,0:T(8,128)S(1)}, u32[]{:S(2)}, u32[]{:S(2)}) collective-permute-start(f32[1,2,2,8,192]{4,3,2,1,0:T(8,128)S(1)} %get-tuple-element.85), channel_id=1, source_target_pairs={{0,64},{32,0},{64,128},{96,32},{128,192},{160,96},{192,256},{224,1... | collective-permute-start | bytes 73736 | tf_op jit(solution)/shard_map/ppermute | solution.py:70
  83.6 4.4 %collective-permute-start.23 = (f32[1,2,2,8,192]{4,3,2,1,0:T(8,128)S(1)}, f32[1,2,2,8,192]{4,3,2,1,0:T(8,128)S(1)}, u32[]{:S(2)}, u32[]{:S(2)}) collective-permute-start(f32[1,2,2,8,192]{4,3,2,1,0:T(8,128)S(1)} %get-tuple-element.86), channel_id=1, source_target_pairs={{64,0},{0,32},{128,64},{32,96},{192,128},{96,160},{256,192},{160,2... | collective-permute-start | bytes 73736 | tf_op jit(solution)/shard_map/ppermute | solution.py:70
  89.0 1.3 %collective-permute-start.25 = (f32[4,4,8,128]{3,2,1,0:T(8,128)S(1)}, f32[4,4,8,128]{3,2,1,0:T(8,128)S(1)}, u32[]{:S(2)}, u32[]{:S(2)}) collective-permute-start(f32[4,4,8,128]{3,2,1,0:T(8,128)S(1)} %bitcast.52), channel_id=1, source_target_pairs={{0,32},{32,1},{1,33},{33,2},{2,34},{34,3},{3,35},{35,0},{8,40},{40... | collective-permute-start | bytes 196616 | tf_op jit(solution)/shard_map/ppermute | solution.py:70
  89.0 4.9 %collective-permute-start.26 = (f32[4,4,8,128]{3,2,1,0:T(8,128)S(1)}, f32[4,4,8,128]{3,2,1,0:T(8,128)S(1)}, u32[]{:S(2)}, u32[]{:S(2)}) collective-permute-start(f32[4,4,8,128]{3,2,1,0:T(8,128)S(1)} %bitcast.51), channel_id=1, source_target_pairs={{32,0},{1,32},{33,1},{2,33},{34,2},{3,34},{35,3},{0,35},{40,8},{9,... | collective-permute-start | bytes 196616 | tf_op jit(solution)/shard_map/ppermute | solution.py:70
  94.0 5.9 %collective-permute-start.29 = (f32[4,1,2,8,128]{4,3,2,1,0:T(8,128)S(1)}, f32[4,1,2,8,128]{4,3,2,1,0:T(8,128)S(1)}, u32[]{:S(2)}, u32[]{:S(2)}) collective-permute-start(f32[4,1,2,8,128]{4,3,2,1,0:T(8,128)S(1)} %get-tuple-element.81), channel_id=1, source_target_pairs={{0,24},{32,56},{64,88},{96,120},{128,152},{160,184},{192,216},{224... | collective-permute-start | bytes 98312 | tf_op jit(solution)/shard_map/ppermute | solution.py:70
  96.8 3.1 %collective-permute-start.27 = (f32[4,1,2,8,128]{4,3,2,1,0:T(8,128)S(1)}, f32[4,1,2,8,128]{4,3,2,1,0:T(8,128)S(1)}, u32[]{:S(2)}, u32[]{:S(2)}) collective-permute-start(f32[4,1,2,8,128]{4,3,2,1,0:T(8,128)S(1)} %get-tuple-element.82), channel_id=1, source_target_pairs={{0,8},{32,0},{64,72},{96,64},{128,136},{160,128},{192,200},{224,19... | collective-permute-start | bytes 98312 | tf_op jit(solution)/shard_map/ppermute | solution.py:70
  96.8 3.1 %collective-permute-start.28 = (f32[4,1,2,8,128]{4,3,2,1,0:T(8,128)S(1)}, f32[4,1,2,8,128]{4,3,2,1,0:T(8,128)S(1)}, u32[]{:S(2)}, u32[]{:S(2)}) collective-permute-start(f32[4,1,2,8,128]{4,3,2,1,0:T(8,128)S(1)} %get-tuple-element.83), channel_id=1, source_target_pairs={{8,0},{0,32},{72,64},{64,96},{136,128},{128,160},{200,192},{192,22... | collective-permute-start | bytes 98312 | tf_op jit(solution)/shard_map/ppermute | solution.py:70
  99.9 3.2 %collective-permute-start.32 = (f32[1,2,2,8,128]{4,3,2,1,0:T(8,128)S(1)}, f32[1,2,2,8,128]{4,3,2,1,0:T(8,128)S(1)}, u32[]{:S(2)}, u32[]{:S(2)}) collective-permute-start(f32[1,2,2,8,128]{4,3,2,1,0:T(8,128)S(1)} %get-tuple-element.100), channel_id=1, source_target_pairs={{0,452},{32,484},{452,0},{484,32},{8,460},{40,492},{460,8},{492,40... | collective-permute-start | bytes 49160 | tf_op jit(solution)/shard_map/ppermute | solution.py:70
  100.6 3.3 %collective-permute-start.30 = (f32[1,2,2,8,128]{4,3,2,1,0:T(8,128)S(1)}, f32[1,2,2,8,128]{4,3,2,1,0:T(8,128)S(1)}, u32[]{:S(2)}, u32[]{:S(2)}) collective-permute-start(f32[1,2,2,8,128]{4,3,2,1,0:T(8,128)S(1)} %get-tuple-element.101), channel_id=1, source_target_pairs={{0,64},{32,0},{64,128},{96,32},{128,192},{160,96},{192,256},{224,1... | collective-permute-start | bytes 49160 | tf_op jit(solution)/shard_map/ppermute | solution.py:70
  103.1 4.8 %collective-permute-start.31 = (f32[1,2,2,8,128]{4,3,2,1,0:T(8,128)S(1)}, f32[1,2,2,8,128]{4,3,2,1,0:T(8,128)S(1)}, u32[]{:S(2)}, u32[]{:S(2)}) collective-permute-start(f32[1,2,2,8,128]{4,3,2,1,0:T(8,128)S(1)} %get-tuple-element.102), channel_id=1, source_target_pairs={{64,0},{0,32},{128,64},{32,96},{192,128},{96,160},{256,192},{160,2... | collective-permute-start | bytes 49160 | tf_op jit(solution)/shard_map/ppermute | solution.py:70
  108.1 9.8 %collective-permute-start.33 = (f32[16,128]{1,0:T(8,128)S(1)}, f32[16,128]{1,0:T(8,128)S(1)}, u32[]{:S(2)}, u32[]{:S(2)}) collective-permute-start(f32[16,128]{1,0:T(8,128)S(1)} %k_force.1), channel_id=1, source_target_pairs={{0,0},{32,1},{1,2},{33,3},{2,4},{34,5},{3,6},{35,7},{8,8},{40,9},{... | collective-permute-start | bytes 24584 | tf_op jit(solution)/shard_map/ppermute | solution.py:70

commit v9 on v6

--- a/solution.py
+++ b/solution.py
@@ -283,7 +283,7 @@
 
 
 def k_features(
-    packed_ref, part_ref, before_ref, after_ref, cells_ref, column_ref, wb_ref, wav_ref, low_ref, high_ref, scal_ref, pre_ref, av_ref
+    packed_ref, part_ref, before_ref, after_ref, cells_ref, column_ref, wb_ref, ec_ref, ep_ref, we_ref, wv_ref, low_ref, high_ref, scal_ref, pre_ref, av_ref
 ):
     packed = packed_ref[...]
     part = part_ref[...]
@@ -311,9 +311,11 @@
     kinds = lax.broadcasted_iota(jnp.int32, (8, 1), 0).astype(F32)
     first = jnp.where(center_kind == kinds, 1.0, 0.0)
     second = jnp.where(partner_kind == kinds, 1.0, 0.0)
-    pre = weighted(wb_ref[...], jnp.concatenate([basis, first, second], axis=0))
+    gap = jnp.zeros((2, 128), F32)
+    kinds_in = jnp.concatenate([wb_ref[...], ec_ref[...], gap, ep_ref[...], gap], axis=0)
+    pre = weighted(kinds_in, jnp.concatenate([basis, first, second], axis=0))
     latent = cut * (pre * jax.nn.sigmoid(pre))
-    av = weighted(wav_ref[...], latent)
+    av = weighted_t(jnp.concatenate([we_ref[...], wv_ref[...]], axis=0), latent)
     a = av[:CHAN]
     terms = jnp.concatenate([unit[k : k + 1] * a for k in range(3)], axis=0)
     named = jnp.where(column_ref[:, 0:1].astype(jnp.int32) == centers_of(packed), 1.0, 0.0).astype(BF16)
@@ -330,7 +332,7 @@
     av_ref[...] = av
 
 
-def k_own_env(packed_ref, scal_ref, pre_ref, av_ref, wb_ref, wav_ref, wm_ref, ei_ref, ej_ref, lat_ref, hid_ref, tan_ref, nav_ref):
+def k_own_env(packed_ref, scal_ref, pre_ref, av_ref, wb_ref, we_ref, wv_ref, wm_ref, ei_ref, ej_ref, lat_ref, hid_ref, tan_ref, nav_ref):
     packed = packed_ref[...]
     scal = scal_ref[...]
     unit, radius, inv, cut, slope = scal[0:3], scal[3:4], scal[4:5], scal[5:6], scal[6:7]
@@ -350,9 +352,9 @@
     orders = lax.broadcasted_iota(jnp.int32, (8, 1), 0).astype(F32) + 1.0
     angle = radius * orders * STEP
     change = (jnp.cos(angle) * (orders * STEP) - jnp.sin(angle) * inv) * inv
-    tangent = slope * act + cut * (gate * (1.0 + pre * (1.0 - gate))) * weighted(wb_ref[0:8], change)
+    tangent = slope * act + cut * (gate * (1.0 + pre * (1.0 - gate))) * weighted(wb_ref[...], change)
     tan_ref[...] = tangent
-    nav_ref[...] = weighted(wav_ref[...], tangent)
+    nav_ref[...] = weighted_t(jnp.concatenate([we_ref[...], wv_ref[...]], axis=0), tangent)
 
 
 def k_energy(
@@ -541,9 +543,7 @@
 ):
     packed = pack(positions, species, send_lists, pair_center, pair_partner, pair_slot_live)
     here = spots()
-    zeros = jnp.zeros((2, 128), F32)
-    wb = jnp.concatenate([w_basis, emb_center, zeros, emb_partner, zeros], axis=0)
-    wav = jnp.concatenate([w_env, w_value], axis=1)
+    channels = (w_env.T, w_value.T)
     wo = w_out.reshape(128, 1)
 
     packed = send(packed, MOVE_IN)
@@ -558,8 +558,10 @@
         part,
         *ghosts,
         column,
-        wb,
-        wav,
+        w_basis,
+        emb_center,
+        emb_partner,
+        *channels,
     )
     ei, ej, latent, hid, tangent, nav = call(
         k_own_env,
@@ -568,8 +570,8 @@
         scal,
         pre,
         av,
-        wb,
-        wav,
+        w_basis,
+        *channels,
         w_mix,
     )
     low, high = low.reshape(1, 2, 2, 8, 192), high.reshape(1, 2, 2, 8, 192)

time: 119 us -> 118 us (level)
  local copies, waits for them, and re-layouts: 1.66 us -> 0.18 us
  waiting for transfers between devices: 41 us -> 42.2 us
    unnamed x16 -> x14, local copies, waits for them, and re-layouts: 1.47 us -> 0.04 us
    ppermute x34, waiting for transfers between devices: 41 us -> 42.2 us  [send(): return lax.ppermute(x, AXES, pairs)]
  transfers between devices with their start and end apart: 34 -> 34, of which waited for: 17 -> 19; matrix products, arithmetic and copies ran while one was open for 0% -> 0% of each run, Pallas kernels for 5% -> 5%
where the time goes in v9:
time: 118 us
  starting transfers between devices  62.2 us (53%)
  waiting for transfers between devices  42.2 us (36%)
  Pallas kernels  12 us (10%)
    ppermute x34, starting transfers between devices, send(): return lax.ppermute(x, AXES, pairs)  62.2 us
    ppermute x34, waiting for transfers between devices, send(): return lax.ppermute(x, AXES, pairs)  42.2 us
    pallas_call x10, Pallas kernels, call(): pl.pallas_call(kernel, out_shape=shapes, in_specs=[spec] * len(args), out...  10.4 us
  transfers between devices with their start and end apart: 34, of which 19 were waited for; matrix products, arithmetic and copies ran while one was open for 0% of the time, Pallas kernels for 5%

profile of v9, /device:TPU:71, one launch (start us, length us, event | category | flops | bytes accessed | tf_op | source)
XLA Modules:
  0.0 118.0 jit_solution(18250510432768649364)
XLA Ops:
  0.6 1.5 %k_pack.1 = f32[48,128]{1,0:T(8,128)} custom-call(f32[3,1,1,1,512]{4,3,2,1,0:T(1,128)} %pos_in.1, s32[1,1,1,512]{3,2,1,0:T(1,128)} %kind_in.1, s32[2,2,2,8]{3,2,1,0:T(2,128)} %names_in.1, s32[1,1,1,8,128]{4,3,2,1,0:T(8,128)} %center_in.1, s32[1,1,1,8,128]{4,3,2,1,0:T(8,128)} %partner_in.1, s32[1,1,1,8,128]{4,3,2,1,0:T(8,128)} %live_in.1), custom_call_target="tpu_custom_call" | custom-call | tf_op jit(solution)/shard_map/k_pack/pallas_call | solution.py:253
  2.1 8.3 %collective-permute-start = (f32[48,128]{1,0:T(8,128)}, f32[48,128]{1,0:T(8,128)S(1)}, u32[]{:S(2)}, u32[]{:S(2)}) collective-permute-start(f32[48,128]{1,0:T(8,128)} %k_pack.1), channel_id=1, source_target_pairs={{0,0},{1,32},{2,1},{3,33},{4,2},{5,34},{6,3},{7,35},{8,8},{9,40},{... | collective-permute-start | bytes 73736 | tf_op jit(solution)/shard_map/ppermute | solution.py:70
  10.5 7.4 %collective-permute-done.packed_ref = f32[48,128]{1,0:T(8,128)S(1)} collective-permute-done((f32[48,128]{1,0:T(8,128)}, f32[48,128]{1,0:T(8,128)S(1)}, u32[]{:S(2)}, u32[]{:S(2)}) %collective-permute-start) | collective-permute-done | bytes 24608 | tf_op jit(solution)/shard_map/ppermute | solution.py:70
  18.2 0.7 collective-permute-start.3
  18.9 1.5 %collective-permute-start.1 = (f32[1,2,2,8,128]{4,3,2,1,0:T(8,128)S(1)}, f32[1,2,2,8,128]{4,3,2,1,0:T(8,128)S(1)}, u32[]{:S(2)}, u32[]{:S(2)}) collective-permute-start(f32[1,2,2,8,128]{4,3,2,1,0:T(8,128)S(1)} %get-tuple-element.107), channel_id=1, source_target_pairs={{0,64},{32,0},{64,128},{96,32},{128,192},{160,96},{192,256},{224,1... | collective-permute-start | bytes 49160 | tf_op jit(solution)/shard_map/ppermute | solution.py:70
  20.3 1.1 collective-permute-done.2
  21.5 4.6 %collective-permute-start.6 = (f32[4,1,2,8,128]{4,3,2,1,0:T(8,128)S(1)}, f32[4,1,2,8,128]{4,3,2,1,0:T(8,128)S(1)}, u32[]{:S(2)}, u32[]{:S(2)}) collective-permute-start(f32[4,1,2,8,128]{4,3,2,1,0:T(8,128)S(1)} %get-tuple-element.98), channel_id=1, source_target_pairs={{0,24},{32,56},{64,88},{96,120},{128,152},{160,184},{192,216},{224... | collective-permute-start | bytes 98312 | tf_op jit(solution)/shard_map/ppermute | solution.py:70
  26.2 3.8 %collective-permute-start.4 = (f32[4,1,2,8,128]{4,3,2,1,0:T(8,128)S(1)}, f32[4,1,2,8,128]{4,3,2,1,0:T(8,128)S(1)}, u32[]{:S(2)}, u32[]{:S(2)}) collective-permute-start(f32[4,1,2,8,128]{4,3,2,1,0:T(8,128)S(1)} %get-tuple-element.99), channel_id=1, source_target_pairs={{0,8},{32,0},{64,72},{96,64},{128,136},{160,128},{192,200},{224,19... | collective-permute-start | bytes 98312 | tf_op jit(solution)/shard_map/ppermute | solution.py:70
  30.0 0.9 collective-permute-done.4
  31.2 2.7 %collective-permute-start.8 = (f32[4,4,8,128]{3,2,1,0:T(8,128)S(1)}, f32[4,4,8,128]{3,2,1,0:T(8,128)S(1)}, u32[]{:S(2)}, u32[]{:S(2)}) collective-permute-start(f32[4,4,8,128]{3,2,1,0:T(8,128)S(1)} %get-tuple-element.82), channel_id=1, source_target_pairs={{32,0},{1,32},{33,1},{2,33},{34,2},{3,34},{35,3},{0,35},{40,8},{9,... | collective-permute-start | bytes 196616 | tf_op jit(solution)/shard_map/ppermute | solution.py:70
  34.0 5.9 %collective-permute-start.7 = (f32[4,4,8,128]{3,2,1,0:T(8,128)S(1)}, f32[4,4,8,128]{3,2,1,0:T(8,128)S(1)}, u32[]{:S(2)}, u32[]{:S(2)}) collective-permute-start(f32[4,4,8,128]{3,2,1,0:T(8,128)S(1)} %get-tuple-element.83), channel_id=1, source_target_pairs={{0,32},{32,1},{1,33},{33,2},{2,34},{34,3},{3,35},{35,0},{8,40},{40... | collective-permute-start | bytes 196616 | tf_op jit(solution)/shard_map/ppermute | solution.py:70
  40.3 1.5 %collective-permute-done.8 = f32[4,4,8,128]{3,2,1,0:T(8,128)S(1)} collective-permute-done((f32[4,4,8,128]{3,2,1,0:T(8,128)S(1)}, f32[4,4,8,128]{3,2,1,0:T(8,128)S(1)}, u32[]{:S(2)}, u32[]{:S(2)}) %collective-permute-start.8) | collective-permute-done | bytes 65568 | tf_op jit(solution)/shard_map/ppermute | solution.py:70
  41.9 1.2 %k_features.1 = (f32[32,192]{1,0:T(8,128)S(1)}, f32[32,192]{1,0:T(8,128)S(1)}, f32[8,1024]{1,0:T(8,128)S(1)}, f32[128,1024]{1,0:T(8,128)S(1)}, f32[128,1024]{1,0:T(8,128)S(1)}) custom-call(f32[48,128]{1,0:T(8,128)S(1)} %collective-permute-done.packed_ref, f32[8,1024]{1,0:T(8,128)S(1)} %k_own_pairs.1.part_ref, f32[128,128]{1,0:T(8,128)S(1)} %bitcast.58, ...), custom_call_target="tpu_custom_call" | custom-call | tf_op jit(solution)/shard_map/k_features/pallas_call | solution.py:519
  43.1 0.7 collective-permute-start.11
  43.8 1.8 %collective-permute-start.9 = (f32[1,2,2,8,192]{4,3,2,1,0:T(8,128)S(1)}, f32[1,2,2,8,192]{4,3,2,1,0:T(8,128)S(1)}, u32[]{:S(2)}, u32[]{:S(2)}) collective-permute-start(f32[1,2,2,8,192]{4,3,2,1,0:T(8,128)S(1)} %get-tuple-element.97), channel_id=1, source_target_pairs={{0,64},{32,0},{64,128},{96,32},{128,192},{160,96},{192,256},{224,1... | collective-permute-start | bytes 73736 | tf_op jit(solution)/shard_map/ppermute | solution.py:70
  45.6 1.3 %collective-permute-done.10 = f32[1,2,2,8,192]{4,3,2,1,0:T(8,128)S(1)} collective-permute-done((f32[1,2,2,8,192]{4,3,2,1,0:T(8,128)S(1)}, f32[1,2,2,8,192]{4,3,2,1,0:T(8,128)S(1)}, u32[]{:S(2)}, u32[]{:S(2)}) %collective-permute-start.10) | collective-permute-done | bytes 24608 | tf_op jit(solution)/shard_map/ppermute | solution.py:70
  46.9 2.8 %collective-permute-start.14 = (f32[4,1,2,8,192]{4,3,2,1,0:T(8,128)S(1)}, f32[4,1,2,8,192]{4,3,2,1,0:T(8,128)S(1)}, u32[]{:S(2)}, u32[]{:S(2)}) collective-permute-start(f32[4,1,2,8,192]{4,3,2,1,0:T(8,128)S(1)} %get-tuple-element.79), channel_id=1, source_target_pairs={{0,24},{32,56},{64,88},{96,120},{128,152},{160,184},{192,216},{224... | collective-permute-start | bytes 147464 | tf_op jit(solution)/shard_map/ppermute | solution.py:70
  49.7 1.6 %collective-permute-start.12 = (f32[4,1,2,8,192]{4,3,2,1,0:T(8,128)S(1)}, f32[4,1,2,8,192]{4,3,2,1,0:T(8,128)S(1)}, u32[]{:S(2)}, u32[]{:S(2)}) collective-permute-start(f32[4,1,2,8,192]{4,3,2,1,0:T(8,128)S(1)} %get-tuple-element.80), channel_id=1, source_target_pairs={{0,8},{32,0},{64,72},{96,64},{128,136},{160,128},{192,200},{224,19... | collective-permute-start | bytes 147464 | tf_op jit(solution)/shard_map/ppermute | solution.py:70
  51.3 1.9 %collective-permute-done.14 = f32[4,1,2,8,192]{4,3,2,1,0:T(8,128)S(1)} collective-permute-done((f32[4,1,2,8,192]{4,3,2,1,0:T(8,128)S(1)}, f32[4,1,2,8,192]{4,3,2,1,0:T(8,128)S(1)}, u32[]{:S(2)}, u32[]{:S(2)}) %collective-permute-start.14) | collective-permute-done | bytes 49184 | tf_op jit(solution)/shard_map/ppermute | solution.py:70
  53.2 2.4 %collective-permute-start.16 = (f32[4,4,8,192]{3,2,1,0:T(8,128)S(1)}, f32[4,4,8,192]{3,2,1,0:T(8,128)S(1)}, u32[]{:S(2)}, u32[]{:S(2)}) collective-permute-start(f32[4,4,8,192]{3,2,1,0:T(8,128)S(1)} %get-tuple-element.67), channel_id=1, source_target_pairs={{32,0},{1,32},{33,1},{2,33},{34,2},{3,34},{35,3},{0,35},{40,8},{9,... | collective-permute-start | bytes 294920 | tf_op jit(solution)/shard_map/ppermute | solution.py:70
  55.7 5.0 %collective-permute-start.15 = (f32[4,4,8,192]{3,2,1,0:T(8,128)S(1)}, f32[4,4,8,192]{3,2,1,0:T(8,128)S(1)}, u32[]{:S(2)}, u32[]{:S(2)}) collective-permute-start(f32[4,4,8,192]{3,2,1,0:T(8,128)S(1)} %get-tuple-element.68), channel_id=1, source_target_pairs={{0,32},{32,1},{1,33},{33,2},{2,34},{34,3},{3,35},{35,0},{8,40},{40... | collective-permute-start | bytes 294920 | tf_op jit(solution)/shard_map/ppermute | solution.py:70
  60.8 2.2 %k_own_env.1 = (f32[192,1024]{1,0:T(8,128)S(1)}, f32[192,1024]{1,0:T(8,128)S(1)}, f32[128,1024]{1,0:T(8,128)S(1)}, f32[128,1024]{1,0:T(8,128)S(1)}, f32[128,1024]{1,0:T(8,128)S(1)}, /*index=5*/f32[128,1024]{1,0:T(8,128)S(1)}) custom-call(f32[48,128]{1,0:T(8,128)S(1)} %collective-permute-done.packed_ref, f32[8,1024]{1,0:T(8,128)S(1)} %get-tuple-element.36.scal_ref, ...), custom_call_target="tpu_custom_call" | custom-call | tf_op jit(solution)/shard_map/k_own_env/pallas_call | solution.py:519
  63.3 1.8 %k_energy.1 = (f32[128,192]{1,0:T(8,128)S(1)}, f32[128,192]{1,0:T(8,128)S(1)}, f32[256,192]{1,0:T(8,128)S(1)}, f32[192,1024]{1,0:T(8,128)S(1)}, f32[128,1024]{1,0:T(8,128)S(1)}, /*index=5*/f32[64,1024]{1,0:T(8,128)S(1)}) custom-call(f32[48,128]{1,0:T(8,128)S(1)} %collective-permute-done.packed_ref, f32[8,1024]{1,0:T(8,128)S(1)} %get-tuple-element.36.scal_ref, ...), custom_call_target="tpu_custom_call" | custom-call | tf_op jit(solution)/shard_map/k_energy/pallas_call | solution.py:519
  65.1 3.0 %collective-permute-start.17 = (f32[4,4,8,192]{3,2,1,0:T(8,128)S(1)}, f32[4,4,8,192]{3,2,1,0:T(8,128)S(1)}, u32[]{:S(2)}, u32[]{:S(2)}) collective-permute-start(f32[4,4,8,192]{3,2,1,0:T(8,128)S(1)} %bitcast.60), channel_id=1, source_target_pairs={{0,32},{32,1},{1,33},{33,2},{2,34},{34,3},{3,35},{35,0},{8,40},{40... | collective-permute-start | bytes 294920 | tf_op jit(solution)/shard_map/ppermute | solution.py:70
  68.1 2.2 %k_direct.1 = (f32[8,1024]{1,0:T(8,128)S(1)}, f32[4,512]{1,0:T(4,128)S(1)}) custom-call(f32[48,128]{1,0:T(8,128)S(1)} %collective-permute-done.packed_ref, f32[8,1024]{1,0:T(8,128)S(1)} %get-tuple-element.36.scal_ref, f32[128,1024]{1,0:T(8,128)S(1)} %get-tuple-element.37.av_ref, f32[128,1024]{1,0:T(8,128)S(1)} %get-tuple-element.39.nav_ref, ...), custom_call_target="tpu_custom_call" | custom-call | tf_op jit(solution)/shard_map/k_direct/pallas_call | solution.py:519
  70.3 3.4 %collective-permute-done.18 = f32[4,4,8,192]{3,2,1,0:T(8,128)S(1)} collective-permute-done((f32[4,4,8,192]{3,2,1,0:T(8,128)S(1)}, f32[4,4,8,192]{3,2,1,0:T(8,128)S(1)}, u32[]{:S(2)}, u32[]{:S(2)}) %collective-permute-start.18) | collective-permute-done | bytes 98336 | tf_op jit(solution)/shard_map/ppermute | solution.py:70
  73.8 3.7 %collective-permute-start.21 = (f32[4,1,2,8,192]{4,3,2,1,0:T(8,128)S(1)}, f32[4,1,2,8,192]{4,3,2,1,0:T(8,128)S(1)}, u32[]{:S(2)}, u32[]{:S(2)}) collective-permute-start(f32[4,1,2,8,192]{4,3,2,1,0:T(8,128)S(1)} %get-tuple-element.64), channel_id=1, source_target_pairs={{0,24},{32,56},{64,88},{96,120},{128,152},{160,184},{192,216},{224... | collective-permute-start | bytes 147464 | tf_op jit(solution)/shard_map/ppermute | solution.py:70
  77.5 1.5 %collective-permute-start.20 = (f32[4,1,2,8,192]{4,3,2,1,0:T(8,128)S(1)}, f32[4,1,2,8,192]{4,3,2,1,0:T(8,128)S(1)}, u32[]{:S(2)}, u32[]{:S(2)}) collective-permute-start(f32[4,1,2,8,192]{4,3,2,1,0:T(8,128)S(1)} %get-tuple-element.66), channel_id=1, source_target_pairs={{8,0},{0,32},{72,64},{64,96},{136,128},{128,160},{200,192},{192,22... | collective-permute-start | bytes 147464 | tf_op jit(solution)/shard_map/ppermute | solution.py:70
  78.9 1.0 collective-permute-done.21
  80.0 0.6 collective-permute-done.19
  80.7 0.7 collective-permute-start.24
  81.3 1.8 %collective-permute-start.22 = (f32[1,2,2,8,192]{4,3,2,1,0:T(8,128)S(1)}, f32[1,2,2,8,192]{4,3,2,1,0:T(8,128)S(1)}, u32[]{:S(2)}, u32[]{:S(2)}) collective-permute-start(f32[1,2,2,8,192]{4,3,2,1,0:T(8,128)S(1)} %get-tuple-element.77), channel_id=1, source_target_pairs={{0,64},{32,0},{64,128},{96,32},{128,192},{160,96},{192,256},{224,1... | collective-permute-start | bytes 73736 | tf_op jit(solution)/shard_map/ppermute | solution.py:70
  83.1 1.0 collective-permute-done.22
  84.1 3.3 %collective-permute-done.23 = f32[1,2,2,8,192]{4,3,2,1,0:T(8,128)S(1)} collective-permute-done((f32[1,2,2,8,192]{4,3,2,1,0:T(8,128)S(1)}, f32[1,2,2,8,192]{4,3,2,1,0:T(8,128)S(1)}, u32[]{:S(2)}, u32[]{:S(2)}) %collective-permute-start.23) | collective-permute-done | bytes 24608 | tf_op jit(solution)/shard_map/ppermute | solution.py:70
  87.5 1.0 k_env_back.1
  88.5 0.5 collective-permute-start.26
  89.0 0.6 k_own_force.1.own_ref
  89.8 3.6 %collective-permute-done.26 = f32[4,4,8,128]{3,2,1,0:T(8,128)S(1)} collective-permute-done((f32[4,4,8,128]{3,2,1,0:T(8,128)S(1)}, f32[4,4,8,128]{3,2,1,0:T(8,128)S(1)}, u32[]{:S(2)}, u32[]{:S(2)}) %collective-permute-start.26) | collective-permute-done | bytes 65568 | tf_op jit(solution)/shard_map/ppermute | solution.py:70
  93.5 2.8 %collective-permute-start.29 = (f32[4,1,2,8,128]{4,3,2,1,0:T(8,128)S(1)}, f32[4,1,2,8,128]{4,3,2,1,0:T(8,128)S(1)}, u32[]{:S(2)}, u32[]{:S(2)}) collective-permute-start(f32[4,1,2,8,128]{4,3,2,1,0:T(8,128)S(1)} %get-tuple-element.73), channel_id=1, source_target_pairs={{0,24},{32,56},{64,88},{96,120},{128,152},{160,184},{192,216},{224... | collective-permute-start | bytes 98312 | tf_op jit(solution)/shard_map/ppermute | solution.py:70
  96.3 1.5 %collective-permute-start.28 = (f32[4,1,2,8,128]{4,3,2,1,0:T(8,128)S(1)}, f32[4,1,2,8,128]{4,3,2,1,0:T(8,128)S(1)}, u32[]{:S(2)}, u32[]{:S(2)}) collective-permute-start(f32[4,1,2,8,128]{4,3,2,1,0:T(8,128)S(1)} %get-tuple-element.75), channel_id=1, source_target_pairs={{8,0},{0,32},{72,64},{64,96},{136,128},{128,160},{200,192},{192,22... | collective-permute-start | bytes 98312 | tf_op jit(solution)/shard_map/ppermute | solution.py:70
  97.7 1.6 %collective-permute-done.29 = f32[4,1,2,8,128]{4,3,2,1,0:T(8,128)S(1)} collective-permute-done((f32[4,1,2,8,128]{4,3,2,1,0:T(8,128)S(1)}, f32[4,1,2,8,128]{4,3,2,1,0:T(8,128)S(1)}, u32[]{:S(2)}, u32[]{:S(2)}) %collective-permute-start.29) | collective-permute-done | bytes 32800 | tf_op jit(solution)/shard_map/ppermute | solution.py:70
  99.4 0.7 collective-permute-start.32
  100.1 2.5 %collective-permute-start.30 = (f32[1,2,2,8,128]{4,3,2,1,0:T(8,128)S(1)}, f32[1,2,2,8,128]{4,3,2,1,0:T(8,128)S(1)}, u32[]{:S(2)}, u32[]{:S(2)}) collective-permute-start(f32[1,2,2,8,128]{4,3,2,1,0:T(8,128)S(1)} %get-tuple-element.93), channel_id=1, source_target_pairs={{0,64},{32,0},{64,128},{96,32},{128,192},{160,96},{192,256},{224,1... | collective-permute-start | bytes 49160 | tf_op jit(solution)/shard_map/ppermute | solution.py:70
  102.5 0.9 collective-permute-done.30
  103.4 4.0 %collective-permute-done.31 = f32[1,2,2,8,128]{4,3,2,1,0:T(8,128)S(1)} collective-permute-done((f32[1,2,2,8,128]{4,3,2,1,0:T(8,128)S(1)}, f32[1,2,2,8,128]{4,3,2,1,0:T(8,128)S(1)}, u32[]{:S(2)}, u32[]{:S(2)}) %collective-permute-start.31) | collective-permute-done | bytes 16416 | tf_op jit(solution)/shard_map/ppermute | solution.py:70
  107.6 1.9 %collective-permute-start.33 = (f32[16,128]{1,0:T(8,128)S(1)}, f32[16,128]{1,0:T(8,128)S(1)}, u32[]{:S(2)}, u32[]{:S(2)}) collective-permute-start(f32[16,128]{1,0:T(8,128)S(1)} %k_force.1), channel_id=1, source_target_pairs={{0,0},{32,1},{1,2},{33,3},{2,4},{34,5},{3,6},{35,7},{8,8},{40,9},{... | collective-permute-start | bytes 24584 | tf_op jit(solution)/shard_map/ppermute | solution.py:70
  109.6 7.9 %collective-permute-done.33.in_ref = f32[16,128]{1,0:T(8,128)S(1)} collective-permute-done((f32[16,128]{1,0:T(8,128)S(1)}, f32[16,128]{1,0:T(8,128)S(1)}, u32[]{:S(2)}, u32[]{:S(2)}) %collective-permute-start.33) | collective-permute-done | bytes 8224 | tf_op jit(solution)/shard_map/ppermute | solution.py:70
  117.4 0.6 k_unpack.1
  (74 shorter events, 2.4 us)
Async XLA Ops:
  2.1 15.8 %collective-permute-start = (f32[48,128]{1,0:T(8,128)}, f32[48,128]{1,0:T(8,128)S(1)}, u32[]{:S(2)}, u32[]{:S(2)}) collective-permute-start(f32[48,128]{1,0:T(8,128)} %k_pack.1), channel_id=1, source_target_pairs={{0,0},{1,32},{2,1},{3,33},{4,2},{5,34},{6,3},{7,35},{8,8},{9,40},{... | collective-permute-start | bytes 73736 | tf_op jit(solution)/shard_map/ppermute | solution.py:70
  18.2 2.2 %collective-permute-start.3 = (f32[1,2,2,8,128]{4,3,2,1,0:T(8,128)S(1)}, f32[1,2,2,8,128]{4,3,2,1,0:T(8,128)S(1)}, u32[]{:S(2)}, u32[]{:S(2)}) collective-permute-start(f32[1,2,2,8,128]{4,3,2,1,0:T(8,128)S(1)} %get-tuple-element.105), channel_id=1, source_target_pairs={{0,452},{32,484},{452,0},{484,32},{8,460},{40,492},{460,8},{492,40... | collective-permute-start | bytes 49160 | tf_op jit(solution)/shard_map/ppermute | solution.py:70
  18.8 2.6 %collective-permute-start.2 = (f32[1,2,2,8,128]{4,3,2,1,0:T(8,128)S(1)}, f32[1,2,2,8,128]{4,3,2,1,0:T(8,128)S(1)}, u32[]{:S(2)}, u32[]{:S(2)}) collective-permute-start(f32[1,2,2,8,128]{4,3,2,1,0:T(8,128)S(1)} %get-tuple-element.106), channel_id=1, source_target_pairs={{64,0},{0,32},{128,64},{32,96},{192,128},{96,160},{256,192},{160,2... | collective-permute-start | bytes 49160 | tf_op jit(solution)/shard_map/ppermute | solution.py:70
  18.9 2.6 %collective-permute-start.1 = (f32[1,2,2,8,128]{4,3,2,1,0:T(8,128)S(1)}, f32[1,2,2,8,128]{4,3,2,1,0:T(8,128)S(1)}, u32[]{:S(2)}, u32[]{:S(2)}) collective-permute-start(f32[1,2,2,8,128]{4,3,2,1,0:T(8,128)S(1)} %get-tuple-element.107), channel_id=1, source_target_pairs={{0,64},{32,0},{64,128},{96,32},{128,192},{160,96},{192,256},{224,1... | collective-permute-start | bytes 49160 | tf_op jit(solution)/shard_map/ppermute | solution.py:70
  21.5 8.4 %collective-permute-start.6 = (f32[4,1,2,8,128]{4,3,2,1,0:T(8,128)S(1)}, f32[4,1,2,8,128]{4,3,2,1,0:T(8,128)S(1)}, u32[]{:S(2)}, u32[]{:S(2)}) collective-permute-start(f32[4,1,2,8,128]{4,3,2,1,0:T(8,128)S(1)} %get-tuple-element.98), channel_id=1, source_target_pairs={{0,24},{32,56},{64,88},{96,120},{128,152},{160,184},{192,216},{224... | collective-permute-start | bytes 98312 | tf_op jit(solution)/shard_map/ppermute | solution.py:70
  26.2 4.6 %collective-permute-start.4 = (f32[4,1,2,8,128]{4,3,2,1,0:T(8,128)S(1)}, f32[4,1,2,8,128]{4,3,2,1,0:T(8,128)S(1)}, u32[]{:S(2)}, u32[]{:S(2)}) collective-permute-start(f32[4,1,2,8,128]{4,3,2,1,0:T(8,128)S(1)} %get-tuple-element.99), channel_id=1, source_target_pairs={{0,8},{32,0},{64,72},{96,64},{128,136},{160,128},{192,200},{224,19... | collective-permute-start | bytes 98312 | tf_op jit(solution)/shard_map/ppermute | solution.py:70
  29.9 1.2 %collective-permute-start.5 = (f32[4,1,2,8,128]{4,3,2,1,0:T(8,128)S(1)}, f32[4,1,2,8,128]{4,3,2,1,0:T(8,128)S(1)}, u32[]{:S(2)}, u32[]{:S(2)}) collective-permute-start(f32[4,1,2,8,128]{4,3,2,1,0:T(8,128)S(1)} %get-tuple-element.100), channel_id=1, source_target_pairs={{8,0},{0,32},{72,64},{64,96},{136,128},{128,160},{200,192},{192,22... | collective-permute-start | bytes 98312 | tf_op jit(solution)/shard_map/ppermute | solution.py:70
  31.2 10.6 %copy-start.3 = (f32[8,128]{1,0:T(8,128)S(1)}, f32[8,128]{1,0:T(8,128)}, u32[]{:S(2)}) copy-start(f32[8,128]{1,0:T(8,128)} %wb_ref.3) | copy-start | bytes 12292
  31.2 10.6 %copy-start.4 = (f32[6,128]{1,0:T(8,128)S(1)}, f32[6,128]{1,0:T(8,128)}, u32[]{:S(2)}) copy-start(f32[6,128]{1,0:T(8,128)} %ec_ref.1) | copy-start | bytes 9220
  31.2 10.6 %copy-start.5 = (f32[6,128]{1,0:T(8,128)S(1)}, f32[6,128]{1,0:T(8,128)}, u32[]{:S(2)}) copy-start(f32[6,128]{1,0:T(8,128)} %ep_ref.1) | copy-start | bytes 9220
  31.2 10.6 %collective-permute-start.8 = (f32[4,4,8,128]{3,2,1,0:T(8,128)S(1)}, f32[4,4,8,128]{3,2,1,0:T(8,128)S(1)}, u32[]{:S(2)}, u32[]{:S(2)}) collective-permute-start(f32[4,4,8,128]{3,2,1,0:T(8,128)S(1)} %get-tuple-element.82), channel_id=1, source_target_pairs={{32,0},{1,32},{33,1},{2,33},{34,2},{3,34},{35,3},{0,35},{40,8},{9,... | collective-permute-start | bytes 196616 | tf_op jit(solution)/shard_map/ppermute | solution.py:70
  34.0 7.8 %copy-start.1 = (f32[128,64]{0,1:T(8,128)S(1)}, f32[128,64]{0,1:T(8,128)}, u32[]{:S(2)}) copy-start(f32[128,64]{0,1:T(8,128)} %param.22) | copy-start | bytes 98308
  34.0 7.9 %copy-start.2 = (f32[128,64]{0,1:T(8,128)S(1)}, f32[128,64]{0,1:T(8,128)}, u32[]{:S(2)}) copy-start(f32[128,64]{0,1:T(8,128)} %param.23) | copy-start | bytes 98308
  34.0 7.8 %collective-permute-start.7 = (f32[4,4,8,128]{3,2,1,0:T(8,128)S(1)}, f32[4,4,8,128]{3,2,1,0:T(8,128)S(1)}, u32[]{:S(2)}, u32[]{:S(2)}) collective-permute-start(f32[4,4,8,128]{3,2,1,0:T(8,128)S(1)} %get-tuple-element.83), channel_id=1, source_target_pairs={{0,32},{32,1},{1,33},{33,2},{2,34},{34,3},{3,35},{35,0},{8,40},{40... | collective-permute-start | bytes 196616 | tf_op jit(solution)/shard_map/ppermute | solution.py:70
  43.1 2.5 %collective-permute-start.11 = (f32[1,2,2,8,192]{4,3,2,1,0:T(8,128)S(1)}, f32[1,2,2,8,192]{4,3,2,1,0:T(8,128)S(1)}, u32[]{:S(2)}, u32[]{:S(2)}) collective-permute-start(f32[1,2,2,8,192]{4,3,2,1,0:T(8,128)S(1)} %get-tuple-element.95), channel_id=1, source_target_pairs={{0,452},{32,484},{452,0},{484,32},{8,460},{40,492},{460,8},{492,40... | collective-permute-start | bytes 73736 | tf_op jit(solution)/shard_map/ppermute | solution.py:70
  43.8 3.1 %collective-permute-start.10 = (f32[1,2,2,8,192]{4,3,2,1,0:T(8,128)S(1)}, f32[1,2,2,8,192]{4,3,2,1,0:T(8,128)S(1)}, u32[]{:S(2)}, u32[]{:S(2)}) collective-permute-start(f32[1,2,2,8,192]{4,3,2,1,0:T(8,128)S(1)} %get-tuple-element.96), channel_id=1, source_target_pairs={{64,0},{0,32},{128,64},{32,96},{192,128},{96,160},{256,192},{160,2... | collective-permute-start | bytes 73736 | tf_op jit(solution)/shard_map/ppermute | solution.py:70
  43.8 3.0 %collective-permute-start.9 = (f32[1,2,2,8,192]{4,3,2,1,0:T(8,128)S(1)}, f32[1,2,2,8,192]{4,3,2,1,0:T(8,128)S(1)}, u32[]{:S(2)}, u32[]{:S(2)}) collective-permute-start(f32[1,2,2,8,192]{4,3,2,1,0:T(8,128)S(1)} %get-tuple-element.97), channel_id=1, source_target_pairs={{0,64},{32,0},{64,128},{96,32},{128,192},{160,96},{192,256},{224,1... | collective-permute-start | bytes 73736 | tf_op jit(solution)/shard_map/ppermute | solution.py:70
  46.9 6.2 %collective-permute-start.14 = (f32[4,1,2,8,192]{4,3,2,1,0:T(8,128)S(1)}, f32[4,1,2,8,192]{4,3,2,1,0:T(8,128)S(1)}, u32[]{:S(2)}, u32[]{:S(2)}) collective-permute-start(f32[4,1,2,8,192]{4,3,2,1,0:T(8,128)S(1)} %get-tuple-element.79), channel_id=1, source_target_pairs={{0,24},{32,56},{64,88},{96,120},{128,152},{160,184},{192,216},{224... | collective-permute-start | bytes 147464 | tf_op jit(solution)/shard_map/ppermute | solution.py:70
  49.7 3.4 %collective-permute-start.12 = (f32[4,1,2,8,192]{4,3,2,1,0:T(8,128)S(1)}, f32[4,1,2,8,192]{4,3,2,1,0:T(8,128)S(1)}, u32[]{:S(2)}, u32[]{:S(2)}) collective-permute-start(f32[4,1,2,8,192]{4,3,2,1,0:T(8,128)S(1)} %get-tuple-element.80), channel_id=1, source_target_pairs={{0,8},{32,0},{64,72},{96,64},{128,136},{160,128},{192,200},{224,19... | collective-permute-start | bytes 147464 | tf_op jit(solution)/shard_map/ppermute | solution.py:70
  51.3 1.9 %collective-permute-start.13 = (f32[4,1,2,8,192]{4,3,2,1,0:T(8,128)S(1)}, f32[4,1,2,8,192]{4,3,2,1,0:T(8,128)S(1)}, u32[]{:S(2)}, u32[]{:S(2)}) collective-permute-start(f32[4,1,2,8,192]{4,3,2,1,0:T(8,128)S(1)} %get-tuple-element.81), channel_id=1, source_target_pairs={{8,0},{0,32},{72,64},{64,96},{136,128},{128,160},{200,192},{192,22... | collective-permute-start | bytes 147464 | tf_op jit(solution)/shard_map/ppermute | solution.py:70
  53.2 7.6 %copy-start = (f32[192,128]{1,0:T(8,128)S(1)}, f32[192,128]{1,0:T(8,128)}, u32[]{:S(2)}) copy-start(f32[192,128]{1,0:T(8,128)} %wm_ref.5) | copy-start | bytes 294916
  53.2 10.1 %collective-permute-start.16 = (f32[4,4,8,192]{3,2,1,0:T(8,128)S(1)}, f32[4,4,8,192]{3,2,1,0:T(8,128)S(1)}, u32[]{:S(2)}, u32[]{:S(2)}) collective-permute-start(f32[4,4,8,192]{3,2,1,0:T(8,128)S(1)} %get-tuple-element.67), channel_id=1, source_target_pairs={{32,0},{1,32},{33,1},{2,33},{34,2},{3,34},{35,3},{0,35},{40,8},{9,... | collective-permute-start | bytes 294920 | tf_op jit(solution)/shard_map/ppermute | solution.py:70
  55.6 5.0 %copy-start.6 = (f32[128]{0:T(128)S(1)}, f32[128]{0:T(128)}, u32[]{:S(2)}) copy-start(f32[128]{0:T(128)} %param.25) | copy-start | bytes 1540
  55.7 7.7 %collective-permute-start.15 = (f32[4,4,8,192]{3,2,1,0:T(8,128)S(1)}, f32[4,4,8,192]{3,2,1,0:T(8,128)S(1)}, u32[]{:S(2)}, u32[]{:S(2)}) collective-permute-start(f32[4,4,8,192]{3,2,1,0:T(8,128)S(1)} %get-tuple-element.68), channel_id=1, source_target_pairs={{0,32},{32,1},{1,33},{33,2},{2,34},{34,3},{3,35},{35,0},{8,40},{40... | collective-permute-start | bytes 294920 | tf_op jit(solution)/shard_map/ppermute | solution.py:70
  65.1 5.2 %collective-permute-start.17 = (f32[4,4,8,192]{3,2,1,0:T(8,128)S(1)}, f32[4,4,8,192]{3,2,1,0:T(8,128)S(1)}, u32[]{:S(2)}, u32[]{:S(2)}) collective-permute-start(f32[4,4,8,192]{3,2,1,0:T(8,128)S(1)} %bitcast.60), channel_id=1, source_target_pairs={{0,32},{32,1},{1,33},{33,2},{2,34},{34,3},{3,35},{35,0},{8,40},{40... | collective-permute-start | bytes 294920 | tf_op jit(solution)/shard_map/ppermute | solution.py:70
  68.1 5.6 %collective-permute-start.18 = (f32[4,4,8,192]{3,2,1,0:T(8,128)S(1)}, f32[4,4,8,192]{3,2,1,0:T(8,128)S(1)}, u32[]{:S(2)}, u32[]{:S(2)}) collective-permute-start(f32[4,4,8,192]{3,2,1,0:T(8,128)S(1)} %bitcast.59), channel_id=1, source_target_pairs={{32,0},{1,32},{33,1},{2,33},{34,2},{3,34},{35,3},{0,35},{40,8},{9,... | collective-permute-start | bytes 294920 | tf_op jit(solution)/shard_map/ppermute | solution.py:70
  73.8 6.2 %collective-permute-start.21 = (f32[4,1,2,8,192]{4,3,2,1,0:T(8,128)S(1)}, f32[4,1,2,8,192]{4,3,2,1,0:T(8,128)S(1)}, u32[]{:S(2)}, u32[]{:S(2)}) collective-permute-start(f32[4,1,2,8,192]{4,3,2,1,0:T(8,128)S(1)} %get-tuple-element.64), channel_id=1, source_target_pairs={{0,24},{32,56},{64,88},{96,120},{128,152},{160,184},{192,216},{224... | collective-permute-start | bytes 147464 | tf_op jit(solution)/shard_map/ppermute | solution.py:70
  77.5 3.1 %collective-permute-start.19 = (f32[4,1,2,8,192]{4,3,2,1,0:T(8,128)S(1)}, f32[4,1,2,8,192]{4,3,2,1,0:T(8,128)S(1)}, u32[]{:S(2)}, u32[]{:S(2)}) collective-permute-start(f32[4,1,2,8,192]{4,3,2,1,0:T(8,128)S(1)} %get-tuple-element.65), channel_id=1, source_target_pairs={{0,8},{32,0},{64,72},{96,64},{128,136},{160,128},{192,200},{224,19... | collective-permute-start | bytes 147464 | tf_op jit(solution)/shard_map/ppermute | solution.py:70
  77.5 3.1 %collective-permute-start.20 = (f32[4,1,2,8,192]{4,3,2,1,0:T(8,128)S(1)}, f32[4,1,2,8,192]{4,3,2,1,0:T(8,128)S(1)}, u32[]{:S(2)}, u32[]{:S(2)}) collective-permute-start(f32[4,1,2,8,192]{4,3,2,1,0:T(8,128)S(1)} %get-tuple-element.66), channel_id=1, source_target_pairs={{8,0},{0,32},{72,64},{64,96},{136,128},{128,160},{200,192},{192,22... | collective-permute-start | bytes 147464 | tf_op jit(solution)/shard_map/ppermute | solution.py:70
  80.7 2.4 %collective-permute-start.24 = (f32[1,2,2,8,192]{4,3,2,1,0:T(8,128)S(1)}, f32[1,2,2,8,192]{4,3,2,1,0:T(8,128)S(1)}, u32[]{:S(2)}, u32[]{:S(2)}) collective-permute-start(f32[1,2,2,8,192]{4,3,2,1,0:T(8,128)S(1)} %get-tuple-element.76), channel_id=1, source_target_pairs={{0,452},{32,484},{452,0},{484,32},{8,460},{40,492},{460,8},{492,40... | collective-permute-start | bytes 73736 | tf_op jit(solution)/shard_map/ppermute | solution.py:70
  81.3 2.8 %collective-permute-start.22 = (f32[1,2,2,8,192]{4,3,2,1,0:T(8,128)S(1)}, f32[1,2,2,8,192]{4,3,2,1,0:T(8,128)S(1)}, u32[]{:S(2)}, u32[]{:S(2)}) collective-permute-start(f32[1,2,2,8,192]{4,3,2,1,0:T(8,128)S(1)} %get-tuple-element.77), channel_id=1, source_target_pairs={{0,64},{32,0},{64,128},{96,32},{128,192},{160,96},{192,256},{224,1... | collective-permute-start | bytes 73736 | tf_op jit(solution)/shard_map/ppermute | solution.py:70
  83.1 4.4 %collective-permute-start.23 = (f32[1,2,2,8,192]{4,3,2,1,0:T(8,128)S(1)}, f32[1,2,2,8,192]{4,3,2,1,0:T(8,128)S(1)}, u32[]{:S(2)}, u32[]{:S(2)}) collective-permute-start(f32[1,2,2,8,192]{4,3,2,1,0:T(8,128)S(1)} %get-tuple-element.78), channel_id=1, source_target_pairs={{64,0},{0,32},{128,64},{32,96},{192,128},{96,160},{256,192},{160,2... | collective-permute-start | bytes 73736 | tf_op jit(solution)/shard_map/ppermute | solution.py:70
  88.5 1.3 %collective-permute-start.25 = (f32[4,4,8,128]{3,2,1,0:T(8,128)S(1)}, f32[4,4,8,128]{3,2,1,0:T(8,128)S(1)}, u32[]{:S(2)}, u32[]{:S(2)}) collective-permute-start(f32[4,4,8,128]{3,2,1,0:T(8,128)S(1)} %bitcast.62), channel_id=1, source_target_pairs={{0,32},{32,1},{1,33},{33,2},{2,34},{34,3},{3,35},{35,0},{8,40},{40... | collective-permute-start | bytes 196616 | tf_op jit(solution)/shard_map/ppermute | solution.py:70
  88.5 4.9 %collective-permute-start.26 = (f32[4,4,8,128]{3,2,1,0:T(8,128)S(1)}, f32[4,4,8,128]{3,2,1,0:T(8,128)S(1)}, u32[]{:S(2)}, u32[]{:S(2)}) collective-permute-start(f32[4,4,8,128]{3,2,1,0:T(8,128)S(1)} %bitcast.61), channel_id=1, source_target_pairs={{32,0},{1,32},{33,1},{2,33},{34,2},{3,34},{35,3},{0,35},{40,8},{9,... | collective-permute-start | bytes 196616 | tf_op jit(solution)/shard_map/ppermute | solution.py:70
  93.5 5.9 %collective-permute-start.29 = (f32[4,1,2,8,128]{4,3,2,1,0:T(8,128)S(1)}, f32[4,1,2,8,128]{4,3,2,1,0:T(8,128)S(1)}, u32[]{:S(2)}, u32[]{:S(2)}) collective-permute-start(f32[4,1,2,8,128]{4,3,2,1,0:T(8,128)S(1)} %get-tuple-element.73), channel_id=1, source_target_pairs={{0,24},{32,56},{64,88},{96,120},{128,152},{160,184},{192,216},{224... | collective-permute-start | bytes 98312 | tf_op jit(solution)/shard_map/ppermute | solution.py:70
  96.3 3.1 %collective-permute-start.27 = (f32[4,1,2,8,128]{4,3,2,1,0:T(8,128)S(1)}, f32[4,1,2,8,128]{4,3,2,1,0:T(8,128)S(1)}, u32[]{:S(2)}, u32[]{:S(2)}) collective-permute-start(f32[4,1,2,8,128]{4,3,2,1,0:T(8,128)S(1)} %get-tuple-element.74), channel_id=1, source_target_pairs={{0,8},{32,0},{64,72},{96,64},{128,136},{160,128},{192,200},{224,19... | collective-permute-start | bytes 98312 | tf_op jit(solution)/shard_map/ppermute | solution.py:70
  96.3 3.0 %collective-permute-start.28 = (f32[4,1,2,8,128]{4,3,2,1,0:T(8,128)S(1)}, f32[4,1,2,8,128]{4,3,2,1,0:T(8,128)S(1)}, u32[]{:S(2)}, u32[]{:S(2)}) collective-permute-start(f32[4,1,2,8,128]{4,3,2,1,0:T(8,128)S(1)} %get-tuple-element.75), channel_id=1, source_target_pairs={{8,0},{0,32},{72,64},{64,96},{136,128},{128,160},{200,192},{192,22... | collective-permute-start | bytes 98312 | tf_op jit(solution)/shard_map/ppermute | solution.py:70
  99.4 3.2 %collective-permute-start.32 = (f32[1,2,2,8,128]{4,3,2,1,0:T(8,128)S(1)}, f32[1,2,2,8,128]{4,3,2,1,0:T(8,128)S(1)}, u32[]{:S(2)}, u32[]{:S(2)}) collective-permute-start(f32[1,2,2,8,128]{4,3,2,1,0:T(8,128)S(1)} %get-tuple-element.92), channel_id=1, source_target_pairs={{0,452},{32,484},{452,0},{484,32},{8,460},{40,492},{460,8},{492,40... | collective-permute-start | bytes 49160 | tf_op jit(solution)/shard_map/ppermute | solution.py:70
  100.1 3.4 %collective-permute-start.30 = (f32[1,2,2,8,128]{4,3,2,1,0:T(8,128)S(1)}, f32[1,2,2,8,128]{4,3,2,1,0:T(8,128)S(1)}, u32[]{:S(2)}, u32[]{:S(2)}) collective-permute-start(f32[1,2,2,8,128]{4,3,2,1,0:T(8,128)S(1)} %get-tuple-element.93), channel_id=1, source_target_pairs={{0,64},{32,0},{64,128},{96,32},{128,192},{160,96},{192,256},{224,1... | collective-permute-start | bytes 49160 | tf_op jit(solution)/shard_map/ppermute | solution.py:70
  102.5 4.8 %collective-permute-start.31 = (f32[1,2,2,8,128]{4,3,2,1,0:T(8,128)S(1)}, f32[1,2,2,8,128]{4,3,2,1,0:T(8,128)S(1)}, u32[]{:S(2)}, u32[]{:S(2)}) collective-permute-start(f32[1,2,2,8,128]{4,3,2,1,0:T(8,128)S(1)} %get-tuple-element.94), channel_id=1, source_target_pairs={{64,0},{0,32},{128,64},{32,96},{192,128},{96,160},{256,192},{160,2... | collective-permute-start | bytes 49160 | tf_op jit(solution)/shard_map/ppermute | solution.py:70
  107.6 9.8 %collective-permute-start.33 = (f32[16,128]{1,0:T(8,128)S(1)}, f32[16,128]{1,0:T(8,128)S(1)}, u32[]{:S(2)}, u32[]{:S(2)}) collective-permute-start(f32[16,128]{1,0:T(8,128)S(1)} %k_force.1), channel_id=1, source_target_pairs={{0,0},{32,1},{1,2},{33,3},{2,4},{34,5},{3,6},{35,7},{8,8},{40,9},{... | collective-permute-start | bytes 24584 | tf_op jit(solution)/shard_map/ppermute | solution.py:70

commit v10 on v9

--- a/solution.py
+++ b/solution.py
@@ -29,7 +29,7 @@
 
 def home(x, y, z):
     x, y, z = x % SHAPE[0], y % SHAPE[1], z % SHAPE[2]
-    return device(z // 2, y, x, z % 2)
+    return device((z // 2 + 1) % 4, y, x, z % 2)
 
 
 CELLS = [(x, y, z) for x in range(SHAPE[0]) for y in range(SHAPE[1]) for z in range(SHAPE[2])]

time: 118 us -> 117 us (level)
  the two profiles are of different devices: /device:TPU:71 before, /device:TPU:33 now
where the time goes in v10:
time: 117 us
  starting transfers between devices  68 us (58%)
  waiting for transfers between devices  35.3 us (30%)
  Pallas kernels  12 us (10%)
    ppermute x34, starting transfers between devices, send(): return lax.ppermute(x, AXES, pairs)  68 us
    ppermute x34, waiting for transfers between devices, send(): return lax.ppermute(x, AXES, pairs)  35.3 us
    pallas_call x10, Pallas kernels, call(): pl.pallas_call(kernel, out_shape=shapes, in_specs=[spec] * len(args), out...  10.5 us
  transfers between devices with their start and end apart: 34, of which 21 were waited for; matrix products, arithmetic and copies ran while one was open for 0% of the time, Pallas kernels for 5%

profile of v10, /device:TPU:33, one launch (start us, length us, event | category | flops | bytes accessed | tf_op | source)
XLA Modules:
  0.0 116.9 jit_solution(12565573271685795242)
XLA Ops:
  0.6 1.5 %k_pack.1 = f32[48,128]{1,0:T(8,128)} custom-call(f32[3,1,1,1,512]{4,3,2,1,0:T(1,128)} %pos_in.1, s32[1,1,1,512]{3,2,1,0:T(1,128)} %kind_in.1, s32[2,2,2,8]{3,2,1,0:T(2,128)} %names_in.1, s32[1,1,1,8,128]{4,3,2,1,0:T(8,128)} %center_in.1, s32[1,1,1,8,128]{4,3,2,1,0:T(8,128)} %partner_in.1, s32[1,1,1,8,128]{4,3,2,1,0:T(8,128)} %live_in.1), custom_call_target="tpu_custom_call" | custom-call | tf_op jit(solution)/shard_map/k_pack/pallas_call | solution.py:253
  2.1 6.4 %collective-permute-start = (f32[48,128]{1,0:T(8,128)}, f32[48,128]{1,0:T(8,128)S(1)}, u32[]{:S(2)}, u32[]{:S(2)}) collective-permute-start(f32[48,128]{1,0:T(8,128)} %k_pack.1), channel_id=1, source_target_pairs={{0,1},{1,33},{2,2},{3,34},{4,3},{5,35},{6,0},{7,32},{8,9},{9,41},{... | collective-permute-start | bytes 73736 | tf_op jit(solution)/shard_map/ppermute | solution.py:70
  8.6 11.6 %collective-permute-done.packed_ref = f32[48,128]{1,0:T(8,128)S(1)} collective-permute-done((f32[48,128]{1,0:T(8,128)}, f32[48,128]{1,0:T(8,128)S(1)}, u32[]{:S(2)}, u32[]{:S(2)}) %collective-permute-start) | collective-permute-done | bytes 24608 | tf_op jit(solution)/shard_map/ppermute | solution.py:70
  20.4 0.7 collective-permute-start.3
  21.1 1.6 %collective-permute-start.2 = (f32[1,2,2,8,128]{4,3,2,1,0:T(8,128)S(1)}, f32[1,2,2,8,128]{4,3,2,1,0:T(8,128)S(1)}, u32[]{:S(2)}, u32[]{:S(2)}) collective-permute-start(f32[1,2,2,8,128]{4,3,2,1,0:T(8,128)S(1)} %get-tuple-element.106), channel_id=1, source_target_pairs={{64,0},{0,32},{128,64},{32,96},{192,128},{96,160},{256,192},{160,2... | collective-permute-start | bytes 49160 | tf_op jit(solution)/shard_map/ppermute | solution.py:70
  22.7 1.4 %collective-permute-start.1 = (f32[1,2,2,8,128]{4,3,2,1,0:T(8,128)S(1)}, f32[1,2,2,8,128]{4,3,2,1,0:T(8,128)S(1)}, u32[]{:S(2)}, u32[]{:S(2)}) collective-permute-start(f32[1,2,2,8,128]{4,3,2,1,0:T(8,128)S(1)} %get-tuple-element.107), channel_id=1, source_target_pairs={{0,64},{32,0},{64,128},{96,32},{128,192},{160,96},{192,256},{224,1... | collective-permute-start | bytes 49160 | tf_op jit(solution)/shard_map/ppermute | solution.py:70
  24.1 1.1 collective-permute-done.2
  25.3 4.9 %collective-permute-start.6 = (f32[4,1,2,8,128]{4,3,2,1,0:T(8,128)S(1)}, f32[4,1,2,8,128]{4,3,2,1,0:T(8,128)S(1)}, u32[]{:S(2)}, u32[]{:S(2)}) collective-permute-start(f32[4,1,2,8,128]{4,3,2,1,0:T(8,128)S(1)} %get-tuple-element.98), channel_id=1, source_target_pairs={{0,24},{32,56},{64,88},{96,120},{128,152},{160,184},{192,216},{224... | collective-permute-start | bytes 98312 | tf_op jit(solution)/shard_map/ppermute | solution.py:70
  30.2 3.8 %collective-permute-start.4 = (f32[4,1,2,8,128]{4,3,2,1,0:T(8,128)S(1)}, f32[4,1,2,8,128]{4,3,2,1,0:T(8,128)S(1)}, u32[]{:S(2)}, u32[]{:S(2)}) collective-permute-start(f32[4,1,2,8,128]{4,3,2,1,0:T(8,128)S(1)} %get-tuple-element.99), channel_id=1, source_target_pairs={{0,8},{32,0},{64,72},{96,64},{128,136},{160,128},{192,200},{224,19... | collective-permute-start | bytes 98312 | tf_op jit(solution)/shard_map/ppermute | solution.py:70
  34.1 0.9 collective-permute-done.4
  35.4 3.1 %collective-permute-start.8 = (f32[4,4,8,128]{3,2,1,0:T(8,128)S(1)}, f32[4,4,8,128]{3,2,1,0:T(8,128)S(1)}, u32[]{:S(2)}, u32[]{:S(2)}) collective-permute-start(f32[4,4,8,128]{3,2,1,0:T(8,128)S(1)} %get-tuple-element.82), channel_id=1, source_target_pairs={{33,1},{2,33},{34,2},{3,34},{35,3},{0,35},{32,0},{1,32},{41,9},{10... | collective-permute-start | bytes 196616 | tf_op jit(solution)/shard_map/ppermute | solution.py:70
  38.5 5.0 %collective-permute-start.7 = (f32[4,4,8,128]{3,2,1,0:T(8,128)S(1)}, f32[4,4,8,128]{3,2,1,0:T(8,128)S(1)}, u32[]{:S(2)}, u32[]{:S(2)}) collective-permute-start(f32[4,4,8,128]{3,2,1,0:T(8,128)S(1)} %get-tuple-element.83), channel_id=1, source_target_pairs={{1,33},{33,2},{2,34},{34,3},{3,35},{35,0},{0,32},{32,1},{9,41},{41... | collective-permute-start | bytes 196616 | tf_op jit(solution)/shard_map/ppermute | solution.py:70
  43.9 1.5 %collective-permute-done.8 = f32[4,4,8,128]{3,2,1,0:T(8,128)S(1)} collective-permute-done((f32[4,4,8,128]{3,2,1,0:T(8,128)S(1)}, f32[4,4,8,128]{3,2,1,0:T(8,128)S(1)}, u32[]{:S(2)}, u32[]{:S(2)}) %collective-permute-start.8) | collective-permute-done | bytes 65568 | tf_op jit(solution)/shard_map/ppermute | solution.py:70
  45.5 1.2 %k_features.1 = (f32[32,192]{1,0:T(8,128)S(1)}, f32[32,192]{1,0:T(8,128)S(1)}, f32[8,1024]{1,0:T(8,128)S(1)}, f32[128,1024]{1,0:T(8,128)S(1)}, f32[128,1024]{1,0:T(8,128)S(1)}) custom-call(f32[48,128]{1,0:T(8,128)S(1)} %collective-permute-done.packed_ref, f32[8,1024]{1,0:T(8,128)S(1)} %k_own_pairs.1.part_ref, f32[128,128]{1,0:T(8,128)S(1)} %bitcast.58, ...), custom_call_target="tpu_custom_call" | custom-call | tf_op jit(solution)/shard_map/k_features/pallas_call | solution.py:519
  46.7 0.7 collective-permute-start.11
  47.4 1.9 %collective-permute-start.9 = (f32[1,2,2,8,192]{4,3,2,1,0:T(8,128)S(1)}, f32[1,2,2,8,192]{4,3,2,1,0:T(8,128)S(1)}, u32[]{:S(2)}, u32[]{:S(2)}) collective-permute-start(f32[1,2,2,8,192]{4,3,2,1,0:T(8,128)S(1)} %get-tuple-element.97), channel_id=1, source_target_pairs={{0,64},{32,0},{64,128},{96,32},{128,192},{160,96},{192,256},{224,1... | collective-permute-start | bytes 73736 | tf_op jit(solution)/shard_map/ppermute | solution.py:70
  49.3 1.3 %collective-permute-done.10 = f32[1,2,2,8,192]{4,3,2,1,0:T(8,128)S(1)} collective-permute-done((f32[1,2,2,8,192]{4,3,2,1,0:T(8,128)S(1)}, f32[1,2,2,8,192]{4,3,2,1,0:T(8,128)S(1)}, u32[]{:S(2)}, u32[]{:S(2)}) %collective-permute-start.10) | collective-permute-done | bytes 24608 | tf_op jit(solution)/shard_map/ppermute | solution.py:70
  50.6 3.1 %collective-permute-start.14 = (f32[4,1,2,8,192]{4,3,2,1,0:T(8,128)S(1)}, f32[4,1,2,8,192]{4,3,2,1,0:T(8,128)S(1)}, u32[]{:S(2)}, u32[]{:S(2)}) collective-permute-start(f32[4,1,2,8,192]{4,3,2,1,0:T(8,128)S(1)} %get-tuple-element.79), channel_id=1, source_target_pairs={{0,24},{32,56},{64,88},{96,120},{128,152},{160,184},{192,216},{224... | collective-permute-start | bytes 147464 | tf_op jit(solution)/shard_map/ppermute | solution.py:70
  53.7 4.1 %collective-permute-start.12 = (f32[4,1,2,8,192]{4,3,2,1,0:T(8,128)S(1)}, f32[4,1,2,8,192]{4,3,2,1,0:T(8,128)S(1)}, u32[]{:S(2)}, u32[]{:S(2)}) collective-permute-start(f32[4,1,2,8,192]{4,3,2,1,0:T(8,128)S(1)} %get-tuple-element.80), channel_id=1, source_target_pairs={{0,8},{32,0},{64,72},{96,64},{128,136},{160,128},{192,200},{224,19... | collective-permute-start | bytes 147464 | tf_op jit(solution)/shard_map/ppermute | solution.py:70
  57.9 0.9 collective-permute-done.12
  58.8 0.8 collective-permute-done.13
  59.7 2.6 %collective-permute-start.16 = (f32[4,4,8,192]{3,2,1,0:T(8,128)S(1)}, f32[4,4,8,192]{3,2,1,0:T(8,128)S(1)}, u32[]{:S(2)}, u32[]{:S(2)}) collective-permute-start(f32[4,4,8,192]{3,2,1,0:T(8,128)S(1)} %get-tuple-element.67), channel_id=1, source_target_pairs={{33,1},{2,33},{34,2},{3,34},{35,3},{0,35},{32,0},{1,32},{41,9},{10... | collective-permute-start | bytes 294920 | tf_op jit(solution)/shard_map/ppermute | solution.py:70
  62.2 0.8 collective-permute-start.15
  63.2 2.2 %k_own_env.1 = (f32[192,1024]{1,0:T(8,128)S(1)}, f32[192,1024]{1,0:T(8,128)S(1)}, f32[128,1024]{1,0:T(8,128)S(1)}, f32[128,1024]{1,0:T(8,128)S(1)}, f32[128,1024]{1,0:T(8,128)S(1)}, /*index=5*/f32[128,1024]{1,0:T(8,128)S(1)}) custom-call(f32[48,128]{1,0:T(8,128)S(1)} %collective-permute-done.packed_ref, f32[8,1024]{1,0:T(8,128)S(1)} %get-tuple-element.36.scal_ref, ...), custom_call_target="tpu_custom_call" | custom-call | tf_op jit(solution)/shard_map/k_own_env/pallas_call | solution.py:519
  65.7 1.8 %k_energy.1 = (f32[128,192]{1,0:T(8,128)S(1)}, f32[128,192]{1,0:T(8,128)S(1)}, f32[256,192]{1,0:T(8,128)S(1)}, f32[192,1024]{1,0:T(8,128)S(1)}, f32[128,1024]{1,0:T(8,128)S(1)}, /*index=5*/f32[64,1024]{1,0:T(8,128)S(1)}) custom-call(f32[48,128]{1,0:T(8,128)S(1)} %collective-permute-done.packed_ref, f32[8,1024]{1,0:T(8,128)S(1)} %get-tuple-element.36.scal_ref, ...), custom_call_target="tpu_custom_call" | custom-call | tf_op jit(solution)/shard_map/k_energy/pallas_call | solution.py:519
  67.5 1.8 %collective-permute-start.17 = (f32[4,4,8,192]{3,2,1,0:T(8,128)S(1)}, f32[4,4,8,192]{3,2,1,0:T(8,128)S(1)}, u32[]{:S(2)}, u32[]{:S(2)}) collective-permute-start(f32[4,4,8,192]{3,2,1,0:T(8,128)S(1)} %bitcast.60), channel_id=1, source_target_pairs={{1,33},{33,2},{2,34},{34,3},{3,35},{35,0},{0,32},{32,1},{9,41},{41... | collective-permute-start | bytes 294920 | tf_op jit(solution)/shard_map/ppermute | solution.py:70
  69.7 2.2 %k_direct.1 = (f32[8,1024]{1,0:T(8,128)S(1)}, f32[4,512]{1,0:T(4,128)S(1)}) custom-call(f32[48,128]{1,0:T(8,128)S(1)} %collective-permute-done.packed_ref, f32[8,1024]{1,0:T(8,128)S(1)} %get-tuple-element.36.scal_ref, f32[128,1024]{1,0:T(8,128)S(1)} %get-tuple-element.37.av_ref, f32[128,1024]{1,0:T(8,128)S(1)} %get-tuple-element.39.nav_ref, ...), custom_call_target="tpu_custom_call" | custom-call | tf_op jit(solution)/shard_map/k_direct/pallas_call | solution.py:519
  71.9 2.0 %collective-permute-done.18 = f32[4,4,8,192]{3,2,1,0:T(8,128)S(1)} collective-permute-done((f32[4,4,8,192]{3,2,1,0:T(8,128)S(1)}, f32[4,4,8,192]{3,2,1,0:T(8,128)S(1)}, u32[]{:S(2)}, u32[]{:S(2)}) %collective-permute-start.18) | collective-permute-done | bytes 98336 | tf_op jit(solution)/shard_map/ppermute | solution.py:70
  74.0 3.7 %collective-permute-start.21 = (f32[4,1,2,8,192]{4,3,2,1,0:T(8,128)S(1)}, f32[4,1,2,8,192]{4,3,2,1,0:T(8,128)S(1)}, u32[]{:S(2)}, u32[]{:S(2)}) collective-permute-start(f32[4,1,2,8,192]{4,3,2,1,0:T(8,128)S(1)} %get-tuple-element.64), channel_id=1, source_target_pairs={{0,24},{32,56},{64,88},{96,120},{128,152},{160,184},{192,216},{224... | collective-permute-start | bytes 147464 | tf_op jit(solution)/shard_map/ppermute | solution.py:70
  77.7 0.7 collective-permute-start.19
  78.4 0.8 collective-permute-start.20
  79.2 1.0 collective-permute-done.21
  80.9 0.7 collective-permute-start.24
  81.6 2.8 %collective-permute-start.22 = (f32[1,2,2,8,192]{4,3,2,1,0:T(8,128)S(1)}, f32[1,2,2,8,192]{4,3,2,1,0:T(8,128)S(1)}, u32[]{:S(2)}, u32[]{:S(2)}) collective-permute-start(f32[1,2,2,8,192]{4,3,2,1,0:T(8,128)S(1)} %get-tuple-element.77), channel_id=1, source_target_pairs={{0,64},{32,0},{64,128},{96,32},{128,192},{160,96},{192,256},{224,1... | collective-permute-start | bytes 73736 | tf_op jit(solution)/shard_map/ppermute | solution.py:70
  84.4 1.0 collective-permute-done.22
  85.4 2.3 %collective-permute-done.23 = f32[1,2,2,8,192]{4,3,2,1,0:T(8,128)S(1)} collective-permute-done((f32[1,2,2,8,192]{4,3,2,1,0:T(8,128)S(1)}, f32[1,2,2,8,192]{4,3,2,1,0:T(8,128)S(1)}, u32[]{:S(2)}, u32[]{:S(2)}) %collective-permute-start.23) | collective-permute-done | bytes 24608 | tf_op jit(solution)/shard_map/ppermute | solution.py:70
  87.7 1.0 k_env_back.1
  88.7 0.7 collective-permute-start.25
  90.1 0.7 collective-permute-done.25
  90.7 2.7 %collective-permute-done.26 = f32[4,4,8,128]{3,2,1,0:T(8,128)S(1)} collective-permute-done((f32[4,4,8,128]{3,2,1,0:T(8,128)S(1)}, f32[4,4,8,128]{3,2,1,0:T(8,128)S(1)}, u32[]{:S(2)}, u32[]{:S(2)}) %collective-permute-start.26) | collective-permute-done | bytes 65568 | tf_op jit(solution)/shard_map/ppermute | solution.py:70
  93.4 2.6 %collective-permute-start.29 = (f32[4,1,2,8,128]{4,3,2,1,0:T(8,128)S(1)}, f32[4,1,2,8,128]{4,3,2,1,0:T(8,128)S(1)}, u32[]{:S(2)}, u32[]{:S(2)}) collective-permute-start(f32[4,1,2,8,128]{4,3,2,1,0:T(8,128)S(1)} %get-tuple-element.73), channel_id=1, source_target_pairs={{0,24},{32,56},{64,88},{96,120},{128,152},{160,184},{192,216},{224... | collective-permute-start | bytes 98312 | tf_op jit(solution)/shard_map/ppermute | solution.py:70
  96.0 1.9 %collective-permute-start.27 = (f32[4,1,2,8,128]{4,3,2,1,0:T(8,128)S(1)}, f32[4,1,2,8,128]{4,3,2,1,0:T(8,128)S(1)}, u32[]{:S(2)}, u32[]{:S(2)}) collective-permute-start(f32[4,1,2,8,128]{4,3,2,1,0:T(8,128)S(1)} %get-tuple-element.74), channel_id=1, source_target_pairs={{0,8},{32,0},{64,72},{96,64},{128,136},{160,128},{192,200},{224,19... | collective-permute-start | bytes 98312 | tf_op jit(solution)/shard_map/ppermute | solution.py:70
  98.0 1.3 %collective-permute-done.29 = f32[4,1,2,8,128]{4,3,2,1,0:T(8,128)S(1)} collective-permute-done((f32[4,1,2,8,128]{4,3,2,1,0:T(8,128)S(1)}, f32[4,1,2,8,128]{4,3,2,1,0:T(8,128)S(1)}, u32[]{:S(2)}, u32[]{:S(2)}) %collective-permute-start.29) | collective-permute-done | bytes 32800 | tf_op jit(solution)/shard_map/ppermute | solution.py:70
  100.0 4.5 %collective-permute-start.30 = (f32[1,2,2,8,128]{4,3,2,1,0:T(8,128)S(1)}, f32[1,2,2,8,128]{4,3,2,1,0:T(8,128)S(1)}, u32[]{:S(2)}, u32[]{:S(2)}) collective-permute-start(f32[1,2,2,8,128]{4,3,2,1,0:T(8,128)S(1)} %get-tuple-element.93), channel_id=1, source_target_pairs={{0,64},{32,0},{64,128},{96,32},{128,192},{160,96},{192,256},{224,1... | collective-permute-start | bytes 49160 | tf_op jit(solution)/shard_map/ppermute | solution.py:70
  104.5 0.9 collective-permute-done.30
  105.4 3.3 %collective-permute-done.31 = f32[1,2,2,8,128]{4,3,2,1,0:T(8,128)S(1)} collective-permute-done((f32[1,2,2,8,128]{4,3,2,1,0:T(8,128)S(1)}, f32[1,2,2,8,128]{4,3,2,1,0:T(8,128)S(1)}, u32[]{:S(2)}, u32[]{:S(2)}) %collective-permute-start.31) | collective-permute-done | bytes 16416 | tf_op jit(solution)/shard_map/ppermute | solution.py:70
  108.9 6.6 %collective-permute-start.33 = (f32[16,128]{1,0:T(8,128)S(1)}, f32[16,128]{1,0:T(8,128)S(1)}, u32[]{:S(2)}, u32[]{:S(2)}) collective-permute-start(f32[16,128]{1,0:T(8,128)S(1)} %k_force.1), channel_id=1, source_target_pairs={{1,0},{33,1},{2,2},{34,3},{3,4},{35,5},{0,6},{32,7},{9,8},{41,9},{... | collective-permute-start | bytes 24584 | tf_op jit(solution)/shard_map/ppermute | solution.py:70
  115.5 0.8 collective-permute-done.33.in_ref
  (74 shorter events, 5.1 us)
Async XLA Ops:
  2.1 18.0 %collective-permute-start = (f32[48,128]{1,0:T(8,128)}, f32[48,128]{1,0:T(8,128)S(1)}, u32[]{:S(2)}, u32[]{:S(2)}) collective-permute-start(f32[48,128]{1,0:T(8,128)} %k_pack.1), channel_id=1, source_target_pairs={{0,1},{1,33},{2,2},{3,34},{4,3},{5,35},{6,0},{7,32},{8,9},{9,41},{... | collective-permute-start | bytes 73736 | tf_op jit(solution)/shard_map/ppermute | solution.py:70
  20.4 3.7 %collective-permute-start.3 = (f32[1,2,2,8,128]{4,3,2,1,0:T(8,128)S(1)}, f32[1,2,2,8,128]{4,3,2,1,0:T(8,128)S(1)}, u32[]{:S(2)}, u32[]{:S(2)}) collective-permute-start(f32[1,2,2,8,128]{4,3,2,1,0:T(8,128)S(1)} %get-tuple-element.105), channel_id=1, source_target_pairs={{0,452},{32,484},{452,0},{484,32},{8,460},{40,492},{460,8},{492,40... | collective-permute-start | bytes 49160 | tf_op jit(solution)/shard_map/ppermute | solution.py:70
  21.1 4.1 %collective-permute-start.2 = (f32[1,2,2,8,128]{4,3,2,1,0:T(8,128)S(1)}, f32[1,2,2,8,128]{4,3,2,1,0:T(8,128)S(1)}, u32[]{:S(2)}, u32[]{:S(2)}) collective-permute-start(f32[1,2,2,8,128]{4,3,2,1,0:T(8,128)S(1)} %get-tuple-element.106), channel_id=1, source_target_pairs={{64,0},{0,32},{128,64},{32,96},{192,128},{96,160},{256,192},{160,2... | collective-permute-start | bytes 49160 | tf_op jit(solution)/shard_map/ppermute | solution.py:70
  22.7 2.6 %collective-permute-start.1 = (f32[1,2,2,8,128]{4,3,2,1,0:T(8,128)S(1)}, f32[1,2,2,8,128]{4,3,2,1,0:T(8,128)S(1)}, u32[]{:S(2)}, u32[]{:S(2)}) collective-permute-start(f32[1,2,2,8,128]{4,3,2,1,0:T(8,128)S(1)} %get-tuple-element.107), channel_id=1, source_target_pairs={{0,64},{32,0},{64,128},{96,32},{128,192},{160,96},{192,256},{224,1... | collective-permute-start | bytes 49160 | tf_op jit(solution)/shard_map/ppermute | solution.py:70
  25.3 8.7 %collective-permute-start.6 = (f32[4,1,2,8,128]{4,3,2,1,0:T(8,128)S(1)}, f32[4,1,2,8,128]{4,3,2,1,0:T(8,128)S(1)}, u32[]{:S(2)}, u32[]{:S(2)}) collective-permute-start(f32[4,1,2,8,128]{4,3,2,1,0:T(8,128)S(1)} %get-tuple-element.98), channel_id=1, source_target_pairs={{0,24},{32,56},{64,88},{96,120},{128,152},{160,184},{192,216},{224... | collective-permute-start | bytes 98312 | tf_op jit(solution)/shard_map/ppermute | solution.py:70
  30.2 4.7 %collective-permute-start.4 = (f32[4,1,2,8,128]{4,3,2,1,0:T(8,128)S(1)}, f32[4,1,2,8,128]{4,3,2,1,0:T(8,128)S(1)}, u32[]{:S(2)}, u32[]{:S(2)}) collective-permute-start(f32[4,1,2,8,128]{4,3,2,1,0:T(8,128)S(1)} %get-tuple-element.99), channel_id=1, source_target_pairs={{0,8},{32,0},{64,72},{96,64},{128,136},{160,128},{192,200},{224,19... | collective-permute-start | bytes 98312 | tf_op jit(solution)/shard_map/ppermute | solution.py:70
  34.1 1.2 %collective-permute-start.5 = (f32[4,1,2,8,128]{4,3,2,1,0:T(8,128)S(1)}, f32[4,1,2,8,128]{4,3,2,1,0:T(8,128)S(1)}, u32[]{:S(2)}, u32[]{:S(2)}) collective-permute-start(f32[4,1,2,8,128]{4,3,2,1,0:T(8,128)S(1)} %get-tuple-element.100), channel_id=1, source_target_pairs={{8,0},{0,32},{72,64},{64,96},{136,128},{128,160},{200,192},{192,22... | collective-permute-start | bytes 98312 | tf_op jit(solution)/shard_map/ppermute | solution.py:70
  35.3 10.1 %copy-start.3 = (f32[8,128]{1,0:T(8,128)S(1)}, f32[8,128]{1,0:T(8,128)}, u32[]{:S(2)}) copy-start(f32[8,128]{1,0:T(8,128)} %wb_ref.3) | copy-start | bytes 12292
  35.3 10.1 %copy-start.4 = (f32[6,128]{1,0:T(8,128)S(1)}, f32[6,128]{1,0:T(8,128)}, u32[]{:S(2)}) copy-start(f32[6,128]{1,0:T(8,128)} %ec_ref.1) | copy-start | bytes 9220
  35.3 10.1 %copy-start.5 = (f32[6,128]{1,0:T(8,128)S(1)}, f32[6,128]{1,0:T(8,128)}, u32[]{:S(2)}) copy-start(f32[6,128]{1,0:T(8,128)} %ep_ref.1) | copy-start | bytes 9220
  35.4 10.1 %collective-permute-start.8 = (f32[4,4,8,128]{3,2,1,0:T(8,128)S(1)}, f32[4,4,8,128]{3,2,1,0:T(8,128)S(1)}, u32[]{:S(2)}, u32[]{:S(2)}) collective-permute-start(f32[4,4,8,128]{3,2,1,0:T(8,128)S(1)} %get-tuple-element.82), channel_id=1, source_target_pairs={{33,1},{2,33},{34,2},{3,34},{35,3},{0,35},{32,0},{1,32},{41,9},{10... | collective-permute-start | bytes 196616 | tf_op jit(solution)/shard_map/ppermute | solution.py:70
  38.5 7.0 %copy-start.1 = (f32[128,64]{0,1:T(8,128)S(1)}, f32[128,64]{0,1:T(8,128)}, u32[]{:S(2)}) copy-start(f32[128,64]{0,1:T(8,128)} %param.22) | copy-start | bytes 98308
  38.5 7.0 %copy-start.2 = (f32[128,64]{0,1:T(8,128)S(1)}, f32[128,64]{0,1:T(8,128)}, u32[]{:S(2)}) copy-start(f32[128,64]{0,1:T(8,128)} %param.23) | copy-start | bytes 98308
  38.5 6.9 %collective-permute-start.7 = (f32[4,4,8,128]{3,2,1,0:T(8,128)S(1)}, f32[4,4,8,128]{3,2,1,0:T(8,128)S(1)}, u32[]{:S(2)}, u32[]{:S(2)}) collective-permute-start(f32[4,4,8,128]{3,2,1,0:T(8,128)S(1)} %get-tuple-element.83), channel_id=1, source_target_pairs={{1,33},{33,2},{2,34},{34,3},{3,35},{35,0},{0,32},{32,1},{9,41},{41... | collective-permute-start | bytes 196616 | tf_op jit(solution)/shard_map/ppermute | solution.py:70
  46.7 2.6 %collective-permute-start.11 = (f32[1,2,2,8,192]{4,3,2,1,0:T(8,128)S(1)}, f32[1,2,2,8,192]{4,3,2,1,0:T(8,128)S(1)}, u32[]{:S(2)}, u32[]{:S(2)}) collective-permute-start(f32[1,2,2,8,192]{4,3,2,1,0:T(8,128)S(1)} %get-tuple-element.95), channel_id=1, source_target_pairs={{0,452},{32,484},{452,0},{484,32},{8,460},{40,492},{460,8},{492,40... | collective-permute-start | bytes 73736 | tf_op jit(solution)/shard_map/ppermute | solution.py:70
  47.4 3.2 %collective-permute-start.10 = (f32[1,2,2,8,192]{4,3,2,1,0:T(8,128)S(1)}, f32[1,2,2,8,192]{4,3,2,1,0:T(8,128)S(1)}, u32[]{:S(2)}, u32[]{:S(2)}) collective-permute-start(f32[1,2,2,8,192]{4,3,2,1,0:T(8,128)S(1)} %get-tuple-element.96), channel_id=1, source_target_pairs={{64,0},{0,32},{128,64},{32,96},{192,128},{96,160},{256,192},{160,2... | collective-permute-start | bytes 73736 | tf_op jit(solution)/shard_map/ppermute | solution.py:70
  47.4 3.2 %collective-permute-start.9 = (f32[1,2,2,8,192]{4,3,2,1,0:T(8,128)S(1)}, f32[1,2,2,8,192]{4,3,2,1,0:T(8,128)S(1)}, u32[]{:S(2)}, u32[]{:S(2)}) collective-permute-start(f32[1,2,2,8,192]{4,3,2,1,0:T(8,128)S(1)} %get-tuple-element.97), channel_id=1, source_target_pairs={{0,64},{32,0},{64,128},{96,32},{128,192},{160,96},{192,256},{224,1... | collective-permute-start | bytes 73736 | tf_op jit(solution)/shard_map/ppermute | solution.py:70
  50.6 7.2 %collective-permute-start.14 = (f32[4,1,2,8,192]{4,3,2,1,0:T(8,128)S(1)}, f32[4,1,2,8,192]{4,3,2,1,0:T(8,128)S(1)}, u32[]{:S(2)}, u32[]{:S(2)}) collective-permute-start(f32[4,1,2,8,192]{4,3,2,1,0:T(8,128)S(1)} %get-tuple-element.79), channel_id=1, source_target_pairs={{0,24},{32,56},{64,88},{96,120},{128,152},{160,184},{192,216},{224... | collective-permute-start | bytes 147464 | tf_op jit(solution)/shard_map/ppermute | solution.py:70
  53.7 5.1 %collective-permute-start.12 = (f32[4,1,2,8,192]{4,3,2,1,0:T(8,128)S(1)}, f32[4,1,2,8,192]{4,3,2,1,0:T(8,128)S(1)}, u32[]{:S(2)}, u32[]{:S(2)}) collective-permute-start(f32[4,1,2,8,192]{4,3,2,1,0:T(8,128)S(1)} %get-tuple-element.80), channel_id=1, source_target_pairs={{0,8},{32,0},{64,72},{96,64},{128,136},{160,128},{192,200},{224,19... | collective-permute-start | bytes 147464 | tf_op jit(solution)/shard_map/ppermute | solution.py:70
  57.8 1.7 %collective-permute-start.13 = (f32[4,1,2,8,192]{4,3,2,1,0:T(8,128)S(1)}, f32[4,1,2,8,192]{4,3,2,1,0:T(8,128)S(1)}, u32[]{:S(2)}, u32[]{:S(2)}) collective-permute-start(f32[4,1,2,8,192]{4,3,2,1,0:T(8,128)S(1)} %get-tuple-element.81), channel_id=1, source_target_pairs={{8,0},{0,32},{72,64},{64,96},{136,128},{128,160},{200,192},{192,22... | collective-permute-start | bytes 147464 | tf_op jit(solution)/shard_map/ppermute | solution.py:70
  59.6 3.6 %copy-start = (f32[192,128]{1,0:T(8,128)S(1)}, f32[192,128]{1,0:T(8,128)}, u32[]{:S(2)}) copy-start(f32[192,128]{1,0:T(8,128)} %wm_ref.5) | copy-start | bytes 294916
  59.7 6.0 %collective-permute-start.16 = (f32[4,4,8,192]{3,2,1,0:T(8,128)S(1)}, f32[4,4,8,192]{3,2,1,0:T(8,128)S(1)}, u32[]{:S(2)}, u32[]{:S(2)}) collective-permute-start(f32[4,4,8,192]{3,2,1,0:T(8,128)S(1)} %get-tuple-element.67), channel_id=1, source_target_pairs={{33,1},{2,33},{34,2},{3,34},{35,3},{0,35},{32,0},{1,32},{41,9},{10... | collective-permute-start | bytes 294920 | tf_op jit(solution)/shard_map/ppermute | solution.py:70
  62.2 0.8 copy-start.6
  62.2 3.4 %collective-permute-start.15 = (f32[4,4,8,192]{3,2,1,0:T(8,128)S(1)}, f32[4,4,8,192]{3,2,1,0:T(8,128)S(1)}, u32[]{:S(2)}, u32[]{:S(2)}) collective-permute-start(f32[4,4,8,192]{3,2,1,0:T(8,128)S(1)} %get-tuple-element.68), channel_id=1, source_target_pairs={{1,33},{33,2},{2,34},{34,3},{3,35},{35,0},{0,32},{32,1},{9,41},{41... | collective-permute-start | bytes 294920 | tf_op jit(solution)/shard_map/ppermute | solution.py:70
  67.5 4.4 %collective-permute-start.17 = (f32[4,4,8,192]{3,2,1,0:T(8,128)S(1)}, f32[4,4,8,192]{3,2,1,0:T(8,128)S(1)}, u32[]{:S(2)}, u32[]{:S(2)}) collective-permute-start(f32[4,4,8,192]{3,2,1,0:T(8,128)S(1)} %bitcast.60), channel_id=1, source_target_pairs={{1,33},{33,2},{2,34},{34,3},{3,35},{35,0},{0,32},{32,1},{9,41},{41... | collective-permute-start | bytes 294920 | tf_op jit(solution)/shard_map/ppermute | solution.py:70
  69.2 4.7 %collective-permute-start.18 = (f32[4,4,8,192]{3,2,1,0:T(8,128)S(1)}, f32[4,4,8,192]{3,2,1,0:T(8,128)S(1)}, u32[]{:S(2)}, u32[]{:S(2)}) collective-permute-start(f32[4,4,8,192]{3,2,1,0:T(8,128)S(1)} %bitcast.59), channel_id=1, source_target_pairs={{33,1},{2,33},{34,2},{3,34},{35,3},{0,35},{32,0},{1,32},{41,9},{10... | collective-permute-start | bytes 294920 | tf_op jit(solution)/shard_map/ppermute | solution.py:70
  74.0 6.2 %collective-permute-start.21 = (f32[4,1,2,8,192]{4,3,2,1,0:T(8,128)S(1)}, f32[4,1,2,8,192]{4,3,2,1,0:T(8,128)S(1)}, u32[]{:S(2)}, u32[]{:S(2)}) collective-permute-start(f32[4,1,2,8,192]{4,3,2,1,0:T(8,128)S(1)} %get-tuple-element.64), channel_id=1, source_target_pairs={{0,24},{32,56},{64,88},{96,120},{128,152},{160,184},{192,216},{224... | collective-permute-start | bytes 147464 | tf_op jit(solution)/shard_map/ppermute | solution.py:70
  77.7 3.1 %collective-permute-start.19 = (f32[4,1,2,8,192]{4,3,2,1,0:T(8,128)S(1)}, f32[4,1,2,8,192]{4,3,2,1,0:T(8,128)S(1)}, u32[]{:S(2)}, u32[]{:S(2)}) collective-permute-start(f32[4,1,2,8,192]{4,3,2,1,0:T(8,128)S(1)} %get-tuple-element.65), channel_id=1, source_target_pairs={{0,8},{32,0},{64,72},{96,64},{128,136},{160,128},{192,200},{224,19... | collective-permute-start | bytes 147464 | tf_op jit(solution)/shard_map/ppermute | solution.py:70
  78.4 2.4 %collective-permute-start.20 = (f32[4,1,2,8,192]{4,3,2,1,0:T(8,128)S(1)}, f32[4,1,2,8,192]{4,3,2,1,0:T(8,128)S(1)}, u32[]{:S(2)}, u32[]{:S(2)}) collective-permute-start(f32[4,1,2,8,192]{4,3,2,1,0:T(8,128)S(1)} %get-tuple-element.66), channel_id=1, source_target_pairs={{8,0},{0,32},{72,64},{64,96},{136,128},{128,160},{200,192},{192,22... | collective-permute-start | bytes 147464 | tf_op jit(solution)/shard_map/ppermute | solution.py:70
  80.9 3.5 %collective-permute-start.24 = (f32[1,2,2,8,192]{4,3,2,1,0:T(8,128)S(1)}, f32[1,2,2,8,192]{4,3,2,1,0:T(8,128)S(1)}, u32[]{:S(2)}, u32[]{:S(2)}) collective-permute-start(f32[1,2,2,8,192]{4,3,2,1,0:T(8,128)S(1)} %get-tuple-element.76), channel_id=1, source_target_pairs={{0,452},{32,484},{452,0},{484,32},{8,460},{40,492},{460,8},{492,40... | collective-permute-start | bytes 73736 | tf_op jit(solution)/shard_map/ppermute | solution.py:70
  81.6 3.8 %collective-permute-start.22 = (f32[1,2,2,8,192]{4,3,2,1,0:T(8,128)S(1)}, f32[1,2,2,8,192]{4,3,2,1,0:T(8,128)S(1)}, u32[]{:S(2)}, u32[]{:S(2)}) collective-permute-start(f32[1,2,2,8,192]{4,3,2,1,0:T(8,128)S(1)} %get-tuple-element.77), channel_id=1, source_target_pairs={{0,64},{32,0},{64,128},{96,32},{128,192},{160,96},{192,256},{224,1... | collective-permute-start | bytes 73736 | tf_op jit(solution)/shard_map/ppermute | solution.py:70
  84.4 3.3 %collective-permute-start.23 = (f32[1,2,2,8,192]{4,3,2,1,0:T(8,128)S(1)}, f32[1,2,2,8,192]{4,3,2,1,0:T(8,128)S(1)}, u32[]{:S(2)}, u32[]{:S(2)}) collective-permute-start(f32[1,2,2,8,192]{4,3,2,1,0:T(8,128)S(1)} %get-tuple-element.78), channel_id=1, source_target_pairs={{64,0},{0,32},{128,64},{32,96},{192,128},{96,160},{256,192},{160,2... | collective-permute-start | bytes 73736 | tf_op jit(solution)/shard_map/ppermute | solution.py:70
  88.7 2.0 %collective-permute-start.25 = (f32[4,4,8,128]{3,2,1,0:T(8,128)S(1)}, f32[4,4,8,128]{3,2,1,0:T(8,128)S(1)}, u32[]{:S(2)}, u32[]{:S(2)}) collective-permute-start(f32[4,4,8,128]{3,2,1,0:T(8,128)S(1)} %bitcast.62), channel_id=1, source_target_pairs={{1,33},{33,2},{2,34},{34,3},{3,35},{35,0},{0,32},{32,1},{9,41},{41... | collective-permute-start | bytes 196616 | tf_op jit(solution)/shard_map/ppermute | solution.py:70
  89.4 4.0 %collective-permute-start.26 = (f32[4,4,8,128]{3,2,1,0:T(8,128)S(1)}, f32[4,4,8,128]{3,2,1,0:T(8,128)S(1)}, u32[]{:S(2)}, u32[]{:S(2)}) collective-permute-start(f32[4,4,8,128]{3,2,1,0:T(8,128)S(1)} %bitcast.61), channel_id=1, source_target_pairs={{33,1},{2,33},{34,2},{3,34},{35,3},{0,35},{32,0},{1,32},{41,9},{10... | collective-permute-start | bytes 196616 | tf_op jit(solution)/shard_map/ppermute | solution.py:70
  93.4 5.9 %collective-permute-start.29 = (f32[4,1,2,8,128]{4,3,2,1,0:T(8,128)S(1)}, f32[4,1,2,8,128]{4,3,2,1,0:T(8,128)S(1)}, u32[]{:S(2)}, u32[]{:S(2)}) collective-permute-start(f32[4,1,2,8,128]{4,3,2,1,0:T(8,128)S(1)} %get-tuple-element.73), channel_id=1, source_target_pairs={{0,24},{32,56},{64,88},{96,120},{128,152},{160,184},{192,216},{224... | collective-permute-start | bytes 98312 | tf_op jit(solution)/shard_map/ppermute | solution.py:70
  96.0 3.3 %collective-permute-start.27 = (f32[4,1,2,8,128]{4,3,2,1,0:T(8,128)S(1)}, f32[4,1,2,8,128]{4,3,2,1,0:T(8,128)S(1)}, u32[]{:S(2)}, u32[]{:S(2)}) collective-permute-start(f32[4,1,2,8,128]{4,3,2,1,0:T(8,128)S(1)} %get-tuple-element.74), channel_id=1, source_target_pairs={{0,8},{32,0},{64,72},{96,64},{128,136},{160,128},{192,200},{224,19... | collective-permute-start | bytes 98312 | tf_op jit(solution)/shard_map/ppermute | solution.py:70
  98.0 1.4 %collective-permute-start.28 = (f32[4,1,2,8,128]{4,3,2,1,0:T(8,128)S(1)}, f32[4,1,2,8,128]{4,3,2,1,0:T(8,128)S(1)}, u32[]{:S(2)}, u32[]{:S(2)}) collective-permute-start(f32[4,1,2,8,128]{4,3,2,1,0:T(8,128)S(1)} %get-tuple-element.75), channel_id=1, source_target_pairs={{8,0},{0,32},{72,64},{64,96},{136,128},{128,160},{200,192},{192,22... | collective-permute-start | bytes 98312 | tf_op jit(solution)/shard_map/ppermute | solution.py:70
  99.4 5.1 %collective-permute-start.32 = (f32[1,2,2,8,128]{4,3,2,1,0:T(8,128)S(1)}, f32[1,2,2,8,128]{4,3,2,1,0:T(8,128)S(1)}, u32[]{:S(2)}, u32[]{:S(2)}) collective-permute-start(f32[1,2,2,8,128]{4,3,2,1,0:T(8,128)S(1)} %get-tuple-element.92), channel_id=1, source_target_pairs={{0,452},{32,484},{452,0},{484,32},{8,460},{40,492},{460,8},{492,40... | collective-permute-start | bytes 49160 | tf_op jit(solution)/shard_map/ppermute | solution.py:70
  100.0 5.3 %collective-permute-start.30 = (f32[1,2,2,8,128]{4,3,2,1,0:T(8,128)S(1)}, f32[1,2,2,8,128]{4,3,2,1,0:T(8,128)S(1)}, u32[]{:S(2)}, u32[]{:S(2)}) collective-permute-start(f32[1,2,2,8,128]{4,3,2,1,0:T(8,128)S(1)} %get-tuple-element.93), channel_id=1, source_target_pairs={{0,64},{32,0},{64,128},{96,32},{128,192},{160,96},{192,256},{224,1... | collective-permute-start | bytes 49160 | tf_op jit(solution)/shard_map/ppermute | solution.py:70
  104.5 4.1 %collective-permute-start.31 = (f32[1,2,2,8,128]{4,3,2,1,0:T(8,128)S(1)}, f32[1,2,2,8,128]{4,3,2,1,0:T(8,128)S(1)}, u32[]{:S(2)}, u32[]{:S(2)}) collective-permute-start(f32[1,2,2,8,128]{4,3,2,1,0:T(8,128)S(1)} %get-tuple-element.94), channel_id=1, source_target_pairs={{64,0},{0,32},{128,64},{32,96},{192,128},{96,160},{256,192},{160,2... | collective-permute-start | bytes 49160 | tf_op jit(solution)/shard_map/ppermute | solution.py:70
  108.9 7.4 %collective-permute-start.33 = (f32[16,128]{1,0:T(8,128)S(1)}, f32[16,128]{1,0:T(8,128)S(1)}, u32[]{:S(2)}, u32[]{:S(2)}) collective-permute-start(f32[16,128]{1,0:T(8,128)S(1)} %k_force.1), channel_id=1, source_target_pairs={{1,0},{33,1},{2,2},{34,3},{3,4},{35,5},{0,6},{32,7},{9,8},{41,9},{... | collective-permute-start | bytes 24584 | tf_op jit(solution)/shard_map/ppermute | solution.py:70

commit v11 on v10

--- a/solution.py
+++ b/solution.py
@@ -29,7 +29,7 @@
 
 def home(x, y, z):
     x, y, z = x % SHAPE[0], y % SHAPE[1], z % SHAPE[2]
-    return device((z // 2 + 1) % 4, y, x, z % 2)
+    return device((z // 2 + 1) % 4, y, -x % 16, z % 2)
 
 
 CELLS = [(x, y, z) for x in range(SHAPE[0]) for y in range(SHAPE[1]) for z in range(SHAPE[2])]
@@ -76,13 +76,23 @@
 
 
 def swap(axis, first, last, here):
+    if axis == 0:
+        return trade(axis, last, first, here)[::-1]
+    return trade(axis, first, last, here)
+
+
+def trade(axis, first, last, here):
     at, upward, count = here[axis], here[2] == 0, RINGS[axis][1]
     forth = send(jnp.where(upward, last, first), FORTH[axis])
     ring = send(jnp.where(at == 0, first, last), ENDS[axis])
     back = send(jnp.where(upward, first, last), BACK[axis])
     start, end = at == 0, at == count - 1
-    before = jnp.where(~start, jnp.where(upward, forth, back), jnp.where(start, ring, back))
-    after = jnp.where(end, jnp.where(end, ring, back), jnp.where(~upward, forth, back))
+    if axis == 0:
+        after = jnp.where(~end, jnp.where(~upward, forth, back), jnp.where(end, ring, back))
+        before = jnp.where(start, jnp.where(start, ring, back), jnp.where(upward, forth, back))
+    else:
+        before = jnp.where(~start, jnp.where(upward, forth, back), jnp.where(start, ring, back))
+        after = jnp.where(end, jnp.where(end, ring, back), jnp.where(~upward, forth, back))
     return before, after
 
 

time: 117 us -> 122 us (1.043)
  the two profiles are of different devices: /device:TPU:33 before, /device:TPU:71 now
where the time goes in v11:
time: 122 us; the launch traced here: 121 us
  starting transfers between devices  66.8 us (55%)
  waiting for transfers between devices  41 us (34%)
  Pallas kernels  12 us (10%)
    ppermute x34, starting transfers between devices, send(): return lax.ppermute(x, AXES, pairs)  66.8 us
    ppermute x34, waiting for transfers between devices, send(): return lax.ppermute(x, AXES, pairs)  41 us
    pallas_call x10, Pallas kernels, call(): pl.pallas_call(kernel, out_shape=shapes, in_specs=[spec] * len(args), out...  10.5 us
  transfers between devices with their start and end apart: 34, of which 21 were waited for; matrix products, arithmetic and copies ran while one was open for 0% of the time, Pallas kernels for 4%

profile of v11, /device:TPU:71, one launch (start us, length us, event | category | flops | bytes accessed | tf_op | source)
XLA Modules:
  0.0 121.4 jit_solution(17402949665356267629)
XLA Ops:
  0.6 1.5 %k_pack.1 = f32[48,128]{1,0:T(8,128)} custom-call(f32[3,1,1,1,512]{4,3,2,1,0:T(1,128)} %pos_in.1, s32[1,1,1,512]{3,2,1,0:T(1,128)} %kind_in.1, s32[2,2,2,8]{3,2,1,0:T(2,128)} %names_in.1, s32[1,1,1,8,128]{4,3,2,1,0:T(8,128)} %center_in.1, s32[1,1,1,8,128]{4,3,2,1,0:T(8,128)} %partner_in.1, s32[1,1,1,8,128]{4,3,2,1,0:T(8,128)} %live_in.1), custom_call_target="tpu_custom_call" | custom-call | tf_op jit(solution)/shard_map/k_pack/pallas_call | solution.py:263
  2.1 13.5 %collective-permute-start = (f32[48,128]{1,0:T(8,128)}, f32[48,128]{1,0:T(8,128)S(1)}, u32[]{:S(2)}, u32[]{:S(2)}) collective-permute-start(f32[48,128]{1,0:T(8,128)} %k_pack.1), channel_id=1, source_target_pairs={{0,1},{1,33},{2,2},{3,34},{4,3},{5,35},{6,0},{7,32},{8,9},{9,41},{... | collective-permute-start | bytes 73736 | tf_op jit(solution)/shard_map/ppermute | solution.py:70
  15.7 1.1 collective-permute-done.packed_ref
  17.0 0.7 collective-permute-start.3
  18.0 1.2 collective-permute-start.1
  19.2 1.1 collective-permute-done.2
  20.3 3.1 %collective-permute-done.1 = f32[1,2,2,8,128]{4,3,2,1,0:T(8,128)S(1)} collective-permute-done((f32[1,2,2,8,128]{4,3,2,1,0:T(8,128)S(1)}, f32[1,2,2,8,128]{4,3,2,1,0:T(8,128)S(1)}, u32[]{:S(2)}, u32[]{:S(2)}) %collective-permute-start.1) | collective-permute-done | bytes 16416 | tf_op jit(solution)/shard_map/ppermute | solution.py:70
  23.4 4.6 %collective-permute-start.6 = (f32[4,1,2,8,128]{4,3,2,1,0:T(8,128)S(1)}, f32[4,1,2,8,128]{4,3,2,1,0:T(8,128)S(1)}, u32[]{:S(2)}, u32[]{:S(2)}) collective-permute-start(f32[4,1,2,8,128]{4,3,2,1,0:T(8,128)S(1)} %get-tuple-element.98), channel_id=1, source_target_pairs={{0,24},{32,56},{64,88},{96,120},{128,152},{160,184},{192,216},{224... | collective-permute-start | bytes 98312 | tf_op jit(solution)/shard_map/ppermute | solution.py:70
  28.1 7.4 %collective-permute-start.4 = (f32[4,1,2,8,128]{4,3,2,1,0:T(8,128)S(1)}, f32[4,1,2,8,128]{4,3,2,1,0:T(8,128)S(1)}, u32[]{:S(2)}, u32[]{:S(2)}) collective-permute-start(f32[4,1,2,8,128]{4,3,2,1,0:T(8,128)S(1)} %get-tuple-element.99), channel_id=1, source_target_pairs={{0,8},{32,0},{64,72},{96,64},{128,136},{160,128},{192,200},{224,19... | collective-permute-start | bytes 98312 | tf_op jit(solution)/shard_map/ppermute | solution.py:70
  35.5 0.9 collective-permute-done.4
  36.8 2.7 %collective-permute-start.8 = (f32[4,4,8,128]{3,2,1,0:T(8,128)S(1)}, f32[4,4,8,128]{3,2,1,0:T(8,128)S(1)}, u32[]{:S(2)}, u32[]{:S(2)}) collective-permute-start(f32[4,4,8,128]{3,2,1,0:T(8,128)S(1)} %get-tuple-element.82), channel_id=1, source_target_pairs={{33,1},{2,33},{34,2},{3,34},{35,3},{0,35},{32,0},{1,32},{41,9},{10... | collective-permute-start | bytes 196616 | tf_op jit(solution)/shard_map/ppermute | solution.py:70
  40.4 1.5 %collective-permute-done.8 = f32[4,4,8,128]{3,2,1,0:T(8,128)S(1)} collective-permute-done((f32[4,4,8,128]{3,2,1,0:T(8,128)S(1)}, f32[4,4,8,128]{3,2,1,0:T(8,128)S(1)}, u32[]{:S(2)}, u32[]{:S(2)}) %collective-permute-start.8) | collective-permute-done | bytes 65568 | tf_op jit(solution)/shard_map/ppermute | solution.py:70
  41.9 1.2 %k_features.1 = (f32[32,192]{1,0:T(8,128)S(1)}, f32[32,192]{1,0:T(8,128)S(1)}, f32[8,1024]{1,0:T(8,128)S(1)}, f32[128,1024]{1,0:T(8,128)S(1)}, f32[128,1024]{1,0:T(8,128)S(1)}) custom-call(f32[48,128]{1,0:T(8,128)S(1)} %collective-permute-done.packed_ref, f32[8,1024]{1,0:T(8,128)S(1)} %k_own_pairs.1.part_ref, f32[128,128]{1,0:T(8,128)S(1)} %bitcast.58, ...), custom_call_target="tpu_custom_call" | custom-call | tf_op jit(solution)/shard_map/k_features/pallas_call | solution.py:529
  43.2 0.7 collective-permute-start.11
  43.9 1.8 %collective-permute-start.9 = (f32[1,2,2,8,192]{4,3,2,1,0:T(8,128)S(1)}, f32[1,2,2,8,192]{4,3,2,1,0:T(8,128)S(1)}, u32[]{:S(2)}, u32[]{:S(2)}) collective-permute-start(f32[1,2,2,8,192]{4,3,2,1,0:T(8,128)S(1)} %get-tuple-element.97), channel_id=1, source_target_pairs={{0,64},{32,0},{64,128},{96,32},{128,192},{160,96},{192,256},{224,1... | collective-permute-start | bytes 73736 | tf_op jit(solution)/shard_map/ppermute | solution.py:70
  45.6 1.3 %collective-permute-done.10 = f32[1,2,2,8,192]{4,3,2,1,0:T(8,128)S(1)} collective-permute-done((f32[1,2,2,8,192]{4,3,2,1,0:T(8,128)S(1)}, f32[1,2,2,8,192]{4,3,2,1,0:T(8,128)S(1)}, u32[]{:S(2)}, u32[]{:S(2)}) %collective-permute-start.10) | collective-permute-done | bytes 24608 | tf_op jit(solution)/shard_map/ppermute | solution.py:70
  47.0 2.8 %collective-permute-start.14 = (f32[4,1,2,8,192]{4,3,2,1,0:T(8,128)S(1)}, f32[4,1,2,8,192]{4,3,2,1,0:T(8,128)S(1)}, u32[]{:S(2)}, u32[]{:S(2)}) collective-permute-start(f32[4,1,2,8,192]{4,3,2,1,0:T(8,128)S(1)} %get-tuple-element.79), channel_id=1, source_target_pairs={{0,24},{32,56},{64,88},{96,120},{128,152},{160,184},{192,216},{224... | collective-permute-start | bytes 147464 | tf_op jit(solution)/shard_map/ppermute | solution.py:70
  49.7 5.0 %collective-permute-start.12 = (f32[4,1,2,8,192]{4,3,2,1,0:T(8,128)S(1)}, f32[4,1,2,8,192]{4,3,2,1,0:T(8,128)S(1)}, u32[]{:S(2)}, u32[]{:S(2)}) collective-permute-start(f32[4,1,2,8,192]{4,3,2,1,0:T(8,128)S(1)} %get-tuple-element.80), channel_id=1, source_target_pairs={{0,8},{32,0},{64,72},{96,64},{128,136},{160,128},{192,200},{224,19... | collective-permute-start | bytes 147464 | tf_op jit(solution)/shard_map/ppermute | solution.py:70
  54.7 0.9 collective-permute-done.12
  55.6 0.8 collective-permute-done.13
  56.5 2.6 %collective-permute-start.16 = (f32[4,4,8,192]{3,2,1,0:T(8,128)S(1)}, f32[4,4,8,192]{3,2,1,0:T(8,128)S(1)}, u32[]{:S(2)}, u32[]{:S(2)}) collective-permute-start(f32[4,4,8,192]{3,2,1,0:T(8,128)S(1)} %get-tuple-element.67), channel_id=1, source_target_pairs={{33,1},{2,33},{34,2},{3,34},{35,3},{0,35},{32,0},{1,32},{41,9},{10... | collective-permute-start | bytes 294920 | tf_op jit(solution)/shard_map/ppermute | solution.py:70
  59.1 1.6 %collective-permute-start.15 = (f32[4,4,8,192]{3,2,1,0:T(8,128)S(1)}, f32[4,4,8,192]{3,2,1,0:T(8,128)S(1)}, u32[]{:S(2)}, u32[]{:S(2)}) collective-permute-start(f32[4,4,8,192]{3,2,1,0:T(8,128)S(1)} %get-tuple-element.68), channel_id=1, source_target_pairs={{1,33},{33,2},{2,34},{34,3},{3,35},{35,0},{0,32},{32,1},{9,41},{41... | collective-permute-start | bytes 294920 | tf_op jit(solution)/shard_map/ppermute | solution.py:70
  60.9 2.2 %k_own_env.1 = (f32[192,1024]{1,0:T(8,128)S(1)}, f32[192,1024]{1,0:T(8,128)S(1)}, f32[128,1024]{1,0:T(8,128)S(1)}, f32[128,1024]{1,0:T(8,128)S(1)}, f32[128,1024]{1,0:T(8,128)S(1)}, /*index=5*/f32[128,1024]{1,0:T(8,128)S(1)}) custom-call(f32[48,128]{1,0:T(8,128)S(1)} %collective-permute-done.packed_ref, f32[8,1024]{1,0:T(8,128)S(1)} %get-tuple-element.36.scal_ref, ...), custom_call_target="tpu_custom_call" | custom-call | tf_op jit(solution)/shard_map/k_own_env/pallas_call | solution.py:529
  63.4 1.8 %k_energy.1 = (f32[128,192]{1,0:T(8,128)S(1)}, f32[128,192]{1,0:T(8,128)S(1)}, f32[256,192]{1,0:T(8,128)S(1)}, f32[192,1024]{1,0:T(8,128)S(1)}, f32[128,1024]{1,0:T(8,128)S(1)}, /*index=5*/f32[64,1024]{1,0:T(8,128)S(1)}) custom-call(f32[48,128]{1,0:T(8,128)S(1)} %collective-permute-done.packed_ref, f32[8,1024]{1,0:T(8,128)S(1)} %get-tuple-element.36.scal_ref, ...), custom_call_target="tpu_custom_call" | custom-call | tf_op jit(solution)/shard_map/k_energy/pallas_call | solution.py:529
  65.1 3.0 %collective-permute-start.17 = (f32[4,4,8,192]{3,2,1,0:T(8,128)S(1)}, f32[4,4,8,192]{3,2,1,0:T(8,128)S(1)}, u32[]{:S(2)}, u32[]{:S(2)}) collective-permute-start(f32[4,4,8,192]{3,2,1,0:T(8,128)S(1)} %bitcast.60), channel_id=1, source_target_pairs={{1,33},{33,2},{2,34},{34,3},{3,35},{35,0},{0,32},{32,1},{9,41},{41... | collective-permute-start | bytes 294920 | tf_op jit(solution)/shard_map/ppermute | solution.py:70
  68.1 2.2 %k_direct.1 = (f32[8,1024]{1,0:T(8,128)S(1)}, f32[4,512]{1,0:T(4,128)S(1)}) custom-call(f32[48,128]{1,0:T(8,128)S(1)} %collective-permute-done.packed_ref, f32[8,1024]{1,0:T(8,128)S(1)} %get-tuple-element.36.scal_ref, f32[128,1024]{1,0:T(8,128)S(1)} %get-tuple-element.37.av_ref, f32[128,1024]{1,0:T(8,128)S(1)} %get-tuple-element.39.nav_ref, ...), custom_call_target="tpu_custom_call" | custom-call | tf_op jit(solution)/shard_map/k_direct/pallas_call | solution.py:529
  70.3 3.4 %collective-permute-done.18 = f32[4,4,8,192]{3,2,1,0:T(8,128)S(1)} collective-permute-done((f32[4,4,8,192]{3,2,1,0:T(8,128)S(1)}, f32[4,4,8,192]{3,2,1,0:T(8,128)S(1)}, u32[]{:S(2)}, u32[]{:S(2)}) %collective-permute-start.18) | collective-permute-done | bytes 98336 | tf_op jit(solution)/shard_map/ppermute | solution.py:70
  73.8 3.7 %collective-permute-start.21 = (f32[4,1,2,8,192]{4,3,2,1,0:T(8,128)S(1)}, f32[4,1,2,8,192]{4,3,2,1,0:T(8,128)S(1)}, u32[]{:S(2)}, u32[]{:S(2)}) collective-permute-start(f32[4,1,2,8,192]{4,3,2,1,0:T(8,128)S(1)} %get-tuple-element.64), channel_id=1, source_target_pairs={{0,24},{32,56},{64,88},{96,120},{128,152},{160,184},{192,216},{224... | collective-permute-start | bytes 147464 | tf_op jit(solution)/shard_map/ppermute | solution.py:70
  77.5 1.5 %collective-permute-start.20 = (f32[4,1,2,8,192]{4,3,2,1,0:T(8,128)S(1)}, f32[4,1,2,8,192]{4,3,2,1,0:T(8,128)S(1)}, u32[]{:S(2)}, u32[]{:S(2)}) collective-permute-start(f32[4,1,2,8,192]{4,3,2,1,0:T(8,128)S(1)} %get-tuple-element.66), channel_id=1, source_target_pairs={{8,0},{0,32},{72,64},{64,96},{136,128},{128,160},{200,192},{192,22... | collective-permute-start | bytes 147464 | tf_op jit(solution)/shard_map/ppermute | solution.py:70
  79.0 1.0 collective-permute-done.21
  80.0 0.6 collective-permute-done.19
  80.7 0.7 collective-permute-start.24
  81.4 1.8 %collective-permute-start.22 = (f32[1,2,2,8,192]{4,3,2,1,0:T(8,128)S(1)}, f32[1,2,2,8,192]{4,3,2,1,0:T(8,128)S(1)}, u32[]{:S(2)}, u32[]{:S(2)}) collective-permute-start(f32[1,2,2,8,192]{4,3,2,1,0:T(8,128)S(1)} %get-tuple-element.77), channel_id=1, source_target_pairs={{0,64},{32,0},{64,128},{96,32},{128,192},{160,96},{192,256},{224,1... | collective-permute-start | bytes 73736 | tf_op jit(solution)/shard_map/ppermute | solution.py:70
  83.2 1.0 collective-permute-done.22
  84.2 3.4 %collective-permute-done.23 = f32[1,2,2,8,192]{4,3,2,1,0:T(8,128)S(1)} collective-permute-done((f32[1,2,2,8,192]{4,3,2,1,0:T(8,128)S(1)}, f32[1,2,2,8,192]{4,3,2,1,0:T(8,128)S(1)}, u32[]{:S(2)}, u32[]{:S(2)}) %collective-permute-start.23) | collective-permute-done | bytes 24608 | tf_op jit(solution)/shard_map/ppermute | solution.py:70
  87.6 1.0 k_env_back.1
  89.1 0.6 k_own_force.1.own_ref
  89.9 3.6 %collective-permute-done.26 = f32[4,4,8,128]{3,2,1,0:T(8,128)S(1)} collective-permute-done((f32[4,4,8,128]{3,2,1,0:T(8,128)S(1)}, f32[4,4,8,128]{3,2,1,0:T(8,128)S(1)}, u32[]{:S(2)}, u32[]{:S(2)}) %collective-permute-start.26) | collective-permute-done | bytes 65568 | tf_op jit(solution)/shard_map/ppermute | solution.py:70
  93.5 2.8 %collective-permute-start.29 = (f32[4,1,2,8,128]{4,3,2,1,0:T(8,128)S(1)}, f32[4,1,2,8,128]{4,3,2,1,0:T(8,128)S(1)}, u32[]{:S(2)}, u32[]{:S(2)}) collective-permute-start(f32[4,1,2,8,128]{4,3,2,1,0:T(8,128)S(1)} %get-tuple-element.73), channel_id=1, source_target_pairs={{0,24},{32,56},{64,88},{96,120},{128,152},{160,184},{192,216},{224... | collective-permute-start | bytes 98312 | tf_op jit(solution)/shard_map/ppermute | solution.py:70
  96.4 1.5 %collective-permute-start.28 = (f32[4,1,2,8,128]{4,3,2,1,0:T(8,128)S(1)}, f32[4,1,2,8,128]{4,3,2,1,0:T(8,128)S(1)}, u32[]{:S(2)}, u32[]{:S(2)}) collective-permute-start(f32[4,1,2,8,128]{4,3,2,1,0:T(8,128)S(1)} %get-tuple-element.75), channel_id=1, source_target_pairs={{8,0},{0,32},{72,64},{64,96},{136,128},{128,160},{200,192},{192,22... | collective-permute-start | bytes 98312 | tf_op jit(solution)/shard_map/ppermute | solution.py:70
  97.8 1.6 %collective-permute-done.29 = f32[4,1,2,8,128]{4,3,2,1,0:T(8,128)S(1)} collective-permute-done((f32[4,1,2,8,128]{4,3,2,1,0:T(8,128)S(1)}, f32[4,1,2,8,128]{4,3,2,1,0:T(8,128)S(1)}, u32[]{:S(2)}, u32[]{:S(2)}) %collective-permute-start.29) | collective-permute-done | bytes 32800 | tf_op jit(solution)/shard_map/ppermute | solution.py:70
  99.5 0.7 collective-permute-start.32
  100.1 2.5 %collective-permute-start.30 = (f32[1,2,2,8,128]{4,3,2,1,0:T(8,128)S(1)}, f32[1,2,2,8,128]{4,3,2,1,0:T(8,128)S(1)}, u32[]{:S(2)}, u32[]{:S(2)}) collective-permute-start(f32[1,2,2,8,128]{4,3,2,1,0:T(8,128)S(1)} %get-tuple-element.93), channel_id=1, source_target_pairs={{0,64},{32,0},{64,128},{96,32},{128,192},{160,96},{192,256},{224,1... | collective-permute-start | bytes 49160 | tf_op jit(solution)/shard_map/ppermute | solution.py:70
  102.6 0.9 collective-permute-done.30
  103.5 4.0 %collective-permute-done.31 = f32[1,2,2,8,128]{4,3,2,1,0:T(8,128)S(1)} collective-permute-done((f32[1,2,2,8,128]{4,3,2,1,0:T(8,128)S(1)}, f32[1,2,2,8,128]{4,3,2,1,0:T(8,128)S(1)}, u32[]{:S(2)}, u32[]{:S(2)}) %collective-permute-start.31) | collective-permute-done | bytes 16416 | tf_op jit(solution)/shard_map/ppermute | solution.py:70
  107.7 3.1 %collective-permute-start.33 = (f32[16,128]{1,0:T(8,128)S(1)}, f32[16,128]{1,0:T(8,128)S(1)}, u32[]{:S(2)}, u32[]{:S(2)}) collective-permute-start(f32[16,128]{1,0:T(8,128)S(1)} %k_force.1), channel_id=1, source_target_pairs={{1,0},{33,1},{2,2},{34,3},{3,4},{35,5},{0,6},{32,7},{9,8},{41,9},{... | collective-permute-start | bytes 24584 | tf_op jit(solution)/shard_map/ppermute | solution.py:70
  110.8 10.0 %collective-permute-done.33.in_ref = f32[16,128]{1,0:T(8,128)S(1)} collective-permute-done((f32[16,128]{1,0:T(8,128)S(1)}, f32[16,128]{1,0:T(8,128)S(1)}, u32[]{:S(2)}, u32[]{:S(2)}) %collective-permute-start.33) | collective-permute-done | bytes 8224 | tf_op jit(solution)/shard_map/ppermute | solution.py:70
  120.8 0.6 k_unpack.1
  (74 shorter events, 3.6 us)
Async XLA Ops:
  2.1 14.6 %collective-permute-start = (f32[48,128]{1,0:T(8,128)}, f32[48,128]{1,0:T(8,128)S(1)}, u32[]{:S(2)}, u32[]{:S(2)}) collective-permute-start(f32[48,128]{1,0:T(8,128)} %k_pack.1), channel_id=1, source_target_pairs={{0,1},{1,33},{2,2},{3,34},{4,3},{5,35},{6,0},{7,32},{8,9},{9,41},{... | collective-permute-start | bytes 73736 | tf_op jit(solution)/shard_map/ppermute | solution.py:70
  17.0 2.2 %collective-permute-start.3 = (f32[1,2,2,8,128]{4,3,2,1,0:T(8,128)S(1)}, f32[1,2,2,8,128]{4,3,2,1,0:T(8,128)S(1)}, u32[]{:S(2)}, u32[]{:S(2)}) collective-permute-start(f32[1,2,2,8,128]{4,3,2,1,0:T(8,128)S(1)} %get-tuple-element.105), channel_id=1, source_target_pairs={{0,452},{32,484},{452,0},{484,32},{8,460},{40,492},{460,8},{492,40... | collective-permute-start | bytes 49160 | tf_op jit(solution)/shard_map/ppermute | solution.py:70
  17.7 2.6 %collective-permute-start.2 = (f32[1,2,2,8,128]{4,3,2,1,0:T(8,128)S(1)}, f32[1,2,2,8,128]{4,3,2,1,0:T(8,128)S(1)}, u32[]{:S(2)}, u32[]{:S(2)}) collective-permute-start(f32[1,2,2,8,128]{4,3,2,1,0:T(8,128)S(1)} %get-tuple-element.106), channel_id=1, source_target_pairs={{64,0},{0,32},{128,64},{32,96},{192,128},{96,160},{256,192},{160,2... | collective-permute-start | bytes 49160 | tf_op jit(solution)/shard_map/ppermute | solution.py:70
  18.0 5.4 %collective-permute-start.1 = (f32[1,2,2,8,128]{4,3,2,1,0:T(8,128)S(1)}, f32[1,2,2,8,128]{4,3,2,1,0:T(8,128)S(1)}, u32[]{:S(2)}, u32[]{:S(2)}) collective-permute-start(f32[1,2,2,8,128]{4,3,2,1,0:T(8,128)S(1)} %get-tuple-element.107), channel_id=1, source_target_pairs={{0,64},{32,0},{64,128},{96,32},{128,192},{160,96},{192,256},{224,1... | collective-permute-start | bytes 49160 | tf_op jit(solution)/shard_map/ppermute | solution.py:70
  23.4 12.1 %collective-permute-start.6 = (f32[4,1,2,8,128]{4,3,2,1,0:T(8,128)S(1)}, f32[4,1,2,8,128]{4,3,2,1,0:T(8,128)S(1)}, u32[]{:S(2)}, u32[]{:S(2)}) collective-permute-start(f32[4,1,2,8,128]{4,3,2,1,0:T(8,128)S(1)} %get-tuple-element.98), channel_id=1, source_target_pairs={{0,24},{32,56},{64,88},{96,120},{128,152},{160,184},{192,216},{224... | collective-permute-start | bytes 98312 | tf_op jit(solution)/shard_map/ppermute | solution.py:70
  28.1 8.3 %collective-permute-start.4 = (f32[4,1,2,8,128]{4,3,2,1,0:T(8,128)S(1)}, f32[4,1,2,8,128]{4,3,2,1,0:T(8,128)S(1)}, u32[]{:S(2)}, u32[]{:S(2)}) collective-permute-start(f32[4,1,2,8,128]{4,3,2,1,0:T(8,128)S(1)} %get-tuple-element.99), channel_id=1, source_target_pairs={{0,8},{32,0},{64,72},{96,64},{128,136},{160,128},{192,200},{224,19... | collective-permute-start | bytes 98312 | tf_op jit(solution)/shard_map/ppermute | solution.py:70
  35.5 1.2 collective-permute-start.5
  36.7 5.1 %copy-start.3 = (f32[8,128]{1,0:T(8,128)S(1)}, f32[8,128]{1,0:T(8,128)}, u32[]{:S(2)}) copy-start(f32[8,128]{1,0:T(8,128)} %wb_ref.3) | copy-start | bytes 12292
  36.8 5.1 %copy-start.4 = (f32[6,128]{1,0:T(8,128)S(1)}, f32[6,128]{1,0:T(8,128)}, u32[]{:S(2)}) copy-start(f32[6,128]{1,0:T(8,128)} %ec_ref.1) | copy-start | bytes 9220
  36.8 5.1 %copy-start.5 = (f32[6,128]{1,0:T(8,128)S(1)}, f32[6,128]{1,0:T(8,128)}, u32[]{:S(2)}) copy-start(f32[6,128]{1,0:T(8,128)} %ep_ref.1) | copy-start | bytes 9220
  36.8 5.1 %collective-permute-start.8 = (f32[4,4,8,128]{3,2,1,0:T(8,128)S(1)}, f32[4,4,8,128]{3,2,1,0:T(8,128)S(1)}, u32[]{:S(2)}, u32[]{:S(2)}) collective-permute-start(f32[4,4,8,128]{3,2,1,0:T(8,128)S(1)} %get-tuple-element.82), channel_id=1, source_target_pairs={{33,1},{2,33},{34,2},{3,34},{35,3},{0,35},{32,0},{1,32},{41,9},{10... | collective-permute-start | bytes 196616 | tf_op jit(solution)/shard_map/ppermute | solution.py:70
  39.5 2.4 %copy-start.1 = (f32[128,64]{0,1:T(8,128)S(1)}, f32[128,64]{0,1:T(8,128)}, u32[]{:S(2)}) copy-start(f32[128,64]{0,1:T(8,128)} %param.22) | copy-start | bytes 98308
  39.6 2.4 %copy-start.2 = (f32[128,64]{0,1:T(8,128)S(1)}, f32[128,64]{0,1:T(8,128)}, u32[]{:S(2)}) copy-start(f32[128,64]{0,1:T(8,128)} %param.23) | copy-start | bytes 98308
  39.6 2.3 %collective-permute-start.7 = (f32[4,4,8,128]{3,2,1,0:T(8,128)S(1)}, f32[4,4,8,128]{3,2,1,0:T(8,128)S(1)}, u32[]{:S(2)}, u32[]{:S(2)}) collective-permute-start(f32[4,4,8,128]{3,2,1,0:T(8,128)S(1)} %get-tuple-element.83), channel_id=1, source_target_pairs={{1,33},{33,2},{2,34},{34,3},{3,35},{35,0},{0,32},{32,1},{9,41},{41... | collective-permute-start | bytes 196616 | tf_op jit(solution)/shard_map/ppermute | solution.py:70
  43.2 2.5 %collective-permute-start.11 = (f32[1,2,2,8,192]{4,3,2,1,0:T(8,128)S(1)}, f32[1,2,2,8,192]{4,3,2,1,0:T(8,128)S(1)}, u32[]{:S(2)}, u32[]{:S(2)}) collective-permute-start(f32[1,2,2,8,192]{4,3,2,1,0:T(8,128)S(1)} %get-tuple-element.95), channel_id=1, source_target_pairs={{0,452},{32,484},{452,0},{484,32},{8,460},{40,492},{460,8},{492,40... | collective-permute-start | bytes 73736 | tf_op jit(solution)/shard_map/ppermute | solution.py:70
  43.8 3.1 %collective-permute-start.10 = (f32[1,2,2,8,192]{4,3,2,1,0:T(8,128)S(1)}, f32[1,2,2,8,192]{4,3,2,1,0:T(8,128)S(1)}, u32[]{:S(2)}, u32[]{:S(2)}) collective-permute-start(f32[1,2,2,8,192]{4,3,2,1,0:T(8,128)S(1)} %get-tuple-element.96), channel_id=1, source_target_pairs={{64,0},{0,32},{128,64},{32,96},{192,128},{96,160},{256,192},{160,2... | collective-permute-start | bytes 73736 | tf_op jit(solution)/shard_map/ppermute | solution.py:70
  43.9 3.0 %collective-permute-start.9 = (f32[1,2,2,8,192]{4,3,2,1,0:T(8,128)S(1)}, f32[1,2,2,8,192]{4,3,2,1,0:T(8,128)S(1)}, u32[]{:S(2)}, u32[]{:S(2)}) collective-permute-start(f32[1,2,2,8,192]{4,3,2,1,0:T(8,128)S(1)} %get-tuple-element.97), channel_id=1, source_target_pairs={{0,64},{32,0},{64,128},{96,32},{128,192},{160,96},{192,256},{224,1... | collective-permute-start | bytes 73736 | tf_op jit(solution)/shard_map/ppermute | solution.py:70
  47.0 7.8 %collective-permute-start.14 = (f32[4,1,2,8,192]{4,3,2,1,0:T(8,128)S(1)}, f32[4,1,2,8,192]{4,3,2,1,0:T(8,128)S(1)}, u32[]{:S(2)}, u32[]{:S(2)}) collective-permute-start(f32[4,1,2,8,192]{4,3,2,1,0:T(8,128)S(1)} %get-tuple-element.79), channel_id=1, source_target_pairs={{0,24},{32,56},{64,88},{96,120},{128,152},{160,184},{192,216},{224... | collective-permute-start | bytes 147464 | tf_op jit(solution)/shard_map/ppermute | solution.py:70
  49.7 5.9 %collective-permute-start.12 = (f32[4,1,2,8,192]{4,3,2,1,0:T(8,128)S(1)}, f32[4,1,2,8,192]{4,3,2,1,0:T(8,128)S(1)}, u32[]{:S(2)}, u32[]{:S(2)}) collective-permute-start(f32[4,1,2,8,192]{4,3,2,1,0:T(8,128)S(1)} %get-tuple-element.80), channel_id=1, source_target_pairs={{0,8},{32,0},{64,72},{96,64},{128,136},{160,128},{192,200},{224,19... | collective-permute-start | bytes 147464 | tf_op jit(solution)/shard_map/ppermute | solution.py:70
  54.7 1.7 %collective-permute-start.13 = (f32[4,1,2,8,192]{4,3,2,1,0:T(8,128)S(1)}, f32[4,1,2,8,192]{4,3,2,1,0:T(8,128)S(1)}, u32[]{:S(2)}, u32[]{:S(2)}) collective-permute-start(f32[4,1,2,8,192]{4,3,2,1,0:T(8,128)S(1)} %get-tuple-element.81), channel_id=1, source_target_pairs={{8,0},{0,32},{72,64},{64,96},{136,128},{128,160},{200,192},{192,22... | collective-permute-start | bytes 147464 | tf_op jit(solution)/shard_map/ppermute | solution.py:70
  56.5 4.4 %copy-start = (f32[192,128]{1,0:T(8,128)S(1)}, f32[192,128]{1,0:T(8,128)}, u32[]{:S(2)}) copy-start(f32[192,128]{1,0:T(8,128)} %wm_ref.5) | copy-start | bytes 294916
  56.5 6.8 %collective-permute-start.16 = (f32[4,4,8,192]{3,2,1,0:T(8,128)S(1)}, f32[4,4,8,192]{3,2,1,0:T(8,128)S(1)}, u32[]{:S(2)}, u32[]{:S(2)}) collective-permute-start(f32[4,4,8,192]{3,2,1,0:T(8,128)S(1)} %get-tuple-element.67), channel_id=1, source_target_pairs={{33,1},{2,33},{34,2},{3,34},{35,3},{0,35},{32,0},{1,32},{41,9},{10... | collective-permute-start | bytes 294920 | tf_op jit(solution)/shard_map/ppermute | solution.py:70
  59.1 1.6 %copy-start.6 = (f32[128]{0:T(128)S(1)}, f32[128]{0:T(128)}, u32[]{:S(2)}) copy-start(f32[128]{0:T(128)} %param.25) | copy-start | bytes 1540
  59.1 4.2 %collective-permute-start.15 = (f32[4,4,8,192]{3,2,1,0:T(8,128)S(1)}, f32[4,4,8,192]{3,2,1,0:T(8,128)S(1)}, u32[]{:S(2)}, u32[]{:S(2)}) collective-permute-start(f32[4,4,8,192]{3,2,1,0:T(8,128)S(1)} %get-tuple-element.68), channel_id=1, source_target_pairs={{1,33},{33,2},{2,34},{34,3},{3,35},{35,0},{0,32},{32,1},{9,41},{41... | collective-permute-start | bytes 294920 | tf_op jit(solution)/shard_map/ppermute | solution.py:70
  65.1 5.2 %collective-permute-start.17 = (f32[4,4,8,192]{3,2,1,0:T(8,128)S(1)}, f32[4,4,8,192]{3,2,1,0:T(8,128)S(1)}, u32[]{:S(2)}, u32[]{:S(2)}) collective-permute-start(f32[4,4,8,192]{3,2,1,0:T(8,128)S(1)} %bitcast.60), channel_id=1, source_target_pairs={{1,33},{33,2},{2,34},{34,3},{3,35},{35,0},{0,32},{32,1},{9,41},{41... | collective-permute-start | bytes 294920 | tf_op jit(solution)/shard_map/ppermute | solution.py:70
  68.1 5.6 %collective-permute-start.18 = (f32[4,4,8,192]{3,2,1,0:T(8,128)S(1)}, f32[4,4,8,192]{3,2,1,0:T(8,128)S(1)}, u32[]{:S(2)}, u32[]{:S(2)}) collective-permute-start(f32[4,4,8,192]{3,2,1,0:T(8,128)S(1)} %bitcast.59), channel_id=1, source_target_pairs={{33,1},{2,33},{34,2},{3,34},{35,3},{0,35},{32,0},{1,32},{41,9},{10... | collective-permute-start | bytes 294920 | tf_op jit(solution)/shard_map/ppermute | solution.py:70
  73.8 6.2 %collective-permute-start.21 = (f32[4,1,2,8,192]{4,3,2,1,0:T(8,128)S(1)}, f32[4,1,2,8,192]{4,3,2,1,0:T(8,128)S(1)}, u32[]{:S(2)}, u32[]{:S(2)}) collective-permute-start(f32[4,1,2,8,192]{4,3,2,1,0:T(8,128)S(1)} %get-tuple-element.64), channel_id=1, source_target_pairs={{0,24},{32,56},{64,88},{96,120},{128,152},{160,184},{192,216},{224... | collective-permute-start | bytes 147464 | tf_op jit(solution)/shard_map/ppermute | solution.py:70
  77.5 3.1 %collective-permute-start.19 = (f32[4,1,2,8,192]{4,3,2,1,0:T(8,128)S(1)}, f32[4,1,2,8,192]{4,3,2,1,0:T(8,128)S(1)}, u32[]{:S(2)}, u32[]{:S(2)}) collective-permute-start(f32[4,1,2,8,192]{4,3,2,1,0:T(8,128)S(1)} %get-tuple-element.65), channel_id=1, source_target_pairs={{0,8},{32,0},{64,72},{96,64},{128,136},{160,128},{192,200},{224,19... | collective-permute-start | bytes 147464 | tf_op jit(solution)/shard_map/ppermute | solution.py:70
  77.5 3.1 %collective-permute-start.20 = (f32[4,1,2,8,192]{4,3,2,1,0:T(8,128)S(1)}, f32[4,1,2,8,192]{4,3,2,1,0:T(8,128)S(1)}, u32[]{:S(2)}, u32[]{:S(2)}) collective-permute-start(f32[4,1,2,8,192]{4,3,2,1,0:T(8,128)S(1)} %get-tuple-element.66), channel_id=1, source_target_pairs={{8,0},{0,32},{72,64},{64,96},{136,128},{128,160},{200,192},{192,22... | collective-permute-start | bytes 147464 | tf_op jit(solution)/shard_map/ppermute | solution.py:70
  80.7 2.4 %collective-permute-start.24 = (f32[1,2,2,8,192]{4,3,2,1,0:T(8,128)S(1)}, f32[1,2,2,8,192]{4,3,2,1,0:T(8,128)S(1)}, u32[]{:S(2)}, u32[]{:S(2)}) collective-permute-start(f32[1,2,2,8,192]{4,3,2,1,0:T(8,128)S(1)} %get-tuple-element.76), channel_id=1, source_target_pairs={{0,452},{32,484},{452,0},{484,32},{8,460},{40,492},{460,8},{492,40... | collective-permute-start | bytes 73736 | tf_op jit(solution)/shard_map/ppermute | solution.py:70
  81.4 2.8 %collective-permute-start.22 = (f32[1,2,2,8,192]{4,3,2,1,0:T(8,128)S(1)}, f32[1,2,2,8,192]{4,3,2,1,0:T(8,128)S(1)}, u32[]{:S(2)}, u32[]{:S(2)}) collective-permute-start(f32[1,2,2,8,192]{4,3,2,1,0:T(8,128)S(1)} %get-tuple-element.77), channel_id=1, source_target_pairs={{0,64},{32,0},{64,128},{96,32},{128,192},{160,96},{192,256},{224,1... | collective-permute-start | bytes 73736 | tf_op jit(solution)/shard_map/ppermute | solution.py:70
  83.1 4.4 %collective-permute-start.23 = (f32[1,2,2,8,192]{4,3,2,1,0:T(8,128)S(1)}, f32[1,2,2,8,192]{4,3,2,1,0:T(8,128)S(1)}, u32[]{:S(2)}, u32[]{:S(2)}) collective-permute-start(f32[1,2,2,8,192]{4,3,2,1,0:T(8,128)S(1)} %get-tuple-element.78), channel_id=1, source_target_pairs={{64,0},{0,32},{128,64},{32,96},{192,128},{96,160},{256,192},{160,2... | collective-permute-start | bytes 73736 | tf_op jit(solution)/shard_map/ppermute | solution.py:70
  88.5 1.3 %collective-permute-start.25 = (f32[4,4,8,128]{3,2,1,0:T(8,128)S(1)}, f32[4,4,8,128]{3,2,1,0:T(8,128)S(1)}, u32[]{:S(2)}, u32[]{:S(2)}) collective-permute-start(f32[4,4,8,128]{3,2,1,0:T(8,128)S(1)} %bitcast.62), channel_id=1, source_target_pairs={{1,33},{33,2},{2,34},{34,3},{3,35},{35,0},{0,32},{32,1},{9,41},{41... | collective-permute-start | bytes 196616 | tf_op jit(solution)/shard_map/ppermute | solution.py:70
  88.6 4.9 %collective-permute-start.26 = (f32[4,4,8,128]{3,2,1,0:T(8,128)S(1)}, f32[4,4,8,128]{3,2,1,0:T(8,128)S(1)}, u32[]{:S(2)}, u32[]{:S(2)}) collective-permute-start(f32[4,4,8,128]{3,2,1,0:T(8,128)S(1)} %bitcast.61), channel_id=1, source_target_pairs={{33,1},{2,33},{34,2},{3,34},{35,3},{0,35},{32,0},{1,32},{41,9},{10... | collective-permute-start | bytes 196616 | tf_op jit(solution)/shard_map/ppermute | solution.py:70
  93.5 5.9 %collective-permute-start.29 = (f32[4,1,2,8,128]{4,3,2,1,0:T(8,128)S(1)}, f32[4,1,2,8,128]{4,3,2,1,0:T(8,128)S(1)}, u32[]{:S(2)}, u32[]{:S(2)}) collective-permute-start(f32[4,1,2,8,128]{4,3,2,1,0:T(8,128)S(1)} %get-tuple-element.73), channel_id=1, source_target_pairs={{0,24},{32,56},{64,88},{96,120},{128,152},{160,184},{192,216},{224... | collective-permute-start | bytes 98312 | tf_op jit(solution)/shard_map/ppermute | solution.py:70
  96.3 3.1 %collective-permute-start.27 = (f32[4,1,2,8,128]{4,3,2,1,0:T(8,128)S(1)}, f32[4,1,2,8,128]{4,3,2,1,0:T(8,128)S(1)}, u32[]{:S(2)}, u32[]{:S(2)}) collective-permute-start(f32[4,1,2,8,128]{4,3,2,1,0:T(8,128)S(1)} %get-tuple-element.74), channel_id=1, source_target_pairs={{0,8},{32,0},{64,72},{96,64},{128,136},{160,128},{192,200},{224,19... | collective-permute-start | bytes 98312 | tf_op jit(solution)/shard_map/ppermute | solution.py:70
  96.4 3.0 %collective-permute-start.28 = (f32[4,1,2,8,128]{4,3,2,1,0:T(8,128)S(1)}, f32[4,1,2,8,128]{4,3,2,1,0:T(8,128)S(1)}, u32[]{:S(2)}, u32[]{:S(2)}) collective-permute-start(f32[4,1,2,8,128]{4,3,2,1,0:T(8,128)S(1)} %get-tuple-element.75), channel_id=1, source_target_pairs={{8,0},{0,32},{72,64},{64,96},{136,128},{128,160},{200,192},{192,22... | collective-permute-start | bytes 98312 | tf_op jit(solution)/shard_map/ppermute | solution.py:70
  99.5 3.2 %collective-permute-start.32 = (f32[1,2,2,8,128]{4,3,2,1,0:T(8,128)S(1)}, f32[1,2,2,8,128]{4,3,2,1,0:T(8,128)S(1)}, u32[]{:S(2)}, u32[]{:S(2)}) collective-permute-start(f32[1,2,2,8,128]{4,3,2,1,0:T(8,128)S(1)} %get-tuple-element.92), channel_id=1, source_target_pairs={{0,452},{32,484},{452,0},{484,32},{8,460},{40,492},{460,8},{492,40... | collective-permute-start | bytes 49160 | tf_op jit(solution)/shard_map/ppermute | solution.py:70
  100.1 3.4 %collective-permute-start.30 = (f32[1,2,2,8,128]{4,3,2,1,0:T(8,128)S(1)}, f32[1,2,2,8,128]{4,3,2,1,0:T(8,128)S(1)}, u32[]{:S(2)}, u32[]{:S(2)}) collective-permute-start(f32[1,2,2,8,128]{4,3,2,1,0:T(8,128)S(1)} %get-tuple-element.93), channel_id=1, source_target_pairs={{0,64},{32,0},{64,128},{96,32},{128,192},{160,96},{192,256},{224,1... | collective-permute-start | bytes 49160 | tf_op jit(solution)/shard_map/ppermute | solution.py:70
  102.6 4.8 %collective-permute-start.31 = (f32[1,2,2,8,128]{4,3,2,1,0:T(8,128)S(1)}, f32[1,2,2,8,128]{4,3,2,1,0:T(8,128)S(1)}, u32[]{:S(2)}, u32[]{:S(2)}) collective-permute-start(f32[1,2,2,8,128]{4,3,2,1,0:T(8,128)S(1)} %get-tuple-element.94), channel_id=1, source_target_pairs={{64,0},{0,32},{128,64},{32,96},{192,128},{96,160},{256,192},{160,2... | collective-permute-start | bytes 49160 | tf_op jit(solution)/shard_map/ppermute | solution.py:70
  107.7 13.1 %collective-permute-start.33 = (f32[16,128]{1,0:T(8,128)S(1)}, f32[16,128]{1,0:T(8,128)S(1)}, u32[]{:S(2)}, u32[]{:S(2)}) collective-permute-start(f32[16,128]{1,0:T(8,128)S(1)} %k_force.1), channel_id=1, source_target_pairs={{1,0},{33,1},{2,2},{34,3},{3,4},{35,5},{0,6},{32,7},{9,8},{41,9},{... | collective-permute-start | bytes 24584 | tf_op jit(solution)/shard_map/ppermute | solution.py:70

commit v12 on v10

--- a/solution.py
+++ b/solution.py
@@ -101,7 +101,7 @@
     last = send(before, DOWN)
     cells = cells + jnp.stack([first, last], axis=2)
     cells, beside = lax.optimization_barrier((cells, beside))
-    for axis in (1, 0):
+    for axis in (0, 1):
         first = lax.slice_in_dim(cells, 0, 1, axis=axis)
         last = lax.slice_in_dim(cells, 3, 4, axis=axis)
         from_before, from_after = swap(axis, first, last, here)

time: 117 us -> 118 us (level)
  the two profiles are of different devices: /device:TPU:33 before, /device:TPU:17 now
where the time goes in v12:
time: 118 us
  starting transfers between devices  62.6 us (53%)
  waiting for transfers between devices  41.6 us (35%)
  Pallas kernels  11.9 us (10%)
    ppermute x34, starting transfers between devices, send(): return lax.ppermute(x, AXES, pairs)  62.6 us
    ppermute x34, waiting for transfers between devices, send(): return lax.ppermute(x, AXES, pairs)  41.6 us
    pallas_call x10, Pallas kernels, call(): pl.pallas_call(kernel, out_shape=shapes, in_specs=[spec] * len(args), out...  10.4 us
  transfers between devices with their start and end apart: 34, of which 22 were waited for; matrix products, arithmetic and copies ran while one was open for 0% of the time, Pallas kernels for 5%

profile of v12, /device:TPU:17, one launch (start us, length us, event | category | flops | bytes accessed | tf_op | source)
XLA Modules:
  0.0 117.8 jit_solution(2523186418918878632)
XLA Ops:
  0.6 1.5 %k_pack.1 = f32[48,128]{1,0:T(8,128)} custom-call(f32[3,1,1,1,512]{4,3,2,1,0:T(1,128)} %pos_in.1, s32[1,1,1,512]{3,2,1,0:T(1,128)} %kind_in.1, s32[2,2,2,8]{3,2,1,0:T(2,128)} %names_in.1, s32[1,1,1,8,128]{4,3,2,1,0:T(8,128)} %center_in.1, s32[1,1,1,8,128]{4,3,2,1,0:T(8,128)} %partner_in.1, s32[1,1,1,8,128]{4,3,2,1,0:T(8,128)} %live_in.1), custom_call_target="tpu_custom_call" | custom-call | tf_op jit(solution)/shard_map/k_pack/pallas_call | solution.py:253
  2.1 5.0 %collective-permute-start = (f32[48,128]{1,0:T(8,128)}, f32[48,128]{1,0:T(8,128)S(1)}, u32[]{:S(2)}, u32[]{:S(2)}) collective-permute-start(f32[48,128]{1,0:T(8,128)} %k_pack.1), channel_id=1, source_target_pairs={{0,1},{1,33},{2,2},{3,34},{4,3},{5,35},{6,0},{7,32},{8,9},{9,41},{... | collective-permute-start | bytes 73736 | tf_op jit(solution)/shard_map/ppermute | solution.py:70
  7.2 15.1 %collective-permute-done.packed_ref = f32[48,128]{1,0:T(8,128)S(1)} collective-permute-done((f32[48,128]{1,0:T(8,128)}, f32[48,128]{1,0:T(8,128)S(1)}, u32[]{:S(2)}, u32[]{:S(2)}) %collective-permute-start) | collective-permute-done | bytes 24608 | tf_op jit(solution)/shard_map/ppermute | solution.py:70
  22.6 1.9 %collective-permute-start.3 = (f32[1,2,2,8,128]{4,3,2,1,0:T(8,128)S(1)}, f32[1,2,2,8,128]{4,3,2,1,0:T(8,128)S(1)}, u32[]{:S(2)}, u32[]{:S(2)}) collective-permute-start(f32[1,2,2,8,128]{4,3,2,1,0:T(8,128)S(1)} %get-tuple-element.105), channel_id=1, source_target_pairs={{0,452},{32,484},{452,0},{484,32},{8,460},{40,492},{460,8},{492,40... | collective-permute-start | bytes 49160 | tf_op jit(solution)/shard_map/ppermute | solution.py:70
  24.6 0.7 collective-permute-start.1
  25.2 3.1 %collective-permute-done.3 = f32[1,2,2,8,128]{4,3,2,1,0:T(8,128)S(1)} collective-permute-done((f32[1,2,2,8,128]{4,3,2,1,0:T(8,128)S(1)}, f32[1,2,2,8,128]{4,3,2,1,0:T(8,128)S(1)}, u32[]{:S(2)}, u32[]{:S(2)}) %collective-permute-start.3) | collective-permute-done | bytes 16416 | tf_op jit(solution)/shard_map/ppermute | solution.py:70
  28.4 0.7 collective-permute-start.6
  29.2 2.1 %collective-permute-start.5 = (f32[4,1,2,8,128]{4,3,2,1,0:T(8,128)S(1)}, f32[4,1,2,8,128]{4,3,2,1,0:T(8,128)S(1)}, u32[]{:S(2)}, u32[]{:S(2)}) collective-permute-start(f32[4,1,2,8,128]{4,3,2,1,0:T(8,128)S(1)} %get-tuple-element.100), channel_id=1, source_target_pairs={{8,0},{0,32},{72,64},{64,96},{136,128},{128,160},{200,192},{192,22... | collective-permute-start | bytes 98312 | tf_op jit(solution)/shard_map/ppermute | solution.py:70
  31.3 1.3 %collective-permute-done.4 = f32[4,1,2,8,128]{4,3,2,1,0:T(8,128)S(1)} collective-permute-done((f32[4,1,2,8,128]{4,3,2,1,0:T(8,128)S(1)}, f32[4,1,2,8,128]{4,3,2,1,0:T(8,128)S(1)}, u32[]{:S(2)}, u32[]{:S(2)}) %collective-permute-start.4) | collective-permute-done | bytes 32800 | tf_op jit(solution)/shard_map/ppermute | solution.py:70
  32.6 2.1 %collective-permute-done.5 = f32[4,1,2,8,128]{4,3,2,1,0:T(8,128)S(1)} collective-permute-done((f32[4,1,2,8,128]{4,3,2,1,0:T(8,128)S(1)}, f32[4,1,2,8,128]{4,3,2,1,0:T(8,128)S(1)}, u32[]{:S(2)}, u32[]{:S(2)}) %collective-permute-start.5) | collective-permute-done | bytes 32800 | tf_op jit(solution)/shard_map/ppermute | solution.py:70
  34.8 5.1 %collective-permute-start.8 = (f32[4,4,8,128]{3,2,1,0:T(8,128)S(1)}, f32[4,4,8,128]{3,2,1,0:T(8,128)S(1)}, u32[]{:S(2)}, u32[]{:S(2)}) collective-permute-start(f32[4,4,8,128]{3,2,1,0:T(8,128)S(1)} %get-tuple-element.82), channel_id=1, source_target_pairs={{33,1},{2,33},{34,2},{3,34},{35,3},{0,35},{32,0},{1,32},{41,9},{10... | collective-permute-start | bytes 196616 | tf_op jit(solution)/shard_map/ppermute | solution.py:70
  39.9 2.0 %collective-permute-start.7 = (f32[4,4,8,128]{3,2,1,0:T(8,128)S(1)}, f32[4,4,8,128]{3,2,1,0:T(8,128)S(1)}, u32[]{:S(2)}, u32[]{:S(2)}) collective-permute-start(f32[4,4,8,128]{3,2,1,0:T(8,128)S(1)} %get-tuple-element.83), channel_id=1, source_target_pairs={{1,33},{33,2},{2,34},{34,3},{3,35},{35,0},{0,32},{32,1},{9,41},{41... | collective-permute-start | bytes 196616 | tf_op jit(solution)/shard_map/ppermute | solution.py:70
  42.3 1.8 %collective-permute-done.8 = f32[4,4,8,128]{3,2,1,0:T(8,128)S(1)} collective-permute-done((f32[4,4,8,128]{3,2,1,0:T(8,128)S(1)}, f32[4,4,8,128]{3,2,1,0:T(8,128)S(1)}, u32[]{:S(2)}, u32[]{:S(2)}) %collective-permute-start.8) | collective-permute-done | bytes 65568 | tf_op jit(solution)/shard_map/ppermute | solution.py:70
  44.1 1.2 %k_features.1 = (f32[32,192]{1,0:T(8,128)S(1)}, f32[32,192]{1,0:T(8,128)S(1)}, f32[8,1024]{1,0:T(8,128)S(1)}, f32[128,1024]{1,0:T(8,128)S(1)}, f32[128,1024]{1,0:T(8,128)S(1)}) custom-call(f32[48,128]{1,0:T(8,128)S(1)} %collective-permute-done.packed_ref, f32[8,1024]{1,0:T(8,128)S(1)} %k_own_pairs.1.part_ref, f32[128,128]{1,0:T(8,128)S(1)} %bitcast.58, ...), custom_call_target="tpu_custom_call" | custom-call | tf_op jit(solution)/shard_map/k_features/pallas_call | solution.py:519
  45.3 2.5 %collective-permute-start.11 = (f32[1,2,2,8,192]{4,3,2,1,0:T(8,128)S(1)}, f32[1,2,2,8,192]{4,3,2,1,0:T(8,128)S(1)}, u32[]{:S(2)}, u32[]{:S(2)}) collective-permute-start(f32[1,2,2,8,192]{4,3,2,1,0:T(8,128)S(1)} %get-tuple-element.95), channel_id=1, source_target_pairs={{0,452},{32,484},{452,0},{484,32},{8,460},{40,492},{460,8},{492,40... | collective-permute-start | bytes 73736 | tf_op jit(solution)/shard_map/ppermute | solution.py:70
  47.9 2.2 %collective-permute-start.9 = (f32[1,2,2,8,192]{4,3,2,1,0:T(8,128)S(1)}, f32[1,2,2,8,192]{4,3,2,1,0:T(8,128)S(1)}, u32[]{:S(2)}, u32[]{:S(2)}) collective-permute-start(f32[1,2,2,8,192]{4,3,2,1,0:T(8,128)S(1)} %get-tuple-element.97), channel_id=1, source_target_pairs={{0,64},{32,0},{64,128},{96,32},{128,192},{160,96},{192,256},{224,1... | collective-permute-start | bytes 73736 | tf_op jit(solution)/shard_map/ppermute | solution.py:70
  50.1 1.1 collective-permute-done.11
  51.3 0.7 collective-permute-start.14
  52.0 3.4 %collective-permute-start.13 = (f32[4,1,2,8,192]{4,3,2,1,0:T(8,128)S(1)}, f32[4,1,2,8,192]{4,3,2,1,0:T(8,128)S(1)}, u32[]{:S(2)}, u32[]{:S(2)}) collective-permute-start(f32[4,1,2,8,192]{4,3,2,1,0:T(8,128)S(1)} %get-tuple-element.81), channel_id=1, source_target_pairs={{8,0},{0,32},{72,64},{64,96},{136,128},{128,160},{200,192},{192,22... | collective-permute-start | bytes 147464 | tf_op jit(solution)/shard_map/ppermute | solution.py:70
  55.4 1.6 %collective-permute-done.12 = f32[4,1,2,8,192]{4,3,2,1,0:T(8,128)S(1)} collective-permute-done((f32[4,1,2,8,192]{4,3,2,1,0:T(8,128)S(1)}, f32[4,1,2,8,192]{4,3,2,1,0:T(8,128)S(1)}, u32[]{:S(2)}, u32[]{:S(2)}) %collective-permute-start.12) | collective-permute-done | bytes 49184 | tf_op jit(solution)/shard_map/ppermute | solution.py:70
  57.1 1.0 collective-permute-done.13
  58.1 3.4 %collective-permute-start.16 = (f32[4,4,8,192]{3,2,1,0:T(8,128)S(1)}, f32[4,4,8,192]{3,2,1,0:T(8,128)S(1)}, u32[]{:S(2)}, u32[]{:S(2)}) collective-permute-start(f32[4,4,8,192]{3,2,1,0:T(8,128)S(1)} %get-tuple-element.67), channel_id=1, source_target_pairs={{33,1},{2,33},{34,2},{3,34},{35,3},{0,35},{32,0},{1,32},{41,9},{10... | collective-permute-start | bytes 294920 | tf_op jit(solution)/shard_map/ppermute | solution.py:70
  61.5 1.7 %collective-permute-start.15 = (f32[4,4,8,192]{3,2,1,0:T(8,128)S(1)}, f32[4,4,8,192]{3,2,1,0:T(8,128)S(1)}, u32[]{:S(2)}, u32[]{:S(2)}) collective-permute-start(f32[4,4,8,192]{3,2,1,0:T(8,128)S(1)} %get-tuple-element.68), channel_id=1, source_target_pairs={{1,33},{33,2},{2,34},{34,3},{3,35},{35,0},{0,32},{32,1},{9,41},{41... | collective-permute-start | bytes 294920 | tf_op jit(solution)/shard_map/ppermute | solution.py:70
  63.4 2.2 %k_own_env.1 = (f32[192,1024]{1,0:T(8,128)S(1)}, f32[192,1024]{1,0:T(8,128)S(1)}, f32[128,1024]{1,0:T(8,128)S(1)}, f32[128,1024]{1,0:T(8,128)S(1)}, f32[128,1024]{1,0:T(8,128)S(1)}, /*index=5*/f32[128,1024]{1,0:T(8,128)S(1)}) custom-call(f32[48,128]{1,0:T(8,128)S(1)} %collective-permute-done.packed_ref, f32[8,1024]{1,0:T(8,128)S(1)} %get-tuple-element.36.scal_ref, ...), custom_call_target="tpu_custom_call" | custom-call | tf_op jit(solution)/shard_map/k_own_env/pallas_call | solution.py:519
  66.2 1.8 %k_energy.1 = (f32[128,192]{1,0:T(8,128)S(1)}, f32[128,192]{1,0:T(8,128)S(1)}, f32[256,192]{1,0:T(8,128)S(1)}, f32[192,1024]{1,0:T(8,128)S(1)}, f32[128,1024]{1,0:T(8,128)S(1)}, /*index=5*/f32[64,1024]{1,0:T(8,128)S(1)}) custom-call(f32[48,128]{1,0:T(8,128)S(1)} %collective-permute-done.packed_ref, f32[8,1024]{1,0:T(8,128)S(1)} %get-tuple-element.36.scal_ref, ...), custom_call_target="tpu_custom_call" | custom-call | tf_op jit(solution)/shard_map/k_energy/pallas_call | solution.py:519
  68.0 1.5 %collective-permute-start.17 = (f32[4,4,8,192]{3,2,1,0:T(8,128)S(1)}, f32[4,4,8,192]{3,2,1,0:T(8,128)S(1)}, u32[]{:S(2)}, u32[]{:S(2)}) collective-permute-start(f32[4,4,8,192]{3,2,1,0:T(8,128)S(1)} %bitcast.60), channel_id=1, source_target_pairs={{1,33},{33,2},{2,34},{34,3},{3,35},{35,0},{0,32},{32,1},{9,41},{41... | collective-permute-start | bytes 294920 | tf_op jit(solution)/shard_map/ppermute | solution.py:70
  69.5 2.2 %k_direct.1 = (f32[8,1024]{1,0:T(8,128)S(1)}, f32[4,512]{1,0:T(4,128)S(1)}) custom-call(f32[48,128]{1,0:T(8,128)S(1)} %collective-permute-done.packed_ref, f32[8,1024]{1,0:T(8,128)S(1)} %get-tuple-element.36.scal_ref, f32[128,1024]{1,0:T(8,128)S(1)} %get-tuple-element.37.av_ref, f32[128,1024]{1,0:T(8,128)S(1)} %get-tuple-element.39.nav_ref, ...), custom_call_target="tpu_custom_call" | custom-call | tf_op jit(solution)/shard_map/k_direct/pallas_call | solution.py:519
  71.7 2.5 %collective-permute-done.18 = f32[4,4,8,192]{3,2,1,0:T(8,128)S(1)} collective-permute-done((f32[4,4,8,192]{3,2,1,0:T(8,128)S(1)}, f32[4,4,8,192]{3,2,1,0:T(8,128)S(1)}, u32[]{:S(2)}, u32[]{:S(2)}) %collective-permute-start.18) | collective-permute-done | bytes 98336 | tf_op jit(solution)/shard_map/ppermute | solution.py:70
  74.2 3.4 %collective-permute-start.21 = (f32[1,4,2,8,192]{4,3,2,1,0:T(8,128)S(1)}, f32[1,4,2,8,192]{4,3,2,1,0:T(8,128)S(1)}, u32[]{:S(2)}, u32[]{:S(2)}) collective-permute-start(f32[1,4,2,8,192]{4,3,2,1,0:T(8,128)S(1)} %get-tuple-element.64), channel_id=1, source_target_pairs={{0,452},{32,484},{452,0},{484,32},{8,460},{40,492},{460,8},{492,40... | collective-permute-start | bytes 147464 | tf_op jit(solution)/shard_map/ppermute | solution.py:70
  78.1 1.1 collective-permute-start.20
  79.2 1.3 %collective-permute-done.21 = f32[1,4,2,8,192]{4,3,2,1,0:T(8,128)S(1)} collective-permute-done((f32[1,4,2,8,192]{4,3,2,1,0:T(8,128)S(1)}, f32[1,4,2,8,192]{4,3,2,1,0:T(8,128)S(1)}, u32[]{:S(2)}, u32[]{:S(2)}) %collective-permute-start.21) | collective-permute-done | bytes 49184 | tf_op jit(solution)/shard_map/ppermute | solution.py:70
  81.2 0.7 collective-permute-start.24
  81.9 1.9 %collective-permute-start.23 = (f32[2,1,2,8,192]{4,3,2,1,0:T(8,128)S(1)}, f32[2,1,2,8,192]{4,3,2,1,0:T(8,128)S(1)}, u32[]{:S(2)}, u32[]{:S(2)}) collective-permute-start(f32[2,1,2,8,192]{4,3,2,1,0:T(8,128)S(1)} %get-tuple-element.78), channel_id=1, source_target_pairs={{8,0},{0,32},{72,64},{64,96},{136,128},{128,160},{200,192},{192,22... | collective-permute-start | bytes 73736 | tf_op jit(solution)/shard_map/ppermute | solution.py:70
  83.8 1.3 %collective-permute-done.22 = f32[2,1,2,8,192]{4,3,2,1,0:T(8,128)S(1)} collective-permute-done((f32[2,1,2,8,192]{4,3,2,1,0:T(8,128)S(1)}, f32[2,1,2,8,192]{4,3,2,1,0:T(8,128)S(1)}, u32[]{:S(2)}, u32[]{:S(2)}) %collective-permute-start.22) | collective-permute-done | bytes 24608 | tf_op jit(solution)/shard_map/ppermute | solution.py:70
  85.0 1.7 %collective-permute-done.23 = f32[2,1,2,8,192]{4,3,2,1,0:T(8,128)S(1)} collective-permute-done((f32[2,1,2,8,192]{4,3,2,1,0:T(8,128)S(1)}, f32[2,1,2,8,192]{4,3,2,1,0:T(8,128)S(1)}, u32[]{:S(2)}, u32[]{:S(2)}) %collective-permute-start.23) | collective-permute-done | bytes 24608 | tf_op jit(solution)/shard_map/ppermute | solution.py:70
  86.8 1.0 k_env_back.1
  87.8 2.8 %collective-permute-start.25 = (f32[4,4,8,128]{3,2,1,0:T(8,128)S(1)}, f32[4,4,8,128]{3,2,1,0:T(8,128)S(1)}, u32[]{:S(2)}, u32[]{:S(2)}) collective-permute-start(f32[4,4,8,128]{3,2,1,0:T(8,128)S(1)} %bitcast.62), channel_id=1, source_target_pairs={{1,33},{33,2},{2,34},{34,3},{3,35},{35,0},{0,32},{32,1},{9,41},{41... | collective-permute-start | bytes 196616 | tf_op jit(solution)/shard_map/ppermute | solution.py:70
  91.1 0.6 k_own_force.1.own_ref
  91.9 2.4 %collective-permute-done.26 = f32[4,4,8,128]{3,2,1,0:T(8,128)S(1)} collective-permute-done((f32[4,4,8,128]{3,2,1,0:T(8,128)S(1)}, f32[4,4,8,128]{3,2,1,0:T(8,128)S(1)}, u32[]{:S(2)}, u32[]{:S(2)}) %collective-permute-start.26) | collective-permute-done | bytes 65568 | tf_op jit(solution)/shard_map/ppermute | solution.py:70
  94.3 3.1 %collective-permute-start.29 = (f32[1,4,2,8,128]{4,3,2,1,0:T(8,128)S(1)}, f32[1,4,2,8,128]{4,3,2,1,0:T(8,128)S(1)}, u32[]{:S(2)}, u32[]{:S(2)}) collective-permute-start(f32[1,4,2,8,128]{4,3,2,1,0:T(8,128)S(1)} %get-tuple-element.73), channel_id=1, source_target_pairs={{0,452},{32,484},{452,0},{484,32},{8,460},{40,492},{460,8},{492,40... | collective-permute-start | bytes 98312 | tf_op jit(solution)/shard_map/ppermute | solution.py:70
  97.4 2.6 %collective-permute-start.27 = (f32[1,4,2,8,128]{4,3,2,1,0:T(8,128)S(1)}, f32[1,4,2,8,128]{4,3,2,1,0:T(8,128)S(1)}, u32[]{:S(2)}, u32[]{:S(2)}) collective-permute-start(f32[1,4,2,8,128]{4,3,2,1,0:T(8,128)S(1)} %get-tuple-element.74), channel_id=1, source_target_pairs={{0,64},{32,0},{64,128},{96,32},{128,192},{160,96},{192,256},{224,1... | collective-permute-start | bytes 98312 | tf_op jit(solution)/shard_map/ppermute | solution.py:70
  100.2 0.7 collective-permute-done.27
  101.3 0.7 collective-permute-start.32
  102.0 2.0 %collective-permute-start.31 = (f32[2,1,2,8,128]{4,3,2,1,0:T(8,128)S(1)}, f32[2,1,2,8,128]{4,3,2,1,0:T(8,128)S(1)}, u32[]{:S(2)}, u32[]{:S(2)}) collective-permute-start(f32[2,1,2,8,128]{4,3,2,1,0:T(8,128)S(1)} %get-tuple-element.94), channel_id=1, source_target_pairs={{8,0},{0,32},{72,64},{64,96},{136,128},{128,160},{200,192},{192,22... | collective-permute-start | bytes 49160 | tf_op jit(solution)/shard_map/ppermute | solution.py:70
  104.0 1.1 collective-permute-done.30
  105.1 1.0 collective-permute-done.31
  106.4 10.0 %collective-permute-start.33 = (f32[16,128]{1,0:T(8,128)S(1)}, f32[16,128]{1,0:T(8,128)S(1)}, u32[]{:S(2)}, u32[]{:S(2)}) collective-permute-start(f32[16,128]{1,0:T(8,128)S(1)} %k_force.1), channel_id=1, source_target_pairs={{1,0},{33,1},{2,2},{34,3},{3,4},{35,5},{0,6},{32,7},{9,8},{41,9},{... | collective-permute-start | bytes 24584 | tf_op jit(solution)/shard_map/ppermute | solution.py:70
  116.4 0.8 collective-permute-done.33.in_ref
  (74 shorter events, 5.2 us)
Async XLA Ops:
  2.1 20.2 %collective-permute-start = (f32[48,128]{1,0:T(8,128)}, f32[48,128]{1,0:T(8,128)S(1)}, u32[]{:S(2)}, u32[]{:S(2)}) collective-permute-start(f32[48,128]{1,0:T(8,128)} %k_pack.1), channel_id=1, source_target_pairs={{0,1},{1,33},{2,2},{3,34},{4,3},{5,35},{6,0},{7,32},{8,9},{9,41},{... | collective-permute-start | bytes 73736 | tf_op jit(solution)/shard_map/ppermute | solution.py:70
  22.6 5.7 %collective-permute-start.3 = (f32[1,2,2,8,128]{4,3,2,1,0:T(8,128)S(1)}, f32[1,2,2,8,128]{4,3,2,1,0:T(8,128)S(1)}, u32[]{:S(2)}, u32[]{:S(2)}) collective-permute-start(f32[1,2,2,8,128]{4,3,2,1,0:T(8,128)S(1)} %get-tuple-element.105), channel_id=1, source_target_pairs={{0,452},{32,484},{452,0},{484,32},{8,460},{40,492},{460,8},{492,40... | collective-permute-start | bytes 49160 | tf_op jit(solution)/shard_map/ppermute | solution.py:70
  24.5 3.8 %collective-permute-start.2 = (f32[1,2,2,8,128]{4,3,2,1,0:T(8,128)S(1)}, f32[1,2,2,8,128]{4,3,2,1,0:T(8,128)S(1)}, u32[]{:S(2)}, u32[]{:S(2)}) collective-permute-start(f32[1,2,2,8,128]{4,3,2,1,0:T(8,128)S(1)} %get-tuple-element.106), channel_id=1, source_target_pairs={{64,0},{0,32},{128,64},{32,96},{192,128},{96,160},{256,192},{160,2... | collective-permute-start | bytes 49160 | tf_op jit(solution)/shard_map/ppermute | solution.py:70
  24.6 3.7 %collective-permute-start.1 = (f32[1,2,2,8,128]{4,3,2,1,0:T(8,128)S(1)}, f32[1,2,2,8,128]{4,3,2,1,0:T(8,128)S(1)}, u32[]{:S(2)}, u32[]{:S(2)}) collective-permute-start(f32[1,2,2,8,128]{4,3,2,1,0:T(8,128)S(1)} %get-tuple-element.107), channel_id=1, source_target_pairs={{0,64},{32,0},{64,128},{96,32},{128,192},{160,96},{192,256},{224,1... | collective-permute-start | bytes 49160 | tf_op jit(solution)/shard_map/ppermute | solution.py:70
  28.4 3.0 %collective-permute-start.6 = (f32[4,1,2,8,128]{4,3,2,1,0:T(8,128)S(1)}, f32[4,1,2,8,128]{4,3,2,1,0:T(8,128)S(1)}, u32[]{:S(2)}, u32[]{:S(2)}) collective-permute-start(f32[4,1,2,8,128]{4,3,2,1,0:T(8,128)S(1)} %get-tuple-element.98), channel_id=1, source_target_pairs={{0,24},{32,56},{64,88},{96,120},{128,152},{160,184},{192,216},{224... | collective-permute-start | bytes 98312 | tf_op jit(solution)/shard_map/ppermute | solution.py:70
  29.0 3.6 %collective-permute-start.4 = (f32[4,1,2,8,128]{4,3,2,1,0:T(8,128)S(1)}, f32[4,1,2,8,128]{4,3,2,1,0:T(8,128)S(1)}, u32[]{:S(2)}, u32[]{:S(2)}) collective-permute-start(f32[4,1,2,8,128]{4,3,2,1,0:T(8,128)S(1)} %get-tuple-element.99), channel_id=1, source_target_pairs={{0,8},{32,0},{64,72},{96,64},{128,136},{160,128},{192,200},{224,19... | collective-permute-start | bytes 98312 | tf_op jit(solution)/shard_map/ppermute | solution.py:70
  29.2 5.5 %collective-permute-start.5 = (f32[4,1,2,8,128]{4,3,2,1,0:T(8,128)S(1)}, f32[4,1,2,8,128]{4,3,2,1,0:T(8,128)S(1)}, u32[]{:S(2)}, u32[]{:S(2)}) collective-permute-start(f32[4,1,2,8,128]{4,3,2,1,0:T(8,128)S(1)} %get-tuple-element.100), channel_id=1, source_target_pairs={{8,0},{0,32},{72,64},{64,96},{136,128},{128,160},{200,192},{192,22... | collective-permute-start | bytes 98312 | tf_op jit(solution)/shard_map/ppermute | solution.py:70
  34.7 9.4 %copy-start.3 = (f32[8,128]{1,0:T(8,128)S(1)}, f32[8,128]{1,0:T(8,128)}, u32[]{:S(2)}) copy-start(f32[8,128]{1,0:T(8,128)} %wb_ref.3) | copy-start | bytes 12292
  34.7 9.4 %copy-start.4 = (f32[6,128]{1,0:T(8,128)S(1)}, f32[6,128]{1,0:T(8,128)}, u32[]{:S(2)}) copy-start(f32[6,128]{1,0:T(8,128)} %ec_ref.1) | copy-start | bytes 9220
  34.7 9.3 %copy-start.5 = (f32[6,128]{1,0:T(8,128)S(1)}, f32[6,128]{1,0:T(8,128)}, u32[]{:S(2)}) copy-start(f32[6,128]{1,0:T(8,128)} %ep_ref.1) | copy-start | bytes 9220
  34.8 9.3 %collective-permute-start.8 = (f32[4,4,8,128]{3,2,1,0:T(8,128)S(1)}, f32[4,4,8,128]{3,2,1,0:T(8,128)S(1)}, u32[]{:S(2)}, u32[]{:S(2)}) collective-permute-start(f32[4,4,8,128]{3,2,1,0:T(8,128)S(1)} %get-tuple-element.82), channel_id=1, source_target_pairs={{33,1},{2,33},{34,2},{3,34},{35,3},{0,35},{32,0},{1,32},{41,9},{10... | collective-permute-start | bytes 196616 | tf_op jit(solution)/shard_map/ppermute | solution.py:70
  39.9 4.2 %copy-start.1 = (f32[128,64]{0,1:T(8,128)S(1)}, f32[128,64]{0,1:T(8,128)}, u32[]{:S(2)}) copy-start(f32[128,64]{0,1:T(8,128)} %param.22) | copy-start | bytes 98308
  39.9 4.2 %copy-start.2 = (f32[128,64]{0,1:T(8,128)S(1)}, f32[128,64]{0,1:T(8,128)}, u32[]{:S(2)}) copy-start(f32[128,64]{0,1:T(8,128)} %param.23) | copy-start | bytes 98308
  39.9 4.2 %collective-permute-start.7 = (f32[4,4,8,128]{3,2,1,0:T(8,128)S(1)}, f32[4,4,8,128]{3,2,1,0:T(8,128)S(1)}, u32[]{:S(2)}, u32[]{:S(2)}) collective-permute-start(f32[4,4,8,128]{3,2,1,0:T(8,128)S(1)} %get-tuple-element.83), channel_id=1, source_target_pairs={{1,33},{33,2},{2,34},{34,3},{3,35},{35,0},{0,32},{32,1},{9,41},{41... | collective-permute-start | bytes 196616 | tf_op jit(solution)/shard_map/ppermute | solution.py:70
  45.3 5.9 %collective-permute-start.11 = (f32[1,2,2,8,192]{4,3,2,1,0:T(8,128)S(1)}, f32[1,2,2,8,192]{4,3,2,1,0:T(8,128)S(1)}, u32[]{:S(2)}, u32[]{:S(2)}) collective-permute-start(f32[1,2,2,8,192]{4,3,2,1,0:T(8,128)S(1)} %get-tuple-element.95), channel_id=1, source_target_pairs={{0,452},{32,484},{452,0},{484,32},{8,460},{40,492},{460,8},{492,40... | collective-permute-start | bytes 73736 | tf_op jit(solution)/shard_map/ppermute | solution.py:70
  47.9 3.4 %collective-permute-start.10 = (f32[1,2,2,8,192]{4,3,2,1,0:T(8,128)S(1)}, f32[1,2,2,8,192]{4,3,2,1,0:T(8,128)S(1)}, u32[]{:S(2)}, u32[]{:S(2)}) collective-permute-start(f32[1,2,2,8,192]{4,3,2,1,0:T(8,128)S(1)} %get-tuple-element.96), channel_id=1, source_target_pairs={{64,0},{0,32},{128,64},{32,96},{192,128},{96,160},{256,192},{160,2... | collective-permute-start | bytes 73736 | tf_op jit(solution)/shard_map/ppermute | solution.py:70
  47.9 3.3 %collective-permute-start.9 = (f32[1,2,2,8,192]{4,3,2,1,0:T(8,128)S(1)}, f32[1,2,2,8,192]{4,3,2,1,0:T(8,128)S(1)}, u32[]{:S(2)}, u32[]{:S(2)}) collective-permute-start(f32[1,2,2,8,192]{4,3,2,1,0:T(8,128)S(1)} %get-tuple-element.97), channel_id=1, source_target_pairs={{0,64},{32,0},{64,128},{96,32},{128,192},{160,96},{192,256},{224,1... | collective-permute-start | bytes 73736 | tf_op jit(solution)/shard_map/ppermute | solution.py:70
  51.3 4.2 %collective-permute-start.14 = (f32[4,1,2,8,192]{4,3,2,1,0:T(8,128)S(1)}, f32[4,1,2,8,192]{4,3,2,1,0:T(8,128)S(1)}, u32[]{:S(2)}, u32[]{:S(2)}) collective-permute-start(f32[4,1,2,8,192]{4,3,2,1,0:T(8,128)S(1)} %get-tuple-element.79), channel_id=1, source_target_pairs={{0,24},{32,56},{64,88},{96,120},{128,152},{160,184},{192,216},{224... | collective-permute-start | bytes 147464 | tf_op jit(solution)/shard_map/ppermute | solution.py:70
  51.9 5.1 %collective-permute-start.12 = (f32[4,1,2,8,192]{4,3,2,1,0:T(8,128)S(1)}, f32[4,1,2,8,192]{4,3,2,1,0:T(8,128)S(1)}, u32[]{:S(2)}, u32[]{:S(2)}) collective-permute-start(f32[4,1,2,8,192]{4,3,2,1,0:T(8,128)S(1)} %get-tuple-element.80), channel_id=1, source_target_pairs={{0,8},{32,0},{64,72},{96,64},{128,136},{160,128},{192,200},{224,19... | collective-permute-start | bytes 147464 | tf_op jit(solution)/shard_map/ppermute | solution.py:70
  52.0 6.0 %collective-permute-start.13 = (f32[4,1,2,8,192]{4,3,2,1,0:T(8,128)S(1)}, f32[4,1,2,8,192]{4,3,2,1,0:T(8,128)S(1)}, u32[]{:S(2)}, u32[]{:S(2)}) collective-permute-start(f32[4,1,2,8,192]{4,3,2,1,0:T(8,128)S(1)} %get-tuple-element.81), channel_id=1, source_target_pairs={{8,0},{0,32},{72,64},{64,96},{136,128},{128,160},{200,192},{192,22... | collective-permute-start | bytes 147464 | tf_op jit(solution)/shard_map/ppermute | solution.py:70
  58.1 5.3 %copy-start = (f32[192,128]{1,0:T(8,128)S(1)}, f32[192,128]{1,0:T(8,128)}, u32[]{:S(2)}) copy-start(f32[192,128]{1,0:T(8,128)} %wm_ref.5) | copy-start | bytes 294916
  58.1 8.1 %collective-permute-start.16 = (f32[4,4,8,192]{3,2,1,0:T(8,128)S(1)}, f32[4,4,8,192]{3,2,1,0:T(8,128)S(1)}, u32[]{:S(2)}, u32[]{:S(2)}) collective-permute-start(f32[4,4,8,192]{3,2,1,0:T(8,128)S(1)} %get-tuple-element.67), channel_id=1, source_target_pairs={{33,1},{2,33},{34,2},{3,34},{35,3},{0,35},{32,0},{1,32},{41,9},{10... | collective-permute-start | bytes 294920 | tf_op jit(solution)/shard_map/ppermute | solution.py:70
  61.5 1.8 %copy-start.6 = (f32[128]{0:T(128)S(1)}, f32[128]{0:T(128)}, u32[]{:S(2)}) copy-start(f32[128]{0:T(128)} %param.25) | copy-start | bytes 1540
  61.5 4.7 %collective-permute-start.15 = (f32[4,4,8,192]{3,2,1,0:T(8,128)S(1)}, f32[4,4,8,192]{3,2,1,0:T(8,128)S(1)}, u32[]{:S(2)}, u32[]{:S(2)}) collective-permute-start(f32[4,4,8,192]{3,2,1,0:T(8,128)S(1)} %get-tuple-element.68), channel_id=1, source_target_pairs={{1,33},{33,2},{2,34},{34,3},{3,35},{35,0},{0,32},{32,1},{9,41},{41... | collective-permute-start | bytes 294920 | tf_op jit(solution)/shard_map/ppermute | solution.py:70
  68.0 3.7 %collective-permute-start.17 = (f32[4,4,8,192]{3,2,1,0:T(8,128)S(1)}, f32[4,4,8,192]{3,2,1,0:T(8,128)S(1)}, u32[]{:S(2)}, u32[]{:S(2)}) collective-permute-start(f32[4,4,8,192]{3,2,1,0:T(8,128)S(1)} %bitcast.60), channel_id=1, source_target_pairs={{1,33},{33,2},{2,34},{34,3},{3,35},{35,0},{0,32},{32,1},{9,41},{41... | collective-permute-start | bytes 294920 | tf_op jit(solution)/shard_map/ppermute | solution.py:70
  69.5 4.7 %collective-permute-start.18 = (f32[4,4,8,192]{3,2,1,0:T(8,128)S(1)}, f32[4,4,8,192]{3,2,1,0:T(8,128)S(1)}, u32[]{:S(2)}, u32[]{:S(2)}) collective-permute-start(f32[4,4,8,192]{3,2,1,0:T(8,128)S(1)} %bitcast.59), channel_id=1, source_target_pairs={{33,1},{2,33},{34,2},{3,34},{35,3},{0,35},{32,0},{1,32},{41,9},{10... | collective-permute-start | bytes 294920 | tf_op jit(solution)/shard_map/ppermute | solution.py:70
  74.2 6.2 %collective-permute-start.21 = (f32[1,4,2,8,192]{4,3,2,1,0:T(8,128)S(1)}, f32[1,4,2,8,192]{4,3,2,1,0:T(8,128)S(1)}, u32[]{:S(2)}, u32[]{:S(2)}) collective-permute-start(f32[1,4,2,8,192]{4,3,2,1,0:T(8,128)S(1)} %get-tuple-element.64), channel_id=1, source_target_pairs={{0,452},{32,484},{452,0},{484,32},{8,460},{40,492},{460,8},{492,40... | collective-permute-start | bytes 147464 | tf_op jit(solution)/shard_map/ppermute | solution.py:70
  77.7 3.4 %collective-permute-start.19 = (f32[1,4,2,8,192]{4,3,2,1,0:T(8,128)S(1)}, f32[1,4,2,8,192]{4,3,2,1,0:T(8,128)S(1)}, u32[]{:S(2)}, u32[]{:S(2)}) collective-permute-start(f32[1,4,2,8,192]{4,3,2,1,0:T(8,128)S(1)} %get-tuple-element.65), channel_id=1, source_target_pairs={{0,64},{32,0},{64,128},{96,32},{128,192},{160,96},{192,256},{224,1... | collective-permute-start | bytes 147464 | tf_op jit(solution)/shard_map/ppermute | solution.py:70
  78.1 3.1 %collective-permute-start.20 = (f32[1,4,2,8,192]{4,3,2,1,0:T(8,128)S(1)}, f32[1,4,2,8,192]{4,3,2,1,0:T(8,128)S(1)}, u32[]{:S(2)}, u32[]{:S(2)}) collective-permute-start(f32[1,4,2,8,192]{4,3,2,1,0:T(8,128)S(1)} %get-tuple-element.66), channel_id=1, source_target_pairs={{64,0},{0,32},{128,64},{32,96},{192,128},{96,160},{256,192},{160,2... | collective-permute-start | bytes 147464 | tf_op jit(solution)/shard_map/ppermute | solution.py:70
  81.2 2.6 %collective-permute-start.24 = (f32[2,1,2,8,192]{4,3,2,1,0:T(8,128)S(1)}, f32[2,1,2,8,192]{4,3,2,1,0:T(8,128)S(1)}, u32[]{:S(2)}, u32[]{:S(2)}) collective-permute-start(f32[2,1,2,8,192]{4,3,2,1,0:T(8,128)S(1)} %get-tuple-element.76), channel_id=1, source_target_pairs={{0,24},{32,56},{64,88},{96,120},{128,152},{160,184},{192,216},{224... | collective-permute-start | bytes 73736 | tf_op jit(solution)/shard_map/ppermute | solution.py:70
  81.9 3.2 %collective-permute-start.22 = (f32[2,1,2,8,192]{4,3,2,1,0:T(8,128)S(1)}, f32[2,1,2,8,192]{4,3,2,1,0:T(8,128)S(1)}, u32[]{:S(2)}, u32[]{:S(2)}) collective-permute-start(f32[2,1,2,8,192]{4,3,2,1,0:T(8,128)S(1)} %get-tuple-element.77), channel_id=1, source_target_pairs={{0,8},{32,0},{64,72},{96,64},{128,136},{160,128},{192,200},{224,19... | collective-permute-start | bytes 73736 | tf_op jit(solution)/shard_map/ppermute | solution.py:70
  81.9 4.8 %collective-permute-start.23 = (f32[2,1,2,8,192]{4,3,2,1,0:T(8,128)S(1)}, f32[2,1,2,8,192]{4,3,2,1,0:T(8,128)S(1)}, u32[]{:S(2)}, u32[]{:S(2)}) collective-permute-start(f32[2,1,2,8,192]{4,3,2,1,0:T(8,128)S(1)} %get-tuple-element.78), channel_id=1, source_target_pairs={{8,0},{0,32},{72,64},{64,96},{136,128},{128,160},{200,192},{192,22... | collective-permute-start | bytes 73736 | tf_op jit(solution)/shard_map/ppermute | solution.py:70
  87.8 4.1 %collective-permute-start.25 = (f32[4,4,8,128]{3,2,1,0:T(8,128)S(1)}, f32[4,4,8,128]{3,2,1,0:T(8,128)S(1)}, u32[]{:S(2)}, u32[]{:S(2)}) collective-permute-start(f32[4,4,8,128]{3,2,1,0:T(8,128)S(1)} %bitcast.62), channel_id=1, source_target_pairs={{1,33},{33,2},{2,34},{34,3},{3,35},{35,0},{0,32},{32,1},{9,41},{41... | collective-permute-start | bytes 196616 | tf_op jit(solution)/shard_map/ppermute | solution.py:70
  90.6 3.7 %collective-permute-start.26 = (f32[4,4,8,128]{3,2,1,0:T(8,128)S(1)}, f32[4,4,8,128]{3,2,1,0:T(8,128)S(1)}, u32[]{:S(2)}, u32[]{:S(2)}) collective-permute-start(f32[4,4,8,128]{3,2,1,0:T(8,128)S(1)} %bitcast.61), channel_id=1, source_target_pairs={{33,1},{2,33},{34,2},{3,34},{35,3},{0,35},{32,0},{1,32},{41,9},{10... | collective-permute-start | bytes 196616 | tf_op jit(solution)/shard_map/ppermute | solution.py:70
  94.3 5.9 %collective-permute-start.29 = (f32[1,4,2,8,128]{4,3,2,1,0:T(8,128)S(1)}, f32[1,4,2,8,128]{4,3,2,1,0:T(8,128)S(1)}, u32[]{:S(2)}, u32[]{:S(2)}) collective-permute-start(f32[1,4,2,8,128]{4,3,2,1,0:T(8,128)S(1)} %get-tuple-element.73), channel_id=1, source_target_pairs={{0,452},{32,484},{452,0},{484,32},{8,460},{40,492},{460,8},{492,40... | collective-permute-start | bytes 98312 | tf_op jit(solution)/shard_map/ppermute | solution.py:70
  97.4 3.5 %collective-permute-start.27 = (f32[1,4,2,8,128]{4,3,2,1,0:T(8,128)S(1)}, f32[1,4,2,8,128]{4,3,2,1,0:T(8,128)S(1)}, u32[]{:S(2)}, u32[]{:S(2)}) collective-permute-start(f32[1,4,2,8,128]{4,3,2,1,0:T(8,128)S(1)} %get-tuple-element.74), channel_id=1, source_target_pairs={{0,64},{32,0},{64,128},{96,32},{128,192},{160,96},{192,256},{224,1... | collective-permute-start | bytes 98312 | tf_op jit(solution)/shard_map/ppermute | solution.py:70
  100.0 1.2 %collective-permute-start.28 = (f32[1,4,2,8,128]{4,3,2,1,0:T(8,128)S(1)}, f32[1,4,2,8,128]{4,3,2,1,0:T(8,128)S(1)}, u32[]{:S(2)}, u32[]{:S(2)}) collective-permute-start(f32[1,4,2,8,128]{4,3,2,1,0:T(8,128)S(1)} %get-tuple-element.75), channel_id=1, source_target_pairs={{64,0},{0,32},{128,64},{32,96},{192,128},{96,160},{256,192},{160,2... | collective-permute-start | bytes 98312 | tf_op jit(solution)/shard_map/ppermute | solution.py:70
  101.3 2.7 %collective-permute-start.32 = (f32[2,1,2,8,128]{4,3,2,1,0:T(8,128)S(1)}, f32[2,1,2,8,128]{4,3,2,1,0:T(8,128)S(1)}, u32[]{:S(2)}, u32[]{:S(2)}) collective-permute-start(f32[2,1,2,8,128]{4,3,2,1,0:T(8,128)S(1)} %get-tuple-element.92), channel_id=1, source_target_pairs={{0,24},{32,56},{64,88},{96,120},{128,152},{160,184},{192,216},{224... | collective-permute-start | bytes 49160 | tf_op jit(solution)/shard_map/ppermute | solution.py:70
  102.0 3.2 %collective-permute-start.30 = (f32[2,1,2,8,128]{4,3,2,1,0:T(8,128)S(1)}, f32[2,1,2,8,128]{4,3,2,1,0:T(8,128)S(1)}, u32[]{:S(2)}, u32[]{:S(2)}) collective-permute-start(f32[2,1,2,8,128]{4,3,2,1,0:T(8,128)S(1)} %get-tuple-element.93), channel_id=1, source_target_pairs={{0,8},{32,0},{64,72},{96,64},{128,136},{160,128},{192,200},{224,19... | collective-permute-start | bytes 49160 | tf_op jit(solution)/shard_map/ppermute | solution.py:70
  102.0 4.2 %collective-permute-start.31 = (f32[2,1,2,8,128]{4,3,2,1,0:T(8,128)S(1)}, f32[2,1,2,8,128]{4,3,2,1,0:T(8,128)S(1)}, u32[]{:S(2)}, u32[]{:S(2)}) collective-permute-start(f32[2,1,2,8,128]{4,3,2,1,0:T(8,128)S(1)} %get-tuple-element.94), channel_id=1, source_target_pairs={{8,0},{0,32},{72,64},{64,96},{136,128},{128,160},{200,192},{192,22... | collective-permute-start | bytes 49160 | tf_op jit(solution)/shard_map/ppermute | solution.py:70
  106.4 10.8 %collective-permute-start.33 = (f32[16,128]{1,0:T(8,128)S(1)}, f32[16,128]{1,0:T(8,128)S(1)}, u32[]{:S(2)}, u32[]{:S(2)}) collective-permute-start(f32[16,128]{1,0:T(8,128)S(1)} %k_force.1), channel_id=1, source_target_pairs={{1,0},{33,1},{2,2},{34,3},{3,4},{35,5},{0,6},{32,7},{9,8},{41,9},{... | collective-permute-start | bytes 24584 | tf_op jit(solution)/shard_map/ppermute | solution.py:70

commit v13 on v10

--- a/solution.py
+++ b/solution.py
@@ -86,14 +86,16 @@
     return before, after
 
 
-def spread(low, high, here):
+def spread(low, high, here, beside=()):
     before, after = swap(0, low, high, here)
     cells = jnp.concatenate([before, low, high, after], axis=0)
+    if beside:
+        cells, *beside = lax.optimization_barrier((cells, *beside))
     before, after = swap(1, cells[:, 0:1], cells[:, 1:2], here)
     cells = jnp.concatenate([before, cells, after], axis=1)
     before = send(cells[:, :, 1], UP)
     after = send(cells[:, :, 0], DOWN)
-    return before, after, cells
+    return (before, after, cells), beside
 
 
 def collect(before, after, cells, here, beside):
@@ -550,7 +552,8 @@
     low, high, column = call(k_lists, [(32, 128), (32, 128), (LIST, 8)], packed)
     (part,) = call(k_own_pairs, [(8, PAIRS)], packed)
     low, high = low.reshape(1, 2, 2, 8, 128), high.reshape(1, 2, 2, 8, 128)
-    ghosts = [g.reshape(-1, 128) for g in spread(low, high, here)]
+    ghosts, (part,) = spread(low, high, here, (part,))
+    ghosts = [g.reshape(-1, 128) for g in ghosts]
     low, high, scal, pre, av = call(
         k_features,
         [(32, 192), (32, 192), (8, PAIRS), (128, PAIRS), (128, PAIRS)],
@@ -575,7 +578,7 @@
         w_mix,
     )
     low, high = low.reshape(1, 2, 2, 8, 192), high.reshape(1, 2, 2, 8, 192)
-    ghosts = [g.reshape(-1, 192) for g in spread(low, high, here)]
+    ghosts = [g.reshape(-1, 192) for g in spread(low, high, here)[0]]
     before, after, cells, ej, h, tbar = call(
         k_energy,
         [(128, 192), (128, 192), (256, 192), (192, PAIRS), (128, PAIRS), (CHAN, PAIRS)],

time: 117 us -> 118 us (level)
  no operation moved by 1% of the time
where the time goes in v13:
time: 118 us
  starting transfers between devices  68 us (58%)
  waiting for transfers between devices  35.3 us (30%)
  Pallas kernels  12 us (10%)
    ppermute x34, starting transfers between devices, send(): return lax.ppermute(x, AXES, pairs)  68 us
    ppermute x34, waiting for transfers between devices, send(): return lax.ppermute(x, AXES, pairs)  35.3 us
    pallas_call x10, Pallas kernels, call(): pl.pallas_call(kernel, out_shape=shapes, in_specs=[spec] * len(args), out...  10.4 us
  transfers between devices with their start and end apart: 34, of which 21 were waited for; matrix products, arithmetic and copies ran while one was open for 0% of the time, Pallas kernels for 5%

profile of v13, /device:TPU:33, one launch (start us, length us, event | category | flops | bytes accessed | tf_op | source)
XLA Modules:
  0.0 117.5 jit_solution(7929030980917720220)
XLA Ops:
  0.6 1.5 %k_pack.1 = f32[48,128]{1,0:T(8,128)} custom-call(f32[3,1,1,1,512]{4,3,2,1,0:T(1,128)} %pos_in.1, s32[1,1,1,512]{3,2,1,0:T(1,128)} %kind_in.1, s32[2,2,2,8]{3,2,1,0:T(2,128)} %names_in.1, s32[1,1,1,8,128]{4,3,2,1,0:T(8,128)} %center_in.1, s32[1,1,1,8,128]{4,3,2,1,0:T(8,128)} %partner_in.1, s32[1,1,1,8,128]{4,3,2,1,0:T(8,128)} %live_in.1), custom_call_target="tpu_custom_call" | custom-call | tf_op jit(solution)/shard_map/k_pack/pallas_call | solution.py:255
  2.1 6.4 %collective-permute-start = (f32[48,128]{1,0:T(8,128)}, f32[48,128]{1,0:T(8,128)S(1)}, u32[]{:S(2)}, u32[]{:S(2)}) collective-permute-start(f32[48,128]{1,0:T(8,128)} %k_pack.1), channel_id=1, source_target_pairs={{0,1},{1,33},{2,2},{3,34},{4,3},{5,35},{6,0},{7,32},{8,9},{9,41},{... | collective-permute-start | bytes 73736 | tf_op jit(solution)/shard_map/ppermute | solution.py:70
  8.6 11.6 %collective-permute-done.packed_ref = f32[48,128]{1,0:T(8,128)S(1)} collective-permute-done((f32[48,128]{1,0:T(8,128)}, f32[48,128]{1,0:T(8,128)S(1)}, u32[]{:S(2)}, u32[]{:S(2)}) %collective-permute-start) | collective-permute-done | bytes 24608 | tf_op jit(solution)/shard_map/ppermute | solution.py:70
  20.4 0.7 collective-permute-start.3
  21.1 1.6 %collective-permute-start.2 = (f32[1,2,2,8,128]{4,3,2,1,0:T(8,128)S(1)}, f32[1,2,2,8,128]{4,3,2,1,0:T(8,128)S(1)}, u32[]{:S(2)}, u32[]{:S(2)}) collective-permute-start(f32[1,2,2,8,128]{4,3,2,1,0:T(8,128)S(1)} %get-tuple-element.110), channel_id=1, source_target_pairs={{64,0},{0,32},{128,64},{32,96},{192,128},{96,160},{256,192},{160,2... | collective-permute-start | bytes 49160 | tf_op jit(solution)/shard_map/ppermute | solution.py:70
  22.7 1.4 %collective-permute-start.1 = (f32[1,2,2,8,128]{4,3,2,1,0:T(8,128)S(1)}, f32[1,2,2,8,128]{4,3,2,1,0:T(8,128)S(1)}, u32[]{:S(2)}, u32[]{:S(2)}) collective-permute-start(f32[1,2,2,8,128]{4,3,2,1,0:T(8,128)S(1)} %get-tuple-element.111), channel_id=1, source_target_pairs={{0,64},{32,0},{64,128},{96,32},{128,192},{160,96},{192,256},{224,1... | collective-permute-start | bytes 49160 | tf_op jit(solution)/shard_map/ppermute | solution.py:70
  24.5 0.7 collective-permute-done.2
  25.3 4.9 %collective-permute-start.6 = (f32[4,1,2,8,128]{4,3,2,1,0:T(8,128)S(1)}, f32[4,1,2,8,128]{4,3,2,1,0:T(8,128)S(1)}, u32[]{:S(2)}, u32[]{:S(2)}) collective-permute-start(f32[4,1,2,8,128]{4,3,2,1,0:T(8,128)S(1)} %get-tuple-element.102), channel_id=1, source_target_pairs={{0,24},{32,56},{64,88},{96,120},{128,152},{160,184},{192,216},{224... | collective-permute-start | bytes 98312 | tf_op jit(solution)/shard_map/ppermute | solution.py:70
  30.2 3.8 %collective-permute-start.4 = (f32[4,1,2,8,128]{4,3,2,1,0:T(8,128)S(1)}, f32[4,1,2,8,128]{4,3,2,1,0:T(8,128)S(1)}, u32[]{:S(2)}, u32[]{:S(2)}) collective-permute-start(f32[4,1,2,8,128]{4,3,2,1,0:T(8,128)S(1)} %get-tuple-element.103), channel_id=1, source_target_pairs={{0,8},{32,0},{64,72},{96,64},{128,136},{160,128},{192,200},{224,19... | collective-permute-start | bytes 98312 | tf_op jit(solution)/shard_map/ppermute | solution.py:70
  34.1 0.9 collective-permute-done.4
  35.4 3.1 %collective-permute-start.8 = (f32[4,4,8,128]{3,2,1,0:T(8,128)S(1)}, f32[4,4,8,128]{3,2,1,0:T(8,128)S(1)}, u32[]{:S(2)}, u32[]{:S(2)}) collective-permute-start(f32[4,4,8,128]{3,2,1,0:T(8,128)S(1)} %get-tuple-element.86), channel_id=1, source_target_pairs={{33,1},{2,33},{34,2},{3,34},{35,3},{0,35},{32,0},{1,32},{41,9},{10... | collective-permute-start | bytes 196616 | tf_op jit(solution)/shard_map/ppermute | solution.py:70
  38.5 5.0 %collective-permute-start.7 = (f32[4,4,8,128]{3,2,1,0:T(8,128)S(1)}, f32[4,4,8,128]{3,2,1,0:T(8,128)S(1)}, u32[]{:S(2)}, u32[]{:S(2)}) collective-permute-start(f32[4,4,8,128]{3,2,1,0:T(8,128)S(1)} %get-tuple-element.87), channel_id=1, source_target_pairs={{1,33},{33,2},{2,34},{34,3},{3,35},{35,0},{0,32},{32,1},{9,41},{41... | collective-permute-start | bytes 196616 | tf_op jit(solution)/shard_map/ppermute | solution.py:70
  43.5 1.9 %collective-permute-done.8 = f32[4,4,8,128]{3,2,1,0:T(8,128)S(1)} collective-permute-done((f32[4,4,8,128]{3,2,1,0:T(8,128)S(1)}, f32[4,4,8,128]{3,2,1,0:T(8,128)S(1)}, u32[]{:S(2)}, u32[]{:S(2)}) %collective-permute-start.8) | collective-permute-done | bytes 65568 | tf_op jit(solution)/shard_map/ppermute | solution.py:70
  46.1 1.2 %k_features.1 = (f32[32,192]{1,0:T(8,128)S(1)}, f32[32,192]{1,0:T(8,128)S(1)}, f32[8,1024]{1,0:T(8,128)S(1)}, f32[128,1024]{1,0:T(8,128)S(1)}, f32[128,1024]{1,0:T(8,128)S(1)}) custom-call(f32[48,128]{1,0:T(8,128)S(1)} %collective-permute-done.packed_ref, f32[8,1024]{1,0:T(8,128)S(1)} %k_own_pairs.1.part_ref, f32[128,128]{1,0:T(8,128)S(1)} %bitcast.52, ...), custom_call_target="tpu_custom_call" | custom-call | tf_op jit(solution)/shard_map/k_features/pallas_call | solution.py:521
  47.4 0.7 collective-permute-start.11
  48.1 1.9 %collective-permute-start.9 = (f32[1,2,2,8,192]{4,3,2,1,0:T(8,128)S(1)}, f32[1,2,2,8,192]{4,3,2,1,0:T(8,128)S(1)}, u32[]{:S(2)}, u32[]{:S(2)}) collective-permute-start(f32[1,2,2,8,192]{4,3,2,1,0:T(8,128)S(1)} %get-tuple-element.101), channel_id=1, source_target_pairs={{0,64},{32,0},{64,128},{96,32},{128,192},{160,96},{192,256},{224,1... | collective-permute-start | bytes 73736 | tf_op jit(solution)/shard_map/ppermute | solution.py:70
  49.9 1.3 %collective-permute-done.10 = f32[1,2,2,8,192]{4,3,2,1,0:T(8,128)S(1)} collective-permute-done((f32[1,2,2,8,192]{4,3,2,1,0:T(8,128)S(1)}, f32[1,2,2,8,192]{4,3,2,1,0:T(8,128)S(1)}, u32[]{:S(2)}, u32[]{:S(2)}) %collective-permute-start.10) | collective-permute-done | bytes 24608 | tf_op jit(solution)/shard_map/ppermute | solution.py:70
  51.3 3.1 %collective-permute-start.14 = (f32[4,1,2,8,192]{4,3,2,1,0:T(8,128)S(1)}, f32[4,1,2,8,192]{4,3,2,1,0:T(8,128)S(1)}, u32[]{:S(2)}, u32[]{:S(2)}) collective-permute-start(f32[4,1,2,8,192]{4,3,2,1,0:T(8,128)S(1)} %get-tuple-element.83), channel_id=1, source_target_pairs={{0,24},{32,56},{64,88},{96,120},{128,152},{160,184},{192,216},{224... | collective-permute-start | bytes 147464 | tf_op jit(solution)/shard_map/ppermute | solution.py:70
  54.4 4.1 %collective-permute-start.12 = (f32[4,1,2,8,192]{4,3,2,1,0:T(8,128)S(1)}, f32[4,1,2,8,192]{4,3,2,1,0:T(8,128)S(1)}, u32[]{:S(2)}, u32[]{:S(2)}) collective-permute-start(f32[4,1,2,8,192]{4,3,2,1,0:T(8,128)S(1)} %get-tuple-element.84), channel_id=1, source_target_pairs={{0,8},{32,0},{64,72},{96,64},{128,136},{160,128},{192,200},{224,19... | collective-permute-start | bytes 147464 | tf_op jit(solution)/shard_map/ppermute | solution.py:70
  58.5 0.9 collective-permute-done.12
  59.4 0.8 collective-permute-done.13
  60.3 2.6 %collective-permute-start.16 = (f32[4,4,8,192]{3,2,1,0:T(8,128)S(1)}, f32[4,4,8,192]{3,2,1,0:T(8,128)S(1)}, u32[]{:S(2)}, u32[]{:S(2)}) collective-permute-start(f32[4,4,8,192]{3,2,1,0:T(8,128)S(1)} %get-tuple-element.71), channel_id=1, source_target_pairs={{33,1},{2,33},{34,2},{3,34},{35,3},{0,35},{32,0},{1,32},{41,9},{10... | collective-permute-start | bytes 294920 | tf_op jit(solution)/shard_map/ppermute | solution.py:70
  62.9 0.8 collective-permute-start.15
  63.8 2.2 %k_own_env.1 = (f32[192,1024]{1,0:T(8,128)S(1)}, f32[192,1024]{1,0:T(8,128)S(1)}, f32[128,1024]{1,0:T(8,128)S(1)}, f32[128,1024]{1,0:T(8,128)S(1)}, f32[128,1024]{1,0:T(8,128)S(1)}, /*index=5*/f32[128,1024]{1,0:T(8,128)S(1)}) custom-call(f32[48,128]{1,0:T(8,128)S(1)} %collective-permute-done.packed_ref, f32[8,1024]{1,0:T(8,128)S(1)} %get-tuple-element.40.scal_ref, ...), custom_call_target="tpu_custom_call" | custom-call | tf_op jit(solution)/shard_map/k_own_env/pallas_call | solution.py:521
  66.3 1.8 %k_energy.1 = (f32[128,192]{1,0:T(8,128)S(1)}, f32[128,192]{1,0:T(8,128)S(1)}, f32[256,192]{1,0:T(8,128)S(1)}, f32[192,1024]{1,0:T(8,128)S(1)}, f32[128,1024]{1,0:T(8,128)S(1)}, /*index=5*/f32[64,1024]{1,0:T(8,128)S(1)}) custom-call(f32[48,128]{1,0:T(8,128)S(1)} %collective-permute-done.packed_ref, f32[8,1024]{1,0:T(8,128)S(1)} %get-tuple-element.40.scal_ref, ...), custom_call_target="tpu_custom_call" | custom-call | tf_op jit(solution)/shard_map/k_energy/pallas_call | solution.py:521
  68.1 1.8 %collective-permute-start.17 = (f32[4,4,8,192]{3,2,1,0:T(8,128)S(1)}, f32[4,4,8,192]{3,2,1,0:T(8,128)S(1)}, u32[]{:S(2)}, u32[]{:S(2)}) collective-permute-start(f32[4,4,8,192]{3,2,1,0:T(8,128)S(1)} %bitcast.58), channel_id=1, source_target_pairs={{1,33},{33,2},{2,34},{34,3},{3,35},{35,0},{0,32},{32,1},{9,41},{41... | collective-permute-start | bytes 294920 | tf_op jit(solution)/shard_map/ppermute | solution.py:70
  70.3 2.2 %k_direct.1 = (f32[8,1024]{1,0:T(8,128)S(1)}, f32[4,512]{1,0:T(4,128)S(1)}) custom-call(f32[48,128]{1,0:T(8,128)S(1)} %collective-permute-done.packed_ref, f32[8,1024]{1,0:T(8,128)S(1)} %get-tuple-element.40.scal_ref, f32[128,1024]{1,0:T(8,128)S(1)} %get-tuple-element.41.av_ref, f32[128,1024]{1,0:T(8,128)S(1)} %get-tuple-element.43.nav_ref, ...), custom_call_target="tpu_custom_call" | custom-call | tf_op jit(solution)/shard_map/k_direct/pallas_call | solution.py:521
  72.5 2.0 %collective-permute-done.18 = f32[4,4,8,192]{3,2,1,0:T(8,128)S(1)} collective-permute-done((f32[4,4,8,192]{3,2,1,0:T(8,128)S(1)}, f32[4,4,8,192]{3,2,1,0:T(8,128)S(1)}, u32[]{:S(2)}, u32[]{:S(2)}) %collective-permute-start.18) | collective-permute-done | bytes 98336 | tf_op jit(solution)/shard_map/ppermute | solution.py:70
  74.7 3.7 %collective-permute-start.21 = (f32[4,1,2,8,192]{4,3,2,1,0:T(8,128)S(1)}, f32[4,1,2,8,192]{4,3,2,1,0:T(8,128)S(1)}, u32[]{:S(2)}, u32[]{:S(2)}) collective-permute-start(f32[4,1,2,8,192]{4,3,2,1,0:T(8,128)S(1)} %get-tuple-element.68), channel_id=1, source_target_pairs={{0,24},{32,56},{64,88},{96,120},{128,152},{160,184},{192,216},{224... | collective-permute-start | bytes 147464 | tf_op jit(solution)/shard_map/ppermute | solution.py:70
  78.4 0.7 collective-permute-start.19
  79.1 0.8 collective-permute-start.20
  79.8 1.0 collective-permute-done.21
  81.6 0.7 collective-permute-start.24
  82.2 2.8 %collective-permute-start.22 = (f32[1,2,2,8,192]{4,3,2,1,0:T(8,128)S(1)}, f32[1,2,2,8,192]{4,3,2,1,0:T(8,128)S(1)}, u32[]{:S(2)}, u32[]{:S(2)}) collective-permute-start(f32[1,2,2,8,192]{4,3,2,1,0:T(8,128)S(1)} %get-tuple-element.81), channel_id=1, source_target_pairs={{0,64},{32,0},{64,128},{96,32},{128,192},{160,96},{192,256},{224,1... | collective-permute-start | bytes 73736 | tf_op jit(solution)/shard_map/ppermute | solution.py:70
  85.0 1.0 collective-permute-done.22
  86.1 2.2 %collective-permute-done.23 = f32[1,2,2,8,192]{4,3,2,1,0:T(8,128)S(1)} collective-permute-done((f32[1,2,2,8,192]{4,3,2,1,0:T(8,128)S(1)}, f32[1,2,2,8,192]{4,3,2,1,0:T(8,128)S(1)}, u32[]{:S(2)}, u32[]{:S(2)}) %collective-permute-start.23) | collective-permute-done | bytes 24608 | tf_op jit(solution)/shard_map/ppermute | solution.py:70
  88.3 1.0 k_env_back.1
  89.3 0.7 collective-permute-start.25
  90.7 0.7 collective-permute-done.25
  91.4 2.7 %collective-permute-done.26 = f32[4,4,8,128]{3,2,1,0:T(8,128)S(1)} collective-permute-done((f32[4,4,8,128]{3,2,1,0:T(8,128)S(1)}, f32[4,4,8,128]{3,2,1,0:T(8,128)S(1)}, u32[]{:S(2)}, u32[]{:S(2)}) %collective-permute-start.26) | collective-permute-done | bytes 65568 | tf_op jit(solution)/shard_map/ppermute | solution.py:70
  94.1 2.6 %collective-permute-start.29 = (f32[4,1,2,8,128]{4,3,2,1,0:T(8,128)S(1)}, f32[4,1,2,8,128]{4,3,2,1,0:T(8,128)S(1)}, u32[]{:S(2)}, u32[]{:S(2)}) collective-permute-start(f32[4,1,2,8,128]{4,3,2,1,0:T(8,128)S(1)} %get-tuple-element.77), channel_id=1, source_target_pairs={{0,24},{32,56},{64,88},{96,120},{128,152},{160,184},{192,216},{224... | collective-permute-start | bytes 98312 | tf_op jit(solution)/shard_map/ppermute | solution.py:70
  96.7 1.9 %collective-permute-start.27 = (f32[4,1,2,8,128]{4,3,2,1,0:T(8,128)S(1)}, f32[4,1,2,8,128]{4,3,2,1,0:T(8,128)S(1)}, u32[]{:S(2)}, u32[]{:S(2)}) collective-permute-start(f32[4,1,2,8,128]{4,3,2,1,0:T(8,128)S(1)} %get-tuple-element.78), channel_id=1, source_target_pairs={{0,8},{32,0},{64,72},{96,64},{128,136},{160,128},{192,200},{224,19... | collective-permute-start | bytes 98312 | tf_op jit(solution)/shard_map/ppermute | solution.py:70
  98.6 1.3 %collective-permute-done.29 = f32[4,1,2,8,128]{4,3,2,1,0:T(8,128)S(1)} collective-permute-done((f32[4,1,2,8,128]{4,3,2,1,0:T(8,128)S(1)}, f32[4,1,2,8,128]{4,3,2,1,0:T(8,128)S(1)}, u32[]{:S(2)}, u32[]{:S(2)}) %collective-permute-start.29) | collective-permute-done | bytes 32800 | tf_op jit(solution)/shard_map/ppermute | solution.py:70
  100.7 4.5 %collective-permute-start.30 = (f32[1,2,2,8,128]{4,3,2,1,0:T(8,128)S(1)}, f32[1,2,2,8,128]{4,3,2,1,0:T(8,128)S(1)}, u32[]{:S(2)}, u32[]{:S(2)}) collective-permute-start(f32[1,2,2,8,128]{4,3,2,1,0:T(8,128)S(1)} %get-tuple-element.97), channel_id=1, source_target_pairs={{0,64},{32,0},{64,128},{96,32},{128,192},{160,96},{192,256},{224,1... | collective-permute-start | bytes 49160 | tf_op jit(solution)/shard_map/ppermute | solution.py:70
  105.1 0.9 collective-permute-done.30
  106.0 3.3 %collective-permute-done.31 = f32[1,2,2,8,128]{4,3,2,1,0:T(8,128)S(1)} collective-permute-done((f32[1,2,2,8,128]{4,3,2,1,0:T(8,128)S(1)}, f32[1,2,2,8,128]{4,3,2,1,0:T(8,128)S(1)}, u32[]{:S(2)}, u32[]{:S(2)}) %collective-permute-start.31) | collective-permute-done | bytes 16416 | tf_op jit(solution)/shard_map/ppermute | solution.py:70
  109.5 6.6 %collective-permute-start.33 = (f32[16,128]{1,0:T(8,128)S(1)}, f32[16,128]{1,0:T(8,128)S(1)}, u32[]{:S(2)}, u32[]{:S(2)}) collective-permute-start(f32[16,128]{1,0:T(8,128)S(1)} %k_force.1), channel_id=1, source_target_pairs={{1,0},{33,1},{2,2},{34,3},{3,4},{35,5},{0,6},{32,7},{9,8},{41,9},{... | collective-permute-start | bytes 24584 | tf_op jit(solution)/shard_map/ppermute | solution.py:70
  116.2 0.8 collective-permute-done.33.in_ref
  (74 shorter events, 5.8 us)
Async XLA Ops:
  2.1 18.0 %collective-permute-start = (f32[48,128]{1,0:T(8,128)}, f32[48,128]{1,0:T(8,128)S(1)}, u32[]{:S(2)}, u32[]{:S(2)}) collective-permute-start(f32[48,128]{1,0:T(8,128)} %k_pack.1), channel_id=1, source_target_pairs={{0,1},{1,33},{2,2},{3,34},{4,3},{5,35},{6,0},{7,32},{8,9},{9,41},{... | collective-permute-start | bytes 73736 | tf_op jit(solution)/shard_map/ppermute | solution.py:70
  20.4 4.1 %collective-permute-start.3 = (f32[1,2,2,8,128]{4,3,2,1,0:T(8,128)S(1)}, f32[1,2,2,8,128]{4,3,2,1,0:T(8,128)S(1)}, u32[]{:S(2)}, u32[]{:S(2)}) collective-permute-start(f32[1,2,2,8,128]{4,3,2,1,0:T(8,128)S(1)} %get-tuple-element.109), channel_id=1, source_target_pairs={{0,452},{32,484},{452,0},{484,32},{8,460},{40,492},{460,8},{492,40... | collective-permute-start | bytes 49160 | tf_op jit(solution)/shard_map/ppermute | solution.py:70
  21.1 4.1 %collective-permute-start.2 = (f32[1,2,2,8,128]{4,3,2,1,0:T(8,128)S(1)}, f32[1,2,2,8,128]{4,3,2,1,0:T(8,128)S(1)}, u32[]{:S(2)}, u32[]{:S(2)}) collective-permute-start(f32[1,2,2,8,128]{4,3,2,1,0:T(8,128)S(1)} %get-tuple-element.110), channel_id=1, source_target_pairs={{64,0},{0,32},{128,64},{32,96},{192,128},{96,160},{256,192},{160,2... | collective-permute-start | bytes 49160 | tf_op jit(solution)/shard_map/ppermute | solution.py:70
  22.7 2.6 %collective-permute-start.1 = (f32[1,2,2,8,128]{4,3,2,1,0:T(8,128)S(1)}, f32[1,2,2,8,128]{4,3,2,1,0:T(8,128)S(1)}, u32[]{:S(2)}, u32[]{:S(2)}) collective-permute-start(f32[1,2,2,8,128]{4,3,2,1,0:T(8,128)S(1)} %get-tuple-element.111), channel_id=1, source_target_pairs={{0,64},{32,0},{64,128},{96,32},{128,192},{160,96},{192,256},{224,1... | collective-permute-start | bytes 49160 | tf_op jit(solution)/shard_map/ppermute | solution.py:70
  25.3 8.7 %collective-permute-start.6 = (f32[4,1,2,8,128]{4,3,2,1,0:T(8,128)S(1)}, f32[4,1,2,8,128]{4,3,2,1,0:T(8,128)S(1)}, u32[]{:S(2)}, u32[]{:S(2)}) collective-permute-start(f32[4,1,2,8,128]{4,3,2,1,0:T(8,128)S(1)} %get-tuple-element.102), channel_id=1, source_target_pairs={{0,24},{32,56},{64,88},{96,120},{128,152},{160,184},{192,216},{224... | collective-permute-start | bytes 98312 | tf_op jit(solution)/shard_map/ppermute | solution.py:70
  30.2 4.7 %collective-permute-start.4 = (f32[4,1,2,8,128]{4,3,2,1,0:T(8,128)S(1)}, f32[4,1,2,8,128]{4,3,2,1,0:T(8,128)S(1)}, u32[]{:S(2)}, u32[]{:S(2)}) collective-permute-start(f32[4,1,2,8,128]{4,3,2,1,0:T(8,128)S(1)} %get-tuple-element.103), channel_id=1, source_target_pairs={{0,8},{32,0},{64,72},{96,64},{128,136},{160,128},{192,200},{224,19... | collective-permute-start | bytes 98312 | tf_op jit(solution)/shard_map/ppermute | solution.py:70
  34.1 1.2 %collective-permute-start.5 = (f32[4,1,2,8,128]{4,3,2,1,0:T(8,128)S(1)}, f32[4,1,2,8,128]{4,3,2,1,0:T(8,128)S(1)}, u32[]{:S(2)}, u32[]{:S(2)}) collective-permute-start(f32[4,1,2,8,128]{4,3,2,1,0:T(8,128)S(1)} %get-tuple-element.104), channel_id=1, source_target_pairs={{8,0},{0,32},{72,64},{64,96},{136,128},{128,160},{200,192},{192,22... | collective-permute-start | bytes 98312 | tf_op jit(solution)/shard_map/ppermute | solution.py:70
  35.3 10.1 %copy-start.1 = (f32[128,64]{0,1:T(8,128)S(1)}, f32[128,64]{0,1:T(8,128)}, u32[]{:S(2)}) copy-start(f32[128,64]{0,1:T(8,128)} %param.22) | copy-start | bytes 98308
  35.3 10.1 %copy-start.2 = (f32[128,64]{0,1:T(8,128)S(1)}, f32[128,64]{0,1:T(8,128)}, u32[]{:S(2)}) copy-start(f32[128,64]{0,1:T(8,128)} %param.23) | copy-start | bytes 98308
  35.3 10.1 %copy-start.5 = (f32[6,128]{1,0:T(8,128)S(1)}, f32[6,128]{1,0:T(8,128)}, u32[]{:S(2)}) copy-start(f32[6,128]{1,0:T(8,128)} %ep_ref.1) | copy-start | bytes 9220
  35.4 10.1 %collective-permute-start.8 = (f32[4,4,8,128]{3,2,1,0:T(8,128)S(1)}, f32[4,4,8,128]{3,2,1,0:T(8,128)S(1)}, u32[]{:S(2)}, u32[]{:S(2)}) collective-permute-start(f32[4,4,8,128]{3,2,1,0:T(8,128)S(1)} %get-tuple-element.86), channel_id=1, source_target_pairs={{33,1},{2,33},{34,2},{3,34},{35,3},{0,35},{32,0},{1,32},{41,9},{10... | collective-permute-start | bytes 196616 | tf_op jit(solution)/shard_map/ppermute | solution.py:70
  38.5 6.9 %collective-permute-start.7 = (f32[4,4,8,128]{3,2,1,0:T(8,128)S(1)}, f32[4,4,8,128]{3,2,1,0:T(8,128)S(1)}, u32[]{:S(2)}, u32[]{:S(2)}) collective-permute-start(f32[4,4,8,128]{3,2,1,0:T(8,128)S(1)} %get-tuple-element.87), channel_id=1, source_target_pairs={{1,33},{33,2},{2,34},{34,3},{3,35},{35,0},{0,32},{32,1},{9,41},{41... | collective-permute-start | bytes 196616 | tf_op jit(solution)/shard_map/ppermute | solution.py:70
  45.4 0.7 copy-start.4
  45.4 0.7 copy-start.3
  47.4 2.6 %collective-permute-start.11 = (f32[1,2,2,8,192]{4,3,2,1,0:T(8,128)S(1)}, f32[1,2,2,8,192]{4,3,2,1,0:T(8,128)S(1)}, u32[]{:S(2)}, u32[]{:S(2)}) collective-permute-start(f32[1,2,2,8,192]{4,3,2,1,0:T(8,128)S(1)} %get-tuple-element.99), channel_id=1, source_target_pairs={{0,452},{32,484},{452,0},{484,32},{8,460},{40,492},{460,8},{492,40... | collective-permute-start | bytes 73736 | tf_op jit(solution)/shard_map/ppermute | solution.py:70
  48.0 3.2 %collective-permute-start.10 = (f32[1,2,2,8,192]{4,3,2,1,0:T(8,128)S(1)}, f32[1,2,2,8,192]{4,3,2,1,0:T(8,128)S(1)}, u32[]{:S(2)}, u32[]{:S(2)}) collective-permute-start(f32[1,2,2,8,192]{4,3,2,1,0:T(8,128)S(1)} %get-tuple-element.100), channel_id=1, source_target_pairs={{64,0},{0,32},{128,64},{32,96},{192,128},{96,160},{256,192},{160,2... | collective-permute-start | bytes 73736 | tf_op jit(solution)/shard_map/ppermute | solution.py:70
  48.1 3.2 %collective-permute-start.9 = (f32[1,2,2,8,192]{4,3,2,1,0:T(8,128)S(1)}, f32[1,2,2,8,192]{4,3,2,1,0:T(8,128)S(1)}, u32[]{:S(2)}, u32[]{:S(2)}) collective-permute-start(f32[1,2,2,8,192]{4,3,2,1,0:T(8,128)S(1)} %get-tuple-element.101), channel_id=1, source_target_pairs={{0,64},{32,0},{64,128},{96,32},{128,192},{160,96},{192,256},{224,1... | collective-permute-start | bytes 73736 | tf_op jit(solution)/shard_map/ppermute | solution.py:70
  51.3 7.2 %collective-permute-start.14 = (f32[4,1,2,8,192]{4,3,2,1,0:T(8,128)S(1)}, f32[4,1,2,8,192]{4,3,2,1,0:T(8,128)S(1)}, u32[]{:S(2)}, u32[]{:S(2)}) collective-permute-start(f32[4,1,2,8,192]{4,3,2,1,0:T(8,128)S(1)} %get-tuple-element.83), channel_id=1, source_target_pairs={{0,24},{32,56},{64,88},{96,120},{128,152},{160,184},{192,216},{224... | collective-permute-start | bytes 147464 | tf_op jit(solution)/shard_map/ppermute | solution.py:70
  54.4 5.0 %collective-permute-start.12 = (f32[4,1,2,8,192]{4,3,2,1,0:T(8,128)S(1)}, f32[4,1,2,8,192]{4,3,2,1,0:T(8,128)S(1)}, u32[]{:S(2)}, u32[]{:S(2)}) collective-permute-start(f32[4,1,2,8,192]{4,3,2,1,0:T(8,128)S(1)} %get-tuple-element.84), channel_id=1, source_target_pairs={{0,8},{32,0},{64,72},{96,64},{128,136},{160,128},{192,200},{224,19... | collective-permute-start | bytes 147464 | tf_op jit(solution)/shard_map/ppermute | solution.py:70
  58.5 1.7 %collective-permute-start.13 = (f32[4,1,2,8,192]{4,3,2,1,0:T(8,128)S(1)}, f32[4,1,2,8,192]{4,3,2,1,0:T(8,128)S(1)}, u32[]{:S(2)}, u32[]{:S(2)}) collective-permute-start(f32[4,1,2,8,192]{4,3,2,1,0:T(8,128)S(1)} %get-tuple-element.85), channel_id=1, source_target_pairs={{8,0},{0,32},{72,64},{64,96},{136,128},{128,160},{200,192},{192,22... | collective-permute-start | bytes 147464 | tf_op jit(solution)/shard_map/ppermute | solution.py:70
  60.3 3.6 %copy-start = (f32[192,128]{1,0:T(8,128)S(1)}, f32[192,128]{1,0:T(8,128)}, u32[]{:S(2)}) copy-start(f32[192,128]{1,0:T(8,128)} %wm_ref.5) | copy-start | bytes 294916
  60.3 6.0 %collective-permute-start.16 = (f32[4,4,8,192]{3,2,1,0:T(8,128)S(1)}, f32[4,4,8,192]{3,2,1,0:T(8,128)S(1)}, u32[]{:S(2)}, u32[]{:S(2)}) collective-permute-start(f32[4,4,8,192]{3,2,1,0:T(8,128)S(1)} %get-tuple-element.71), channel_id=1, source_target_pairs={{33,1},{2,33},{34,2},{3,34},{35,3},{0,35},{32,0},{1,32},{41,9},{10... | collective-permute-start | bytes 294920 | tf_op jit(solution)/shard_map/ppermute | solution.py:70
  62.9 0.8 copy-start.6
  62.9 3.4 %collective-permute-start.15 = (f32[4,4,8,192]{3,2,1,0:T(8,128)S(1)}, f32[4,4,8,192]{3,2,1,0:T(8,128)S(1)}, u32[]{:S(2)}, u32[]{:S(2)}) collective-permute-start(f32[4,4,8,192]{3,2,1,0:T(8,128)S(1)} %get-tuple-element.72), channel_id=1, source_target_pairs={{1,33},{33,2},{2,34},{34,3},{3,35},{35,0},{0,32},{32,1},{9,41},{41... | collective-permute-start | bytes 294920 | tf_op jit(solution)/shard_map/ppermute | solution.py:70
  68.1 4.4 %collective-permute-start.17 = (f32[4,4,8,192]{3,2,1,0:T(8,128)S(1)}, f32[4,4,8,192]{3,2,1,0:T(8,128)S(1)}, u32[]{:S(2)}, u32[]{:S(2)}) collective-permute-start(f32[4,4,8,192]{3,2,1,0:T(8,128)S(1)} %bitcast.58), channel_id=1, source_target_pairs={{1,33},{33,2},{2,34},{34,3},{3,35},{35,0},{0,32},{32,1},{9,41},{41... | collective-permute-start | bytes 294920 | tf_op jit(solution)/shard_map/ppermute | solution.py:70
  69.9 4.7 %collective-permute-start.18 = (f32[4,4,8,192]{3,2,1,0:T(8,128)S(1)}, f32[4,4,8,192]{3,2,1,0:T(8,128)S(1)}, u32[]{:S(2)}, u32[]{:S(2)}) collective-permute-start(f32[4,4,8,192]{3,2,1,0:T(8,128)S(1)} %bitcast.57), channel_id=1, source_target_pairs={{33,1},{2,33},{34,2},{3,34},{35,3},{0,35},{32,0},{1,32},{41,9},{10... | collective-permute-start | bytes 294920 | tf_op jit(solution)/shard_map/ppermute | solution.py:70
  74.7 6.2 %collective-permute-start.21 = (f32[4,1,2,8,192]{4,3,2,1,0:T(8,128)S(1)}, f32[4,1,2,8,192]{4,3,2,1,0:T(8,128)S(1)}, u32[]{:S(2)}, u32[]{:S(2)}) collective-permute-start(f32[4,1,2,8,192]{4,3,2,1,0:T(8,128)S(1)} %get-tuple-element.68), channel_id=1, source_target_pairs={{0,24},{32,56},{64,88},{96,120},{128,152},{160,184},{192,216},{224... | collective-permute-start | bytes 147464 | tf_op jit(solution)/shard_map/ppermute | solution.py:70
  78.4 3.1 %collective-permute-start.19 = (f32[4,1,2,8,192]{4,3,2,1,0:T(8,128)S(1)}, f32[4,1,2,8,192]{4,3,2,1,0:T(8,128)S(1)}, u32[]{:S(2)}, u32[]{:S(2)}) collective-permute-start(f32[4,1,2,8,192]{4,3,2,1,0:T(8,128)S(1)} %get-tuple-element.69), channel_id=1, source_target_pairs={{0,8},{32,0},{64,72},{96,64},{128,136},{160,128},{192,200},{224,19... | collective-permute-start | bytes 147464 | tf_op jit(solution)/shard_map/ppermute | solution.py:70
  79.1 2.4 %collective-permute-start.20 = (f32[4,1,2,8,192]{4,3,2,1,0:T(8,128)S(1)}, f32[4,1,2,8,192]{4,3,2,1,0:T(8,128)S(1)}, u32[]{:S(2)}, u32[]{:S(2)}) collective-permute-start(f32[4,1,2,8,192]{4,3,2,1,0:T(8,128)S(1)} %get-tuple-element.70), channel_id=1, source_target_pairs={{8,0},{0,32},{72,64},{64,96},{136,128},{128,160},{200,192},{192,22... | collective-permute-start | bytes 147464 | tf_op jit(solution)/shard_map/ppermute | solution.py:70
  81.6 3.5 %collective-permute-start.24 = (f32[1,2,2,8,192]{4,3,2,1,0:T(8,128)S(1)}, f32[1,2,2,8,192]{4,3,2,1,0:T(8,128)S(1)}, u32[]{:S(2)}, u32[]{:S(2)}) collective-permute-start(f32[1,2,2,8,192]{4,3,2,1,0:T(8,128)S(1)} %get-tuple-element.80), channel_id=1, source_target_pairs={{0,452},{32,484},{452,0},{484,32},{8,460},{40,492},{460,8},{492,40... | collective-permute-start | bytes 73736 | tf_op jit(solution)/shard_map/ppermute | solution.py:70
  82.2 3.8 %collective-permute-start.22 = (f32[1,2,2,8,192]{4,3,2,1,0:T(8,128)S(1)}, f32[1,2,2,8,192]{4,3,2,1,0:T(8,128)S(1)}, u32[]{:S(2)}, u32[]{:S(2)}) collective-permute-start(f32[1,2,2,8,192]{4,3,2,1,0:T(8,128)S(1)} %get-tuple-element.81), channel_id=1, source_target_pairs={{0,64},{32,0},{64,128},{96,32},{128,192},{160,96},{192,256},{224,1... | collective-permute-start | bytes 73736 | tf_op jit(solution)/shard_map/ppermute | solution.py:70
  85.0 3.3 %collective-permute-start.23 = (f32[1,2,2,8,192]{4,3,2,1,0:T(8,128)S(1)}, f32[1,2,2,8,192]{4,3,2,1,0:T(8,128)S(1)}, u32[]{:S(2)}, u32[]{:S(2)}) collective-permute-start(f32[1,2,2,8,192]{4,3,2,1,0:T(8,128)S(1)} %get-tuple-element.82), channel_id=1, source_target_pairs={{64,0},{0,32},{128,64},{32,96},{192,128},{96,160},{256,192},{160,2... | collective-permute-start | bytes 73736 | tf_op jit(solution)/shard_map/ppermute | solution.py:70
  89.3 2.1 %collective-permute-start.25 = (f32[4,4,8,128]{3,2,1,0:T(8,128)S(1)}, f32[4,4,8,128]{3,2,1,0:T(8,128)S(1)}, u32[]{:S(2)}, u32[]{:S(2)}) collective-permute-start(f32[4,4,8,128]{3,2,1,0:T(8,128)S(1)} %bitcast.60), channel_id=1, source_target_pairs={{1,33},{33,2},{2,34},{34,3},{3,35},{35,0},{0,32},{32,1},{9,41},{41... | collective-permute-start | bytes 196616 | tf_op jit(solution)/shard_map/ppermute | solution.py:70
  90.1 4.0 %collective-permute-start.26 = (f32[4,4,8,128]{3,2,1,0:T(8,128)S(1)}, f32[4,4,8,128]{3,2,1,0:T(8,128)S(1)}, u32[]{:S(2)}, u32[]{:S(2)}) collective-permute-start(f32[4,4,8,128]{3,2,1,0:T(8,128)S(1)} %bitcast.59), channel_id=1, source_target_pairs={{33,1},{2,33},{34,2},{3,34},{35,3},{0,35},{32,0},{1,32},{41,9},{10... | collective-permute-start | bytes 196616 | tf_op jit(solution)/shard_map/ppermute | solution.py:70
  94.1 5.9 %collective-permute-start.29 = (f32[4,1,2,8,128]{4,3,2,1,0:T(8,128)S(1)}, f32[4,1,2,8,128]{4,3,2,1,0:T(8,128)S(1)}, u32[]{:S(2)}, u32[]{:S(2)}) collective-permute-start(f32[4,1,2,8,128]{4,3,2,1,0:T(8,128)S(1)} %get-tuple-element.77), channel_id=1, source_target_pairs={{0,24},{32,56},{64,88},{96,120},{128,152},{160,184},{192,216},{224... | collective-permute-start | bytes 98312 | tf_op jit(solution)/shard_map/ppermute | solution.py:70
  96.7 3.3 %collective-permute-start.27 = (f32[4,1,2,8,128]{4,3,2,1,0:T(8,128)S(1)}, f32[4,1,2,8,128]{4,3,2,1,0:T(8,128)S(1)}, u32[]{:S(2)}, u32[]{:S(2)}) collective-permute-start(f32[4,1,2,8,128]{4,3,2,1,0:T(8,128)S(1)} %get-tuple-element.78), channel_id=1, source_target_pairs={{0,8},{32,0},{64,72},{96,64},{128,136},{160,128},{192,200},{224,19... | collective-permute-start | bytes 98312 | tf_op jit(solution)/shard_map/ppermute | solution.py:70
  98.6 1.4 %collective-permute-start.28 = (f32[4,1,2,8,128]{4,3,2,1,0:T(8,128)S(1)}, f32[4,1,2,8,128]{4,3,2,1,0:T(8,128)S(1)}, u32[]{:S(2)}, u32[]{:S(2)}) collective-permute-start(f32[4,1,2,8,128]{4,3,2,1,0:T(8,128)S(1)} %get-tuple-element.79), channel_id=1, source_target_pairs={{8,0},{0,32},{72,64},{64,96},{136,128},{128,160},{200,192},{192,22... | collective-permute-start | bytes 98312 | tf_op jit(solution)/shard_map/ppermute | solution.py:70
  100.0 5.1 %collective-permute-start.32 = (f32[1,2,2,8,128]{4,3,2,1,0:T(8,128)S(1)}, f32[1,2,2,8,128]{4,3,2,1,0:T(8,128)S(1)}, u32[]{:S(2)}, u32[]{:S(2)}) collective-permute-start(f32[1,2,2,8,128]{4,3,2,1,0:T(8,128)S(1)} %get-tuple-element.96), channel_id=1, source_target_pairs={{0,452},{32,484},{452,0},{484,32},{8,460},{40,492},{460,8},{492,40... | collective-permute-start | bytes 49160 | tf_op jit(solution)/shard_map/ppermute | solution.py:70
  100.7 5.3 %collective-permute-start.30 = (f32[1,2,2,8,128]{4,3,2,1,0:T(8,128)S(1)}, f32[1,2,2,8,128]{4,3,2,1,0:T(8,128)S(1)}, u32[]{:S(2)}, u32[]{:S(2)}) collective-permute-start(f32[1,2,2,8,128]{4,3,2,1,0:T(8,128)S(1)} %get-tuple-element.97), channel_id=1, source_target_pairs={{0,64},{32,0},{64,128},{96,32},{128,192},{160,96},{192,256},{224,1... | collective-permute-start | bytes 49160 | tf_op jit(solution)/shard_map/ppermute | solution.py:70
  105.1 4.1 %collective-permute-start.31 = (f32[1,2,2,8,128]{4,3,2,1,0:T(8,128)S(1)}, f32[1,2,2,8,128]{4,3,2,1,0:T(8,128)S(1)}, u32[]{:S(2)}, u32[]{:S(2)}) collective-permute-start(f32[1,2,2,8,128]{4,3,2,1,0:T(8,128)S(1)} %get-tuple-element.98), channel_id=1, source_target_pairs={{64,0},{0,32},{128,64},{32,96},{192,128},{96,160},{256,192},{160,2... | collective-permute-start | bytes 49160 | tf_op jit(solution)/shard_map/ppermute | solution.py:70
  109.5 7.4 %collective-permute-start.33 = (f32[16,128]{1,0:T(8,128)S(1)}, f32[16,128]{1,0:T(8,128)S(1)}, u32[]{:S(2)}, u32[]{:S(2)}) collective-permute-start(f32[16,128]{1,0:T(8,128)S(1)} %k_force.1), channel_id=1, source_target_pairs={{1,0},{33,1},{2,2},{34,3},{3,4},{35,5},{0,6},{32,7},{9,8},{41,9},{... | collective-permute-start | bytes 24584 | tf_op jit(solution)/shard_map/ppermute | solution.py:70
